TPU v7x, 32 devices: a whole 2x2x4 slice. The times are simulated.
32 devices in a mesh: dom: 8 (over z, x), tile: 4 (over y, core).
Axes of the slice: x: 2, y: 2, z: 4, core: 2. Of those that a mesh axis runs over, the one named last changes fastest.
Arguments:
- krylov_block: float32 [96, 32, 128], P('dom'), may hold values from -6 to 6
- diag_block: float32 [96, 128, 128], P(('dom', 'tile')), may hold values from -0.031819805 to 4.03182
- inverse_prev: float32 [96, 128, 128], P(('dom', 'tile')), may hold values from -0.01767767 to 0.951011
- coupling_tiles: float32 [96, 8, 128, 128], P('dom', 'tile'), may hold values from -0.14142136 to 0.14142136
- slot_kind: int32 [96, 8], P('dom', 'tile'), may hold values from 0 to 2, as said below
- slot_link: int32 [96, 8], P('dom', 'tile'), may hold values from 0 to 31, as said below
- send_slots: int32 [8, 4, 4, 4], P('dom', 'tile'), may hold values from 0 to 23, as said below
Outputs:
- inverse_new: float32 [96, 128, 128], P(('dom', 'tile'))
- applied: float32 [96, 32, 128], P('dom')
Inputs may be any that keep to these rules, and one draw needn't show every extreme that they name: `slot_kind`: every live slot has exactly one partner as stated, in the same tile group and in a partition at most two away; partners never lie outside the partitions 0 .. 7. `slot_link`: links of empty slots are 0. `send_slots`: entry [p, g, l, j] is a slot position of partition p in group g. Lists 0 and 1 name upper slots whose partners lie in partition p + 1 and p + 2, lists 2 and 3 lower slots whose partners lie in p - 1 and p - 2; the four lists and the partition's own pairs use distinct positions. Some list reaches 4 live entries in every draw.
All inputs are finite; a program needn't handle non-finite values.
Results may differ from a plain program's by a relative error of at most 0.0003.
Values sent between devices are 32-bit elements; how exact they have to be, the bound alone decides.
No kernel may reach another device: no remote copies, remote signals or barrier semaphores. Data moves between devices by JAX's collectives and lax.ppermute only.
A program may use at most 64 MiB of HBM per device.

v0:
```python
import jax
import jax.numpy as jnp
from jax import lax
from jax.sharding import PartitionSpec as P

FSWEEPS = 2
LSWEEPS = 3
USWEEPS = 3


precise = lax.Precision.HIGHEST


def passed_along(block, axis, distance):
    devices = range(lax.axis_size(axis))
    route = [(i - distance, i) for i in devices if i - distance in devices]
    return lax.ppermute(block, axis, route)


def newton_step(inverse, pivot):
    product = jnp.matmul(inverse, pivot, precision=precise)
    return 2.0 * inverse - jnp.matmul(product, inverse, precision=precise)


def apply_inverse(inverse, vectors):
    return jnp.einsum("rvj,rij->rvi", vectors, inverse, precision=precise)


def local(krylov_block, diag_block, inverse_prev, coupling_tiles, slot_kind, slot_link, send_slots):
    row_count = coupling_tiles.shape[0]
    slot_width = coupling_tiles.shape[1]
    block_size = coupling_tiles.shape[2]
    slot_total = row_count * slot_width
    capacity = send_slots.shape[3]
    partner = slot_link.reshape(slot_total)
    send_table = send_slots.reshape(4, capacity)
    send_rows = send_table // slot_width
    row_source = jnp.where(
        partner < slot_total, partner // slot_width, partner - slot_total + row_count
    )
    tiles_lower = coupling_tiles * (slot_kind == 1).astype(jnp.float32)[:, :, None, None]
    tiles_upper = coupling_tiles * (slot_kind == 2).astype(jnp.float32)[:, :, None, None]

    def spread(inverse_mine):
        return lax.all_gather(inverse_mine, "tile", axis=0, tiled=True)

    inverse_mine = inverse_prev
    inverse_all = spread(inverse_mine)
    for sweep_no in range(FSWEEPS):
        upper_products = jnp.einsum("rij,rwjk->rwik", inverse_all, tiles_upper, precision=precise)
        upper_products = upper_products.reshape(slot_total, block_size, block_size)
        near_out = upper_products[send_table[0]]
        far_out = upper_products[send_table[1]]
        pivot_near_in = passed_along(near_out, "dom", 1)
        pivot_far_in = passed_along(far_out, "dom", 2)
        pivot_lookup = jnp.concatenate([upper_products, pivot_near_in, pivot_far_in], 0)
        pivot_gathered = pivot_lookup[partner].reshape(
            row_count, slot_width, block_size, block_size
        )
        shares = lax.psum_scatter(
            jnp.einsum("rwij,rwjk->rik", tiles_lower, pivot_gathered, precision=precise),
            "tile",
            scatter_dimension=0,
            tiled=True,
        )
        inverse_mine = newton_step(inverse_mine, diag_block - shares)
        inverse_all = spread(inverse_mine)
    slot_shape = (row_count, slot_width) + krylov_block.shape[1:]
    lower_y = krylov_block
    for sweep_no in range(LSWEEPS):
        scaled = apply_inverse(inverse_all, lower_y)
        near_in = passed_along(scaled[send_rows[0]], "dom", 1)
        far_in = passed_along(scaled[send_rows[1]], "dom", 2)
        lookup = jnp.concatenate([scaled, near_in, far_in], 0)
        gathered = lookup[row_source].reshape(slot_shape)
        partial_value = jnp.einsum("rwvj,rwij->rvi", gathered, tiles_lower, precision=precise)
        lower_y = krylov_block - lax.psum(partial_value, "tile")
    solved = apply_inverse(inverse_all, lower_y)
    for sweep_no in range(USWEEPS):
        near_in = passed_along(solved[send_rows[2]], "dom", -1)
        far_in = passed_along(solved[send_rows[3]], "dom", -2)
        lookup = jnp.concatenate([solved, near_in, far_in], 0)
        gathered = lookup[row_source].reshape(slot_shape)
        partial_value = jnp.einsum("rwvj,rwij->rvi", gathered, tiles_upper, precision=precise)
        solved = apply_inverse(inverse_all, lower_y - lax.psum(partial_value, "tile"))
    return (inverse_mine, solved)


def solution(mesh):
    placed = (
        P("dom", None, None),
        P(("dom", "tile"), None, None),
        P(("dom", "tile"), None, None),
        P("dom", "tile", None, None),
        P("dom", "tile"),
        P("dom", "tile"),
        P("dom", "tile", None, None),
    )
    return jax.shard_map(
        local,
        mesh=mesh,
        in_specs=placed,
        out_specs=(P(("dom", "tile"), None, None), P("dom", None, None)),
        check_vma=False,
    )
```

profile of v0, /device:TPU:18, one launch (start us, length us, event | category | flops | bytes accessed | tf_op | source)
XLA Modules:
  0.0 429.7 jit_solution(3771218208445821040)
XLA Ops:
  8.0 8.8 %all_gather.9 = f32[12,128,128]{2,1,0:T(8,128)S(1)} all-gather(f32[3,128,128]{2,1,0:T(8,128)} %param.9), channel_id=1, replica_groups=mesh['dom'=8,'tile'=4] {'tile'}, dimensions={0}, use_global_device_ids=true | all-gather | bytes 983040 | tf_op jit(solution)/shard_map/all_gather | solution.py:45
  17.6 4.3 %fusion.8 = f32[12,2,128,128]{3,2,1,0:T(8,128)S(1)} fusion(f32[12,2,128,128]{3,2,1,0:T(8,128)} %param.10, f32[12,128,128]{2,1,0:T(8,128)S(1)} %all_gather.9, f32[12,2]{1,0:T(8,128)S(1)} %copy.20), kind=kOutput, calls=%fused_computation.36 | convolution fusion | flops 604372992 | bytes 3932256 | tf_op jit(solution)/shard_map/rij,rwjk->rwik/dot_general | solution.py:50
  22.5 3.5 collective-permute-start
  30.0 3.0 collective-permute-done
  33.0 5.6 %collective-permute-done.1 = f32[4,128,128]{1,2,0:T(8,128)S(1)} collective-permute-done((f32[4,128,128]{1,2,0:T(8,128)S(1)}, f32[4,128,128]{1,2,0:T(8,128)S(1)}, u32[]{:S(2)}, u32[]{:S(2)}) %collective-permute-start.1) | collective-permute-done | bytes 262176 | tf_op jit(solution)/shard_map/ppermute | solution.py:17
  40.1 2.4 gather_fusion.2
  42.5 2.6 convolution_bitcast_fusion.1
  45.1 24.0 %reduce-scatter.3.cloned.1.call-done = f32[3,128,128]{2,1,0:T(8,128)} async-done(((f32[12,128,128]{2,1,0:T(8,128)}), f32[3,128,128]{2,1,0:T(8,128)}) %reduce-scatter.3.cloned.1.call-update) | async-done | bytes 196624 | tf_op jit(solution)/shard_map/reduce_scatter | solution.py:60
  70.7 8.2 %all_gather.10 = f32[12,128,128]{2,1,0:T(8,128)S(1)} all-gather(f32[3,128,128]{2,1,0:T(8,128)S(1)} %convolution_subtract_fusion.1), channel_id=1, replica_groups=mesh['dom'=8,'tile'=4] {'tile'}, dimensions={0}, use_global_device_ids=true | all-gather | bytes 983040 | tf_op jit(solution)/shard_map/all_gather | solution.py:45
  78.9 2.9 fusion.6
  84.6 3.4 collective-permute-start.2
  89.9 5.3 %collective-permute-done.2 = f32[4,128,128]{1,2,0:T(8,128)S(1)} collective-permute-done((f32[4,128,128]{1,2,0:T(8,128)}, f32[4,128,128]{1,2,0:T(8,128)S(1)}, u32[]{:S(2)}, u32[]{:S(2)}) %collective-permute-start.2) | collective-permute-done | bytes 262176 | tf_op jit(solution)/shard_map/ppermute | solution.py:17
  95.2 5.6 %collective-permute-done.3 = f32[4,128,128]{1,2,0:T(8,128)S(1)} collective-permute-done((f32[4,128,128]{1,2,0:T(8,128)}, f32[4,128,128]{1,2,0:T(8,128)S(1)}, u32[]{:S(2)}, u32[]{:S(2)}) %collective-permute-start.3) | collective-permute-done | bytes 262176 | tf_op jit(solution)/shard_map/ppermute | solution.py:17
  102.4 2.4 gather_fusion.5
  104.7 2.6 convolution_bitcast_fusion
  108.9 22.2 %reduce-scatter.5.cloned.1.call-done = f32[3,128,128]{2,1,0:T(8,128)} async-done(((f32[12,128,128]{2,1,0:T(8,128)}), f32[3,128,128]{2,1,0:T(8,128)}) %reduce-scatter.5.cloned.1.call-update) | async-done | bytes 196624 | tf_op jit(solution)/shard_map/reduce_scatter | solution.py:60
  133.4 8.2 %all_gather.11 = f32[12,128,128]{2,1,0:T(8,128)S(1)} all-gather(f32[3,128,128]{2,1,0:T(8,128)S(1)} %convolution_subtract_fusion), channel_id=1, replica_groups=mesh['dom'=8,'tile'=4] {'tile'}, dimensions={0}, use_global_device_ids=true | all-gather | bytes 983040 | tf_op jit(solution)/shard_map/all_gather | solution.py:45
  143.5 3.4 collective-permute-start.4
  149.8 3.9 collective-permute-done.5
  154.3 2.3 fusion.18
  156.7 31.3 %all-reduce.7.cloned.1.call-done = f32[12,32,128]{2,1,0:T(8,128)} async-done(((f32[12,32,128]{2,1,0:T(8,128)}), f32[12,32,128]{2,1,0:T(8,128)}) %all-reduce.7.cloned.1.call-update) | async-done | bytes 196624 | tf_op jit(solution)/shard_map/psum | solution.py:77
  187.9 2.2 fusion.56
  191.5 3.4 collective-permute-start.6
  197.7 3.4 collective-permute-done.7
  201.7 2.3 fusion.21
  204.1 30.9 %all-reduce.9.cloned.1.call-done = f32[12,32,128]{2,1,0:T(8,128)} async-done(((f32[12,32,128]{2,1,0:T(8,128)}), f32[12,32,128]{2,1,0:T(8,128)}) %all-reduce.9.cloned.1.call-update) | async-done | bytes 196624 | tf_op jit(solution)/shard_map/psum | solution.py:77
  235.0 2.2 fusion.54
  238.7 3.4 collective-permute-start.8
  244.8 3.4 collective-permute-done.9
  248.8 2.3 fusion.24
  251.3 30.9 %all-reduce.11.cloned.1.call-done = f32[12,32,128]{2,1,0:T(8,128)} async-done(((f32[12,32,128]{2,1,0:T(8,128)}), f32[12,32,128]{2,1,0:T(8,128)}) %all-reduce.11.cloned.1.call-update) | async-done | bytes 196624 | tf_op jit(solution)/shard_map/psum | solution.py:77
  285.0 2.5 collective-permute-start.10
  288.0 2.4 collective-permute-start.11
  294.8 2.3 fusion.27
  297.2 30.9 %all-reduce.13.cloned.1.call-done = f32[12,32,128]{2,1,0:T(8,128)} async-done(((f32[12,32,128]{2,1,0:T(8,128)}), f32[12,32,128]{2,1,0:T(8,128)}) %all-reduce.13.cloned.1.call-update) | async-done | bytes 196624 | tf_op jit(solution)/shard_map/psum | solution.py:85
  328.1 2.2 fusion.52
  331.5 2.5 collective-permute-start.12
  333.9 2.7 collective-permute-start.13
  336.6 2.6 collective-permute-done.12
  340.7 2.3 fusion.30
  343.1 30.9 %all-reduce.15.cloned.1.call-done = f32[12,32,128]{2,1,0:T(8,128)} async-done(((f32[12,32,128]{2,1,0:T(8,128)}), f32[12,32,128]{2,1,0:T(8,128)}) %all-reduce.15.cloned.1.call-update) | async-done | bytes 196624 | tf_op jit(solution)/shard_map/psum | solution.py:85
  374.0 2.2 fusion.50
  377.4 2.5 collective-permute-start.14
  379.8 2.4 collective-permute-start.15
  382.3 2.8 collective-permute-done.14
  386.6 2.3 fusion.33
  389.0 30.9 %all-reduce.17.cloned.1.call-done = f32[12,32,128]{2,1,0:T(8,128)} async-done(((f32[12,32,128]{2,1,0:T(8,128)}), f32[12,32,128]{2,1,0:T(8,128)}) %all-reduce.17.cloned.1.call-update) | async-done | bytes 196624 | tf_op jit(solution)/shard_map/psum | solution.py:85
  419.9 2.9 fusion.48
  (112 shorter events, 47.3 us)
Async XLA Ops:
  7.2 61.9 %reduce-scatter.3.cloned.1.call-start = ((), (), s32[]{:S(2)}) async-start(), calls=%async_computation.2 | async-start | bytes 983040 | tf_op jit(solution)/shard_map/reduce_scatter | solution.py:60
  17.6 4.4 %copy-start.8 = (s32[1024]{0:T(1024)}, s32[1024]{0:T(1024)S(1)}, u32[]{:S(2)}) copy-start(s32[1024]{0:T(1024)S(1)} %pad_clamp_fusion.7) | copy-start | bytes 12292
  17.6 11.5 %copy-start.13 = (s32[12,2]{0,1:T(2,128)S(1)}, s32[12,2]{0,1:T(2,128)}, u32[]{:S(2)}) copy-start(s32[12,2]{0,1:T(2,128)} %param.12) | copy-start | bytes 292
  22.5 10.5 %collective-permute-start = (f32[4,128,128]{1,2,0:T(8,128)S(1)}, f32[4,128,128]{1,2,0:T(8,128)S(1)}, u32[]{:S(2)}, u32[]{:S(2)}) collective-permute-start(f32[4,128,128]{1,2,0:T(8,128)S(1)} %gather_fusion), channel_id=1, source_target_pairs={{0,4},{4,8},{8,12},{12,16},{16,20},{20,24},{24,28},{1,5},{5,9},{9,... | collective-permute-start | bytes 786440 | tf_op jit(solution)/shard_map/ppermute | solution.py:17
  26.0 0.6 copy-start.9
  27.2 11.4 %collective-permute-start.1 = (f32[4,128,128]{1,2,0:T(8,128)S(1)}, f32[4,128,128]{1,2,0:T(8,128)S(1)}, u32[]{:S(2)}, u32[]{:S(2)}) collective-permute-start(f32[4,128,128]{1,2,0:T(8,128)S(1)} %gather_fusion.1), channel_id=1, source_target_pairs={{0,8},{4,12},{8,16},{12,20},{16,24},{20,28},{1,9},{5,13},{9,17},{1... | collective-permute-start | bytes 786440 | tf_op jit(solution)/shard_map/ppermute | solution.py:17
  30.0 10.1 %copy-start.10 = (s32[1024]{0:T(1024)}, s32[1024]{0:T(1024)S(1)}, u32[]{:S(2)}) copy-start(s32[1024]{0:T(1024)S(1)} %pad_clamp_fusion.5) | copy-start | bytes 12292
  40.1 2.4 copy-start
  42.4 26.7 %copy-start.2 = (f32[3,128,128]{2,1,0:T(8,128)S(1)}, f32[3,128,128]{2,1,0:T(8,128)}, u32[]{:S(2)}) copy-start(f32[3,128,128]{2,1,0:T(8,128)} %param.9) | copy-start | bytes 589828
  42.4 26.6 %copy-start.3 = (f32[3,128,128]{2,1,0:T(8,128)S(1)}, f32[3,128,128]{2,1,0:T(8,128)}, u32[]{:S(2)}) copy-start(f32[3,128,128]{2,1,0:T(8,128)} %param.8) | copy-start | bytes 589828
  45.0 86.1 %reduce-scatter.5.cloned.1.call-start = ((), (), s32[]{:S(2)}) async-start(), calls=%async_computation.3 | async-start | bytes 983040 | tf_op jit(solution)/shard_map/reduce_scatter | solution.py:60
  84.6 10.7 %collective-permute-start.2 = (f32[4,128,128]{1,2,0:T(8,128)}, f32[4,128,128]{1,2,0:T(8,128)S(1)}, u32[]{:S(2)}, u32[]{:S(2)}) collective-permute-start(f32[4,128,128]{1,2,0:T(8,128)} %gather_fusion.3), channel_id=1, source_target_pairs={{0,4},{4,8},{8,12},{12,16},{16,20},{20,24},{24,28},{1,5},{5,9},{9,... | collective-permute-start | bytes 786440 | tf_op jit(solution)/shard_map/ppermute | solution.py:17
  88.0 12.9 %collective-permute-start.3 = (f32[4,128,128]{1,2,0:T(8,128)}, f32[4,128,128]{1,2,0:T(8,128)S(1)}, u32[]{:S(2)}, u32[]{:S(2)}) collective-permute-start(f32[4,128,128]{1,2,0:T(8,128)} %gather_fusion.4), channel_id=1, source_target_pairs={{0,8},{4,12},{8,16},{12,20},{16,24},{20,28},{1,9},{5,13},{9,17},{1... | collective-permute-start | bytes 786440 | tf_op jit(solution)/shard_map/ppermute | solution.py:17
  104.7 26.4 %copy-start.4 = (f32[3,128,128]{2,1,0:T(8,128)S(1)}, f32[3,128,128]{2,1,0:T(8,128)}, u32[]{:S(2)}) copy-start(f32[3,128,128]{2,1,0:T(8,128)} %param.8) | copy-start | bytes 589828
  107.3 34.3 %copy-start.1 = (f32[12,32,128]{2,1,0:T(8,128)S(1)}, f32[12,32,128]{2,1,0:T(8,128)}, u32[]{:S(2)}) copy-start(f32[12,32,128]{2,1,0:T(8,128)} %param.7) | copy-start | bytes 589828
  107.3 80.6 %all-reduce.7.cloned.1.call-start = ((), (), s32[]{:S(2)}) async-start(), calls=%async_computation.4 | async-start | bytes 393216 | tf_op jit(solution)/shard_map/psum | solution.py:77
  108.8 34.1 %copy-start.6 = (s32[1024]{0:T(1024)}, s32[1024]{0:T(1024)S(1)}, u32[]{:S(2)}) copy-start(s32[1024]{0:T(1024)S(1)} %pad_clamp_fusion.4) | copy-start | bytes 12292
  108.9 38.1 %copy-start.7 = (s32[1024]{0:T(1024)}, s32[1024]{0:T(1024)S(1)}, u32[]{:S(2)}) copy-start(s32[1024]{0:T(1024)S(1)} %pad_clamp_fusion.3) | copy-start | bytes 12292
  132.4 17.0 %copy-start.14 = (s32[24]{0:T(128)S(1)}, s32[24]{0:T(128)}, u32[]{:S(2)}) copy-start(s32[24]{0:T(128)} %get-tuple-element.10) | copy-start | bytes 292
  132.7 0.7 copy-start.5
  143.5 6.2 %collective-permute-start.4 = (f32[4,32,128]{2,1,0:T(8,128)S(1)}, f32[4,32,128]{2,1,0:T(8,128)S(1)}, u32[]{:S(2)}, u32[]{:S(2)}) collective-permute-start(f32[4,32,128]{2,1,0:T(8,128)S(1)} %gather_fusion.6), channel_id=1, source_target_pairs={{0,4},{4,8},{8,12},{12,16},{16,20},{20,24},{24,28},{1,5},{5,9},{9,... | collective-permute-start | bytes 196616 | tf_op jit(solution)/shard_map/ppermute | solution.py:17
  147.5 6.2 %collective-permute-start.5 = (f32[4,32,128]{2,1,0:T(8,128)S(1)}, f32[4,32,128]{2,1,0:T(8,128)S(1)}, u32[]{:S(2)}, u32[]{:S(2)}) collective-permute-start(f32[4,32,128]{2,1,0:T(8,128)S(1)} %gather_fusion.7), channel_id=1, source_target_pairs={{0,8},{4,12},{8,16},{12,20},{16,24},{20,28},{1,9},{5,13},{9,17},{1... | collective-permute-start | bytes 196616 | tf_op jit(solution)/shard_map/ppermute | solution.py:17
  156.6 78.4 %all-reduce.9.cloned.1.call-start = ((), (), s32[]{:S(2)}) async-start(), calls=%async_computation.5 | async-start | bytes 393216 | tf_op jit(solution)/shard_map/psum | solution.py:77
  191.5 6.2 %collective-permute-start.6 = (f32[4,32,128]{2,1,0:T(8,128)S(1)}, f32[4,32,128]{2,1,0:T(8,128)S(1)}, u32[]{:S(2)}, u32[]{:S(2)}) collective-permute-start(f32[4,32,128]{2,1,0:T(8,128)S(1)} %gather_fusion.9), channel_id=1, source_target_pairs={{0,4},{4,8},{8,12},{12,16},{16,20},{20,24},{24,28},{1,5},{5,9},{9,... | collective-permute-start | bytes 196616 | tf_op jit(solution)/shard_map/ppermute | solution.py:17
  194.9 6.2 %collective-permute-start.7 = (f32[4,32,128]{2,1,0:T(8,128)S(1)}, f32[4,32,128]{2,1,0:T(8,128)S(1)}, u32[]{:S(2)}, u32[]{:S(2)}) collective-permute-start(f32[4,32,128]{2,1,0:T(8,128)S(1)} %gather_fusion.10), channel_id=1, source_target_pairs={{0,8},{4,12},{8,16},{12,20},{16,24},{20,28},{1,9},{5,13},{9,17},{1... | collective-permute-start | bytes 196616 | tf_op jit(solution)/shard_map/ppermute | solution.py:17
  201.7 42.3 %copy-start.12 = (s32[4]{0:T(128)S(1)}, s32[4]{0:T(128)}, u32[]{:S(2)}) copy-start(s32[4]{0:T(128)} %get-tuple-element.2) | copy-start | bytes 52
  204.1 78.0 %all-reduce.11.cloned.1.call-start = ((), (), s32[]{:S(2)}) async-start(), calls=%async_computation.6 | async-start | bytes 393216 | tf_op jit(solution)/shard_map/psum | solution.py:77
  238.7 6.2 %collective-permute-start.8 = (f32[4,32,128]{2,1,0:T(8,128)S(1)}, f32[4,32,128]{2,1,0:T(8,128)S(1)}, u32[]{:S(2)}, u32[]{:S(2)}) collective-permute-start(f32[4,32,128]{2,1,0:T(8,128)S(1)} %gather_fusion.12), channel_id=1, source_target_pairs={{0,4},{4,8},{8,12},{12,16},{16,20},{20,24},{24,28},{1,5},{5,9},{9,... | collective-permute-start | bytes 196616 | tf_op jit(solution)/shard_map/ppermute | solution.py:17
  242.1 6.2 %collective-permute-start.9 = (f32[4,32,128]{2,1,0:T(8,128)S(1)}, f32[4,32,128]{2,1,0:T(8,128)S(1)}, u32[]{:S(2)}, u32[]{:S(2)}) collective-permute-start(f32[4,32,128]{2,1,0:T(8,128)S(1)} %gather_fusion.13), channel_id=1, source_target_pairs={{0,8},{4,12},{8,16},{12,20},{16,24},{20,28},{1,9},{5,13},{9,17},{1... | collective-permute-start | bytes 196616 | tf_op jit(solution)/shard_map/ppermute | solution.py:17
  248.2 3.0 copy-start.11
  251.2 76.9 %all-reduce.13.cloned.1.call-start = ((), (), s32[]{:S(2)}) async-start(), calls=%async_computation.7 | async-start | bytes 393216 | tf_op jit(solution)/shard_map/psum | solution.py:85
  285.0 7.3 %collective-permute-start.10 = (f32[4,32,128]{2,1,0:T(8,128)S(1)}, f32[4,32,128]{2,1,0:T(8,128)S(1)}, u32[]{:S(2)}, u32[]{:S(2)}) collective-permute-start(f32[4,32,128]{2,1,0:T(8,128)S(1)} %gather_fusion.15), channel_id=1, source_target_pairs={{4,0},{8,4},{12,8},{16,12},{20,16},{24,20},{28,24},{5,1},{9,5},{13... | collective-permute-start | bytes 196616 | tf_op jit(solution)/shard_map/ppermute | solution.py:17
  288.0 6.2 %collective-permute-start.11 = (f32[4,32,128]{2,1,0:T(8,128)S(1)}, f32[4,32,128]{2,1,0:T(8,128)S(1)}, u32[]{:S(2)}, u32[]{:S(2)}) collective-permute-start(f32[4,32,128]{2,1,0:T(8,128)S(1)} %gather_fusion.16), channel_id=1, source_target_pairs={{8,0},{12,4},{16,8},{20,12},{24,16},{28,20},{9,1},{13,5},{17,9},{2... | collective-permute-start | bytes 196616 | tf_op jit(solution)/shard_map/ppermute | solution.py:17
  297.1 76.9 %all-reduce.15.cloned.1.call-start = ((), (), s32[]{:S(2)}) async-start(), calls=%async_computation.8 | async-start | bytes 393216 | tf_op jit(solution)/shard_map/psum | solution.py:85
  331.5 7.7 %collective-permute-start.12 = (f32[4,32,128]{2,1,0:T(8,128)S(1)}, f32[4,32,128]{2,1,0:T(8,128)S(1)}, u32[]{:S(2)}, u32[]{:S(2)}) collective-permute-start(f32[4,32,128]{2,1,0:T(8,128)S(1)} %gather_fusion.18), channel_id=1, source_target_pairs={{4,0},{8,4},{12,8},{16,12},{20,16},{24,20},{28,24},{5,1},{9,5},{13... | collective-permute-start | bytes 196616 | tf_op jit(solution)/shard_map/ppermute | solution.py:17
  333.9 6.2 %collective-permute-start.13 = (f32[4,32,128]{2,1,0:T(8,128)S(1)}, f32[4,32,128]{2,1,0:T(8,128)S(1)}, u32[]{:S(2)}, u32[]{:S(2)}) collective-permute-start(f32[4,32,128]{2,1,0:T(8,128)S(1)} %gather_fusion.19), channel_id=1, source_target_pairs={{8,0},{12,4},{16,8},{20,12},{24,16},{28,20},{9,1},{13,5},{17,9},{2... | collective-permute-start | bytes 196616 | tf_op jit(solution)/shard_map/ppermute | solution.py:17
  343.1 76.9 %all-reduce.17.cloned.1.call-start = ((), (), s32[]{:S(2)}) async-start(), calls=%async_computation.9 | async-start | bytes 393216 | tf_op jit(solution)/shard_map/psum | solution.py:85
  377.4 7.7 %collective-permute-start.14 = (f32[4,32,128]{2,1,0:T(8,128)S(1)}, f32[4,32,128]{2,1,0:T(8,128)S(1)}, u32[]{:S(2)}, u32[]{:S(2)}) collective-permute-start(f32[4,32,128]{2,1,0:T(8,128)S(1)} %gather_fusion.21), channel_id=1, source_target_pairs={{4,0},{8,4},{12,8},{16,12},{20,16},{24,20},{28,24},{5,1},{9,5},{13... | collective-permute-start | bytes 196616 | tf_op jit(solution)/shard_map/ppermute | solution.py:17
  379.8 6.2 %collective-permute-start.15 = (f32[4,32,128]{2,1,0:T(8,128)S(1)}, f32[4,32,128]{2,1,0:T(8,128)S(1)}, u32[]{:S(2)}, u32[]{:S(2)}) collective-permute-start(f32[4,32,128]{2,1,0:T(8,128)S(1)} %gather_fusion.22), channel_id=1, source_target_pairs={{8,0},{12,4},{16,8},{20,12},{24,16},{28,20},{9,1},{13,5},{17,9},{2... | collective-permute-start | bytes 196616 | tf_op jit(solution)/shard_map/ppermute | solution.py:17
Sparse Core Ops, SparseCore 0:
  45.2 23.8 reduce-scatter.2
  107.4 23.6 reduce-scatter.4
  156.7 31.1 all-reduce.6
  204.2 30.7 all-reduce.8
  251.3 30.7 all-reduce.10
  297.3 30.7 all-reduce.12
  343.2 30.7 all-reduce.14
  389.1 30.7 all-reduce.16
where the time goes:
time: 432 us; the launch traced here: 430 us
  waiting for transfers between devices  275 us (64%)
  matrix products  44.1 us (10%)
  starting transfers between devices  42.1 us (10%)
  blocking collectives  25.2 us (6%)
  local copies, waits for them, and re-layouts  21 us (5%)
  between operations  14.7 us (3%)
  other arithmetic  7.46 us (2%)
    psum x3, waiting for transfers between devices, local(): lower_y = krylov_block - lax.psum(partial_value, 'tile')  93 us
    psum x3, waiting for transfers between devices, local(): lax.psum(partial_value, 'tile')  92.7 us
    reduce_scatter x2, waiting for transfers between devices, local(): lax.psum_scatter(jnp.einsum('rwij,rwjk->rik', tiles_lower, pivot_gathered...  46.2 us
    ppermute x16, waiting for transfers between devices, passed_along(): return lax.ppermute(block, axis, route)  43.1 us
    ppermute x16, starting transfers between devices, passed_along(): return lax.ppermute(block, axis, route)  41.6 us
    all_gather x3, blocking collectives, spread(): return lax.all_gather(inverse_mine, 'tile', axis=0, tiled=True)  25.2 us
    dot_general x7, matrix products, apply_inverse(): return jnp.einsum('rvj,rij->rvi', vectors, inverse, precision=precise)  14.5 us
  transfers between devices with their start and end apart: 24, of which 24 were waited for; matrix products, arithmetic and copies ran while one was open for 1% of the time, Pallas kernels for 0%

commit v1 on v0

v1 whole, which is shorter than its diff:
```python
import functools

import jax
import jax.numpy as jnp
from jax import lax
from jax.experimental import pallas as pl
from jax.experimental.pallas import tpu as pltpu
from jax.sharding import PartitionSpec as P

FSWEEPS = 2
LSWEEPS = 3
USWEEPS = 3
F32 = jnp.float32
BF16 = jnp.bfloat16


def split(a):
    hi = a.astype(BF16)
    return hi, (a - hi.astype(F32)).astype(BF16)


def matmul_parts(ah, al, bh, bl):
    lhs = jnp.concatenate([ah, al], 1)
    pair = jnp.concatenate([bh, bl], 1)
    rhs = jnp.concatenate([pair, pair], 0)
    out = jnp.dot(lhs, rhs, preferred_element_type=F32)
    n = bh.shape[1]
    return out[:, :n] + out[:, n:]


def matmul(a, b):
    return matmul_parts(*split(a), *split(b))


def times_tile(x, wide):
    v, n = x.shape
    stacked = jnp.concatenate(split(x), 0)
    out = lax.dot_general(stacked, wide, (((1,), (1,)), ((), ())), preferred_element_type=F32)
    return out[:v, :n] + (out[v:, :n] + out[:v, n:])


def widen(a):
    return jnp.concatenate(split(a), 0)


class Layout:
    def __init__(self, rows, width, cap, n_tile):
        self.rows, self.width, self.cap, self.n_tile = rows, width, cap, n_tile
        self.slots = rows * width
        self.own_rows = rows // n_tile
        self.n_link = self.slots
        self.n_send = 2 * self.slots

    def kind(self, meta, s):
        return meta[s]

    def link(self, meta, s):
        return meta[self.n_link + s]

    def listed(self, meta, which, j):
        return meta[self.n_send + which * self.cap + j]

    def place(self, r, me):
        far = (r // self.own_rows) ^ me
        return ((far & 1) * (self.n_tile // 2) + (far >> 1)) * self.own_rows + r % self.own_rows

    def lookup(self, meta, role, base_list, side, j):
        s = self.listed(meta, base_list + role, j)
        v = self.link(meta, s) - self.slots - role * self.cap
        live = (self.kind(meta, s) == side) & (v >= 0) & (v < self.cap)
        return s, s // self.width, live, jnp.clip(v, 0, self.cap - 1)


def smem():
    return pl.BlockSpec(memory_space=pltpu.SMEM)


def vmem():
    return pl.BlockSpec(memory_space=pltpu.VMEM)


def call(body, outs, scalars, arrays, flops=0, scratch=()):
    moved = sum(a.size * a.dtype.itemsize for a in arrays) + sum(o.size * o.dtype.itemsize for o in outs)
    return pl.pallas_call(
        body,
        out_shape=outs,
        in_specs=[smem()] * len(scalars) + [vmem()] * len(arrays),
        out_specs=[vmem()] * len(outs),
        scratch_shapes=list(scratch),
        compiler_params=pltpu.CompilerParams(vmem_limit_bytes=24 << 20),
        cost_estimate=pl.CostEstimate(flops=flops, bytes_accessed=moved, transcendentals=0),
    )(*scalars, *arrays)


def pack_kernel(lay, me, mine, mates, tiles, mate_tiles, lower, upper):
    role = me[0] % 2
    for base, side, out in ((2, 1, lower), (0, 2, upper)):
        for g, (meta, source) in enumerate(((mine, tiles), (mates, mate_tiles))):
            for j in range(lay.cap):
                s, _, live, _ = lay.lookup(meta, role, base, side, j)
                out[g * lay.cap + j] = widen(jnp.where(live, source[s], 0.0))


def outgoing_kernel(lay, me, mine, mates, inverse, upper, out):
    role = me[0] % 2
    n = inverse.shape[1]
    for g, meta in enumerate((mine, mates)):
        for j in range(lay.cap):
            _, r, _, _ = lay.lookup(meta, role, 0, 2, j)
            k = g * lay.cap + j
            out[k] = matmul_parts(*split(inverse[lay.place(r, me[0])]), upper[k, :n], upper[k, n:])


def local_pivot_kernel(lay, me, mine, inverse, tiles, out):
    out[...] = jnp.zeros_like(out)

    @pl.loop(0, lay.slots)
    def _(s):
        v = lay.link(mine, s)

        @pl.when((lay.kind(mine, s) == 1) & (v < lay.slots))
        def _():
            q = matmul(inverse[lay.place(v // lay.width, me[0])], tiles[v])
            out[lay.place(s // lay.width, me[0])] += matmul(tiles[s], q)


def incoming_kernel(lay, me, mine, mates, local, lower, arrived, keep, give, total):
    role = me[0] % 2
    n = lower.shape[2]
    total[...] = local[...]
    for g, meta in enumerate((mine, mates)):
        for j in range(lay.cap):
            _, r, _, v = lay.lookup(meta, role, 2, 1, j)
            k = g * lay.cap + j
            total[lay.place(r, me[0])] += matmul_parts(
                lower[k, :n], lower[k, n:], *split(arrived[g * lay.cap + v])
            )
    half = keep.shape[0]
    keep[...] = total[:half]
    give[...] = total[half:]


def newton_kernel(inverse, diag, sums, out):
    for i in range(out.shape[0]):
        x = inverse[i]
        xh, xl = split(x)
        product = matmul_parts(xh, xl, *split(diag[i] - sums[i]))
        out[i] = 2.0 * x - matmul_parts(*split(product), xh, xl)


def apply_kernel(lay, list_base, n_sums, me, mine, mates, base, *refs):
    sums, (inverse, out, send, rest) = refs[:n_sums], refs[n_sums:]
    role = me[0] % 2
    for r in range(lay.rows):
        u = base[r]
        if sums:
            u = u - sum(s[r] for s in sums)
        rest[r] = u
        out[r] = times_tile(u, widen(inverse[lay.place(r, me[0])]))
    if send is not None:
        for g, meta in enumerate((mine, mates)):
            for j in range(lay.cap):
                r = lay.listed(meta, list_base + role, j) // lay.width
                send[g * lay.cap + j] = out[r]


def last_apply_kernel(lay, n_sums, me, base, *refs):
    sums, (inverse, out) = refs[:n_sums], refs[n_sums:]
    for r in range(lay.rows):
        u = base[r] - sum(s[r] for s in sums)
        out[r] = times_tile(u, widen(inverse[lay.place(r, me[0])]))


def local_vector_kernel(lay, side, mine, x, tiles, out):
    out[...] = jnp.zeros_like(out)

    @pl.loop(0, lay.slots)
    def _(s):
        v = lay.link(mine, s)

        @pl.when((lay.kind(mine, s) == side) & (v < lay.slots))
        def _():
            out[s // lay.width] += times_tile(x[v // lay.width], widen(tiles[s]))


def arrived_vector_kernel(lay, list_base, side, me, mine, mates, local, tiles, arrived, out):
    role = me[0] % 2
    out[...] = local[...]
    for g, meta in enumerate((mine, mates)):
        for j in range(lay.cap):
            _, r, _, v = lay.lookup(meta, role, list_base, side, j)
            k = g * lay.cap + j
            out[r] += times_tile(arrived[g * lay.cap + v], tiles[k])


def local(krylov_block, diag_block, inverse_prev, coupling_tiles, slot_kind, slot_link, send_slots):
    rows, width, n, _ = coupling_tiles.shape
    cap = send_slots.shape[3]
    n_dom, n_tile = lax.axis_size("dom"), lax.axis_size("tile")
    lay = Layout(rows, width, cap, n_tile)
    vectors = krylov_block.shape[1]
    upper_bits = [1 << b for b in range(1, n_tile.bit_length() - 1)]

    me = lax.axis_index("tile").astype(jnp.int32).reshape(1)
    mine = jnp.concatenate([slot_kind.reshape(-1), slot_link.reshape(-1), send_slots.reshape(-1)])
    tiles = coupling_tiles.reshape(lay.slots, n, n)

    def swap(x, bit):
        return lax.ppermute(x, "tile", [(i, i ^ bit) for i in range(n_tile)])

    def along(x, sign):
        route = []
        for d in range(n_dom):
            for t in range(n_tile):
                to = d + sign * (1 + t % 2)
                if 0 <= to < n_dom:
                    route.append((d * n_tile + t, to * n_tile + t))
        return lax.ppermute(x, ("dom", "tile"), route)

    def spread(x):
        for bit in upper_bits:
            x = jnp.concatenate([x, swap(x, bit)], 0)
        return x

    def summed(x, chunked):
        for bit in upper_bits:
            got = swap(x, bit)
            if chunked:
                near = bit // 2
                got = got.reshape((n_tile // 2 // (2 * near), 2, near * lay.own_rows) + x.shape[1:])
                got = jnp.concatenate([got[:, 1:], got[:, :1]], 1).reshape(x.shape)
            x = x + got
        return x

    def shape(*dims, dtype=F32):
        return jax.ShapeDtypeStruct(dims, dtype)

    kernel = lambda body, *bound: functools.partial(body, lay, *bound)

    mates = swap(mine, 1)
    mate_tiles = swap(tiles, 1)
    kept = spread(inverse_prev)
    diag = spread(diag_block)
    lower, upper = call(
        kernel(pack_kernel),
        [shape(2 * cap, 2 * n, n, dtype=BF16)] * 2,
        (me, mine, mates),
        (tiles, mate_tiles),
    )
    half = rows // 2
    for _ in range(FSWEEPS):
        inverse = jnp.concatenate([kept, swap(kept, 1)], 0)
        (out,) = call(kernel(outgoing_kernel), [shape(2 * cap, n, n)], (me, mine, mates), (inverse, upper))
        arrived = along(out, 1)
        (here,) = call(
            kernel(local_pivot_kernel), [shape(rows, n, n)], (me, mine), (inverse, tiles), flops=8 * 2 * n**3 * rows
        )
        keep, give = call(
            kernel(incoming_kernel),
            [shape(half, n, n)] * 2,
            (me, mine, mates),
            (here, lower, arrived),
            scratch=(pltpu.VMEM((rows, n, n), F32),),
        )
        sums = summed(keep + swap(give, 1), True)
        (kept,) = call(newton_kernel, [shape(half, n, n)], (), (kept, diag, sums))
    inverse = jnp.concatenate([kept, swap(kept, 1)], 0)

    block = shape(rows, vectors, n)
    sent = shape(2 * cap, vectors, n)

    def apply(base, sums, list_base):
        return call(
            kernel(apply_kernel, list_base, len(sums)),
            [block, sent, block],
            (me, mine, mates),
            (base, *sums, inverse),
        )

    def neighbour_sum(x, send, side):
        arrived = along(send, 1 if side == 1 else -1)
        (here,) = call(
            kernel(local_vector_kernel, side), [block], (mine,), (x, tiles), flops=4 * 2 * n**2 * vectors * rows
        )
        (part,) = call(
            kernel(arrived_vector_kernel, 2 if side == 1 else 0, side),
            [block],
            (me, mine, mates),
            (here, lower if side == 1 else upper, arrived),
        )
        part = part + swap(part, 1)
        for bit in upper_bits[:-1]:
            part = part + swap(part, bit)
        return part, swap(part, upper_bits[-1])

    x, send, _ = apply(krylov_block, (), 0)
    for sweep in range(LSWEEPS):
        sums = neighbour_sum(x, send, 1)
        x, send, y = apply(krylov_block, sums, 0 if sweep < LSWEEPS - 1 else 2)
    for sweep in range(USWEEPS):
        sums = neighbour_sum(x, send, 2)
        if sweep < USWEEPS - 1:
            x, send, _ = apply(y, sums, 2)
        else:
            (x,) = call(kernel(last_apply_kernel, len(sums)), [block], (me,), (y, *sums, inverse))
    return (kept[: lay.own_rows], x)


def solution(mesh):
    placed = (
        P("dom", None, None),
        P(("dom", "tile"), None, None),
        P(("dom", "tile"), None, None),
        P("dom", "tile", None, None),
        P("dom", "tile"),
        P("dom", "tile"),
        P("dom", "tile", None, None),
    )
    return jax.shard_map(
        local,
        mesh=mesh,
        in_specs=placed,
        out_specs=(P(("dom", "tile"), None, None), P("dom", None, None)),
        check_vma=False,
    )
```

time: 432 us -> 196 us (0.45)
  waiting for transfers between devices: 275 us -> 110 us
  matrix products: 44.1 us -> 0 us
  Pallas kernels: 0 us -> 30.5 us
  blocking collectives: 25.2 us -> 0 us
  local copies, waits for them, and re-layouts: 21 us -> 4.3 us
  between operations: 14.7 us -> 1.09 us
  starting transfers between devices: 42.1 us -> 49.7 us
  other arithmetic: 7.46 us -> 0.61 us
    psum x6 -> x0, waiting for transfers between devices: 186 us -> none  [the longest x3 93 us: local(): lower_y = krylov_block - lax.psum(partial_value, 'tile')]
    ppermute x16 -> x31, waiting for transfers between devices: 43.1 us -> 110 us  [the longest x23 75.8 us: swap(): return lax.ppermute(x, 'tile', [(i, i ^ bit) for i in range(n_tile)])]
    reduce_scatter x2 -> x0, waiting for transfers between devices: 46.2 us -> none  [local(): lax.psum_scatter(jnp.einsum('rwij,rwjk->rik', tiles_lower, pivot_gathered...]
    dot_general x21 -> x0, matrix products: 44.1 us -> none  [the longest x7 14.5 us: apply_inverse(): return jnp.einsum('rvj,rij->rvi', vectors, inverse, precision=precise)]
    pallas_call x0 -> x28, Pallas kernels: none -> 30.5 us  [call(): pl.pallas_call(body, out_shape=outs, in_specs=[smem()] * len(scalars) + [...]
    all_gather x3 -> x0, blocking collectives: 25.2 us -> none  [spread(): return lax.all_gather(inverse_mine, 'tile', axis=0, tiled=True)]
    gather x24 -> x0, local copies, waits for them, and re-layouts: 19.3 us -> none  [the longest x2 4.71 us: local(): pivot_lookup[partner].reshape(row_count, slot_width, block_size, block_size)]
    ppermute x16 -> x31, starting transfers between devices: 41.6 us -> 49.7 us  [the longest x8 33.4 us: along(): return lax.ppermute(x, ('dom', 'tile'), route)]
  transfers between devices with their start and end apart: 24 -> 31, of which waited for: 24 -> 28; matrix products, arithmetic and copies ran while one was open for 1% -> 2% of each run, Pallas kernels for 0% -> 5%
where the time goes in v1:
time: 196 us
  waiting for transfers between devices  110 us (56%)
  starting transfers between devices  49.7 us (25%)
  Pallas kernels  30.5 us (16%)
  local copies, waits for them, and re-layouts  4.3 us (2%)
    ppermute x23, waiting for transfers between devices, swap(): return lax.ppermute(x, 'tile', [(i, i ^ bit) for i in range(n_tile)])  75.8 us
    ppermute x8, waiting for transfers between devices, along(): return lax.ppermute(x, ('dom', 'tile'), route)  34.1 us
    ppermute x8, starting transfers between devices, along(): return lax.ppermute(x, ('dom', 'tile'), route)  33.4 us
    pallas_call x28, Pallas kernels, call(): pl.pallas_call(body, out_shape=outs, in_specs=[smem()] * len(scalars) + [...  30.5 us
    ppermute x23, starting transfers between devices, swap(): return lax.ppermute(x, 'tile', [(i, i ^ bit) for i in range(n_tile)])  16.3 us
  transfers between devices with their start and end apart: 31, of which 28 were waited for; matrix products, arithmetic and copies ran while one was open for 2% of the time, Pallas kernels for 5%

profile of v1, /device:TPU:18, one launch (start us, length us, event | category | flops | bytes accessed | tf_op | source)
XLA Modules:
  0.0 196.1 jit_solution(1747288810455694176)
XLA Ops:
  0.7 1.6 collective-permute-start
  3.3 5.0 %collective-permute-done = f32[3,128,128]{2,1,0:T(8,128)S(1)} collective-permute-done((f32[3,128,128]{2,1,0:T(8,128)}, f32[3,128,128]{2,1,0:T(8,128)S(1)}, u32[]{:S(2)}, u32[]{:S(2)}) %collective-permute-start) | collective-permute-done | bytes 196640 | tf_op jit(solution)/shard_map/ppermute | solution.py:209
  12.2 1.6 shard_map.87
  14.7 3.5 %collective-permute-start.5 = (f32[8,128,128]{2,1,0:T(8,128)S(1)}, f32[8,128,128]{2,1,0:T(8,128)S(1)}, u32[]{:S(2)}, u32[]{:S(2)}) collective-permute-start(f32[8,128,128]{2,1,0:T(8,128)S(1)} %shard_map.88), channel_id=1, source_target_pairs={{0,4},{1,9},{2,6},{3,11},{4,8},{5,13},{6,10},{7,15},{8,12},{9,17},... | collective-permute-start | bytes 1572872 | tf_op jit(solution)/shard_map/ppermute | solution.py:218
  18.1 1.6 shard_map.86.local
  19.8 10.0 %collective-permute-done.5.arrived = f32[8,128,128]{2,1,0:T(8,128)S(1)} collective-permute-done((f32[8,128,128]{2,1,0:T(8,128)S(1)}, f32[8,128,128]{2,1,0:T(8,128)S(1)}, u32[]{:S(2)}, u32[]{:S(2)}) %collective-permute-start.5) | collective-permute-done | bytes 524320 | tf_op jit(solution)/shard_map/ppermute | solution.py:218
  31.0 1.6 collective-permute-done.6
  32.7 1.6 collective-permute-start.7
  34.8 13.3 %collective-permute-done.1 = f32[3,128,128]{2,1,0:T(8,128)S(1)} collective-permute-done((f32[3,128,128]{2,1,0:T(8,128)S(1)}, f32[3,128,128]{2,1,0:T(8,128)S(1)}, u32[]{:S(2)}, u32[]{:S(2)}) %collective-permute-start.1) | collective-permute-done | bytes 196640 | tf_op jit(solution)/shard_map/ppermute | solution.py:209
  48.8 1.7 collective-permute-done.8
  51.5 5.3 %collective-permute-start.9 = (f32[8,128,128]{2,1,0:T(8,128)S(1)}, f32[8,128,128]{2,1,0:T(8,128)S(1)}, u32[]{:S(2)}, u32[]{:S(2)}) collective-permute-start(f32[8,128,128]{2,1,0:T(8,128)S(1)} %shard_map.92), channel_id=1, source_target_pairs={{0,4},{1,9},{2,6},{3,11},{4,8},{5,13},{6,10},{7,15},{8,12},{9,17},... | collective-permute-start | bytes 1572872 | tf_op jit(solution)/shard_map/ppermute | solution.py:218
  56.8 1.6 shard_map.91.local
  58.4 8.0 %collective-permute-done.9.arrived = f32[8,128,128]{2,1,0:T(8,128)S(1)} collective-permute-done((f32[8,128,128]{2,1,0:T(8,128)S(1)}, f32[8,128,128]{2,1,0:T(8,128)S(1)}, u32[]{:S(2)}, u32[]{:S(2)}) %collective-permute-start.9) | collective-permute-done | bytes 524320 | tf_op jit(solution)/shard_map/ppermute | solution.py:218
  67.5 1.7 collective-permute-done.10
  69.3 1.6 collective-permute-start.11
  70.9 9.6 %collective-permute-done.11 = f32[6,128,128]{2,1,0:T(8,128)S(1)} collective-permute-done((f32[6,128,128]{2,1,0:T(8,128)S(1)}, f32[6,128,128]{2,1,0:T(8,128)S(1)}, u32[]{:S(2)}, u32[]{:S(2)}) %collective-permute-start.11) | collective-permute-done | bytes 393248 | tf_op jit(solution)/shard_map/ppermute | solution.py:209
  81.2 1.7 collective-permute-done.12
  83.0 1.5 shard_map.95
  84.5 5.3 %collective-permute-start.13 = (f32[8,32,128]{2,1,0:T(8,128)S(1)}, f32[8,32,128]{2,1,0:T(8,128)S(1)}, u32[]{:S(2)}, u32[]{:S(2)}) collective-permute-start(f32[8,32,128]{2,1,0:T(8,128)S(1)} %get-tuple-element.28), channel_id=1, source_target_pairs={{0,4},{1,9},{2,6},{3,11},{4,8},{5,13},{6,10},{7,15},{8,12},{9,17},... | collective-permute-start | bytes 393224 | tf_op jit(solution)/shard_map/ppermute | solution.py:218
  93.2 1.4 collective-permute-done.14
  94.7 1.6 collective-permute-start.15
  96.3 5.4 %collective-permute-done.15.refs_1_ = f32[12,32,128]{2,1,0:T(8,128)S(1)} collective-permute-done((f32[12,32,128]{2,1,0:T(8,128)S(1)}, f32[12,32,128]{2,1,0:T(8,128)S(1)}, u32[]{:S(2)}, u32[]{:S(2)}) %collective-permute-start.15) | collective-permute-done | bytes 196640 | tf_op jit(solution)/shard_map/ppermute | solution.py:209
  101.7 1.5 shard_map.98
  103.2 5.2 %collective-permute-start.16 = (f32[8,32,128]{2,1,0:T(8,128)S(1)}, f32[8,32,128]{2,1,0:T(8,128)S(1)}, u32[]{:S(2)}, u32[]{:S(2)}) collective-permute-start(f32[8,32,128]{2,1,0:T(8,128)S(1)} %get-tuple-element.30), channel_id=1, source_target_pairs={{0,4},{1,9},{2,6},{3,11},{4,8},{5,13},{6,10},{7,15},{8,12},{9,17},... | collective-permute-start | bytes 393224 | tf_op jit(solution)/shard_map/ppermute | solution.py:218
  111.8 1.4 collective-permute-done.17
  113.3 1.6 collective-permute-start.18
  114.9 5.4 %collective-permute-done.18.refs_1_ = f32[12,32,128]{2,1,0:T(8,128)S(1)} collective-permute-done((f32[12,32,128]{2,1,0:T(8,128)S(1)}, f32[12,32,128]{2,1,0:T(8,128)S(1)}, u32[]{:S(2)}, u32[]{:S(2)}) %collective-permute-start.18) | collective-permute-done | bytes 196640 | tf_op jit(solution)/shard_map/ppermute | solution.py:209
  120.3 1.5 shard_map.101
  121.8 5.2 %collective-permute-start.19 = (f32[8,32,128]{2,1,0:T(8,128)S(1)}, f32[8,32,128]{2,1,0:T(8,128)S(1)}, u32[]{:S(2)}, u32[]{:S(2)}) collective-permute-start(f32[8,32,128]{2,1,0:T(8,128)S(1)} %get-tuple-element.32), channel_id=1, source_target_pairs={{0,4},{1,9},{2,6},{3,11},{4,8},{5,13},{6,10},{7,15},{8,12},{9,17},... | collective-permute-start | bytes 393224 | tf_op jit(solution)/shard_map/ppermute | solution.py:218
  130.5 1.4 collective-permute-done.20
  131.9 1.6 collective-permute-start.21
  133.5 5.4 %collective-permute-done.21.refs_1_ = f32[12,32,128]{2,1,0:T(8,128)S(1)} collective-permute-done((f32[12,32,128]{2,1,0:T(8,128)S(1)}, f32[12,32,128]{2,1,0:T(8,128)S(1)}, u32[]{:S(2)}, u32[]{:S(2)}) %collective-permute-start.21) | collective-permute-done | bytes 196640 | tf_op jit(solution)/shard_map/ppermute | solution.py:209
  139.9 4.3 %collective-permute-start.22 = (f32[8,32,128]{2,1,0:T(8,128)S(1)}, f32[8,32,128]{2,1,0:T(8,128)S(1)}, u32[]{:S(2)}, u32[]{:S(2)}) collective-permute-start(f32[8,32,128]{2,1,0:T(8,128)S(1)} %get-tuple-element.35), channel_id=1, source_target_pairs={{4,0},{6,2},{8,4},{9,1},{10,6},{11,3},{12,8},{13,5},{14,10},{15,7}... | collective-permute-start | bytes 393224 | tf_op jit(solution)/shard_map/ppermute | solution.py:218
  145.2 3.1 %collective-permute-done.22.arrived = f32[8,32,128]{2,1,0:T(8,128)S(1)} collective-permute-done((f32[8,32,128]{2,1,0:T(8,128)S(1)}, f32[8,32,128]{2,1,0:T(8,128)S(1)}, u32[]{:S(2)}, u32[]{:S(2)}) %collective-permute-start.22) | collective-permute-done | bytes 131104 | tf_op jit(solution)/shard_map/ppermute | solution.py:218
  149.2 1.4 collective-permute-done.23
  150.7 1.6 collective-permute-start.24
  152.3 5.4 %collective-permute-done.24.refs_1_ = f32[12,32,128]{2,1,0:T(8,128)S(1)} collective-permute-done((f32[12,32,128]{2,1,0:T(8,128)S(1)}, f32[12,32,128]{2,1,0:T(8,128)S(1)}, u32[]{:S(2)}, u32[]{:S(2)}) %collective-permute-start.24) | collective-permute-done | bytes 196640 | tf_op jit(solution)/shard_map/ppermute | solution.py:209
  157.7 1.5 shard_map.107
  159.2 2.7 %collective-permute-start.25 = (f32[8,32,128]{2,1,0:T(8,128)S(1)}, f32[8,32,128]{2,1,0:T(8,128)S(1)}, u32[]{:S(2)}, u32[]{:S(2)}) collective-permute-start(f32[8,32,128]{2,1,0:T(8,128)S(1)} %get-tuple-element.37), channel_id=1, source_target_pairs={{4,0},{6,2},{8,4},{9,1},{10,6},{11,3},{12,8},{13,5},{14,10},{15,7}... | collective-permute-start | bytes 393224 | tf_op jit(solution)/shard_map/ppermute | solution.py:218
  162.9 4.0 %collective-permute-done.25.arrived = f32[8,32,128]{2,1,0:T(8,128)S(1)} collective-permute-done((f32[8,32,128]{2,1,0:T(8,128)S(1)}, f32[8,32,128]{2,1,0:T(8,128)S(1)}, u32[]{:S(2)}, u32[]{:S(2)}) %collective-permute-start.25) | collective-permute-done | bytes 131104 | tf_op jit(solution)/shard_map/ppermute | solution.py:218
  167.9 1.4 collective-permute-done.26
  169.3 1.6 collective-permute-start.27
  170.9 5.4 %collective-permute-done.27.refs_1_ = f32[12,32,128]{2,1,0:T(8,128)S(1)} collective-permute-done((f32[12,32,128]{2,1,0:T(8,128)S(1)}, f32[12,32,128]{2,1,0:T(8,128)S(1)}, u32[]{:S(2)}, u32[]{:S(2)}) %collective-permute-start.27) | collective-permute-done | bytes 196640 | tf_op jit(solution)/shard_map/ppermute | solution.py:209
  176.3 1.5 shard_map.110
  177.8 1.9 collective-permute-start.28
  180.8 4.8 %collective-permute-done.28.arrived = f32[8,32,128]{2,1,0:T(8,128)S(1)} collective-permute-done((f32[8,32,128]{2,1,0:T(8,128)S(1)}, f32[8,32,128]{2,1,0:T(8,128)S(1)}, u32[]{:S(2)}, u32[]{:S(2)}) %collective-permute-start.28) | collective-permute-done | bytes 131104 | tf_op jit(solution)/shard_map/ppermute | solution.py:218
  188.0 1.6 collective-permute-start.30
  190.3 4.7 %collective-permute-done.30.refs_1_ = f32[12,32,128]{2,1,0:T(8,128)S(1)} collective-permute-done((f32[12,32,128]{2,1,0:T(8,128)S(1)}, f32[12,32,128]{2,1,0:T(8,128)S(1)}, u32[]{:S(2)}, u32[]{:S(2)}) %collective-permute-start.30) | collective-permute-done | bytes 196640 | tf_op jit(solution)/shard_map/ppermute | solution.py:209
  (76 shorter events, 31.5 us)
Async XLA Ops:
  0.6 11.6 %copy-start = (f32[12,2,128,128]{3,2,1,0:T(8,128)S(1)}, f32[12,2,128,128]{3,2,1,0:T(8,128)}, u32[]{:S(2)}) copy-start(f32[12,2,128,128]{3,2,1,0:T(8,128)} %param.10) | copy-start | bytes 4718596
  0.6 11.6 %collective-permute-start.4 = (f32[24,128,128]{2,1,0:T(8,128)}, f32[24,128,128]{2,1,0:T(8,128)}, u32[]{:S(2)}, u32[]{:S(2)}) collective-permute-start(f32[24,128,128]{2,1,0:T(8,128)} %bitcast.8), channel_id=1, source_target_pairs={{0,1},{1,0},{2,3},{3,2},{4,5},{5,4},{6,7},{7,6},{8,9},{9,8},{10,11... | collective-permute-start | bytes 4718600 | tf_op jit(solution)/shard_map/ppermute | solution.py:209
  0.7 7.5 %collective-permute-start = (f32[3,128,128]{2,1,0:T(8,128)}, f32[3,128,128]{2,1,0:T(8,128)S(1)}, u32[]{:S(2)}, u32[]{:S(2)}) collective-permute-start(f32[3,128,128]{2,1,0:T(8,128)} %param.9), channel_id=1, source_target_pairs={{0,2},{1,3},{2,0},{3,1},{4,6},{5,7},{6,4},{7,5},{8,10},{9,11},{10,... | collective-permute-start | bytes 589832 | tf_op jit(solution)/shard_map/ppermute | solution.py:209
  8.3 3.1 %collective-permute-start.3 = (f32[6,128,128]{2,1,0:T(8,128)S(1)}, f32[6,128,128]{2,1,0:T(8,128)S(1)}, u32[]{:S(2)}, u32[]{:S(2)}) collective-permute-start(f32[6,128,128]{2,1,0:T(8,128)S(1)} %get-tuple-element.45.inverse), channel_id=1, source_target_pairs={{0,1},{1,0},{2,3},{3,2},{4,5},{5,4},{6,7},{7,6},{8,9},{9,8},{10,11... | collective-permute-start | bytes 1179656 | tf_op jit(solution)/shard_map/ppermute | solution.py:209
  10.9 1.3 collective-permute-start.2
  14.7 15.1 %collective-permute-start.5 = (f32[8,128,128]{2,1,0:T(8,128)S(1)}, f32[8,128,128]{2,1,0:T(8,128)S(1)}, u32[]{:S(2)}, u32[]{:S(2)}) collective-permute-start(f32[8,128,128]{2,1,0:T(8,128)S(1)} %shard_map.88), channel_id=1, source_target_pairs={{0,4},{1,9},{2,6},{3,11},{4,8},{5,13},{6,10},{7,15},{8,12},{9,17},... | collective-permute-start | bytes 1572872 | tf_op jit(solution)/shard_map/ppermute | solution.py:218
  19.8 14.5 %copy-start.2 = (f32[3,128,128]{2,1,0:T(8,128)S(1)}, f32[3,128,128]{2,1,0:T(8,128)}, u32[]{:S(2)}) copy-start(f32[3,128,128]{2,1,0:T(8,128)} %param.8) | copy-start | bytes 589828
  30.8 1.8 collective-permute-start.6
  32.7 15.5 %collective-permute-start.7 = (f32[6,128,128]{2,1,0:T(8,128)S(1)}, f32[6,128,128]{2,1,0:T(8,128)S(1)}, u32[]{:S(2)}, u32[]{:S(2)}) collective-permute-start(f32[6,128,128]{2,1,0:T(8,128)S(1)} %add.30), channel_id=1, source_target_pairs={{0,2},{1,3},{2,0},{3,1},{4,6},{5,7},{6,4},{7,5},{8,10},{9,11},{10,... | collective-permute-start | bytes 1179656 | tf_op jit(solution)/shard_map/ppermute | solution.py:209
  34.3 13.8 %collective-permute-start.1 = (f32[3,128,128]{2,1,0:T(8,128)S(1)}, f32[3,128,128]{2,1,0:T(8,128)S(1)}, u32[]{:S(2)}, u32[]{:S(2)}) collective-permute-start(f32[3,128,128]{2,1,0:T(8,128)S(1)} %copy-done.2), channel_id=1, source_target_pairs={{0,2},{1,3},{2,0},{3,1},{4,6},{5,7},{6,4},{7,5},{8,10},{9,11},{10,... | collective-permute-start | bytes 589832 | tf_op jit(solution)/shard_map/ppermute | solution.py:209
  48.8 1.8 collective-permute-start.8
  51.5 14.9 %collective-permute-start.9 = (f32[8,128,128]{2,1,0:T(8,128)S(1)}, f32[8,128,128]{2,1,0:T(8,128)S(1)}, u32[]{:S(2)}, u32[]{:S(2)}) collective-permute-start(f32[8,128,128]{2,1,0:T(8,128)S(1)} %shard_map.92), channel_id=1, source_target_pairs={{0,4},{1,9},{2,6},{3,11},{4,8},{5,13},{6,10},{7,15},{8,12},{9,17},... | collective-permute-start | bytes 1572872 | tf_op jit(solution)/shard_map/ppermute | solution.py:218
  67.5 1.8 collective-permute-start.10
  69.3 11.2 %collective-permute-start.11 = (f32[6,128,128]{2,1,0:T(8,128)S(1)}, f32[6,128,128]{2,1,0:T(8,128)S(1)}, u32[]{:S(2)}, u32[]{:S(2)}) collective-permute-start(f32[6,128,128]{2,1,0:T(8,128)S(1)} %add.32), channel_id=1, source_target_pairs={{0,2},{1,3},{2,0},{3,1},{4,6},{5,7},{6,4},{7,5},{8,10},{9,11},{10,... | collective-permute-start | bytes 1179656 | tf_op jit(solution)/shard_map/ppermute | solution.py:209
  80.6 2.4 %copy-start.1 = (f32[12,32,128]{2,1,0:T(8,128)S(1)}, f32[12,32,128]{2,1,0:T(8,128)}, u32[]{:S(2)}) copy-start(f32[12,32,128]{2,1,0:T(8,128)} %base.7) | copy-start | bytes 589828
  81.1 1.8 collective-permute-start.12
  84.5 7.8 %collective-permute-start.13 = (f32[8,32,128]{2,1,0:T(8,128)S(1)}, f32[8,32,128]{2,1,0:T(8,128)S(1)}, u32[]{:S(2)}, u32[]{:S(2)}) collective-permute-start(f32[8,32,128]{2,1,0:T(8,128)S(1)} %get-tuple-element.28), channel_id=1, source_target_pairs={{0,4},{1,9},{2,6},{3,11},{4,8},{5,13},{6,10},{7,15},{8,12},{9,17},... | collective-permute-start | bytes 393224 | tf_op jit(solution)/shard_map/ppermute | solution.py:218
  93.1 1.5 collective-permute-start.14
  94.7 7.0 %collective-permute-start.15 = (f32[12,32,128]{2,1,0:T(8,128)S(1)}, f32[12,32,128]{2,1,0:T(8,128)S(1)}, u32[]{:S(2)}, u32[]{:S(2)}) collective-permute-start(f32[12,32,128]{2,1,0:T(8,128)S(1)} %add.34.refs_0_), channel_id=1, source_target_pairs={{0,2},{1,3},{2,0},{3,1},{4,6},{5,7},{6,4},{7,5},{8,10},{9,11},{10,... | collective-permute-start | bytes 589832 | tf_op jit(solution)/shard_map/ppermute | solution.py:209
  103.2 7.7 %collective-permute-start.16 = (f32[8,32,128]{2,1,0:T(8,128)S(1)}, f32[8,32,128]{2,1,0:T(8,128)S(1)}, u32[]{:S(2)}, u32[]{:S(2)}) collective-permute-start(f32[8,32,128]{2,1,0:T(8,128)S(1)} %get-tuple-element.30), channel_id=1, source_target_pairs={{0,4},{1,9},{2,6},{3,11},{4,8},{5,13},{6,10},{7,15},{8,12},{9,17},... | collective-permute-start | bytes 393224 | tf_op jit(solution)/shard_map/ppermute | solution.py:218
  111.8 1.5 collective-permute-start.17
  113.3 7.0 %collective-permute-start.18 = (f32[12,32,128]{2,1,0:T(8,128)S(1)}, f32[12,32,128]{2,1,0:T(8,128)S(1)}, u32[]{:S(2)}, u32[]{:S(2)}) collective-permute-start(f32[12,32,128]{2,1,0:T(8,128)S(1)} %add.35.refs_0_), channel_id=1, source_target_pairs={{0,2},{1,3},{2,0},{3,1},{4,6},{5,7},{6,4},{7,5},{8,10},{9,11},{10,... | collective-permute-start | bytes 589832 | tf_op jit(solution)/shard_map/ppermute | solution.py:209
  121.8 7.7 %collective-permute-start.19 = (f32[8,32,128]{2,1,0:T(8,128)S(1)}, f32[8,32,128]{2,1,0:T(8,128)S(1)}, u32[]{:S(2)}, u32[]{:S(2)}) collective-permute-start(f32[8,32,128]{2,1,0:T(8,128)S(1)} %get-tuple-element.32), channel_id=1, source_target_pairs={{0,4},{1,9},{2,6},{3,11},{4,8},{5,13},{6,10},{7,15},{8,12},{9,17},... | collective-permute-start | bytes 393224 | tf_op jit(solution)/shard_map/ppermute | solution.py:218
  130.4 1.5 collective-permute-start.20
  131.9 7.0 %collective-permute-start.21 = (f32[12,32,128]{2,1,0:T(8,128)S(1)}, f32[12,32,128]{2,1,0:T(8,128)S(1)}, u32[]{:S(2)}, u32[]{:S(2)}) collective-permute-start(f32[12,32,128]{2,1,0:T(8,128)S(1)} %add.36.refs_0_), channel_id=1, source_target_pairs={{0,2},{1,3},{2,0},{3,1},{4,6},{5,7},{6,4},{7,5},{8,10},{9,11},{10,... | collective-permute-start | bytes 589832 | tf_op jit(solution)/shard_map/ppermute | solution.py:209
  139.9 8.4 %collective-permute-start.22 = (f32[8,32,128]{2,1,0:T(8,128)S(1)}, f32[8,32,128]{2,1,0:T(8,128)S(1)}, u32[]{:S(2)}, u32[]{:S(2)}) collective-permute-start(f32[8,32,128]{2,1,0:T(8,128)S(1)} %get-tuple-element.35), channel_id=1, source_target_pairs={{4,0},{6,2},{8,4},{9,1},{10,6},{11,3},{12,8},{13,5},{14,10},{15,7}... | collective-permute-start | bytes 393224 | tf_op jit(solution)/shard_map/ppermute | solution.py:218
  149.2 1.5 collective-permute-start.23
  150.7 7.0 %collective-permute-start.24 = (f32[12,32,128]{2,1,0:T(8,128)S(1)}, f32[12,32,128]{2,1,0:T(8,128)S(1)}, u32[]{:S(2)}, u32[]{:S(2)}) collective-permute-start(f32[12,32,128]{2,1,0:T(8,128)S(1)} %add.37.refs_0_), channel_id=1, source_target_pairs={{0,2},{1,3},{2,0},{3,1},{4,6},{5,7},{6,4},{7,5},{8,10},{9,11},{10,... | collective-permute-start | bytes 589832 | tf_op jit(solution)/shard_map/ppermute | solution.py:209
  159.2 7.7 %collective-permute-start.25 = (f32[8,32,128]{2,1,0:T(8,128)S(1)}, f32[8,32,128]{2,1,0:T(8,128)S(1)}, u32[]{:S(2)}, u32[]{:S(2)}) collective-permute-start(f32[8,32,128]{2,1,0:T(8,128)S(1)} %get-tuple-element.37), channel_id=1, source_target_pairs={{4,0},{6,2},{8,4},{9,1},{10,6},{11,3},{12,8},{13,5},{14,10},{15,7}... | collective-permute-start | bytes 393224 | tf_op jit(solution)/shard_map/ppermute | solution.py:218
  167.8 1.5 collective-permute-start.26
  169.3 7.0 %collective-permute-start.27 = (f32[12,32,128]{2,1,0:T(8,128)S(1)}, f32[12,32,128]{2,1,0:T(8,128)S(1)}, u32[]{:S(2)}, u32[]{:S(2)}) collective-permute-start(f32[12,32,128]{2,1,0:T(8,128)S(1)} %add.38.refs_0_), channel_id=1, source_target_pairs={{0,2},{1,3},{2,0},{3,1},{4,6},{5,7},{6,4},{7,5},{8,10},{9,11},{10,... | collective-permute-start | bytes 589832 | tf_op jit(solution)/shard_map/ppermute | solution.py:209
  177.8 7.7 %collective-permute-start.28 = (f32[8,32,128]{2,1,0:T(8,128)S(1)}, f32[8,32,128]{2,1,0:T(8,128)S(1)}, u32[]{:S(2)}, u32[]{:S(2)}) collective-permute-start(f32[8,32,128]{2,1,0:T(8,128)S(1)} %get-tuple-element.39), channel_id=1, source_target_pairs={{4,0},{6,2},{8,4},{9,1},{10,6},{11,3},{12,8},{13,5},{14,10},{15,7}... | collective-permute-start | bytes 393224 | tf_op jit(solution)/shard_map/ppermute | solution.py:218
  186.4 1.5 collective-permute-start.29
  188.0 7.0 %collective-permute-start.30 = (f32[12,32,128]{2,1,0:T(8,128)S(1)}, f32[12,32,128]{2,1,0:T(8,128)S(1)}, u32[]{:S(2)}, u32[]{:S(2)}) collective-permute-start(f32[12,32,128]{2,1,0:T(8,128)S(1)} %add.39.refs_0_), channel_id=1, source_target_pairs={{0,2},{1,3},{2,0},{3,1},{4,6},{5,7},{6,4},{7,5},{8,10},{9,11},{10,... | collective-permute-start | bytes 589832 | tf_op jit(solution)/shard_map/ppermute | solution.py:209

commit v2 on v1

v2 whole, which is shorter than its diff:
```python
import functools

import jax
import jax.numpy as jnp
from jax import lax
from jax.experimental import pallas as pl
from jax.experimental.pallas import tpu as pltpu
from jax.sharding import PartitionSpec as P

FSWEEPS = 2
LSWEEPS = 3
USWEEPS = 3
F32 = jnp.float32
BF16 = jnp.bfloat16


def split(a):
    hi = a.astype(BF16)
    return hi, (a - hi.astype(F32)).astype(BF16)


def matmul_parts(ah, al, bh, bl):
    lhs = jnp.concatenate([ah, al], 1)
    pair = jnp.concatenate([bh, bl], 1)
    rhs = jnp.concatenate([pair, pair], 0)
    out = jnp.dot(lhs, rhs, preferred_element_type=F32)
    n = bh.shape[1]
    return out[:, :n] + out[:, n:]


def matmul(a, b):
    return matmul_parts(*split(a), *split(b))


def times_tile(x, wide):
    v, n = x.shape
    stacked = jnp.concatenate(split(x), 0)
    out = lax.dot_general(stacked, wide, (((1,), (1,)), ((), ())), preferred_element_type=F32)
    return out[:v, :n] + (out[v:, :n] + out[:v, n:])


def widen(a):
    return jnp.concatenate(split(a), 0)


class Layout:
    def __init__(self, rows, width, cap, n_tile):
        self.rows, self.width, self.cap, self.n_tile = rows, width, cap, n_tile
        self.slots = rows * width
        self.own_rows = rows // n_tile
        self.n_link = self.slots
        self.n_send = 2 * self.slots
        self.listed_slots = n_tile * cap
        self.pairs = self.slots // 2
        self.usual = min(self.pairs, max(1, (self.slots - 4 * cap) // 2))
        self.table = 3 * self.listed_slots + n_tile * self.pairs + n_tile // 2

    def kind(self, meta, s):
        return meta[s]

    def link(self, meta, s):
        return meta[self.n_link + s]

    def listed(self, meta, which, j):
        return meta[self.n_send + which * self.cap + j]

    def place(self, r, me):
        far = (r // self.own_rows) ^ me
        return ((far & 1) * (self.n_tile // 2) + (far >> 1)) * self.own_rows + r % self.own_rows

    def lookup(self, meta, role, base_list, side, j):
        s = self.listed(meta, base_list + role, j)
        v = self.link(meta, s) - self.slots - role * self.cap
        live = (self.kind(meta, s) == side) & (v >= 0) & (v < self.cap)
        return s, s // self.width, live, jnp.clip(v, 0, self.cap - 1)


def smem():
    return pl.BlockSpec(memory_space=pltpu.SMEM)


def vmem():
    return pl.BlockSpec(memory_space=pltpu.VMEM)


def call(body, outs, scalars, arrays, flops=0, scratch=(), early=()):
    moved = sum(a.size * a.dtype.itemsize for a in arrays) + sum(o.size * o.dtype.itemsize for o in outs)
    return pl.pallas_call(
        body if not early else lambda *refs: body(*refs[len(early) :]),
        out_shape=outs,
        in_specs=[pl.BlockSpec(memory_space=pl.ANY)] * len(early) + [smem()] * len(scalars) + [vmem()] * len(arrays),
        out_specs=[vmem()] * len(outs),
        scratch_shapes=list(scratch),
        compiler_params=pltpu.CompilerParams(vmem_limit_bytes=8 << 20),
        cost_estimate=pl.CostEstimate(flops=flops, bytes_accessed=moved, transcendentals=0),
    )(*early, *scalars, *arrays)


def outgoing_kernel(lay, me, mine, mates, inverse, tiles, mate_tiles, out):
    role = me[0] % 2
    for g, (meta, source) in enumerate(((mine, tiles), (mates, mate_tiles))):
        for j in range(lay.cap):
            s, r, live, _ = lay.lookup(meta, role, 0, 2, j)
            out[g * lay.cap + j] = matmul(inverse[lay.place(r, me[0])], jnp.where(live, source[s], 0.0))


def local_pivot_kernel(lay, me, mine, inverse, diag, tiles, out):
    out[: lay.own_rows] = -diag[...]
    out[lay.own_rows :] = jnp.zeros((lay.rows - lay.own_rows,) + diag.shape[1:], F32)

    @pl.loop(0, lay.slots)
    def _(s):
        v = lay.link(mine, s)

        @pl.when((lay.kind(mine, s) == 1) & (v < lay.slots))
        def _():
            q = matmul(inverse[lay.place(v // lay.width, me[0])], tiles[v])
            out[lay.place(s // lay.width, me[0])] += matmul(tiles[s], q)


def incoming_kernel(lay, me, mine, mates, local, tiles, mate_tiles, arrived, keep, give, total):
    role = me[0] % 2
    places, terms = [], []
    for g, (meta, source) in enumerate(((mine, tiles), (mates, mate_tiles))):
        for j in range(lay.cap):
            s, r, live, v = lay.lookup(meta, role, 2, 1, j)
            places.append(lay.place(r, me[0]))
            terms.append(matmul(jnp.where(live, source[s], 0.0), arrived[g * lay.cap + v]))
    total[...] = local[...]
    for place, term in zip(places, terms):
        total[place] += term
    half = keep.shape[0]
    keep[...] = total[:half]
    give[...] = total[half:]


def newton_kernel(inverse, sums, out):
    for i in range(out.shape[0]):
        x = inverse[i]
        xh, xl = split(x)
        product = matmul_parts(xh, xl, *split(sums[i]))
        out[i] = 2.0 * x + matmul_parts(*split(product), xh, xl)


def table_kernel(lay, me, metas, peers_below, peers_above, out):
    role = me[0] % 2
    for side in (1, 2):
        start = (side - 1) * lay.table
        base, peers = ((2, peers_below), (0, peers_above))[side - 1]
        for q in range(lay.n_tile):
            a, meta, peer = q ^ me[0], metas.at[q], peers.at[q]
            for j in range(lay.cap):
                s, _, live, v = lay.lookup(meta, role, base, side, j)
                k = start + a * lay.cap + j
                out[k] = s
                out[lay.listed_slots + k] = live.astype(jnp.int32)
                out[2 * lay.listed_slots + k] = lay.listed(peer, 2 - base + role, v) // lay.width
        for q in range(0, lay.n_tile, 2):
            meta, a = metas.at[q], (q ^ me[0]) >> 1
            begin = start + 3 * lay.listed_slots + a * (2 * lay.pairs)
            for i in range(2 * lay.pairs):
                out[begin + i] = 0

            def step(s, count, meta=meta, begin=begin, side=side):
                v = lay.link(meta, s)
                found = (lay.kind(meta, s) == side) & (v < lay.slots)

                @pl.when(found)
                def _():
                    out[begin + count] = s
                    out[begin + lay.pairs + count] = v // lay.width

                return count + found.astype(jnp.int32)

            out[start + 3 * lay.listed_slots + lay.n_tile * lay.pairs + a] = lax.fori_loop(0, lay.slots, step, 0)


def scaled_kernel(lay, side, pieces, me, table, inverse, *refs):
    sources, (listed, local) = refs[:-2], refs[-2:]
    groups, at = [], 0
    for count in pieces:
        groups.append(sources[at : at + count])
        at += count
    start = (side - 1) * lay.table

    def scaled(q, s, live):
        tile = jnp.concatenate([ref[s] for ref in groups[q]], 0)
        return widen(matmul(inverse[lay.place(s // lay.width, me[0])], jnp.where(live, tile, 0.0)))

    for q in range(lay.n_tile):
        for j in range(lay.cap):
            k = (q ^ me[0]) * lay.cap + j
            listed[k] = scaled(q, table[start + k], table[start + lay.listed_slots + k] != 0)
    for q in range(0, lay.n_tile, 2):
        a = (q ^ me[0]) >> 1
        begin = start + 3 * lay.listed_slots + a * (2 * lay.pairs)
        count = table[start + 3 * lay.listed_slots + lay.n_tile * lay.pairs + a]
        for i in range(lay.usual):
            local[a * lay.pairs + i] = scaled(q, table[begin + i], i < count)

        @pl.loop(lay.usual, count)
        def _(i, q=q, a=a, begin=begin):
            local[a * lay.pairs + i] = scaled(q, table[begin + i], True)


def first_kernel(lay, me, base, inverse, out):
    for r in range(lay.rows):
        out[r] = times_tile(base[r], widen(inverse[lay.place(r, me[0])]))


def local_sum_kernel(lay, side, table, x, tiles, out):
    start = (side - 1) * lay.table + 3 * lay.listed_slots
    groups = lay.n_tile // 2

    def term(a, i):
        return times_tile(x[table[start + a * (2 * lay.pairs) + lay.pairs + i]], tiles[a * lay.pairs + i])

    def row(a, i):
        return table[start + a * (2 * lay.pairs) + i] // lay.width

    usual = [(a, i) for a in range(groups) for i in range(lay.usual)]
    terms = [term(a, i) for a, i in usual]
    out[...] = jnp.zeros_like(out)
    for (a, i), value in zip(usual, terms):
        out[row(a, i)] += value
    for a in range(groups):

        @pl.loop(lay.usual, table[start + lay.n_tile * lay.pairs + a])
        def _(i, a=a):
            out[row(a, i)] += term(a, i)


def listed_sum_kernel(lay, side, table, local, tiles, arrived, out):
    start = (side - 1) * lay.table
    terms = [
        times_tile(arrived[table[start + 2 * lay.listed_slots + k]], tiles[k]) for k in range(lay.listed_slots)
    ]
    out[...] = local[...]
    for k, value in enumerate(terms):
        out[table[start + k] // lay.width] += value


def local(krylov_block, diag_block, inverse_prev, coupling_tiles, slot_kind, slot_link, send_slots):
    rows, width, n, _ = coupling_tiles.shape
    cap = send_slots.shape[3]
    n_dom, n_tile = lax.axis_size("dom"), lax.axis_size("tile")
    lay = Layout(rows, width, cap, n_tile)
    vectors = krylov_block.shape[1]
    upper_bits = [1 << b for b in range(1, n_tile.bit_length() - 1)]

    me = lax.axis_index("tile").astype(jnp.int32).reshape(1)
    mine = jnp.concatenate([slot_kind.reshape(-1), slot_link.reshape(-1), send_slots.reshape(-1)])
    tiles = coupling_tiles.reshape(lay.slots, n, n)

    def swap(x, bit):
        return lax.ppermute(x, "tile", [(i, i ^ bit) for i in range(n_tile)])

    def along(x, sign):
        route = []
        for d in range(n_dom):
            for t in range(n_tile):
                to = d + sign * (1 + t % 2)
                if 0 <= to < n_dom:
                    route.append((d * n_tile + t, to * n_tile + t))
        return lax.ppermute(x, ("dom", "tile"), route)

    def spread(x):
        for bit in upper_bits:
            x = jnp.concatenate([x, swap(x, bit)], 0)
        return x

    def summed(x):
        for bit in upper_bits:
            got = swap(x, bit)
            near = bit // 2
            got = got.reshape((n_tile // 2 // (2 * near), 2, near * lay.own_rows) + x.shape[1:])
            x = x + jnp.concatenate([got[:, 1:], got[:, :1]], 1).reshape(x.shape)
        return x

    def after(x, *others):
        return lax.optimization_barrier((x, others))[0]

    def shape(*dims, dtype=F32):
        return jax.ShapeDtypeStruct(dims, dtype)

    kernel = lambda body, *bound: functools.partial(body, lay, *bound)
    product = 8 * n**3

    mate_tiles = swap(tiles, 1)
    arriving = spread(inverse_prev)
    mates = swap(mine, 1)
    kept, mine, mates = lax.optimization_barrier((arriving, mine, mates))
    half = rows // 2
    cuts = [slice(i * n // FSWEEPS, (i + 1) * n // FSWEEPS) for i in range(FSWEEPS)]
    metas = jnp.stack([mine, mates])
    far_tiles, far_mate_tiles = [], []
    for sweep in range(FSWEEPS):
        inverse = jnp.concatenate([kept, swap(kept, 1)], 0)
        (out,) = call(
            kernel(outgoing_kernel), [shape(2 * cap, n, n)], (me, mine, mates), (inverse, tiles, mate_tiles)
        )
        arrived = along(out, 1)
        (here,) = call(
            kernel(local_pivot_kernel),
            [shape(rows, n, n)],
            (me, mine),
            (inverse, diag_block, tiles),
            flops=product * rows,
        )
        part = [tiles[:, cuts[sweep]]]
        for bit in upper_bits:
            part += [swap(x, bit) for x in part]
        far_tiles.append(part[1:])
        early = list(part[1:])
        if sweep == 0:
            for bit in upper_bits:
                metas = jnp.concatenate([metas, swap(metas, bit)], 0)
            early.append(metas)
        if sweep == FSWEEPS - 1:
            below, above = along(metas, 1), along(metas, -1)
            table = pl.pallas_call(
                kernel(table_kernel),
                out_shape=shape(2 * lay.table, dtype=jnp.int32),
                in_specs=[smem()] * 4,
                out_specs=smem(),
            )(me, metas, below, above)
            early.append(table)
        keep, give = call(
            kernel(incoming_kernel),
            [shape(half, n, n)] * 2,
            (me, mine, mates),
            (here, tiles, mate_tiles, arrived),
            scratch=(pltpu.VMEM((rows, n, n), F32),),
            early=early,
        )
        sums = summed(keep + swap(give, 1))
        far_mate_tiles.append([swap(x, 1) for x in part[1:]])
        (kept,) = call(newton_kernel, [shape(half, n, n)], (), (kept, sums), early=far_mate_tiles[-1])
    inverse = jnp.concatenate([kept, swap(kept, 1)], 0)

    groups = [[tiles], [mate_tiles]]
    for i in range(n_tile // 2 - 1):
        groups += [[part[i] for part in far_tiles], [part[i] for part in far_mate_tiles]]
    flat = [x for group in groups for x in group]

    def scale(side):
        return call(
            kernel(scaled_kernel, side, [len(group) for group in groups]),
            [
                shape(lay.listed_slots, 2 * n, n, dtype=BF16),
                shape(n_tile // 2 * lay.pairs, 2 * n, n, dtype=BF16),
            ],
            (me, table),
            (inverse, *flat),
            flops=product * 24,
        )

    block = shape(rows, vectors, n)
    (first,) = call(kernel(first_kernel), [block], (me,), (krylov_block, inverse))

    def sweeps(x, side, count, listed, local):
        base = x
        for _ in range(count):
            arrived = along(x, 1 if side == 1 else -1)
            (here,) = call(
                kernel(local_sum_kernel, side), [block], (table,), (x, local), flops=8 * n**2 * vectors * rows
            )
            (part,) = call(kernel(listed_sum_kernel, side), [block], (table,), (here, listed, arrived))
            x = base - (part + swap(part, 1))
        return x

    lower, upper = scale(1), scale(2)
    solved = sweeps(sweeps(first, 1, LSWEEPS, *lower), 2, USWEEPS, *upper)
    return (kept[: lay.own_rows], solved)


def solution(mesh):
    placed = (
        P("dom", None, None),
        P(("dom", "tile"), None, None),
        P(("dom", "tile"), None, None),
        P("dom", "tile", None, None),
        P("dom", "tile"),
        P("dom", "tile"),
        P("dom", "tile", None, None),
    )
    return jax.shard_map(
        local,
        mesh=mesh,
        in_specs=placed,
        out_specs=(P(("dom", "tile"), None, None), P("dom", None, None)),
        check_vma=False,
    )
```

time: 196 us -> 163 us (0.83)
  waiting for transfers between devices: 110 us -> 72.8 us
  local copies, waits for them, and re-layouts: 4.3 us -> 9.3 us
    ppermute x23 -> x21, waiting for transfers between devices: 75.8 us -> 48 us  [swap(): return lax.ppermute(x, 'tile', [(i, i ^ bit) for i in range(n_tile)])]
    ppermute x8 -> x10, waiting for transfers between devices: 34.1 us -> 24.8 us  [along(): return lax.ppermute(x, ('dom', 'tile'), route)]
    ppermute x23 -> x21, starting transfers between devices: 16.3 us -> 11.5 us  [swap(): return lax.ppermute(x, 'tile', [(i, i ^ bit) for i in range(n_tile)])]
    ppermute x8 -> x10, starting transfers between devices: 33.4 us -> 36.3 us  [along(): return lax.ppermute(x, ('dom', 'tile'), route)]
    slice x3 -> x4, local copies, waits for them, and re-layouts: 0.74 us -> 3.46 us  [the longest x1 2.72 us: local(): part = [tiles[:, cuts[sweep]]]]
    pallas_call x28 -> x24, Pallas kernels: 30.5 us -> 28.8 us  [the longest x23 25.8 us: call(): pl.pallas_call(body if not early else lambda *refs: body(*refs[len(early)...]
  transfers between devices with their start and end apart: 31 -> 31, of which waited for: 28 -> 19; matrix products, arithmetic and copies ran while one was open for 2% -> 5% of each run, Pallas kernels for 5% -> 12%
where the time goes in v2:
time: 163 us; the launch traced here: 162 us
  waiting for transfers between devices  72.8 us (45%)
  starting transfers between devices  47.8 us (29%)
  Pallas kernels  28.8 us (18%)
  local copies, waits for them, and re-layouts  9.3 us (6%)
  other arithmetic  2.39 us (1%)
    ppermute x21, waiting for transfers between devices, swap(): return lax.ppermute(x, 'tile', [(i, i ^ bit) for i in range(n_tile)])  48 us
    ppermute x10, starting transfers between devices, along(): return lax.ppermute(x, ('dom', 'tile'), route)  36.3 us
    pallas_call x23, Pallas kernels, call(): pl.pallas_call(body if not early else lambda *refs: body(*refs[len(early)...  25.8 us
    ppermute x10, waiting for transfers between devices, along(): return lax.ppermute(x, ('dom', 'tile'), route)  24.8 us
    ppermute x21, starting transfers between devices, swap(): return lax.ppermute(x, 'tile', [(i, i ^ bit) for i in range(n_tile)])  11.5 us
    unnamed x31, local copies, waits for them, and re-layouts  3.89 us
  transfers between devices with their start and end apart: 31, of which 19 were waited for; matrix products, arithmetic and copies ran while one was open for 5% of the time, Pallas kernels for 12%

profile of v2, /device:TPU:18, one launch (start us, length us, event | category | flops | bytes accessed | tf_op | source)
XLA Modules:
  0.0 162.4 jit_solution(1917403441753664836)
XLA Ops:
  0.7 1.6 collective-permute-start.4
  5.0 3.2 %collective-permute-done.4 = f32[3,128,128]{2,1,0:T(8,128)S(1)} collective-permute-done((f32[3,128,128]{2,1,0:T(8,128)}, f32[3,128,128]{2,1,0:T(8,128)S(1)}, u32[]{:S(2)}, u32[]{:S(2)}) %collective-permute-start.4) | collective-permute-done | bytes 196640 | tf_op jit(solution)/shard_map/ppermute | solution.py:256
  9.3 2.7 %fusion = (f32[24,64,128]{2,1,0:T(8,128)}, f32[24,64,128]{2,1,0:T(8,128)}) fusion(f32[24,128,128]{2,1,0:T(8,128)} %bitcast.11), kind=kLoop, calls=%fused_computation.18 | loop fusion | bytes 3145728 | tf_op jit(solution)/shard_map/slice | solution.py:310
  12.0 1.5 collective-permute-start.2
  15.5 3.5 %collective-permute-start.9 = (f32[8,128,128]{2,1,0:T(8,128)S(1)}, f32[8,128,128]{2,1,0:T(8,128)S(1)}, u32[]{:S(2)}, u32[]{:S(2)}) collective-permute-start(f32[8,128,128]{2,1,0:T(8,128)S(1)} %shard_map.87), channel_id=1, source_target_pairs={{0,4},{1,9},{2,6},{3,11},{4,8},{5,13},{6,10},{7,15},{8,12},{9,17},... | collective-permute-start | bytes 1572872 | tf_op jit(solution)/shard_map/ppermute | solution.py:265
  19.6 12.7 %collective-permute-done.6 = s32[2,64]{1,0:T(2,128)S(1)} collective-permute-done((s32[2,64]{1,0:T(2,128)S(1)}, s32[2,64]{1,0:T(2,128)S(1)}, u32[]{:S(2)}, u32[]{:S(2)}) %collective-permute-start.6) | collective-permute-done | bytes 544 | tf_op jit(solution)/shard_map/ppermute | solution.py:256
  32.3 1.6 %shard_map.86.refs_5_ = f32[12,128,128]{2,1,0:T(8,128)S(1)} custom-call(s32[1]{0:T(128)} %bitcast.3.me.refs_2_, s32[64]{0:T(128)S(1)} %pad_add_fusion.2.mine.refs_3_, f32[12,128,128]{2,1,0:T(8,128)S(1)} %constant_dynamic-update-slice_fusion.inverse, f32[3,128,128]{2,1,0:T(8,128)S(1)} %copy-done.7, f32[24,128,128]{2,1,0:T(8,128)S(1)} %bitcast.13), custom_call_target="tpu_custom_call" | custom-call | flops 201326592 | bytes 3342336 | tf_op jit(solution)/shard_map/pallas_call | solution.py:88
  34.0 1.1 shard_map.88
  35.2 1.7 %collective-permute-done.10 = f32[6,128,128]{2,1,0:T(8,128)S(1)} collective-permute-done((f32[6,128,128]{2,1,0:T(8,128)S(1)}, f32[6,128,128]{2,1,0:T(8,128)S(1)}, u32[]{:S(2)}, u32[]{:S(2)}) %collective-permute-start.10) | collective-permute-done | bytes 393248 | tf_op jit(solution)/shard_map/ppermute | solution.py:256
  36.9 2.3 %collective-permute-start.11 = (f32[6,128,128]{2,1,0:T(8,128)S(1)}, f32[6,128,128]{2,1,0:T(8,128)S(1)}, u32[]{:S(2)}, u32[]{:S(2)}) collective-permute-start(f32[6,128,128]{2,1,0:T(8,128)S(1)} %add.30), channel_id=1, source_target_pairs={{0,2},{1,3},{2,0},{3,1},{4,6},{5,7},{6,4},{7,5},{8,10},{9,11},{10,... | collective-permute-start | bytes 1179656 | tf_op jit(solution)/shard_map/ppermute | solution.py:256
  39.2 9.4 %collective-permute-done.11 = f32[6,128,128]{2,1,0:T(8,128)S(1)} collective-permute-done((f32[6,128,128]{2,1,0:T(8,128)S(1)}, f32[6,128,128]{2,1,0:T(8,128)S(1)}, u32[]{:S(2)}, u32[]{:S(2)}) %collective-permute-start.11) | collective-permute-done | bytes 393248 | tf_op jit(solution)/shard_map/ppermute | solution.py:256
  49.3 1.8 %collective-permute-start = (f32[24,64,128]{2,1,0:T(8,128)}, f32[24,64,128]{2,1,0:T(8,128)}, u32[]{:S(2)}, u32[]{:S(2)}) collective-permute-start(f32[24,64,128]{2,1,0:T(8,128)} %get-tuple-element.25), channel_id=1, source_target_pairs={{0,2},{1,3},{2,0},{3,1},{4,6},{5,7},{6,4},{7,5},{8,10},{9,11},{10,... | collective-permute-start | bytes 2359304 | tf_op jit(solution)/shard_map/ppermute | solution.py:256
  51.2 1.7 %shard_map.92 = f32[8,128,128]{2,1,0:T(8,128)} custom-call(s32[1]{0:T(128)} %bitcast.3.me.refs_2_, s32[64]{0:T(128)S(1)} %pad_add_fusion.2.mine.refs_3_, s32[64]{0:T(128)S(1)} %collective-permute-done.5.mates.refs_4_, f32[12,128,128]{2,1,0:T(8,128)S(1)} %pad_maximum_fusion.inverse, f32[24,128,128]{2,1,0:T(8,128)S(1)} %bitcast.15, ...), custom_call_target="tpu_custom_call" | custom-call | bytes 4456448 | tf_op jit(solution)/shard_map/pallas_call | solution.py:88
  52.9 3.6 %collective-permute-start.15 = (f32[8,128,128]{2,1,0:T(8,128)}, f32[8,128,128]{2,1,0:T(8,128)}, u32[]{:S(2)}, u32[]{:S(2)}) collective-permute-start(f32[8,128,128]{2,1,0:T(8,128)} %shard_map.92), channel_id=1, source_target_pairs={{0,4},{1,9},{2,6},{3,11},{4,8},{5,13},{6,10},{7,15},{8,12},{9,17},... | collective-permute-start | bytes 1572872 | tf_op jit(solution)/shard_map/ppermute | solution.py:265
  56.5 3.1 %collective-permute-start.12 = (s32[4,64]{1,0:T(4,128)S(1)}, s32[4,64]{1,0:T(4,128)S(1)}, u32[]{:S(2)}, u32[]{:S(2)}) collective-permute-start(s32[4,64]{1,0:T(4,128)S(1)} %pad_add_fusion.refs_1_.metas), channel_id=1, source_target_pairs={{0,4},{1,9},{2,6},{3,11},{4,8},{5,13},{6,10},{7,15},{8,12},{9,17},... | collective-permute-start | bytes 3080 | tf_op jit(solution)/shard_map/ppermute | solution.py:265
  59.5 2.8 %collective-permute-start.13 = (s32[4,64]{1,0:T(4,128)S(1)}, s32[4,64]{1,0:T(4,128)S(1)}, u32[]{:S(2)}, u32[]{:S(2)}) collective-permute-start(s32[4,64]{1,0:T(4,128)S(1)} %pad_add_fusion.refs_1_.metas), channel_id=1, source_target_pairs={{4,0},{6,2},{8,4},{9,1},{10,6},{11,3},{12,8},{13,5},{14,10},{15,7}... | collective-permute-start | bytes 3080 | tf_op jit(solution)/shard_map/ppermute | solution.py:265
  62.3 5.6 %collective-permute-done.12.peers_below = s32[4,64]{1,0:T(4,128)S(1)} collective-permute-done((s32[4,64]{1,0:T(4,128)S(1)}, s32[4,64]{1,0:T(4,128)S(1)}, u32[]{:S(2)}, u32[]{:S(2)}) %collective-permute-start.12) | collective-permute-done | bytes 1056 | tf_op jit(solution)/shard_map/ppermute | solution.py:265
  69.1 3.1 %shard_map.90.refs_1_.table = s32[196]{0:T(256)} custom-call(s32[1]{0:T(128)} %bitcast.3.me.refs_2_, s32[4,64]{1,0:T(4,128)} %copy-done.11, s32[4,64]{1,0:T(4,128)} %copy-done.12, s32[4,64]{1,0:T(4,128)} %copy-done.13), custom_call_target="tpu_custom_call" | custom-call | tf_op jit(solution)/shard_map/pallas_call | solution.py:321
  72.2 1.1 copy-done.2
  73.3 1.6 %shard_map.91.refs_5_ = f32[12,128,128]{2,1,0:T(8,128)S(1)} custom-call(s32[1]{0:T(128)} %bitcast.3.me.refs_2_, s32[64]{0:T(128)S(1)} %pad_add_fusion.2.mine.refs_3_, f32[12,128,128]{2,1,0:T(8,128)S(1)} %copy-done.2, f32[3,128,128]{2,1,0:T(8,128)S(1)} %copy-done.8, f32[24,128,128]{2,1,0:T(8,128)S(1)} %bitcast.16), custom_call_target="tpu_custom_call" | custom-call | flops 201326592 | bytes 3342336 | tf_op jit(solution)/shard_map/pallas_call | solution.py:88
  75.0 1.6 shard_map.93
  76.6 1.4 collective-permute-start.16
  77.9 1.3 collective-permute-done.16
  79.4 1.3 collective-permute-start.17
  80.7 10.1 %collective-permute-done.17 = f32[6,128,128]{2,1,0:T(8,128)S(1)} collective-permute-done((f32[6,128,128]{2,1,0:T(8,128)S(1)}, f32[6,128,128]{2,1,0:T(8,128)S(1)}, u32[]{:S(2)}, u32[]{:S(2)}) %collective-permute-start.17) | collective-permute-done | bytes 393248 | tf_op jit(solution)/shard_map/ppermute | solution.py:256
  91.6 1.7 %collective-permute-done.18 = f32[6,128,128]{2,1,0:T(8,128)S(1)} collective-permute-done((f32[6,128,128]{2,1,0:T(8,128)S(1)}, f32[6,128,128]{2,1,0:T(8,128)S(1)}, u32[]{:S(2)}, u32[]{:S(2)}) %collective-permute-start.18) | collective-permute-done | bytes 393248 | tf_op jit(solution)/shard_map/ppermute | solution.py:256
  93.8 4.8 %collective-permute-start.19 = (f32[12,32,128]{2,1,0:T(8,128)S(1)}, f32[12,32,128]{2,1,0:T(8,128)S(1)}, u32[]{:S(2)}, u32[]{:S(2)}) collective-permute-start(f32[12,32,128]{2,1,0:T(8,128)S(1)} %shard_map.95.x), channel_id=1, source_target_pairs={{0,4},{1,9},{2,6},{3,11},{4,8},{5,13},{6,10},{7,15},{8,12},{9,17},... | collective-permute-start | bytes 589832 | tf_op jit(solution)/shard_map/ppermute | solution.py:265
  98.6 2.3 %shard_map.96 = (bf16[16,256,128]{2,1,0:T(8,128)(2,1)S(1)}, bf16[24,256,128]{2,1,0:T(8,128)(2,1)S(1)}) custom-call(s32[1]{0:T(128)} %bitcast.3.me.refs_2_, s32[196]{0:T(256)S(1)} %copy-done.9, f32[12,128,128]{2,1,0:T(8,128)S(1)} %pad_maximum_fusion.1.inverse, f32[24,128,128]{2,1,0:T(8,128)S(1)} %bitcast.18, ...), custom_call_target="tpu_custom_call" | custom-call | flops 402653184 | bytes 9699328 | tf_op jit(solution)/shard_map/pallas_call | solution.py:88
  101.8 1.0 shard_map.98
  102.9 1.4 collective-permute-done.20
  104.4 5.3 %collective-permute-start.21 = (f32[12,32,128]{2,1,0:T(8,128)S(1)}, f32[12,32,128]{2,1,0:T(8,128)S(1)}, u32[]{:S(2)}, u32[]{:S(2)}) collective-permute-start(f32[12,32,128]{2,1,0:T(8,128)S(1)} %add_subtract_fusion.5.x), channel_id=1, source_target_pairs={{0,4},{1,9},{2,6},{3,11},{4,8},{5,13},{6,10},{7,15},{8,12},{9,17},... | collective-permute-start | bytes 589832 | tf_op jit(solution)/shard_map/ppermute | solution.py:265
  110.5 2.3 %collective-permute-done.21.arrived = f32[12,32,128]{2,1,0:T(8,128)S(1)} collective-permute-done((f32[12,32,128]{2,1,0:T(8,128)S(1)}, f32[12,32,128]{2,1,0:T(8,128)S(1)}, u32[]{:S(2)}, u32[]{:S(2)}) %collective-permute-start.21) | collective-permute-done | bytes 196640 | tf_op jit(solution)/shard_map/ppermute | solution.py:265
  112.8 1.0 shard_map.100
  113.9 1.4 collective-permute-done.22
  115.4 5.3 %collective-permute-start.23 = (f32[12,32,128]{2,1,0:T(8,128)S(1)}, f32[12,32,128]{2,1,0:T(8,128)S(1)}, u32[]{:S(2)}, u32[]{:S(2)}) collective-permute-start(f32[12,32,128]{2,1,0:T(8,128)S(1)} %add_subtract_fusion.4.x), channel_id=1, source_target_pairs={{0,4},{1,9},{2,6},{3,11},{4,8},{5,13},{6,10},{7,15},{8,12},{9,17},... | collective-permute-start | bytes 589832 | tf_op jit(solution)/shard_map/ppermute | solution.py:265
  121.5 2.3 %collective-permute-done.23.arrived = f32[12,32,128]{2,1,0:T(8,128)S(1)} collective-permute-done((f32[12,32,128]{2,1,0:T(8,128)S(1)}, f32[12,32,128]{2,1,0:T(8,128)S(1)}, u32[]{:S(2)}, u32[]{:S(2)}) %collective-permute-start.23) | collective-permute-done | bytes 196640 | tf_op jit(solution)/shard_map/ppermute | solution.py:265
  123.9 1.0 shard_map.102
  125.0 1.4 collective-permute-done.24
  126.4 4.2 %collective-permute-start.25 = (f32[12,32,128]{2,1,0:T(8,128)S(1)}, f32[12,32,128]{2,1,0:T(8,128)S(1)}, u32[]{:S(2)}, u32[]{:S(2)}) collective-permute-start(f32[12,32,128]{2,1,0:T(8,128)S(1)} %add_subtract_fusion.3.x), channel_id=1, source_target_pairs={{4,0},{6,2},{8,4},{9,1},{10,6},{11,3},{12,8},{13,5},{14,10},{15,7}... | collective-permute-start | bytes 589832 | tf_op jit(solution)/shard_map/ppermute | solution.py:265
  130.7 2.3 %shard_map.103 = (bf16[16,256,128]{2,1,0:T(8,128)(2,1)S(1)}, bf16[24,256,128]{2,1,0:T(8,128)(2,1)S(1)}) custom-call(s32[1]{0:T(128)} %bitcast.3.me.refs_2_, s32[196]{0:T(256)S(1)} %copy-done.9, f32[12,128,128]{2,1,0:T(8,128)S(1)} %pad_maximum_fusion.1.inverse, f32[24,128,128]{2,1,0:T(8,128)S(1)} %bitcast.19, ...), custom_call_target="tpu_custom_call" | custom-call | flops 402653184 | bytes 9699328 | tf_op jit(solution)/shard_map/pallas_call | solution.py:88
  133.8 3.2 %collective-permute-done.25.arrived = f32[12,32,128]{2,1,0:T(8,128)S(1)} collective-permute-done((f32[12,32,128]{2,1,0:T(8,128)S(1)}, f32[12,32,128]{2,1,0:T(8,128)S(1)}, u32[]{:S(2)}, u32[]{:S(2)}) %collective-permute-start.25) | collective-permute-done | bytes 196640 | tf_op jit(solution)/shard_map/ppermute | solution.py:265
  137.0 1.0 shard_map.105
  138.1 1.4 collective-permute-done.26
  139.6 1.9 %collective-permute-start.27 = (f32[12,32,128]{2,1,0:T(8,128)S(1)}, f32[12,32,128]{2,1,0:T(8,128)S(1)}, u32[]{:S(2)}, u32[]{:S(2)}) collective-permute-start(f32[12,32,128]{2,1,0:T(8,128)S(1)} %add_subtract_fusion.2.x), channel_id=1, source_target_pairs={{4,0},{6,2},{8,4},{9,1},{10,6},{11,3},{12,8},{13,5},{14,10},{15,7}... | collective-permute-start | bytes 589832 | tf_op jit(solution)/shard_map/ppermute | solution.py:265
  142.4 5.7 %collective-permute-done.27.arrived = f32[12,32,128]{2,1,0:T(8,128)S(1)} collective-permute-done((f32[12,32,128]{2,1,0:T(8,128)S(1)}, f32[12,32,128]{2,1,0:T(8,128)S(1)}, u32[]{:S(2)}, u32[]{:S(2)}) %collective-permute-start.27) | collective-permute-done | bytes 196640 | tf_op jit(solution)/shard_map/ppermute | solution.py:265
  149.2 1.4 collective-permute-done.28
  150.7 1.9 %collective-permute-start.29 = (f32[12,32,128]{2,1,0:T(8,128)S(1)}, f32[12,32,128]{2,1,0:T(8,128)S(1)}, u32[]{:S(2)}, u32[]{:S(2)}) collective-permute-start(f32[12,32,128]{2,1,0:T(8,128)S(1)} %add_subtract_fusion.1.x), channel_id=1, source_target_pairs={{4,0},{6,2},{8,4},{9,1},{10,6},{11,3},{12,8},{13,5},{14,10},{15,7}... | collective-permute-start | bytes 589832 | tf_op jit(solution)/shard_map/ppermute | solution.py:265
  153.5 5.7 %collective-permute-done.29.arrived = f32[12,32,128]{2,1,0:T(8,128)S(1)} collective-permute-done((f32[12,32,128]{2,1,0:T(8,128)S(1)}, f32[12,32,128]{2,1,0:T(8,128)S(1)}, u32[]{:S(2)}, u32[]{:S(2)}) %collective-permute-start.29) | collective-permute-done | bytes 196640 | tf_op jit(solution)/shard_map/ppermute | solution.py:265
  (95 shorter events, 19.7 us)
Async XLA Ops:
  0.6 14.0 %collective-permute-start.8 = (f32[24,128,128]{2,1,0:T(8,128)}, f32[24,128,128]{2,1,0:T(8,128)S(1)}, u32[]{:S(2)}, u32[]{:S(2)}) collective-permute-start(f32[24,128,128]{2,1,0:T(8,128)} %bitcast.10), channel_id=1, source_target_pairs={{0,1},{1,0},{2,3},{3,2},{4,5},{5,4},{6,7},{7,6},{8,9},{9,8},{10,11... | collective-permute-start | bytes 4718600 | tf_op jit(solution)/shard_map/ppermute | solution.py:256
  0.7 7.5 %collective-permute-start.4 = (f32[3,128,128]{2,1,0:T(8,128)}, f32[3,128,128]{2,1,0:T(8,128)S(1)}, u32[]{:S(2)}, u32[]{:S(2)}) collective-permute-start(f32[3,128,128]{2,1,0:T(8,128)} %param.9), channel_id=1, source_target_pairs={{0,2},{1,3},{2,0},{3,1},{4,6},{5,7},{6,4},{7,5},{8,10},{9,11},{10,... | collective-permute-start | bytes 589832 | tf_op jit(solution)/shard_map/ppermute | solution.py:256
  4.8 4.4 %collective-permute-start.5 = (s32[64]{0:T(128)S(1)}, s32[64]{0:T(128)S(1)}, u32[]{:S(2)}, u32[]{:S(2)}) collective-permute-start(s32[64]{0:T(128)S(1)} %pad_add_fusion.2.mine.refs_3_), channel_id=1, source_target_pairs={{0,1},{1,0},{2,3},{3,2},{4,5},{5,4},{6,7},{7,6},{8,9},{9,8},{10,11... | collective-permute-start | bytes 776 | tf_op jit(solution)/shard_map/ppermute | solution.py:256
  9.2 4.3 %collective-permute-start.7 = (f32[6,128,128]{2,1,0:T(8,128)S(1)}, f32[6,128,128]{2,1,0:T(8,128)}, u32[]{:S(2)}, u32[]{:S(2)}) collective-permute-start(f32[6,128,128]{2,1,0:T(8,128)S(1)} %pad_maximum_fusion.2.refs_1_), channel_id=1, source_target_pairs={{0,1},{1,0},{2,3},{3,2},{4,5},{5,4},{6,7},{7,6},{8,9},{9,8},{10,11... | collective-permute-start | bytes 1179656 | tf_op jit(solution)/shard_map/ppermute | solution.py:256
  12.0 2.6 %copy-start = (f32[12,2,128,128]{3,2,1,0:T(8,128)S(1)}, f32[12,2,128,128]{3,2,1,0:T(8,128)}, u32[]{:S(2)}) copy-start(f32[12,2,128,128]{3,2,1,0:T(8,128)} %param.10) | copy-start | bytes 4718596
  12.0 21.9 %collective-permute-start.2 = (f32[24,64,128]{2,1,0:T(8,128)}, f32[24,64,128]{2,1,0:T(8,128)}, u32[]{:S(2)}, u32[]{:S(2)}) collective-permute-start(f32[24,64,128]{2,1,0:T(8,128)} %get-tuple-element.24), channel_id=1, source_target_pairs={{0,2},{1,3},{2,0},{3,1},{4,6},{5,7},{6,4},{7,5},{8,10},{9,11},{10,... | collective-permute-start | bytes 2359304 | tf_op jit(solution)/shard_map/ppermute | solution.py:256
  14.6 17.7 %copy-start.7 = (f32[3,128,128]{2,1,0:T(8,128)S(1)}, f32[3,128,128]{2,1,0:T(8,128)}, u32[]{:S(2)}) copy-start(f32[3,128,128]{2,1,0:T(8,128)} %diag.3) | copy-start | bytes 589828
  15.5 18.4 %collective-permute-start.9 = (f32[8,128,128]{2,1,0:T(8,128)S(1)}, f32[8,128,128]{2,1,0:T(8,128)S(1)}, u32[]{:S(2)}, u32[]{:S(2)}) collective-permute-start(f32[8,128,128]{2,1,0:T(8,128)S(1)} %shard_map.87), channel_id=1, source_target_pairs={{0,4},{1,9},{2,6},{3,11},{4,8},{5,13},{6,10},{7,15},{8,12},{9,17},... | collective-permute-start | bytes 1572872 | tf_op jit(solution)/shard_map/ppermute | solution.py:265
  19.0 13.3 %collective-permute-start.6 = (s32[2,64]{1,0:T(2,128)S(1)}, s32[2,64]{1,0:T(2,128)S(1)}, u32[]{:S(2)}, u32[]{:S(2)}) collective-permute-start(s32[2,64]{1,0:T(2,128)S(1)} %pad_add_fusion.1), channel_id=1, source_target_pairs={{0,2},{1,3},{2,0},{3,1},{4,6},{5,7},{6,4},{7,5},{8,10},{9,11},{10,... | collective-permute-start | bytes 1544 | tf_op jit(solution)/shard_map/ppermute | solution.py:256
  32.3 27.2 %copy-start.11 = (s32[4,64]{1,0:T(4,128)}, s32[4,64]{1,0:T(4,128)S(1)}, u32[]{:S(2)}) copy-start(s32[4,64]{1,0:T(4,128)S(1)} %pad_add_fusion.refs_1_.metas) | copy-start | bytes 3076
  35.0 1.8 %collective-permute-start.10 = (f32[6,128,128]{2,1,0:T(8,128)S(1)}, f32[6,128,128]{2,1,0:T(8,128)S(1)}, u32[]{:S(2)}, u32[]{:S(2)}) collective-permute-start(f32[6,128,128]{2,1,0:T(8,128)S(1)} %get-tuple-element.17), channel_id=1, source_target_pairs={{0,1},{1,0},{2,3},{3,2},{4,5},{5,4},{6,7},{7,6},{8,9},{9,8},{10,11... | collective-permute-start | bytes 1179656 | tf_op jit(solution)/shard_map/ppermute | solution.py:256
  36.9 11.7 %collective-permute-start.11 = (f32[6,128,128]{2,1,0:T(8,128)S(1)}, f32[6,128,128]{2,1,0:T(8,128)S(1)}, u32[]{:S(2)}, u32[]{:S(2)}) collective-permute-start(f32[6,128,128]{2,1,0:T(8,128)S(1)} %add.30), channel_id=1, source_target_pairs={{0,2},{1,3},{2,0},{3,1},{4,6},{5,7},{6,4},{7,5},{8,10},{9,11},{10,... | collective-permute-start | bytes 1179656 | tf_op jit(solution)/shard_map/ppermute | solution.py:256
  39.2 9.5 %collective-permute-start.3 = (f32[24,64,128]{2,1,0:T(8,128)}, f32[24,64,128]{2,1,0:T(8,128)S(1)}, u32[]{:S(2)}, u32[]{:S(2)}) collective-permute-start(f32[24,64,128]{2,1,0:T(8,128)} %collective-permute-done.2.refs_0_.refs_2_), channel_id=1, source_target_pairs={{0,1},{1,0},{2,3},{3,2},{4,5},{5,4},{6,7},{7,6},{8,9},{9,8},{10,11... | collective-permute-start | bytes 2359304 | tf_op jit(solution)/shard_map/ppermute | solution.py:256
  48.7 2.4 %copy-start.3 = (f32[24,64,128]{2,1,0:T(8,128)}, f32[24,64,128]{2,1,0:T(8,128)S(1)}, u32[]{:S(2)}) copy-start(f32[24,64,128]{2,1,0:T(8,128)S(1)} %collective-permute-done.3.refs_0_.refs_4_) | copy-start | bytes 2359300
  49.2 3.7 %copy-start.5 = (f32[6,128,128]{2,1,0:T(8,128)}, f32[6,128,128]{2,1,0:T(8,128)S(1)}, u32[]{:S(2)}) copy-start(f32[6,128,128]{2,1,0:T(8,128)S(1)} %shard_map.89.refs_1_) | copy-start | bytes 1179652
  49.2 1.9 %collective-permute-start.14 = (f32[6,128,128]{2,1,0:T(8,128)S(1)}, f32[6,128,128]{2,1,0:T(8,128)S(1)}, u32[]{:S(2)}, u32[]{:S(2)}) collective-permute-start(f32[6,128,128]{2,1,0:T(8,128)S(1)} %shard_map.89.refs_1_), channel_id=1, source_target_pairs={{0,1},{1,0},{2,3},{3,2},{4,5},{5,4},{6,7},{7,6},{8,9},{9,8},{10,11... | collective-permute-start | bytes 1179656 | tf_op jit(solution)/shard_map/ppermute | solution.py:256
  49.3 25.7 %collective-permute-start = (f32[24,64,128]{2,1,0:T(8,128)}, f32[24,64,128]{2,1,0:T(8,128)}, u32[]{:S(2)}, u32[]{:S(2)}) collective-permute-start(f32[24,64,128]{2,1,0:T(8,128)} %get-tuple-element.25), channel_id=1, source_target_pairs={{0,2},{1,3},{2,0},{3,1},{4,6},{5,7},{6,4},{7,5},{8,10},{9,11},{10,... | collective-permute-start | bytes 2359304 | tf_op jit(solution)/shard_map/ppermute | solution.py:256
  51.2 1.7 %copy-start.1 = (f32[12,128,128]{2,1,0:T(8,128)}, f32[12,128,128]{2,1,0:T(8,128)S(1)}, u32[]{:S(2)}) copy-start(f32[12,128,128]{2,1,0:T(8,128)S(1)} %pad_maximum_fusion.inverse) | copy-start | bytes 2359300
  51.2 21.0 %copy-start.8 = (f32[3,128,128]{2,1,0:T(8,128)S(1)}, f32[3,128,128]{2,1,0:T(8,128)}, u32[]{:S(2)}) copy-start(f32[3,128,128]{2,1,0:T(8,128)} %diag.3) | copy-start | bytes 589828
  52.9 22.1 %collective-permute-start.15 = (f32[8,128,128]{2,1,0:T(8,128)}, f32[8,128,128]{2,1,0:T(8,128)}, u32[]{:S(2)}, u32[]{:S(2)}) collective-permute-start(f32[8,128,128]{2,1,0:T(8,128)} %shard_map.92), channel_id=1, source_target_pairs={{0,4},{1,9},{2,6},{3,11},{4,8},{5,13},{6,10},{7,15},{8,12},{9,17},... | collective-permute-start | bytes 1572872 | tf_op jit(solution)/shard_map/ppermute | solution.py:265
  56.5 11.5 %collective-permute-start.12 = (s32[4,64]{1,0:T(4,128)S(1)}, s32[4,64]{1,0:T(4,128)S(1)}, u32[]{:S(2)}, u32[]{:S(2)}) collective-permute-start(s32[4,64]{1,0:T(4,128)S(1)} %pad_add_fusion.refs_1_.metas), channel_id=1, source_target_pairs={{0,4},{1,9},{2,6},{3,11},{4,8},{5,13},{6,10},{7,15},{8,12},{9,17},... | collective-permute-start | bytes 3080 | tf_op jit(solution)/shard_map/ppermute | solution.py:265
  59.5 8.4 %collective-permute-start.13 = (s32[4,64]{1,0:T(4,128)S(1)}, s32[4,64]{1,0:T(4,128)S(1)}, u32[]{:S(2)}, u32[]{:S(2)}) collective-permute-start(s32[4,64]{1,0:T(4,128)S(1)} %pad_add_fusion.refs_1_.metas), channel_id=1, source_target_pairs={{4,0},{6,2},{8,4},{9,1},{10,6},{11,3},{12,8},{13,5},{14,10},{15,7}... | collective-permute-start | bytes 3080 | tf_op jit(solution)/shard_map/ppermute | solution.py:265
  68.0 0.6 copy-start.12
  68.5 0.6 copy-start.13
  72.2 1.1 copy-start.2
  73.3 1.7 %copy-start.9 = (s32[196]{0:T(256)S(1)}, s32[196]{0:T(256)}, u32[]{:S(2)}) copy-start(s32[196]{0:T(256)} %shard_map.90.refs_1_.table) | copy-start | bytes 2356
  76.6 2.7 %collective-permute-start.16 = (f32[6,128,128]{2,1,0:T(8,128)S(1)}, f32[6,128,128]{2,1,0:T(8,128)S(1)}, u32[]{:S(2)}, u32[]{:S(2)}) collective-permute-start(f32[6,128,128]{2,1,0:T(8,128)S(1)} %get-tuple-element.19), channel_id=1, source_target_pairs={{0,1},{1,0},{2,3},{3,2},{4,5},{5,4},{6,7},{7,6},{8,9},{9,8},{10,11... | collective-permute-start | bytes 1179656 | tf_op jit(solution)/shard_map/ppermute | solution.py:256
  79.3 11.6 %copy-start.6 = (f32[6,128,128]{2,1,0:T(8,128)S(1)}, f32[6,128,128]{2,1,0:T(8,128)}, u32[]{:S(2)}) copy-start(f32[6,128,128]{2,1,0:T(8,128)} %copy-done.5) | copy-start | bytes 1179652
  79.4 11.5 %collective-permute-start.17 = (f32[6,128,128]{2,1,0:T(8,128)S(1)}, f32[6,128,128]{2,1,0:T(8,128)S(1)}, u32[]{:S(2)}, u32[]{:S(2)}) collective-permute-start(f32[6,128,128]{2,1,0:T(8,128)S(1)} %add.32), channel_id=1, source_target_pairs={{0,2},{1,3},{2,0},{3,1},{4,6},{5,7},{6,4},{7,5},{8,10},{9,11},{10,... | collective-permute-start | bytes 1179656 | tf_op jit(solution)/shard_map/ppermute | solution.py:256
  80.7 10.3 %collective-permute-start.1 = (f32[24,64,128]{2,1,0:T(8,128)}, f32[24,64,128]{2,1,0:T(8,128)S(1)}, u32[]{:S(2)}, u32[]{:S(2)}) collective-permute-start(f32[24,64,128]{2,1,0:T(8,128)} %collective-permute-done.refs_0_.refs_3_), channel_id=1, source_target_pairs={{0,1},{1,0},{2,3},{3,2},{4,5},{5,4},{6,7},{7,6},{8,9},{9,8},{10,11... | collective-permute-start | bytes 2359304 | tf_op jit(solution)/shard_map/ppermute | solution.py:256
  91.0 2.4 %copy-start.10 = (f32[12,32,128]{2,1,0:T(8,128)S(1)}, f32[12,32,128]{2,1,0:T(8,128)}, u32[]{:S(2)}) copy-start(f32[12,32,128]{2,1,0:T(8,128)} %base.1) | copy-start | bytes 589828
  91.5 7.1 %copy-start.4 = (f32[24,64,128]{2,1,0:T(8,128)S(1)}, f32[24,64,128]{2,1,0:T(8,128)}, u32[]{:S(2)}) copy-start(f32[24,64,128]{2,1,0:T(8,128)} %copy-done.3) | copy-start | bytes 2359300
  91.5 1.8 %collective-permute-start.18 = (f32[6,128,128]{2,1,0:T(8,128)S(1)}, f32[6,128,128]{2,1,0:T(8,128)S(1)}, u32[]{:S(2)}, u32[]{:S(2)}) collective-permute-start(f32[6,128,128]{2,1,0:T(8,128)S(1)} %shard_map.94), channel_id=1, source_target_pairs={{0,1},{1,0},{2,3},{3,2},{4,5},{5,4},{6,7},{7,6},{8,9},{9,8},{10,11... | collective-permute-start | bytes 1179656 | tf_op jit(solution)/shard_map/ppermute | solution.py:256
  93.8 8.0 %collective-permute-start.19 = (f32[12,32,128]{2,1,0:T(8,128)S(1)}, f32[12,32,128]{2,1,0:T(8,128)S(1)}, u32[]{:S(2)}, u32[]{:S(2)}) collective-permute-start(f32[12,32,128]{2,1,0:T(8,128)S(1)} %shard_map.95.x), channel_id=1, source_target_pairs={{0,4},{1,9},{2,6},{3,11},{4,8},{5,13},{6,10},{7,15},{8,12},{9,17},... | collective-permute-start | bytes 589832 | tf_op jit(solution)/shard_map/ppermute | solution.py:265
  102.8 1.5 collective-permute-start.20
  104.4 8.4 %collective-permute-start.21 = (f32[12,32,128]{2,1,0:T(8,128)S(1)}, f32[12,32,128]{2,1,0:T(8,128)S(1)}, u32[]{:S(2)}, u32[]{:S(2)}) collective-permute-start(f32[12,32,128]{2,1,0:T(8,128)S(1)} %add_subtract_fusion.5.x), channel_id=1, source_target_pairs={{0,4},{1,9},{2,6},{3,11},{4,8},{5,13},{6,10},{7,15},{8,12},{9,17},... | collective-permute-start | bytes 589832 | tf_op jit(solution)/shard_map/ppermute | solution.py:265
  113.8 1.5 collective-permute-start.22
  115.4 8.5 %collective-permute-start.23 = (f32[12,32,128]{2,1,0:T(8,128)S(1)}, f32[12,32,128]{2,1,0:T(8,128)S(1)}, u32[]{:S(2)}, u32[]{:S(2)}) collective-permute-start(f32[12,32,128]{2,1,0:T(8,128)S(1)} %add_subtract_fusion.4.x), channel_id=1, source_target_pairs={{0,4},{1,9},{2,6},{3,11},{4,8},{5,13},{6,10},{7,15},{8,12},{9,17},... | collective-permute-start | bytes 589832 | tf_op jit(solution)/shard_map/ppermute | solution.py:265
  124.9 1.5 collective-permute-start.24
  126.4 10.6 %collective-permute-start.25 = (f32[12,32,128]{2,1,0:T(8,128)S(1)}, f32[12,32,128]{2,1,0:T(8,128)S(1)}, u32[]{:S(2)}, u32[]{:S(2)}) collective-permute-start(f32[12,32,128]{2,1,0:T(8,128)S(1)} %add_subtract_fusion.3.x), channel_id=1, source_target_pairs={{4,0},{6,2},{8,4},{9,1},{10,6},{11,3},{12,8},{13,5},{14,10},{15,7}... | collective-permute-start | bytes 589832 | tf_op jit(solution)/shard_map/ppermute | solution.py:265
  138.1 1.5 collective-permute-start.26
  139.6 8.5 %collective-permute-start.27 = (f32[12,32,128]{2,1,0:T(8,128)S(1)}, f32[12,32,128]{2,1,0:T(8,128)S(1)}, u32[]{:S(2)}, u32[]{:S(2)}) collective-permute-start(f32[12,32,128]{2,1,0:T(8,128)S(1)} %add_subtract_fusion.2.x), channel_id=1, source_target_pairs={{4,0},{6,2},{8,4},{9,1},{10,6},{11,3},{12,8},{13,5},{14,10},{15,7}... | collective-permute-start | bytes 589832 | tf_op jit(solution)/shard_map/ppermute | solution.py:265
  149.1 1.5 collective-permute-start.28
  150.7 8.5 %collective-permute-start.29 = (f32[12,32,128]{2,1,0:T(8,128)S(1)}, f32[12,32,128]{2,1,0:T(8,128)S(1)}, u32[]{:S(2)}, u32[]{:S(2)}) collective-permute-start(f32[12,32,128]{2,1,0:T(8,128)S(1)} %add_subtract_fusion.1.x), channel_id=1, source_target_pairs={{4,0},{6,2},{8,4},{9,1},{10,6},{11,3},{12,8},{13,5},{14,10},{15,7}... | collective-permute-start | bytes 589832 | tf_op jit(solution)/shard_map/ppermute | solution.py:265
  160.2 1.5 collective-permute-start.30

commit v3 on v2

v3 whole, which is shorter than its diff:
```python
import functools

import jax
import jax.numpy as jnp
from jax import lax
from jax.experimental import pallas as pl
from jax.experimental.pallas import tpu as pltpu
from jax.sharding import PartitionSpec as P

FSWEEPS = 2
LSWEEPS = 3
USWEEPS = 3
F32 = jnp.float32
BF16 = jnp.bfloat16


def split(a):
    hi = a.astype(BF16)
    return hi, (a - hi.astype(F32)).astype(BF16)


def matmul_parts(ah, al, bh, bl):
    lhs = jnp.concatenate([ah, al], 1)
    pair = jnp.concatenate([bh, bl], 1)
    rhs = jnp.concatenate([pair, pair], 0)
    out = jnp.dot(lhs, rhs, preferred_element_type=F32)
    n = bh.shape[1]
    return out[:, :n] + out[:, n:]


def matmul(a, b):
    return matmul_parts(*split(a), *split(b))


def times_tile(x, wide):
    v, n = x.shape
    stacked = jnp.concatenate(split(x), 0)
    out = lax.dot_general(stacked, wide, (((1,), (1,)), ((), ())), preferred_element_type=F32)
    return out[:v, :n] + (out[v:, :n] + out[:v, n:])


def widen(a):
    return jnp.concatenate(split(a), 0)


class Layout:
    def __init__(self, rows, width, cap, n_tile):
        self.rows, self.width, self.cap, self.n_tile = rows, width, cap, n_tile
        self.slots = rows * width
        self.own_rows = rows // n_tile
        self.pairs = max(1, (self.slots - 4 * cap) // 2)
        self.listed_slots = n_tile * cap
        self.local_slots = n_tile // 2 * self.pairs
        self.table = 2 * (self.listed_slots + self.local_slots)

    def kind(self, meta, s):
        return meta[s]

    def link(self, meta, s):
        return meta[self.slots + s]

    def listed(self, meta, which, j):
        return meta[2 * self.slots + which * self.cap + j]

    def place(self, r, me):
        far = (r // self.own_rows) ^ me
        return ((far & 1) * (self.n_tile // 2) + (far >> 1)) * self.own_rows + r % self.own_rows

    def lookup(self, meta, which, side, j):
        s = self.listed(meta, which, j)
        v = self.link(meta, s) - self.slots - (which % 2) * self.cap
        live = (self.kind(meta, s) == side) & (v >= 0) & (v < self.cap)
        return s, live, jnp.clip(v, 0, self.cap - 1)

    def is_local(self, meta, s, side):
        return (self.kind(meta, s) == side) & (self.link(meta, s) < self.slots)

    def scan(self, meta, side, found):
        def step(s, count):
            hit = self.is_local(meta, s, side)

            @pl.when(hit & (count < self.pairs))
            def _():
                found(s, count)

            return count + hit.astype(jnp.int32)

        return lax.fori_loop(0, self.slots, step, 0)


def smem():
    return pl.BlockSpec(memory_space=pltpu.SMEM)


def vmem():
    return pl.BlockSpec(memory_space=pltpu.VMEM)


def call(body, outs, scalars, arrays, flops=0, scratch=(), early=()):
    moved = sum(a.size * a.dtype.itemsize for a in arrays) + sum(o.size * o.dtype.itemsize for o in outs)
    return pl.pallas_call(
        body if not early else lambda *refs: body(*refs[len(early) :]),
        out_shape=outs,
        in_specs=[pl.BlockSpec(memory_space=pl.ANY)] * len(early) + [smem()] * len(scalars) + [vmem()] * len(arrays),
        out_specs=[vmem()] * len(outs),
        scratch_shapes=list(scratch),
        compiler_params=pltpu.CompilerParams(vmem_limit_bytes=8 << 20),
        cost_estimate=pl.CostEstimate(flops=flops, bytes_accessed=moved, transcendentals=0),
    )(*early, *scalars, *arrays)


def gather_kernel(lay, mine, tiles, lower, lower_local, upper, places):
    for side, base, out in ((1, 2, lower), (2, 0, upper)):
        for which in range(2):
            for j in range(lay.cap):
                s, live, _ = lay.lookup(mine, base + which, side, j)
                out[which * lay.cap + j] = jnp.where(live, tiles[s], 0.0)
    for side, out, start in ((1, lower_local, 0), (2, upper, 2 * lay.cap)):
        for i in range(lay.pairs):
            places[i] = 0

        def found(s, i):
            places[i] = s

        count = lay.scan(mine, side, found)
        for i in range(lay.pairs):
            out[start + i] = jnp.where(i < count, tiles[places[i]], 0.0)


def outgoing_kernel(lay, me, mine, mates, inverse, upper, mate_upper, out):
    role = me[0] % 2
    for g, (meta, source) in enumerate(((mine, upper), (mates, mate_upper))):
        for j in range(lay.cap):
            r = lay.listed(meta, role, j) // lay.width
            out[g * lay.cap + j] = matmul(inverse[lay.place(r, me[0])], source[role * lay.cap + j])


def local_pivot_kernel(lay, me, mine, inverse, diag, tiles, out):
    out[: lay.own_rows] = -diag[...]
    out[lay.own_rows :] = jnp.zeros((lay.rows - lay.own_rows,) + diag.shape[1:], F32)

    @pl.loop(0, lay.slots)
    def _(s):
        @pl.when(lay.is_local(mine, s, 1))
        def _():
            v = lay.link(mine, s)
            q = matmul(inverse[lay.place(v // lay.width, me[0])], tiles[v])
            out[lay.place(s // lay.width, me[0])] += matmul(tiles[s], q)


def incoming_kernel(lay, me, mine, mates, local, lower, mate_lower, arrived, keep, give, total):
    role = me[0] % 2
    places, terms = [], []
    for g, (meta, source) in enumerate(((mine, lower), (mates, mate_lower))):
        for j in range(lay.cap):
            s, _, v = lay.lookup(meta, 2 + role, 1, j)
            places.append(lay.place(s // lay.width, me[0]))
            terms.append(matmul(source[role * lay.cap + j], arrived[g * lay.cap + v]))
    total[...] = local[...]
    for place, term in zip(places, terms):
        total[place] += term
    half = keep.shape[0]
    keep[...] = total[:half]
    give[...] = total[half:]


def newton_kernel(inverse, sums, out):
    for i in range(out.shape[0]):
        x = inverse[i]
        xh, xl = split(x)
        product = matmul_parts(xh, xl, *split(sums[i]))
        out[i] = 2.0 * x + matmul_parts(*split(product), xh, xl)


def table_kernel(lay, me, metas, peers_below, peers_above, out):
    role = me[0] % 2
    for side in (1, 2):
        start = (side - 1) * lay.table
        base, peers = ((2, peers_below), (0, peers_above))[side - 1]
        for q in range(lay.n_tile):
            a, meta, peer = q ^ me[0], metas.at[q], peers.at[q]
            for j in range(lay.cap):
                s, _, v = lay.lookup(meta, base + role, side, j)
                k = start + a * lay.cap + j
                out[k] = s // lay.width
                out[lay.listed_slots + k] = lay.listed(peer, 2 - base + role, v) // lay.width
        for q in range(0, lay.n_tile, 2):
            meta = metas.at[q]
            begin = start + 2 * lay.listed_slots + ((q ^ me[0]) >> 1) * lay.pairs
            for i in range(lay.pairs):
                out[begin + i] = 0
                out[begin + lay.local_slots + i] = 0

            def found(s, i, meta=meta, begin=begin):
                out[begin + i] = s // lay.width
                out[begin + lay.local_slots + i] = lay.link(meta, s) // lay.width

            lay.scan(meta, side, found)


def scaled_kernel(lay, side, me, table, inverse, *refs):
    sources, (listed, local) = refs[:-2], refs[-2:]
    role = me[0] % 2
    start = (side - 1) * lay.table

    def scaled(row, tile):
        return widen(matmul(inverse[lay.place(row, me[0])], tile))

    at = 0
    for q in range(lay.n_tile):
        lists = sources[at]
        for j in range(lay.cap):
            k = (q ^ me[0]) * lay.cap + j
            listed[k] = scaled(table[start + k], lists[role * lay.cap + j])
        at += 1
        if q % 2 == 0:
            pairs, first = (lists, 2 * lay.cap) if side == 2 else (sources[at], 0)
            at += side == 1
            for i in range(lay.pairs):
                k = ((q ^ me[0]) >> 1) * lay.pairs + i
                local[k] = scaled(table[start + 2 * lay.listed_slots + k], pairs[first + i])


def first_kernel(lay, me, base, inverse, out):
    count = out.shape[1]
    mine = pl.ds(pl.multiple_of((me[0] >> 1) * count, count), count)
    for r in range(lay.rows):
        out[r] = times_tile(base[r, mine], widen(inverse[lay.place(r, me[0])]))


def local_sum_kernel(lay, side, table, x, tiles, out):
    start = (side - 1) * lay.table + 2 * lay.listed_slots
    terms = [times_tile(x[table[start + lay.local_slots + k]], tiles[k]) for k in range(lay.local_slots)]
    out[...] = jnp.zeros_like(out)
    for k, value in enumerate(terms):
        out[table[start + k]] += value


def listed_sum_kernel(lay, side, table, local, tiles, arrived, out):
    start = (side - 1) * lay.table
    terms = [times_tile(arrived[table[start + lay.listed_slots + k]], tiles[k]) for k in range(lay.listed_slots)]
    out[...] = local[...]
    for k, value in enumerate(terms):
        out[table[start + k]] += value


def local(krylov_block, diag_block, inverse_prev, coupling_tiles, slot_kind, slot_link, send_slots):
    rows, width, n, _ = coupling_tiles.shape
    cap = send_slots.shape[3]
    n_dom, n_tile = lax.axis_size("dom"), lax.axis_size("tile")
    lay = Layout(rows, width, cap, n_tile)
    vectors = krylov_block.shape[1]
    upper_bits = [1 << b for b in range(1, n_tile.bit_length() - 1)]

    me = lax.axis_index("tile").astype(jnp.int32).reshape(1)
    mine = jnp.concatenate([slot_kind.reshape(-1), slot_link.reshape(-1), send_slots.reshape(-1)])
    tiles = coupling_tiles.reshape(lay.slots, n, n)

    def swap(x, bit):
        return lax.ppermute(x, "tile", [(i, i ^ bit) for i in range(n_tile)])

    def along(x, sign):
        route = []
        for d in range(n_dom):
            for t in range(n_tile):
                to = d + sign * (1 + t % 2)
                if 0 <= to < n_dom:
                    route.append((d * n_tile + t, to * n_tile + t))
        return lax.ppermute(x, ("dom", "tile"), route)

    def summed(x):
        for bit in upper_bits:
            got = swap(x, bit)
            near = bit // 2
            got = got.reshape((n_tile // 2 // (2 * near), 2, near * lay.own_rows) + x.shape[1:])
            x = x + jnp.concatenate([got[:, 1:], got[:, :1]], 1).reshape(x.shape)
        return x

    def shape(*dims, dtype=F32):
        return jax.ShapeDtypeStruct(dims, dtype)

    kernel = lambda body, *bound: functools.partial(body, lay, *bound)
    product = 8 * n**3

    def over_chips(x):
        held = [x]
        for bit in upper_bits:
            held += [swap(one, bit) for one in held]
        return held

    arriving = over_chips(inverse_prev)
    held = over_chips(mine)
    both = [swap(x, 1) for x in held]
    lower, lower_local, upper = call(
        kernel(gather_kernel),
        [shape(2 * cap, n, n), shape(lay.pairs, n, n), shape(2 * cap + lay.pairs, n, n)],
        (mine,),
        (tiles,),
        scratch=(pltpu.SMEM((lay.pairs,), jnp.int32),),
    )
    mate_lower, mate_upper = swap(lower, 1), swap(upper, 1)
    arriving, held, both, lower, lower_local, upper = lax.optimization_barrier(
        (arriving, held, both, lower, lower_local, upper)
    )
    mates = both[0]
    metas = jnp.stack([one for pair in zip(held, both) for one in pair])
    kept = jnp.concatenate(arriving, 0)
    mated = jnp.concatenate([swap(x, 1) for x in arriving], 0)
    half = rows // 2
    for sweep in range(FSWEEPS):
        inverse = jnp.concatenate([kept, mated], 0)
        (out,) = call(
            kernel(outgoing_kernel), [shape(2 * cap, n, n)], (me, mine, mates), (inverse, upper, mate_upper)
        )
        arrived = along(out, 1)
        (here,) = call(
            kernel(local_pivot_kernel),
            [shape(rows, n, n)],
            (me, mine),
            (inverse, diag_block, tiles),
            flops=product * rows,
        )
        early = []
        if sweep == 0:
            lowers = over_chips(lower)
            below, above = along(metas, 1), along(metas, -1)
            early += [*lowers[1:], below, above]
        if sweep == FSWEEPS - 1:
            lower_locals = over_chips(lower_local)
            mate_lowers = [mate_lower] + [swap(x, 1) for x in lowers[1:]]
            table = pl.pallas_call(
                kernel(table_kernel),
                out_shape=shape(2 * lay.table, dtype=jnp.int32),
                in_specs=[smem()] * 4,
                out_specs=smem(),
            )(me, metas, below, above)
            early += [*lower_locals[1:], *mate_lowers[1:], table]
        keep, give = call(
            kernel(incoming_kernel),
            [shape(half, n, n)] * 2,
            (me, mine, mates),
            (here, lower, mate_lower, arrived),
            scratch=(pltpu.VMEM((rows, n, n), F32),),
            early=early,
        )
        sums = summed(keep + swap(give, 1))
        (kept,) = call(newton_kernel, [shape(half, n, n)], (), (kept, sums))
        mated = swap(kept, 1)
    inverse = jnp.concatenate([kept, mated], 0)

    def scale(side, sources):
        return call(
            kernel(scaled_kernel, side),
            [
                shape(lay.listed_slots, 2 * n, n, dtype=BF16),
                shape(lay.local_slots, 2 * n, n, dtype=BF16),
            ],
            (me, table),
            (inverse, *sources),
            flops=product * 24,
        )

    share = vectors // (n_tile // 2)
    block = shape(rows, share, n)
    (first,) = call(kernel(first_kernel), [block], (me,), (krylov_block, inverse))

    def sweeps(x, side, count, listed, local, early=()):
        base = x
        for sweep in range(count):
            arrived = along(x, 1 if side == 1 else -1)
            (here,) = call(
                kernel(local_sum_kernel, side), [block], (table,), (x, local), flops=8 * n**2 * vectors * rows
            )
            (part,) = call(
                kernel(listed_sum_kernel, side),
                [block],
                (table,),
                (here, listed, arrived),
                early=early if sweep == count - 1 else (),
            )
            x = base - (part + swap(part, 1))
        return x

    uppers = over_chips(upper)
    mate_uppers = [mate_upper] + [swap(x, 1) for x in uppers[1:]]
    low = [x for three in zip(lowers, lower_locals, mate_lowers) for x in three]
    up = [x for pair in zip(uppers, mate_uppers) for x in pair]
    solved = sweeps(first, 1, LSWEEPS, *scale(1, low), early=uppers[1:])
    solved = sweeps(solved, 2, USWEEPS, *scale(2, up))
    for bit in upper_bits:
        got = swap(solved, bit)
        solved = jnp.where(
            (me[0] & bit) == 0, jnp.concatenate([solved, got], 1), jnp.concatenate([got, solved], 1)
        )
    return (kept[: lay.own_rows], solved)


def solution(mesh):
    placed = (
        P("dom", None, None),
        P(("dom", "tile"), None, None),
        P(("dom", "tile"), None, None),
        P("dom", "tile", None, None),
        P("dom", "tile"),
        P("dom", "tile"),
        P("dom", "tile", None, None),
    )
    return jax.shard_map(
        local,
        mesh=mesh,
        in_specs=placed,
        out_specs=(P(("dom", "tile"), None, None), P("dom", None, None)),
        check_vma=False,
    )
```

time: 163 us -> 154 us (0.945)
  waiting for transfers between devices: 72.8 us -> 63.8 us
  Pallas kernels: 28.8 us -> 32.2 us
    ppermute x10, waiting for transfers between devices: 24.8 us -> 18.8 us  [along(): return lax.ppermute(x, ('dom', 'tile'), route)]
    ppermute x21 -> x26, waiting for transfers between devices: 48 us -> 45 us  [swap(): return lax.ppermute(x, 'tile', [(i, i ^ bit) for i in range(n_tile)])]
    pallas_call x23 -> x24, Pallas kernels: 25.8 us -> 28.7 us  [call(): pl.pallas_call(body if not early else lambda *refs: body(*refs[len(early)...]
    slice x1 -> x0, local copies, waits for them, and re-layouts: 2.72 us -> none  [local(): part = [tiles[:, cuts[sweep]]]]
    ppermute x21 -> x26, starting transfers between devices: 11.5 us -> 9.17 us  [swap(): return lax.ppermute(x, 'tile', [(i, i ^ bit) for i in range(n_tile)])]
    unnamed x31 -> x35, local copies, waits for them, and re-layouts: 3.89 us -> 6.01 us
  transfers between devices with their start and end apart: 31 -> 36, of which waited for: 19 -> 24; matrix products, arithmetic and copies ran while one was open for 5% -> 1% of each run, Pallas kernels for 12% -> 15%
where the time goes in v3:
time: 154 us; the launch traced here: 153 us
  waiting for transfers between devices  63.8 us (41%)
  starting transfers between devices  46.8 us (30%)
  Pallas kernels  32.2 us (21%)
  local copies, waits for them, and re-layouts  7.7 us (5%)
    ppermute x26, waiting for transfers between devices, swap(): return lax.ppermute(x, 'tile', [(i, i ^ bit) for i in range(n_tile)])  45 us
    ppermute x10, starting transfers between devices, along(): return lax.ppermute(x, ('dom', 'tile'), route)  37.6 us
    pallas_call x24, Pallas kernels, call(): pl.pallas_call(body if not early else lambda *refs: body(*refs[len(early)...  28.7 us
    ppermute x10, waiting for transfers between devices, along(): return lax.ppermute(x, ('dom', 'tile'), route)  18.8 us
    ppermute x26, starting transfers between devices, swap(): return lax.ppermute(x, 'tile', [(i, i ^ bit) for i in range(n_tile)])  9.17 us
    unnamed x35, local copies, waits for them, and re-layouts  6.01 us
    pallas_call x1, Pallas kernels, local(): pl.pallas_call(kernel(table_kernel), out_shape=shape(2 * lay.table, dtype...  3.53 us
  transfers between devices with their start and end apart: 36, of which 24 were waited for; matrix products, arithmetic and copies ran while one was open for 1% of the time, Pallas kernels for 15%

profile of v3, /device:TPU:18, one launch (start us, length us, event | category | flops | bytes accessed | tf_op | source)
XLA Modules:
  0.0 153.0 jit_solution(9647923493855150928)
XLA Ops:
  3.2 1.4 copy-done
  4.6 2.2 %shard_map.86 = (f32[8,128,128]{2,1,0:T(8,128)}, f32[4,128,128]{2,1,0:T(8,128)}, f32[12,128,128]{2,1,0:T(8,128)S(1)}) custom-call(s32[64]{0:T(128)S(1)} %pad_add_fusion.1.mine.refs_4_, f32[24,128,128]{2,1,0:T(8,128)S(1)} %bitcast.12), custom_call_target="tpu_custom_call" | custom-call | bytes 3145728 | tf_op jit(solution)/shard_map/pallas_call | solution.py:101
  6.8 1.5 collective-permute-start
  9.4 4.8 %collective-permute-done.1 = s32[64]{0:T(128)S(1)} collective-permute-done((s32[64]{0:T(128)S(1)}, s32[64]{0:T(128)S(1)}, u32[]{:S(2)}, u32[]{:S(2)}) %collective-permute-start.1) | collective-permute-done | bytes 288 | tf_op jit(solution)/shard_map/ppermute | solution.py:260
  14.2 1.1 collective-permute-done.3
  15.3 1.5 collective-permute-start.4
  19.5 3.5 %collective-permute-start.11 = (f32[8,128,128]{2,1,0:T(8,128)S(1)}, f32[8,128,128]{2,1,0:T(8,128)S(1)}, u32[]{:S(2)}, u32[]{:S(2)}) collective-permute-start(f32[8,128,128]{2,1,0:T(8,128)S(1)} %shard_map.88), channel_id=1, source_target_pairs={{0,4},{1,9},{2,6},{3,11},{4,8},{5,13},{6,10},{7,15},{8,12},{9,17},... | collective-permute-start | bytes 1572872 | tf_op jit(solution)/shard_map/ppermute | solution.py:269
  23.0 3.4 %collective-permute-start.5 = (s32[4,64]{1,0:T(4,128)S(1)}, s32[4,64]{1,0:T(4,128)S(1)}, u32[]{:S(2)}, u32[]{:S(2)}) collective-permute-start(s32[4,64]{1,0:T(4,128)S(1)} %pad_add_fusion.metas), channel_id=1, source_target_pairs={{0,4},{1,9},{2,6},{3,11},{4,8},{5,13},{6,10},{7,15},{8,12},{9,17},... | collective-permute-start | bytes 3080 | tf_op jit(solution)/shard_map/ppermute | solution.py:269
  26.4 2.4 %collective-permute-start.6 = (s32[4,64]{1,0:T(4,128)S(1)}, s32[4,64]{1,0:T(4,128)S(1)}, u32[]{:S(2)}, u32[]{:S(2)}) collective-permute-start(s32[4,64]{1,0:T(4,128)S(1)} %pad_add_fusion.metas), channel_id=1, source_target_pairs={{4,0},{6,2},{8,4},{9,1},{10,6},{11,3},{12,8},{13,5},{14,10},{15,7}... | collective-permute-start | bytes 3080 | tf_op jit(solution)/shard_map/ppermute | solution.py:269
  28.9 2.3 %shard_map.87.refs_6_ = f32[12,128,128]{2,1,0:T(8,128)S(1)} custom-call(s32[1]{0:T(128)} %bitcast.5.me.refs_3_, s32[64]{0:T(128)S(1)} %pad_add_fusion.1.mine.refs_4_, f32[12,128,128]{2,1,0:T(8,128)S(1)} %constant_dynamic-update-slice_fusion.inverse, f32[3,128,128]{2,1,0:T(8,128)S(1)} %copy-done.4, f32[24,128,128]{2,1,0:T(8,128)S(1)} %bitcast.13), custom_call_target="tpu_custom_call" | custom-call | flops 201326592 | bytes 3342336 | tf_op jit(solution)/shard_map/pallas_call | solution.py:101
  31.3 3.3 %collective-permute-done.5.refs_1_.peers_below = s32[4,64]{1,0:T(4,128)S(1)} collective-permute-done((s32[4,64]{1,0:T(4,128)S(1)}, s32[4,64]{1,0:T(4,128)S(1)}, u32[]{:S(2)}, u32[]{:S(2)}) %collective-permute-start.5) | collective-permute-done | bytes 1056 | tf_op jit(solution)/shard_map/ppermute | solution.py:269
  34.6 1.7 %shard_map.89 = (f32[6,128,128]{2,1,0:T(8,128)S(1)}, f32[6,128,128]{2,1,0:T(8,128)S(1)}) custom-call(f32[8,128,128]{2,1,0:T(8,128)} %collective-permute-done.4.refs_0_.refs_3_, s32[4,64]{1,0:T(4,128)S(1)} %collective-permute-done.5.refs_1_.peers_below, s32[4,64]{1,0:T(4,128)S(1)} %collective-permute-done.6.refs_2_.peers_above, s32[1]{0:T(128)} %bitcast.5.me.refs_3_, ...), custom_call_target="tpu_custom_call" | custom-call | bytes 3145728 | tf_op jit(solution)/shard_map/pallas_call | solution.py:101
  36.5 1.7 %collective-permute-done.12 = f32[6,128,128]{2,1,0:T(8,128)S(1)} collective-permute-done((f32[6,128,128]{2,1,0:T(8,128)S(1)}, f32[6,128,128]{2,1,0:T(8,128)S(1)}, u32[]{:S(2)}, u32[]{:S(2)}) %collective-permute-start.12) | collective-permute-done | bytes 393248 | tf_op jit(solution)/shard_map/ppermute | solution.py:260
  38.8 10.6 %collective-permute-done.13 = f32[6,128,128]{2,1,0:T(8,128)S(1)} collective-permute-done((f32[6,128,128]{2,1,0:T(8,128)S(1)}, f32[6,128,128]{2,1,0:T(8,128)S(1)}, u32[]{:S(2)}, u32[]{:S(2)}) %collective-permute-start.13) | collective-permute-done | bytes 393248 | tf_op jit(solution)/shard_map/ppermute | solution.py:260
  50.6 1.2 collective-permute-done.16
  51.9 1.7 %shard_map.93 = f32[8,128,128]{2,1,0:T(8,128)} custom-call(s32[1]{0:T(128)} %bitcast.5.me.refs_3_, s32[64]{0:T(128)S(1)} %pad_add_fusion.1.mine.refs_4_, s32[64]{0:T(128)S(1)} %collective-permute-done.2.mates.refs_5_, f32[12,128,128]{2,1,0:T(8,128)S(1)} %pad_maximum_fusion.inverse, f32[12,128,128]{2,1,0:T(8,128)S(1)} %get-tuple-element.32.upper.refs_0_, ...), custom_call_target="tpu_custom_call" | custom-call | bytes 2883584 | tf_op jit(solution)/shard_map/pallas_call | solution.py:101
  54.4 5.3 %collective-permute-start.17 = (f32[8,128,128]{2,1,0:T(8,128)}, f32[8,128,128]{2,1,0:T(8,128)}, u32[]{:S(2)}, u32[]{:S(2)}) collective-permute-start(f32[8,128,128]{2,1,0:T(8,128)} %shard_map.93), channel_id=1, source_target_pairs={{0,4},{1,9},{2,6},{3,11},{4,8},{5,13},{6,10},{7,15},{8,12},{9,17},... | collective-permute-start | bytes 1572872 | tf_op jit(solution)/shard_map/ppermute | solution.py:269
  60.3 3.5 %shard_map.91.refs_2_.table.refs_1_ = s32[96]{0:T(128)} custom-call(s32[1]{0:T(128)} %bitcast.5.me.refs_3_, s32[4,64]{1,0:T(4,128)} %copy-done.14, s32[4,64]{1,0:T(4,128)} %copy-done.8, s32[4,64]{1,0:T(4,128)} %copy-done.9), custom_call_target="tpu_custom_call" | custom-call | tf_op jit(solution)/shard_map/pallas_call | solution.py:331
  63.8 1.1 copy-done.3
  65.9 2.3 %shard_map.92.refs_6_ = f32[12,128,128]{2,1,0:T(8,128)S(1)} custom-call(s32[1]{0:T(128)} %bitcast.5.me.refs_3_, s32[64]{0:T(128)S(1)} %pad_add_fusion.1.mine.refs_4_, f32[12,128,128]{2,1,0:T(8,128)S(1)} %copy-done.3, f32[3,128,128]{2,1,0:T(8,128)S(1)} %copy-done.5, f32[24,128,128]{2,1,0:T(8,128)S(1)} %bitcast.14), custom_call_target="tpu_custom_call" | custom-call | flops 201326592 | bytes 3342336 | tf_op jit(solution)/shard_map/pallas_call | solution.py:101
  68.3 1.4 collective-permute-done.17.refs_9_
  69.6 1.9 %shard_map.94 = (f32[6,128,128]{2,1,0:T(8,128)S(1)}, f32[6,128,128]{2,1,0:T(8,128)S(1)}) custom-call(f32[4,128,128]{2,1,0:T(8,128)} %collective-permute-done.14.refs_0_.refs_4_, f32[8,128,128]{2,1,0:T(8,128)} %collective-permute-done.15.refs_1_.refs_5_, s32[96]{0:T(128)S(1)} %copy-done.7, s32[1]{0:T(128)} %bitcast.5.me.refs_3_, ...), custom_call_target="tpu_custom_call" | custom-call | bytes 3145728 | tf_op jit(solution)/shard_map/pallas_call | solution.py:101
  71.6 1.7 %collective-permute-done.18 = f32[6,128,128]{2,1,0:T(8,128)S(1)} collective-permute-done((f32[6,128,128]{2,1,0:T(8,128)S(1)}, f32[6,128,128]{2,1,0:T(8,128)S(1)}, u32[]{:S(2)}, u32[]{:S(2)}) %collective-permute-start.18) | collective-permute-done | bytes 393248 | tf_op jit(solution)/shard_map/ppermute | solution.py:260
  73.9 10.7 %collective-permute-done.19 = f32[6,128,128]{2,1,0:T(8,128)S(1)} collective-permute-done((f32[6,128,128]{2,1,0:T(8,128)S(1)}, f32[6,128,128]{2,1,0:T(8,128)S(1)}, u32[]{:S(2)}, u32[]{:S(2)}) %collective-permute-start.19) | collective-permute-done | bytes 393248 | tf_op jit(solution)/shard_map/ppermute | solution.py:260
  85.8 1.1 collective-permute-done.20
  87.4 5.3 %collective-permute-start.22 = (f32[12,16,128]{2,1,0:T(8,128)S(1)}, f32[12,16,128]{2,1,0:T(8,128)S(1)}, u32[]{:S(2)}, u32[]{:S(2)}) collective-permute-start(f32[12,16,128]{2,1,0:T(8,128)S(1)} %shard_map.96.x), channel_id=1, source_target_pairs={{0,4},{1,9},{2,6},{3,11},{4,8},{5,13},{6,10},{7,15},{8,12},{9,17},... | collective-permute-start | bytes 294920 | tf_op jit(solution)/shard_map/ppermute | solution.py:269
  92.7 2.4 %shard_map.97 = (bf16[16,256,128]{2,1,0:T(8,128)(2,1)S(1)}, bf16[8,256,128]{2,1,0:T(8,128)(2,1)S(1)}) custom-call(s32[1]{0:T(128)} %bitcast.5.me.refs_3_, s32[96]{0:T(128)S(1)} %copy-done.7, f32[12,128,128]{2,1,0:T(8,128)S(1)} %pad_maximum_fusion.1.inverse, f32[8,128,128]{2,1,0:T(8,128)} %get-tuple-element.27.refs_7_.refs_0_, ...), custom_call_target="tpu_custom_call" | custom-call | flops 402653184 | bytes 4980736 | tf_op jit(solution)/shard_map/pallas_call | solution.py:101
  95.9 1.0 shard_map.99
  97.0 1.3 collective-permute-done.23
  98.3 4.2 %collective-permute-start.24 = (f32[12,16,128]{2,1,0:T(8,128)S(1)}, f32[12,16,128]{2,1,0:T(8,128)S(1)}, u32[]{:S(2)}, u32[]{:S(2)}) collective-permute-start(f32[12,16,128]{2,1,0:T(8,128)S(1)} %add_subtract_fusion.5.x), channel_id=1, source_target_pairs={{0,4},{1,9},{2,6},{3,11},{4,8},{5,13},{6,10},{7,15},{8,12},{9,17},... | collective-permute-start | bytes 294920 | tf_op jit(solution)/shard_map/ppermute | solution.py:269
  103.3 1.5 collective-permute-done.24.arrived
  104.8 1.0 shard_map.101
  107.2 5.1 %collective-permute-start.26 = (f32[12,16,128]{2,1,0:T(8,128)S(1)}, f32[12,16,128]{2,1,0:T(8,128)S(1)}, u32[]{:S(2)}, u32[]{:S(2)}) collective-permute-start(f32[12,16,128]{2,1,0:T(8,128)S(1)} %add_subtract_fusion.4.x), channel_id=1, source_target_pairs={{0,4},{1,9},{2,6},{3,11},{4,8},{5,13},{6,10},{7,15},{8,12},{9,17},... | collective-permute-start | bytes 294920 | tf_op jit(solution)/shard_map/ppermute | solution.py:269
  113.1 1.4 collective-permute-done.26.refs_4_
  115.6 1.3 collective-permute-done.27
  116.9 4.3 %collective-permute-start.29 = (f32[12,16,128]{2,1,0:T(8,128)S(1)}, f32[12,16,128]{2,1,0:T(8,128)S(1)}, u32[]{:S(2)}, u32[]{:S(2)}) collective-permute-start(f32[12,16,128]{2,1,0:T(8,128)S(1)} %add_subtract_fusion.3.x), channel_id=1, source_target_pairs={{4,0},{6,2},{8,4},{9,1},{10,6},{11,3},{12,8},{13,5},{14,10},{15,7}... | collective-permute-start | bytes 294920 | tf_op jit(solution)/shard_map/ppermute | solution.py:269
  121.2 1.2 shard_map.104
  123.2 2.2 %collective-permute-done.29.arrived = f32[12,16,128]{2,1,0:T(8,128)S(1)} collective-permute-done((f32[12,16,128]{2,1,0:T(8,128)S(1)}, f32[12,16,128]{2,1,0:T(8,128)S(1)}, u32[]{:S(2)}, u32[]{:S(2)}) %collective-permute-start.29) | collective-permute-done | bytes 98336 | tf_op jit(solution)/shard_map/ppermute | solution.py:269
  126.5 1.3 collective-permute-done.30
  127.8 2.2 %collective-permute-start.31 = (f32[12,16,128]{2,1,0:T(8,128)S(1)}, f32[12,16,128]{2,1,0:T(8,128)S(1)}, u32[]{:S(2)}, u32[]{:S(2)}) collective-permute-start(f32[12,16,128]{2,1,0:T(8,128)S(1)} %add_subtract_fusion.2.x), channel_id=1, source_target_pairs={{4,0},{6,2},{8,4},{9,1},{10,6},{11,3},{12,8},{13,5},{14,10},{15,7}... | collective-permute-start | bytes 294920 | tf_op jit(solution)/shard_map/ppermute | solution.py:269
  130.9 4.3 %collective-permute-done.31.arrived = f32[12,16,128]{2,1,0:T(8,128)S(1)} collective-permute-done((f32[12,16,128]{2,1,0:T(8,128)S(1)}, f32[12,16,128]{2,1,0:T(8,128)S(1)}, u32[]{:S(2)}, u32[]{:S(2)}) %collective-permute-start.31) | collective-permute-done | bytes 98336 | tf_op jit(solution)/shard_map/ppermute | solution.py:269
  135.2 1.0 shard_map.108
  136.3 1.3 collective-permute-done.32
  137.6 1.9 %collective-permute-start.33 = (f32[12,16,128]{2,1,0:T(8,128)S(1)}, f32[12,16,128]{2,1,0:T(8,128)S(1)}, u32[]{:S(2)}, u32[]{:S(2)}) collective-permute-start(f32[12,16,128]{2,1,0:T(8,128)S(1)} %add_subtract_fusion.1.x), channel_id=1, source_target_pairs={{4,0},{6,2},{8,4},{9,1},{10,6},{11,3},{12,8},{13,5},{14,10},{15,7}... | collective-permute-start | bytes 294920 | tf_op jit(solution)/shard_map/ppermute | solution.py:269
  140.4 4.7 %collective-permute-done.33.arrived = f32[12,16,128]{2,1,0:T(8,128)S(1)} collective-permute-done((f32[12,16,128]{2,1,0:T(8,128)S(1)}, f32[12,16,128]{2,1,0:T(8,128)S(1)}, u32[]{:S(2)}, u32[]{:S(2)}) %collective-permute-start.33) | collective-permute-done | bytes 98336 | tf_op jit(solution)/shard_map/ppermute | solution.py:269
  145.0 1.0 shard_map.110
  146.1 1.3 collective-permute-done.34
  148.7 3.7 %collective-permute-done.35 = f32[12,16,128]{2,1,0:T(8,128)S(1)} collective-permute-done((f32[12,16,128]{2,1,0:T(8,128)S(1)}, f32[12,16,128]{2,1,0:T(8,128)S(1)}, u32[]{:S(2)}, u32[]{:S(2)}) %collective-permute-start.35) | collective-permute-done | bytes 98336 | tf_op jit(solution)/shard_map/ppermute | solution.py:260
  (109 shorter events, 23.5 us)
Async XLA Ops:
  3.2 1.4 copy-start
  4.6 2.2 %copy-start.10 = (f32[3,128,128]{2,1,0:T(8,128)S(1)}, f32[3,128,128]{2,1,0:T(8,128)}, u32[]{:S(2)}) copy-start(f32[3,128,128]{2,1,0:T(8,128)} %param.9) | copy-start | bytes 589828
  6.8 11.8 %collective-permute-start.10 = (f32[12,128,128]{2,1,0:T(8,128)S(1)}, f32[12,128,128]{2,1,0:T(8,128)S(1)}, u32[]{:S(2)}, u32[]{:S(2)}) collective-permute-start(f32[12,128,128]{2,1,0:T(8,128)S(1)} %get-tuple-element.32.upper.refs_0_), channel_id=1, source_target_pairs={{0,1},{1,0},{2,3},{3,2},{4,5},{5,4},{6,7},{7,6},{8,9},{9,8},{10,11... | collective-permute-start | bytes 2359304 | tf_op jit(solution)/shard_map/ppermute | solution.py:260
  6.8 8.5 %collective-permute-start = (f32[3,128,128]{2,1,0:T(8,128)S(1)}, f32[3,128,128]{2,1,0:T(8,128)S(1)}, u32[]{:S(2)}, u32[]{:S(2)}) collective-permute-start(f32[3,128,128]{2,1,0:T(8,128)S(1)} %copy-done.10), channel_id=1, source_target_pairs={{0,2},{1,3},{2,0},{3,1},{4,6},{5,7},{6,4},{7,5},{8,10},{9,11},{10,... | collective-permute-start | bytes 589832 | tf_op jit(solution)/shard_map/ppermute | solution.py:260
  8.3 5.9 %collective-permute-start.1 = (s32[64]{0:T(128)S(1)}, s32[64]{0:T(128)S(1)}, u32[]{:S(2)}, u32[]{:S(2)}) collective-permute-start(s32[64]{0:T(128)S(1)} %pad_add_fusion.1.mine.refs_4_), channel_id=1, source_target_pairs={{0,2},{1,3},{2,0},{3,1},{4,6},{5,7},{6,4},{7,5},{8,10},{9,11},{10,... | collective-permute-start | bytes 776 | tf_op jit(solution)/shard_map/ppermute | solution.py:260
  8.9 5.4 %collective-permute-start.2 = (s32[64]{0:T(128)S(1)}, s32[64]{0:T(128)S(1)}, u32[]{:S(2)}, u32[]{:S(2)}) collective-permute-start(s32[64]{0:T(128)S(1)} %pad_add_fusion.1.mine.refs_4_), channel_id=1, source_target_pairs={{0,1},{1,0},{2,3},{3,2},{4,5},{5,4},{6,7},{7,6},{8,9},{9,8},{10,11... | collective-permute-start | bytes 776 | tf_op jit(solution)/shard_map/ppermute | solution.py:260
  8.9 25.7 %collective-permute-start.9 = (f32[8,128,128]{2,1,0:T(8,128)}, f32[8,128,128]{2,1,0:T(8,128)}, u32[]{:S(2)}, u32[]{:S(2)}) collective-permute-start(f32[8,128,128]{2,1,0:T(8,128)} %get-tuple-element.27.refs_7_.refs_0_), channel_id=1, source_target_pairs={{0,1},{1,0},{2,3},{3,2},{4,5},{5,4},{6,7},{7,6},{8,9},{9,8},{10,11... | collective-permute-start | bytes 1572872 | tf_op jit(solution)/shard_map/ppermute | solution.py:260
  14.2 1.1 collective-permute-start.3
  15.3 4.2 %copy-start.12 = (f32[3,128,128]{2,1,0:T(8,128)}, f32[3,128,128]{2,1,0:T(8,128)S(1)}, u32[]{:S(2)}) copy-start(f32[3,128,128]{2,1,0:T(8,128)S(1)} %collective-permute-done) | copy-start | bytes 589828
  15.3 19.3 %collective-permute-start.4 = (f32[8,128,128]{2,1,0:T(8,128)}, f32[8,128,128]{2,1,0:T(8,128)}, u32[]{:S(2)}, u32[]{:S(2)}) collective-permute-start(f32[8,128,128]{2,1,0:T(8,128)} %get-tuple-element.27.refs_7_.refs_0_), channel_id=1, source_target_pairs={{0,2},{1,3},{2,0},{3,1},{4,6},{5,7},{6,4},{7,5},{8,10},{9,11},{10,... | collective-permute-start | bytes 1572872 | tf_op jit(solution)/shard_map/ppermute | solution.py:260
  16.9 1.4 collective-permute-start.7
  16.9 1.7 %collective-permute-start.8 = (f32[3,128,128]{2,1,0:T(8,128)S(1)}, f32[3,128,128]{2,1,0:T(8,128)S(1)}, u32[]{:S(2)}, u32[]{:S(2)}) collective-permute-start(f32[3,128,128]{2,1,0:T(8,128)S(1)} %collective-permute-done), channel_id=1, source_target_pairs={{0,1},{1,0},{2,3},{3,2},{4,5},{5,4},{6,7},{7,6},{8,9},{9,8},{10,11... | collective-permute-start | bytes 589832 | tf_op jit(solution)/shard_map/ppermute | solution.py:260
  18.3 10.5 %copy-start.1 = (f32[12,2,128,128]{3,2,1,0:T(8,128)S(1)}, f32[12,2,128,128]{3,2,1,0:T(8,128)}, u32[]{:S(2)}) copy-start(f32[12,2,128,128]{3,2,1,0:T(8,128)} %param.10) | copy-start | bytes 4718596
  18.3 10.5 %copy-start.4 = (f32[3,128,128]{2,1,0:T(8,128)S(1)}, f32[3,128,128]{2,1,0:T(8,128)}, u32[]{:S(2)}) copy-start(f32[3,128,128]{2,1,0:T(8,128)} %diag.3) | copy-start | bytes 589828
  19.5 15.1 %collective-permute-start.11 = (f32[8,128,128]{2,1,0:T(8,128)S(1)}, f32[8,128,128]{2,1,0:T(8,128)S(1)}, u32[]{:S(2)}, u32[]{:S(2)}) collective-permute-start(f32[8,128,128]{2,1,0:T(8,128)S(1)} %shard_map.88), channel_id=1, source_target_pairs={{0,4},{1,9},{2,6},{3,11},{4,8},{5,13},{6,10},{7,15},{8,12},{9,17},... | collective-permute-start | bytes 1572872 | tf_op jit(solution)/shard_map/ppermute | solution.py:269
  23.0 8.2 %copy-start.14 = (s32[4,64]{1,0:T(4,128)}, s32[4,64]{1,0:T(4,128)S(1)}, u32[]{:S(2)}) copy-start(s32[4,64]{1,0:T(4,128)S(1)} %pad_add_fusion.metas) | copy-start | bytes 3076
  23.0 11.6 %collective-permute-start.5 = (s32[4,64]{1,0:T(4,128)S(1)}, s32[4,64]{1,0:T(4,128)S(1)}, u32[]{:S(2)}, u32[]{:S(2)}) collective-permute-start(s32[4,64]{1,0:T(4,128)S(1)} %pad_add_fusion.metas), channel_id=1, source_target_pairs={{0,4},{1,9},{2,6},{3,11},{4,8},{5,13},{6,10},{7,15},{8,12},{9,17},... | collective-permute-start | bytes 3080 | tf_op jit(solution)/shard_map/ppermute | solution.py:269
  26.4 8.2 %collective-permute-start.6 = (s32[4,64]{1,0:T(4,128)S(1)}, s32[4,64]{1,0:T(4,128)S(1)}, u32[]{:S(2)}, u32[]{:S(2)}) collective-permute-start(s32[4,64]{1,0:T(4,128)S(1)} %pad_add_fusion.metas), channel_id=1, source_target_pairs={{4,0},{6,2},{8,4},{9,1},{10,6},{11,3},{12,8},{13,5},{14,10},{15,7}... | collective-permute-start | bytes 3080 | tf_op jit(solution)/shard_map/ppermute | solution.py:269
  31.2 7.6 %copy-start.11 = (f32[3,128,128]{2,1,0:T(8,128)S(1)}, f32[3,128,128]{2,1,0:T(8,128)}, u32[]{:S(2)}) copy-start(f32[3,128,128]{2,1,0:T(8,128)} %param.9) | copy-start | bytes 589828
  31.2 7.5 %copy-start.13 = (f32[3,128,128]{2,1,0:T(8,128)S(1)}, f32[3,128,128]{2,1,0:T(8,128)}, u32[]{:S(2)}) copy-start(f32[3,128,128]{2,1,0:T(8,128)} %copy-done.12) | copy-start | bytes 589828
  34.6 3.6 %copy-start.8 = (s32[4,64]{1,0:T(4,128)}, s32[4,64]{1,0:T(4,128)S(1)}, u32[]{:S(2)}) copy-start(s32[4,64]{1,0:T(4,128)S(1)} %collective-permute-done.5.refs_1_.peers_below) | copy-start | bytes 3076
  34.6 3.6 %copy-start.9 = (s32[4,64]{1,0:T(4,128)}, s32[4,64]{1,0:T(4,128)S(1)}, u32[]{:S(2)}) copy-start(s32[4,64]{1,0:T(4,128)S(1)} %collective-permute-done.6.refs_2_.peers_above) | copy-start | bytes 3076
  36.3 1.8 %collective-permute-start.12 = (f32[6,128,128]{2,1,0:T(8,128)S(1)}, f32[6,128,128]{2,1,0:T(8,128)S(1)}, u32[]{:S(2)}, u32[]{:S(2)}) collective-permute-start(f32[6,128,128]{2,1,0:T(8,128)S(1)} %get-tuple-element.34), channel_id=1, source_target_pairs={{0,1},{1,0},{2,3},{3,2},{4,5},{5,4},{6,7},{7,6},{8,9},{9,8},{10,11... | collective-permute-start | bytes 1179656 | tf_op jit(solution)/shard_map/ppermute | solution.py:260
  38.2 11.2 %collective-permute-start.13 = (f32[6,128,128]{2,1,0:T(8,128)S(1)}, f32[6,128,128]{2,1,0:T(8,128)S(1)}, u32[]{:S(2)}, u32[]{:S(2)}) collective-permute-start(f32[6,128,128]{2,1,0:T(8,128)S(1)} %add.30), channel_id=1, source_target_pairs={{0,2},{1,3},{2,0},{3,1},{4,6},{5,7},{6,4},{7,5},{8,10},{9,11},{10,... | collective-permute-start | bytes 1179656 | tf_op jit(solution)/shard_map/ppermute | solution.py:260
  50.0 1.8 %collective-permute-start.16 = (f32[6,128,128]{2,1,0:T(8,128)S(1)}, f32[6,128,128]{2,1,0:T(8,128)S(1)}, u32[]{:S(2)}, u32[]{:S(2)}) collective-permute-start(f32[6,128,128]{2,1,0:T(8,128)S(1)} %shard_map.90.inverse), channel_id=1, source_target_pairs={{0,1},{1,0},{2,3},{3,2},{4,5},{5,4},{6,7},{7,6},{8,9},{9,8},{10,11... | collective-permute-start | bytes 1179656 | tf_op jit(solution)/shard_map/ppermute | solution.py:260
  50.1 18.2 %collective-permute-start.15 = (f32[8,128,128]{2,1,0:T(8,128)}, f32[8,128,128]{2,1,0:T(8,128)}, u32[]{:S(2)}, u32[]{:S(2)}) collective-permute-start(f32[8,128,128]{2,1,0:T(8,128)} %collective-permute-done.4.refs_0_.refs_3_), channel_id=1, source_target_pairs={{0,1},{1,0},{2,3},{3,2},{4,5},{5,4},{6,7},{7,6},{8,9},{9,8},{10,11... | collective-permute-start | bytes 1572872 | tf_op jit(solution)/shard_map/ppermute | solution.py:260
  54.4 15.2 %collective-permute-start.17 = (f32[8,128,128]{2,1,0:T(8,128)}, f32[8,128,128]{2,1,0:T(8,128)}, u32[]{:S(2)}, u32[]{:S(2)}) collective-permute-start(f32[8,128,128]{2,1,0:T(8,128)} %shard_map.93), channel_id=1, source_target_pairs={{0,4},{1,9},{2,6},{3,11},{4,8},{5,13},{6,10},{7,15},{8,12},{9,17},... | collective-permute-start | bytes 1572872 | tf_op jit(solution)/shard_map/ppermute | solution.py:269
  59.7 8.5 %collective-permute-start.14 = (f32[4,128,128]{2,1,0:T(8,128)}, f32[4,128,128]{2,1,0:T(8,128)}, u32[]{:S(2)}, u32[]{:S(2)}) collective-permute-start(f32[4,128,128]{2,1,0:T(8,128)} %get-tuple-element.35.refs_1_), channel_id=1, source_target_pairs={{0,2},{1,3},{2,0},{3,1},{4,6},{5,7},{6,4},{7,5},{8,10},{9,11},{10,... | collective-permute-start | bytes 786440 | tf_op jit(solution)/shard_map/ppermute | solution.py:260
  65.9 3.7 %copy-start.7 = (s32[96]{0:T(128)S(1)}, s32[96]{0:T(128)}, u32[]{:S(2)}) copy-start(s32[96]{0:T(128)} %shard_map.91.refs_2_.table.refs_1_) | copy-start | bytes 1156
  71.5 1.8 %collective-permute-start.18 = (f32[6,128,128]{2,1,0:T(8,128)S(1)}, f32[6,128,128]{2,1,0:T(8,128)S(1)}, u32[]{:S(2)}, u32[]{:S(2)}) collective-permute-start(f32[6,128,128]{2,1,0:T(8,128)S(1)} %get-tuple-element.37), channel_id=1, source_target_pairs={{0,1},{1,0},{2,3},{3,2},{4,5},{5,4},{6,7},{7,6},{8,9},{9,8},{10,11... | collective-permute-start | bytes 1179656 | tf_op jit(solution)/shard_map/ppermute | solution.py:260
  73.3 11.2 %collective-permute-start.19 = (f32[6,128,128]{2,1,0:T(8,128)S(1)}, f32[6,128,128]{2,1,0:T(8,128)S(1)}, u32[]{:S(2)}, u32[]{:S(2)}) collective-permute-start(f32[6,128,128]{2,1,0:T(8,128)S(1)} %add.32), channel_id=1, source_target_pairs={{0,2},{1,3},{2,0},{3,1},{4,6},{5,7},{6,4},{7,5},{8,10},{9,11},{10,... | collective-permute-start | bytes 1179656 | tf_op jit(solution)/shard_map/ppermute | solution.py:260
  84.7 2.3 %copy-start.6 = (f32[12,32,128]{2,1,0:T(8,128)S(1)}, f32[12,32,128]{2,1,0:T(8,128)}, u32[]{:S(2)}) copy-start(f32[12,32,128]{2,1,0:T(8,128)} %base.1) | copy-start | bytes 589828
  85.2 1.8 %collective-permute-start.20 = (f32[6,128,128]{2,1,0:T(8,128)S(1)}, f32[6,128,128]{2,1,0:T(8,128)S(1)}, u32[]{:S(2)}, u32[]{:S(2)}) collective-permute-start(f32[6,128,128]{2,1,0:T(8,128)S(1)} %shard_map.95), channel_id=1, source_target_pairs={{0,1},{1,0},{2,3},{3,2},{4,5},{5,4},{6,7},{7,6},{8,9},{9,8},{10,11... | collective-permute-start | bytes 1179656 | tf_op jit(solution)/shard_map/ppermute | solution.py:260
  85.3 20.6 %collective-permute-start.21 = (f32[12,128,128]{2,1,0:T(8,128)S(1)}, f32[12,128,128]{2,1,0:T(8,128)S(1)}, u32[]{:S(2)}, u32[]{:S(2)}) collective-permute-start(f32[12,128,128]{2,1,0:T(8,128)S(1)} %get-tuple-element.32.upper.refs_0_), channel_id=1, source_target_pairs={{0,2},{1,3},{2,0},{3,1},{4,6},{5,7},{6,4},{7,5},{8,10},{9,11},{10,... | collective-permute-start | bytes 2359304 | tf_op jit(solution)/shard_map/ppermute | solution.py:260
  87.4 8.5 %collective-permute-start.22 = (f32[12,16,128]{2,1,0:T(8,128)S(1)}, f32[12,16,128]{2,1,0:T(8,128)S(1)}, u32[]{:S(2)}, u32[]{:S(2)}) collective-permute-start(f32[12,16,128]{2,1,0:T(8,128)S(1)} %shard_map.96.x), channel_id=1, source_target_pairs={{0,4},{1,9},{2,6},{3,11},{4,8},{5,13},{6,10},{7,15},{8,12},{9,17},... | collective-permute-start | bytes 294920 | tf_op jit(solution)/shard_map/ppermute | solution.py:269
  96.9 1.4 collective-permute-start.23
  98.3 6.5 %collective-permute-start.24 = (f32[12,16,128]{2,1,0:T(8,128)S(1)}, f32[12,16,128]{2,1,0:T(8,128)S(1)}, u32[]{:S(2)}, u32[]{:S(2)}) collective-permute-start(f32[12,16,128]{2,1,0:T(8,128)S(1)} %add_subtract_fusion.5.x), channel_id=1, source_target_pairs={{0,4},{1,9},{2,6},{3,11},{4,8},{5,13},{6,10},{7,15},{8,12},{9,17},... | collective-permute-start | bytes 294920 | tf_op jit(solution)/shard_map/ppermute | solution.py:269
  105.8 1.4 collective-permute-start.25
  105.9 15.3 %collective-permute-start.28 = (f32[12,128,128]{2,1,0:T(8,128)S(1)}, f32[12,128,128]{2,1,0:T(8,128)S(1)}, u32[]{:S(2)}, u32[]{:S(2)}) collective-permute-start(f32[12,128,128]{2,1,0:T(8,128)S(1)} %collective-permute-done.21.refs_0_.refs_2_), channel_id=1, source_target_pairs={{0,1},{1,0},{2,3},{3,2},{4,5},{5,4},{6,7},{7,6},{8,9},{9,8},{10,11... | collective-permute-start | bytes 2359304 | tf_op jit(solution)/shard_map/ppermute | solution.py:260
  107.2 7.3 %collective-permute-start.26 = (f32[12,16,128]{2,1,0:T(8,128)S(1)}, f32[12,16,128]{2,1,0:T(8,128)S(1)}, u32[]{:S(2)}, u32[]{:S(2)}) collective-permute-start(f32[12,16,128]{2,1,0:T(8,128)S(1)} %add_subtract_fusion.4.x), channel_id=1, source_target_pairs={{0,4},{1,9},{2,6},{3,11},{4,8},{5,13},{6,10},{7,15},{8,12},{9,17},... | collective-permute-start | bytes 294920 | tf_op jit(solution)/shard_map/ppermute | solution.py:269
  115.5 1.4 collective-permute-start.27
  116.9 8.6 %collective-permute-start.29 = (f32[12,16,128]{2,1,0:T(8,128)S(1)}, f32[12,16,128]{2,1,0:T(8,128)S(1)}, u32[]{:S(2)}, u32[]{:S(2)}) collective-permute-start(f32[12,16,128]{2,1,0:T(8,128)S(1)} %add_subtract_fusion.3.x), channel_id=1, source_target_pairs={{4,0},{6,2},{8,4},{9,1},{10,6},{11,3},{12,8},{13,5},{14,10},{15,7}... | collective-permute-start | bytes 294920 | tf_op jit(solution)/shard_map/ppermute | solution.py:269
  126.4 1.4 collective-permute-start.30
  127.8 7.4 %collective-permute-start.31 = (f32[12,16,128]{2,1,0:T(8,128)S(1)}, f32[12,16,128]{2,1,0:T(8,128)S(1)}, u32[]{:S(2)}, u32[]{:S(2)}) collective-permute-start(f32[12,16,128]{2,1,0:T(8,128)S(1)} %add_subtract_fusion.2.x), channel_id=1, source_target_pairs={{4,0},{6,2},{8,4},{9,1},{10,6},{11,3},{12,8},{13,5},{14,10},{15,7}... | collective-permute-start | bytes 294920 | tf_op jit(solution)/shard_map/ppermute | solution.py:269
  136.2 1.4 collective-permute-start.32
  137.6 7.4 %collective-permute-start.33 = (f32[12,16,128]{2,1,0:T(8,128)S(1)}, f32[12,16,128]{2,1,0:T(8,128)S(1)}, u32[]{:S(2)}, u32[]{:S(2)}) collective-permute-start(f32[12,16,128]{2,1,0:T(8,128)S(1)} %add_subtract_fusion.1.x), channel_id=1, source_target_pairs={{4,0},{6,2},{8,4},{9,1},{10,6},{11,3},{12,8},{13,5},{14,10},{15,7}... | collective-permute-start | bytes 294920 | tf_op jit(solution)/shard_map/ppermute | solution.py:269
  146.0 1.4 collective-permute-start.34
  147.4 4.9 %collective-permute-start.35 = (f32[12,16,128]{2,1,0:T(8,128)S(1)}, f32[12,16,128]{2,1,0:T(8,128)S(1)}, u32[]{:S(2)}, u32[]{:S(2)}) collective-permute-start(f32[12,16,128]{2,1,0:T(8,128)S(1)} %add_subtract_fusion), channel_id=1, source_target_pairs={{0,2},{1,3},{2,0},{3,1},{4,6},{5,7},{6,4},{7,5},{8,10},{9,11},{10,... | collective-permute-start | bytes 294920 | tf_op jit(solution)/shard_map/ppermute | solution.py:260
  (3 other events, 3.0 us)

commit v4 on v3

--- a/solution.py
+++ b/solution.py
@@ -75,17 +75,12 @@
     def is_local(self, meta, s, side):
         return (self.kind(meta, s) == side) & (self.link(meta, s) < self.slots)
 
-    def scan(self, meta, side, found):
-        def step(s, count):
-            hit = self.is_local(meta, s, side)
-
-            @pl.when(hit & (count < self.pairs))
-            def _():
-                found(s, count)
-
-            return count + hit.astype(jnp.int32)
-
-        return lax.fori_loop(0, self.slots, step, 0)
+    def scan(self, meta, side, places):
+        count = jnp.int32(0)
+        for s in range(self.slots):
+            places[count] = s
+            count = count + self.is_local(meta, s, side).astype(jnp.int32)
+        return count
 
 
 def smem():
@@ -96,38 +91,37 @@
     return pl.BlockSpec(memory_space=pltpu.VMEM)
 
 
-def call(body, outs, scalars, arrays, flops=0, scratch=(), early=()):
+def call(body, outs, scalars, arrays, flops=0, scratch=(), early=(), to_smem=False):
     moved = sum(a.size * a.dtype.itemsize for a in arrays) + sum(o.size * o.dtype.itemsize for o in outs)
     return pl.pallas_call(
         body if not early else lambda *refs: body(*refs[len(early) :]),
         out_shape=outs,
         in_specs=[pl.BlockSpec(memory_space=pl.ANY)] * len(early) + [smem()] * len(scalars) + [vmem()] * len(arrays),
-        out_specs=[vmem()] * len(outs),
+        out_specs=[smem() if to_smem else vmem()] * len(outs),
         scratch_shapes=list(scratch),
         compiler_params=pltpu.CompilerParams(vmem_limit_bytes=8 << 20),
         cost_estimate=pl.CostEstimate(flops=flops, bytes_accessed=moved, transcendentals=0),
     )(*early, *scalars, *arrays)
 
 
-def gather_kernel(lay, mine, tiles, lower, lower_local, upper, places):
-    for side, base, out in ((1, 2, lower), (2, 0, upper)):
-        for which in range(2):
-            for j in range(lay.cap):
-                s, live, _ = lay.lookup(mine, base + which, side, j)
-                out[which * lay.cap + j] = jnp.where(live, tiles[s], 0.0)
-    for side, out, start in ((1, lower_local, 0), (2, upper, 2 * lay.cap)):
-        for i in range(lay.pairs):
-            places[i] = 0
-
-        def found(s, i):
-            places[i] = s
-
-        count = lay.scan(mine, side, found)
-        for i in range(lay.pairs):
-            out[start + i] = jnp.where(i < count, tiles[places[i]], 0.0)
-
-
-def outgoing_kernel(lay, me, mine, mates, inverse, upper, mate_upper, out):
+def listed_tiles(lay, meta, side, tiles, out):
+    for which in range(2):
+        for j in range(lay.cap):
+            s, live, _ = lay.lookup(meta, 4 - 2 * side + which, side, j)
+            out[which * lay.cap + j] = jnp.where(live, tiles[s], 0.0)
+
+
+def outgoing_kernel(lay, me, mine, mates, inverse, tiles, mate_tiles, out, lower):
+    role = me[0] % 2
+    for g, (meta, source) in enumerate(((mine, tiles), (mates, mate_tiles))):
+        for j in range(lay.cap):
+            s, live, _ = lay.lookup(meta, role, 2, j)
+            tile = jnp.where(live, source[s], 0.0)
+            out[g * lay.cap + j] = matmul(inverse[lay.place(s // lay.width, me[0])], tile)
+    listed_tiles(lay, mine, 1, tiles, lower)
+
+
+def next_outgoing_kernel(lay, me, mine, mates, inverse, upper, mate_upper, out):
     role = me[0] % 2
     for g, (meta, source) in enumerate(((mine, upper), (mates, mate_upper))):
         for j in range(lay.cap):
@@ -135,7 +129,7 @@
             out[g * lay.cap + j] = matmul(inverse[lay.place(r, me[0])], source[role * lay.cap + j])
 
 
-def local_pivot_kernel(lay, me, mine, inverse, diag, tiles, out):
+def local_terms(lay, me, mine, inverse, diag, tiles, out):
     out[: lay.own_rows] = -diag[...]
     out[lay.own_rows :] = jnp.zeros((lay.rows - lay.own_rows,) + diag.shape[1:], F32)
 
@@ -146,6 +140,24 @@
             v = lay.link(mine, s)
             q = matmul(inverse[lay.place(v // lay.width, me[0])], tiles[v])
             out[lay.place(s // lay.width, me[0])] += matmul(tiles[s], q)
+
+
+def local_pivot_kernel(
+    lay, me, mine, mates, inverse, diag, tiles, mate_tiles, out, mate_lower, lower_local, upper, mate_upper, places
+):
+    local_terms(lay, me, mine, inverse, diag, tiles, out)
+    listed_tiles(lay, mates, 1, mate_tiles, mate_lower)
+    listed_tiles(lay, mates, 2, mate_tiles, mate_upper)
+    listed_tiles(lay, mine, 2, tiles, upper)
+    for side, target, start in ((1, lower_local, 0), (2, upper, 2 * lay.cap)):
+        count = lay.scan(mine, side, places)
+        for i in range(lay.pairs):
+            live = i < count
+            target[start + i] = jnp.where(live, tiles[jnp.where(live, places[i], 0)], 0.0)
+
+
+def next_local_pivot_kernel(lay, me, mine, inverse, diag, tiles, out):
+    local_terms(lay, me, mine, inverse, diag, tiles, out)
 
 
 def incoming_kernel(lay, me, mine, mates, local, lower, mate_lower, arrived, keep, give, total):
@@ -172,7 +184,7 @@
         out[i] = 2.0 * x + matmul_parts(*split(product), xh, xl)
 
 
-def table_kernel(lay, me, metas, peers_below, peers_above, out):
+def table_kernel(lay, me, metas, peers_below, peers_above, out, places):
     role = me[0] % 2
     for side in (1, 2):
         start = (side - 1) * lay.table
@@ -187,15 +199,12 @@
         for q in range(0, lay.n_tile, 2):
             meta = metas.at[q]
             begin = start + 2 * lay.listed_slots + ((q ^ me[0]) >> 1) * lay.pairs
+            count = lay.scan(meta, side, places)
             for i in range(lay.pairs):
-                out[begin + i] = 0
-                out[begin + lay.local_slots + i] = 0
-
-            def found(s, i, meta=meta, begin=begin):
+                s = jnp.where(i < count, places[i], 0)
                 out[begin + i] = s // lay.width
-                out[begin + lay.local_slots + i] = lay.link(meta, s) // lay.width
-
-            lay.scan(meta, side, found)
+                v = jnp.where(i < count, lay.link(meta, s), 0)
+                out[begin + lay.local_slots + i] = v // lay.width
 
 
 def scaled_kernel(lay, side, me, table, inverse, *refs):
@@ -288,53 +297,62 @@
             held += [swap(one, bit) for one in held]
         return held
 
+    mate_tiles = swap(tiles, 1)
     arriving = over_chips(inverse_prev)
     held = over_chips(mine)
     both = [swap(x, 1) for x in held]
-    lower, lower_local, upper = call(
-        kernel(gather_kernel),
-        [shape(2 * cap, n, n), shape(lay.pairs, n, n), shape(2 * cap + lay.pairs, n, n)],
-        (mine,),
-        (tiles,),
-        scratch=(pltpu.SMEM((lay.pairs,), jnp.int32),),
-    )
-    mate_lower, mate_upper = swap(lower, 1), swap(upper, 1)
-    arriving, held, both, lower, lower_local, upper = lax.optimization_barrier(
-        (arriving, held, both, lower, lower_local, upper)
-    )
+    arriving, held, both = lax.optimization_barrier((arriving, held, both))
     mates = both[0]
     metas = jnp.stack([one for pair in zip(held, both) for one in pair])
     kept = jnp.concatenate(arriving, 0)
     mated = jnp.concatenate([swap(x, 1) for x in arriving], 0)
     half = rows // 2
+    lists, local_list = shape(2 * cap, n, n), shape(lay.pairs, n, n)
+    places = pltpu.SMEM((lay.slots + 1,), jnp.int32)
     for sweep in range(FSWEEPS):
         inverse = jnp.concatenate([kept, mated], 0)
-        (out,) = call(
-            kernel(outgoing_kernel), [shape(2 * cap, n, n)], (me, mine, mates), (inverse, upper, mate_upper)
-        )
-        arrived = along(out, 1)
-        (here,) = call(
-            kernel(local_pivot_kernel),
-            [shape(rows, n, n)],
-            (me, mine),
-            (inverse, diag_block, tiles),
-            flops=product * rows,
-        )
-        early = []
+        early, later = [], []
         if sweep == 0:
+            out, lower = call(
+                kernel(outgoing_kernel), [lists] * 2, (me, mine, mates), (inverse, tiles, mate_tiles)
+            )
+            arrived = along(out, 1)
             lowers = over_chips(lower)
-            below, above = along(metas, 1), along(metas, -1)
-            early += [*lowers[1:], below, above]
+            here, mate_lower, lower_local, upper, mate_upper = call(
+                kernel(local_pivot_kernel),
+                [shape(rows, n, n), lists, local_list, shape(2 * cap + lay.pairs, n, n), lists],
+                (me, mine, mates),
+                (inverse, diag_block, tiles, mate_tiles),
+                flops=product * rows,
+                scratch=(places,),
+            )
+            early += lowers[1:]
+        else:
+            (out,) = call(
+                kernel(next_outgoing_kernel), [lists], (me, mine, mates), (inverse, upper, mate_upper)
+            )
+            arrived = along(out, 1)
+            (here,) = call(
+                kernel(next_local_pivot_kernel),
+                [shape(rows, n, n)],
+                (me, mine),
+                (inverse, diag_block, tiles),
+                flops=product * rows,
+            )
         if sweep == FSWEEPS - 1:
             lower_locals = over_chips(lower_local)
             mate_lowers = [mate_lower] + [swap(x, 1) for x in lowers[1:]]
-            table = pl.pallas_call(
+            below, above = along(metas, 1), along(metas, -1)
+            (table,) = call(
                 kernel(table_kernel),
-                out_shape=shape(2 * lay.table, dtype=jnp.int32),
-                in_specs=[smem()] * 4,
-                out_specs=smem(),
-            )(me, metas, below, above)
-            early += [*lower_locals[1:], *mate_lowers[1:], table]
+                [shape(2 * lay.table, dtype=jnp.int32)],
+                (me, metas, below, above),
+                (),
+                scratch=(places,),
+                to_smem=True,
+            )
+            early += [*lower_locals[1:], *mate_lowers[1:], below, above]
+            later += [table]
         keep, give = call(
             kernel(incoming_kernel),
             [shape(half, n, n)] * 2,
@@ -344,7 +362,7 @@
             early=early,
         )
         sums = summed(keep + swap(give, 1))
-        (kept,) = call(newton_kernel, [shape(half, n, n)], (), (kept, sums))
+        (kept,) = call(newton_kernel, [shape(half, n, n)], (), (kept, sums), early=later)
         mated = swap(kept, 1)
     inverse = jnp.concatenate([kept, mated], 0)
 

time: 154 us -> 145 us (0.942)
  Pallas kernels: 32.2 us -> 25.6 us
  starting transfers between devices: 46.8 us -> 51.7 us
  waiting for transfers between devices: 63.8 us -> 59.6 us
  local copies, waits for them, and re-layouts: 7.7 us -> 4.21 us
    ppermute x26 -> x25, waiting for transfers between devices: 45 us -> 38.6 us  [swap(): return lax.ppermute(x, 'tile', [(i, i ^ bit) for i in range(n_tile)])]
    ppermute x26 -> x25, starting transfers between devices: 9.17 us -> 14.6 us  [swap(): return lax.ppermute(x, 'tile', [(i, i ^ bit) for i in range(n_tile)])]
    pallas_call x1 -> x0, Pallas kernels: 3.53 us -> none  [local(): pl.pallas_call(kernel(table_kernel), out_shape=shape(2 * lay.table, dtype...]
    unnamed x35 -> x13, local copies, waits for them, and re-layouts: 6.01 us -> 2.53 us
    pallas_call x24, Pallas kernels: 28.7 us -> 25.6 us  [call(): pl.pallas_call(body if not early else lambda *refs: body(*refs[len(early)...]
    ppermute x10, waiting for transfers between devices: 18.8 us -> 21 us  [along(): return lax.ppermute(x, ('dom', 'tile'), route)]
  transfers between devices with their start and end apart: 36 -> 35, of which waited for: 24 -> 26; matrix products, arithmetic and copies ran while one was open for 1% -> 3% of each run, Pallas kernels for 15% -> 13%
where the time goes in v4:
time: 145 us; the launch traced here: 144 us
  waiting for transfers between devices  59.6 us (41%)
  starting transfers between devices  51.7 us (36%)
  Pallas kernels  25.6 us (18%)
  local copies, waits for them, and re-layouts  4.21 us (3%)
    ppermute x25, waiting for transfers between devices, swap(): return lax.ppermute(x, 'tile', [(i, i ^ bit) for i in range(n_tile)])  38.6 us
    ppermute x10, starting transfers between devices, along(): return lax.ppermute(x, ('dom', 'tile'), route)  37 us
    pallas_call x24, Pallas kernels, call(): pl.pallas_call(body if not early else lambda *refs: body(*refs[len(early)...  25.6 us
    ppermute x10, waiting for transfers between devices, along(): return lax.ppermute(x, ('dom', 'tile'), route)  21 us
    ppermute x25, starting transfers between devices, swap(): return lax.ppermute(x, 'tile', [(i, i ^ bit) for i in range(n_tile)])  14.6 us
  transfers between devices with their start and end apart: 35, of which 26 were waited for; matrix products, arithmetic and copies ran while one was open for 3% of the time, Pallas kernels for 13%

profile of v4, /device:TPU:18, one launch (start us, length us, event | category | flops | bytes accessed | tf_op | source)
XLA Modules:
  0.0 143.6 jit_solution(10814230194727648086)
XLA Ops:
  0.7 1.6 %collective-permute-start = (f32[3,128,128]{2,1,0:T(8,128)}, f32[3,128,128]{2,1,0:T(8,128)S(1)}, u32[]{:S(2)}, u32[]{:S(2)}) collective-permute-start(f32[3,128,128]{2,1,0:T(8,128)} %param.9), channel_id=1, source_target_pairs={{0,2},{1,3},{2,0},{3,1},{4,6},{5,7},{6,4},{7,5},{8,10},{9,11},{10,... | collective-permute-start | bytes 589832 | tf_op jit(solution)/shard_map/ppermute | solution.py:269
  5.4 3.0 %collective-permute-done.1 = s32[64]{0:T(128)S(1)} collective-permute-done((s32[64]{0:T(128)S(1)}, s32[64]{0:T(128)S(1)}, u32[]{:S(2)}, u32[]{:S(2)}) %collective-permute-start.1) | collective-permute-done | bytes 288 | tf_op jit(solution)/shard_map/ppermute | solution.py:269
  8.4 1.1 collective-permute-done.3
  12.2 3.5 %collective-permute-start.10 = (f32[8,128,128]{2,1,0:T(8,128)S(1)}, f32[8,128,128]{2,1,0:T(8,128)S(1)}, u32[]{:S(2)}, u32[]{:S(2)}) collective-permute-start(f32[8,128,128]{2,1,0:T(8,128)S(1)} %get-tuple-element.32), channel_id=1, source_target_pairs={{0,4},{1,9},{2,6},{3,11},{4,8},{5,13},{6,10},{7,15},{8,12},{9,17},... | collective-permute-start | bytes 1572872 | tf_op jit(solution)/shard_map/ppermute | solution.py:278
  15.7 1.5 %collective-permute-start.9 = (f32[8,128,128]{2,1,0:T(8,128)S(1)}, f32[8,128,128]{2,1,0:T(8,128)S(1)}, u32[]{:S(2)}, u32[]{:S(2)}) collective-permute-start(f32[8,128,128]{2,1,0:T(8,128)S(1)} %get-tuple-element.29.refs_5_.refs_8_.refs_0_), channel_id=1, source_target_pairs={{0,2},{1,3},{2,0},{3,1},{4,6},{5,7},{6,4},{7,5},{8,10},{9,11},{10,... | collective-permute-start | bytes 1572872 | tf_op jit(solution)/shard_map/ppermute | solution.py:269
  17.2 2.8 %shard_map.88 = (f32[12,128,128]{2,1,0:T(8,128)S(1)}, f32[8,128,128]{2,1,0:T(8,128)S(1)}, f32[4,128,128]{2,1,0:T(8,128)S(1)}, f32[12,128,128]{2,1,0:T(8,128)S(1)}, f32[8,128,128]{2,1,0:T(8,128)S(1)}) custom-call(s32[1]{0:T(128)} %bitcast.me.refs_1_.refs_4_, s32[64]{0:T(128)S(1)} %pad_add_fusion.1.mine.refs_2_.refs_5_, ...), custom_call_target="tpu_custom_call" | custom-call | flops 201326592 | bytes 7012352 | tf_op jit(solution)/shard_map/pallas_call | solution.py:96
  20.0 7.3 %collective-permute-done.10.refs_7_ = f32[8,128,128]{2,1,0:T(8,128)S(1)} collective-permute-done((f32[8,128,128]{2,1,0:T(8,128)S(1)}, f32[8,128,128]{2,1,0:T(8,128)S(1)}, u32[]{:S(2)}, u32[]{:S(2)}) %collective-permute-start.10) | collective-permute-done | bytes 524320 | tf_op jit(solution)/shard_map/ppermute | solution.py:278
  27.3 2.3 %collective-permute-done.9.refs_0_.refs_3_ = f32[8,128,128]{2,1,0:T(8,128)S(1)} collective-permute-done((f32[8,128,128]{2,1,0:T(8,128)S(1)}, f32[8,128,128]{2,1,0:T(8,128)S(1)}, u32[]{:S(2)}, u32[]{:S(2)}) %collective-permute-start.9) | collective-permute-done | bytes 524320 | tf_op jit(solution)/shard_map/ppermute | solution.py:269
  29.6 1.0 shard_map.89
  30.7 1.7 %collective-permute-done.11 = f32[6,128,128]{2,1,0:T(8,128)S(1)} collective-permute-done((f32[6,128,128]{2,1,0:T(8,128)S(1)}, f32[6,128,128]{2,1,0:T(8,128)S(1)}, u32[]{:S(2)}, u32[]{:S(2)}) %collective-permute-start.11) | collective-permute-done | bytes 393248 | tf_op jit(solution)/shard_map/ppermute | solution.py:269
  32.5 1.5 %collective-permute-start.12 = (f32[6,128,128]{2,1,0:T(8,128)S(1)}, f32[6,128,128]{2,1,0:T(8,128)S(1)}, u32[]{:S(2)}, u32[]{:S(2)}) collective-permute-start(f32[6,128,128]{2,1,0:T(8,128)S(1)} %add.30), channel_id=1, source_target_pairs={{0,2},{1,3},{2,0},{3,1},{4,6},{5,7},{6,4},{7,5},{8,10},{9,11},{10,... | collective-permute-start | bytes 1179656 | tf_op jit(solution)/shard_map/ppermute | solution.py:269
  34.0 9.7 %collective-permute-done.12 = f32[6,128,128]{2,1,0:T(8,128)S(1)} collective-permute-done((f32[6,128,128]{2,1,0:T(8,128)S(1)}, f32[6,128,128]{2,1,0:T(8,128)S(1)}, u32[]{:S(2)}, u32[]{:S(2)}) %collective-permute-start.12) | collective-permute-done | bytes 393248 | tf_op jit(solution)/shard_map/ppermute | solution.py:269
  44.9 1.2 collective-permute-done.15
  47.0 3.0 %collective-permute-start.16 = (f32[8,128,128]{2,1,0:T(8,128)S(1)}, f32[8,128,128]{2,1,0:T(8,128)S(1)}, u32[]{:S(2)}, u32[]{:S(2)}) collective-permute-start(f32[8,128,128]{2,1,0:T(8,128)S(1)} %shard_map.92), channel_id=1, source_target_pairs={{0,4},{1,9},{2,6},{3,11},{4,8},{5,13},{6,10},{7,15},{8,12},{9,17},... | collective-permute-start | bytes 1572872 | tf_op jit(solution)/shard_map/ppermute | solution.py:278
  50.0 1.5 %collective-permute-start.13 = (f32[4,128,128]{2,1,0:T(8,128)S(1)}, f32[4,128,128]{2,1,0:T(8,128)S(1)}, u32[]{:S(2)}, u32[]{:S(2)}) collective-permute-start(f32[4,128,128]{2,1,0:T(8,128)S(1)} %get-tuple-element.35.refs_1_), channel_id=1, source_target_pairs={{0,2},{1,3},{2,0},{3,1},{4,6},{5,7},{6,4},{7,5},{8,10},{9,11},{10,... | collective-permute-start | bytes 786440 | tf_op jit(solution)/shard_map/ppermute | solution.py:269
  51.5 2.8 %collective-permute-start.5 = (s32[4,64]{1,0:T(4,128)S(1)}, s32[4,64]{1,0:T(4,128)S(1)}, u32[]{:S(2)}, u32[]{:S(2)}) collective-permute-start(s32[4,64]{1,0:T(4,128)S(1)} %pad_add_fusion.metas), channel_id=1, source_target_pairs={{4,0},{6,2},{8,4},{9,1},{10,6},{11,3},{12,8},{13,5},{14,10},{15,7}... | collective-permute-start | bytes 3080 | tf_op jit(solution)/shard_map/ppermute | solution.py:278
  54.4 3.9 %collective-permute-start.4 = (s32[4,64]{1,0:T(4,128)S(1)}, s32[4,64]{1,0:T(4,128)S(1)}, u32[]{:S(2)}, u32[]{:S(2)}) collective-permute-start(s32[4,64]{1,0:T(4,128)S(1)} %pad_add_fusion.metas), channel_id=1, source_target_pairs={{0,4},{1,9},{2,6},{3,11},{4,8},{5,13},{6,10},{7,15},{8,12},{9,17},... | collective-permute-start | bytes 3080 | tf_op jit(solution)/shard_map/ppermute | solution.py:278
  58.3 2.3 %shard_map.91.refs_7_ = f32[12,128,128]{2,1,0:T(8,128)S(1)} custom-call(s32[1]{0:T(128)} %bitcast.me.refs_1_.refs_4_, s32[64]{0:T(128)S(1)} %pad_add_fusion.1.mine.refs_2_.refs_5_, f32[12,128,128]{2,1,0:T(8,128)S(1)} %pad_maximum_fusion.inverse, f32[3,128,128]{2,1,0:T(8,128)S(1)} %copy-done.1, f32[24,128,128]{2,1,0:T(8,128)S(1)} %bitcast.15), custom_call_target="tpu_custom_call" | custom-call | flops 201326592 | bytes 3342336 | tf_op jit(solution)/shard_map/pallas_call | solution.py:96
  60.7 1.1 shard_map.93
  61.8 1.3 collective-permute-start.17
  63.1 1.3 collective-permute-done.17
  64.5 1.5 %collective-permute-start.18 = (f32[6,128,128]{2,1,0:T(8,128)S(1)}, f32[6,128,128]{2,1,0:T(8,128)S(1)}, u32[]{:S(2)}, u32[]{:S(2)}) collective-permute-start(f32[6,128,128]{2,1,0:T(8,128)S(1)} %add.32), channel_id=1, source_target_pairs={{0,2},{1,3},{2,0},{3,1},{4,6},{5,7},{6,4},{7,5},{8,10},{9,11},{10,... | collective-permute-start | bytes 1179656 | tf_op jit(solution)/shard_map/ppermute | solution.py:269
  66.0 2.1 %shard_map.86.refs_0_.table.refs_1_ = s32[96]{0:T(128)S(1)} custom-call(s32[1]{0:T(128)} %bitcast.me.refs_1_.refs_4_, s32[4,64]{1,0:T(4,128)S(1)} %pad_add_fusion.metas, s32[4,64]{1,0:T(4,128)S(1)} %collective-permute-done.4.peers_below.refs_2_, s32[4,64]{1,0:T(4,128)S(1)} %collective-permute-done.5.peers_above.refs_3_), custom_call_target="tpu_custom_call" | custom-call | bytes 384 | tf_op jit(solution)/shard_map/pallas_call | solution.py:96
  68.1 7.8 %collective-permute-done.18 = f32[6,128,128]{2,1,0:T(8,128)S(1)} collective-permute-done((f32[6,128,128]{2,1,0:T(8,128)S(1)}, f32[6,128,128]{2,1,0:T(8,128)S(1)}, u32[]{:S(2)}, u32[]{:S(2)}) %collective-permute-start.18) | collective-permute-done | bytes 393248 | tf_op jit(solution)/shard_map/ppermute | solution.py:269
  76.6 1.5 %collective-permute-start.20 = (f32[12,128,128]{2,1,0:T(8,128)S(1)}, f32[12,128,128]{2,1,0:T(8,128)S(1)}, u32[]{:S(2)}, u32[]{:S(2)}) collective-permute-start(f32[12,128,128]{2,1,0:T(8,128)S(1)} %get-tuple-element.36.upper.refs_0_), channel_id=1, source_target_pairs={{0,2},{1,3},{2,0},{3,1},{4,6},{5,7},{6,4},{7,5},{8,10},{9,11},{10,... | collective-permute-start | bytes 2359304 | tf_op jit(solution)/shard_map/ppermute | solution.py:269
  78.8 4.2 %collective-permute-start.21 = (f32[12,16,128]{2,1,0:T(8,128)S(1)}, f32[12,16,128]{2,1,0:T(8,128)S(1)}, u32[]{:S(2)}, u32[]{:S(2)}) collective-permute-start(f32[12,16,128]{2,1,0:T(8,128)S(1)} %shard_map.95.x), channel_id=1, source_target_pairs={{0,4},{1,9},{2,6},{3,11},{4,8},{5,13},{6,10},{7,15},{8,12},{9,17},... | collective-permute-start | bytes 294920 | tf_op jit(solution)/shard_map/ppermute | solution.py:278
  83.0 1.3 shard_map.96
  86.9 1.3 collective-permute-done.22
  88.2 4.6 %collective-permute-start.23 = (f32[12,16,128]{2,1,0:T(8,128)S(1)}, f32[12,16,128]{2,1,0:T(8,128)S(1)}, u32[]{:S(2)}, u32[]{:S(2)}) collective-permute-start(f32[12,16,128]{2,1,0:T(8,128)S(1)} %add_subtract_fusion.5.x), channel_id=1, source_target_pairs={{0,4},{1,9},{2,6},{3,11},{4,8},{5,13},{6,10},{7,15},{8,12},{9,17},... | collective-permute-start | bytes 294920 | tf_op jit(solution)/shard_map/ppermute | solution.py:278
  93.6 2.0 %collective-permute-done.23.arrived = f32[12,16,128]{2,1,0:T(8,128)S(1)} collective-permute-done((f32[12,16,128]{2,1,0:T(8,128)S(1)}, f32[12,16,128]{2,1,0:T(8,128)S(1)}, u32[]{:S(2)}, u32[]{:S(2)}) %collective-permute-start.23) | collective-permute-done | bytes 98336 | tf_op jit(solution)/shard_map/ppermute | solution.py:278
  95.7 1.0 shard_map.100
  98.0 4.6 %collective-permute-start.25 = (f32[12,16,128]{2,1,0:T(8,128)S(1)}, f32[12,16,128]{2,1,0:T(8,128)S(1)}, u32[]{:S(2)}, u32[]{:S(2)}) collective-permute-start(f32[12,16,128]{2,1,0:T(8,128)S(1)} %add_subtract_fusion.4.x), channel_id=1, source_target_pairs={{0,4},{1,9},{2,6},{3,11},{4,8},{5,13},{6,10},{7,15},{8,12},{9,17},... | collective-permute-start | bytes 294920 | tf_op jit(solution)/shard_map/ppermute | solution.py:278
  103.4 2.0 %collective-permute-done.25.refs_4_ = f32[12,16,128]{2,1,0:T(8,128)S(1)} collective-permute-done((f32[12,16,128]{2,1,0:T(8,128)S(1)}, f32[12,16,128]{2,1,0:T(8,128)S(1)}, u32[]{:S(2)}, u32[]{:S(2)}) %collective-permute-start.25) | collective-permute-done | bytes 98336 | tf_op jit(solution)/shard_map/ppermute | solution.py:278
  106.5 1.3 collective-permute-done.26
  107.8 4.8 %collective-permute-start.28 = (f32[12,16,128]{2,1,0:T(8,128)S(1)}, f32[12,16,128]{2,1,0:T(8,128)S(1)}, u32[]{:S(2)}, u32[]{:S(2)}) collective-permute-start(f32[12,16,128]{2,1,0:T(8,128)S(1)} %add_subtract_fusion.3.x), channel_id=1, source_target_pairs={{4,0},{6,2},{8,4},{9,1},{10,6},{11,3},{12,8},{13,5},{14,10},{15,7}... | collective-permute-start | bytes 294920 | tf_op jit(solution)/shard_map/ppermute | solution.py:278
  112.7 1.2 shard_map.103
  115.7 1.0 shard_map.105
  116.8 1.3 collective-permute-done.29
  118.1 3.5 %collective-permute-start.30 = (f32[12,16,128]{2,1,0:T(8,128)S(1)}, f32[12,16,128]{2,1,0:T(8,128)S(1)}, u32[]{:S(2)}, u32[]{:S(2)}) collective-permute-start(f32[12,16,128]{2,1,0:T(8,128)S(1)} %add_subtract_fusion.2.x), channel_id=1, source_target_pairs={{4,0},{6,2},{8,4},{9,1},{10,6},{11,3},{12,8},{13,5},{14,10},{15,7}... | collective-permute-start | bytes 294920 | tf_op jit(solution)/shard_map/ppermute | solution.py:278
  122.4 3.4 %collective-permute-done.30.arrived = f32[12,16,128]{2,1,0:T(8,128)S(1)} collective-permute-done((f32[12,16,128]{2,1,0:T(8,128)S(1)}, f32[12,16,128]{2,1,0:T(8,128)S(1)}, u32[]{:S(2)}, u32[]{:S(2)}) %collective-permute-start.30) | collective-permute-done | bytes 98336 | tf_op jit(solution)/shard_map/ppermute | solution.py:278
  125.8 1.0 shard_map.107
  126.9 1.3 collective-permute-done.31
  128.2 2.2 %collective-permute-start.32 = (f32[12,16,128]{2,1,0:T(8,128)S(1)}, f32[12,16,128]{2,1,0:T(8,128)S(1)}, u32[]{:S(2)}, u32[]{:S(2)}) collective-permute-start(f32[12,16,128]{2,1,0:T(8,128)S(1)} %add_subtract_fusion.1.x), channel_id=1, source_target_pairs={{4,0},{6,2},{8,4},{9,1},{10,6},{11,3},{12,8},{13,5},{14,10},{15,7}... | collective-permute-start | bytes 294920 | tf_op jit(solution)/shard_map/ppermute | solution.py:278
  131.3 4.3 %collective-permute-done.32.arrived = f32[12,16,128]{2,1,0:T(8,128)S(1)} collective-permute-done((f32[12,16,128]{2,1,0:T(8,128)S(1)}, f32[12,16,128]{2,1,0:T(8,128)S(1)}, u32[]{:S(2)}, u32[]{:S(2)}) %collective-permute-start.32) | collective-permute-done | bytes 98336 | tf_op jit(solution)/shard_map/ppermute | solution.py:278
  135.6 1.0 shard_map.109
  136.7 1.3 collective-permute-done.33
  138.0 1.5 %collective-permute-start.34 = (f32[12,16,128]{2,1,0:T(8,128)S(1)}, f32[12,16,128]{2,1,0:T(8,128)S(1)}, u32[]{:S(2)}, u32[]{:S(2)}) collective-permute-start(f32[12,16,128]{2,1,0:T(8,128)S(1)} %add_subtract_fusion), channel_id=1, source_target_pairs={{0,2},{1,3},{2,0},{3,1},{4,6},{5,7},{6,4},{7,5},{8,10},{9,11},{10,... | collective-permute-start | bytes 294920 | tf_op jit(solution)/shard_map/ppermute | solution.py:269
  140.2 2.7 %collective-permute-done.34 = f32[12,16,128]{2,1,0:T(8,128)S(1)} collective-permute-done((f32[12,16,128]{2,1,0:T(8,128)S(1)}, f32[12,16,128]{2,1,0:T(8,128)S(1)}, u32[]{:S(2)}, u32[]{:S(2)}) %collective-permute-start.34) | collective-permute-done | bytes 98336 | tf_op jit(solution)/shard_map/ppermute | solution.py:269
  (84 shorter events, 21.2 us)
Async XLA Ops:
  0.6 10.7 %copy-start = (f32[12,2,128,128]{3,2,1,0:T(8,128)S(1)}, f32[12,2,128,128]{3,2,1,0:T(8,128)}, u32[]{:S(2)}) copy-start(f32[12,2,128,128]{3,2,1,0:T(8,128)} %param.10) | copy-start | bytes 4718596
  0.6 10.6 %collective-permute-start.8 = (f32[24,128,128]{2,1,0:T(8,128)}, f32[24,128,128]{2,1,0:T(8,128)S(1)}, u32[]{:S(2)}, u32[]{:S(2)}) collective-permute-start(f32[24,128,128]{2,1,0:T(8,128)} %bitcast.12), channel_id=1, source_target_pairs={{0,1},{1,0},{2,3},{3,2},{4,5},{5,4},{6,7},{7,6},{8,9},{9,8},{10,11... | collective-permute-start | bytes 4718600 | tf_op jit(solution)/shard_map/ppermute | solution.py:269
  0.7 8.8 %collective-permute-start = (f32[3,128,128]{2,1,0:T(8,128)}, f32[3,128,128]{2,1,0:T(8,128)S(1)}, u32[]{:S(2)}, u32[]{:S(2)}) collective-permute-start(f32[3,128,128]{2,1,0:T(8,128)} %param.9), channel_id=1, source_target_pairs={{0,2},{1,3},{2,0},{3,1},{4,6},{5,7},{6,4},{7,5},{8,10},{9,11},{10,... | collective-permute-start | bytes 589832 | tf_op jit(solution)/shard_map/ppermute | solution.py:269
  4.9 3.5 %collective-permute-start.1 = (s32[64]{0:T(128)S(1)}, s32[64]{0:T(128)S(1)}, u32[]{:S(2)}, u32[]{:S(2)}) collective-permute-start(s32[64]{0:T(128)S(1)} %pad_add_fusion.1.mine.refs_2_.refs_5_), channel_id=1, source_target_pairs={{0,2},{1,3},{2,0},{3,1},{4,6},{5,7},{6,4},{7,5},{8,10},{9,11},{10,... | collective-permute-start | bytes 776 | tf_op jit(solution)/shard_map/ppermute | solution.py:269
  5.4 3.0 %collective-permute-start.2 = (s32[64]{0:T(128)S(1)}, s32[64]{0:T(128)S(1)}, u32[]{:S(2)}, u32[]{:S(2)}) collective-permute-start(s32[64]{0:T(128)S(1)} %pad_add_fusion.1.mine.refs_2_.refs_5_), channel_id=1, source_target_pairs={{0,1},{1,0},{2,3},{3,2},{4,5},{5,4},{6,7},{7,6},{8,9},{9,8},{10,11... | collective-permute-start | bytes 776 | tf_op jit(solution)/shard_map/ppermute | solution.py:269
  8.4 1.1 collective-permute-start.3
  9.5 1.7 %collective-permute-start.6 = (f32[3,128,128]{2,1,0:T(8,128)}, f32[3,128,128]{2,1,0:T(8,128)S(1)}, u32[]{:S(2)}, u32[]{:S(2)}) collective-permute-start(f32[3,128,128]{2,1,0:T(8,128)} %param.9), channel_id=1, source_target_pairs={{0,1},{1,0},{2,3},{3,2},{4,5},{5,4},{6,7},{7,6},{8,9},{9,8},{10,11... | collective-permute-start | bytes 589832 | tf_op jit(solution)/shard_map/ppermute | solution.py:269
  9.7 1.5 %collective-permute-start.7 = (f32[3,128,128]{2,1,0:T(8,128)S(1)}, f32[3,128,128]{2,1,0:T(8,128)S(1)}, u32[]{:S(2)}, u32[]{:S(2)}) collective-permute-start(f32[3,128,128]{2,1,0:T(8,128)S(1)} %collective-permute-done), channel_id=1, source_target_pairs={{0,1},{1,0},{2,3},{3,2},{4,5},{5,4},{6,7},{7,6},{8,9},{9,8},{10,11... | collective-permute-start | bytes 589832 | tf_op jit(solution)/shard_map/ppermute | solution.py:269
  11.3 5.9 %copy-start.1 = (f32[3,128,128]{2,1,0:T(8,128)S(1)}, f32[3,128,128]{2,1,0:T(8,128)}, u32[]{:S(2)}) copy-start(f32[3,128,128]{2,1,0:T(8,128)} %diag.3) | copy-start | bytes 589828
  12.2 15.0 %collective-permute-start.10 = (f32[8,128,128]{2,1,0:T(8,128)S(1)}, f32[8,128,128]{2,1,0:T(8,128)S(1)}, u32[]{:S(2)}, u32[]{:S(2)}) collective-permute-start(f32[8,128,128]{2,1,0:T(8,128)S(1)} %get-tuple-element.32), channel_id=1, source_target_pairs={{0,4},{1,9},{2,6},{3,11},{4,8},{5,13},{6,10},{7,15},{8,12},{9,17},... | collective-permute-start | bytes 1572872 | tf_op jit(solution)/shard_map/ppermute | solution.py:278
  15.7 13.9 %collective-permute-start.9 = (f32[8,128,128]{2,1,0:T(8,128)S(1)}, f32[8,128,128]{2,1,0:T(8,128)S(1)}, u32[]{:S(2)}, u32[]{:S(2)}) collective-permute-start(f32[8,128,128]{2,1,0:T(8,128)S(1)} %get-tuple-element.29.refs_5_.refs_8_.refs_0_), channel_id=1, source_target_pairs={{0,2},{1,3},{2,0},{3,1},{4,6},{5,7},{6,4},{7,5},{8,10},{9,11},{10,... | collective-permute-start | bytes 1572872 | tf_op jit(solution)/shard_map/ppermute | solution.py:269
  29.6 4.4 %copy-start.3 = (f32[3,128,128]{2,1,0:T(8,128)S(1)}, f32[3,128,128]{2,1,0:T(8,128)}, u32[]{:S(2)}) copy-start(f32[3,128,128]{2,1,0:T(8,128)} %param.9) | copy-start | bytes 589828
  30.6 1.8 %collective-permute-start.11 = (f32[6,128,128]{2,1,0:T(8,128)S(1)}, f32[6,128,128]{2,1,0:T(8,128)S(1)}, u32[]{:S(2)}, u32[]{:S(2)}) collective-permute-start(f32[6,128,128]{2,1,0:T(8,128)S(1)} %get-tuple-element.34), channel_id=1, source_target_pairs={{0,1},{1,0},{2,3},{3,2},{4,5},{5,4},{6,7},{7,6},{8,9},{9,8},{10,11... | collective-permute-start | bytes 1179656 | tf_op jit(solution)/shard_map/ppermute | solution.py:269
  32.5 11.2 %collective-permute-start.12 = (f32[6,128,128]{2,1,0:T(8,128)S(1)}, f32[6,128,128]{2,1,0:T(8,128)S(1)}, u32[]{:S(2)}, u32[]{:S(2)}) collective-permute-start(f32[6,128,128]{2,1,0:T(8,128)S(1)} %add.30), channel_id=1, source_target_pairs={{0,2},{1,3},{2,0},{3,1},{4,6},{5,7},{6,4},{7,5},{8,10},{9,11},{10,... | collective-permute-start | bytes 1179656 | tf_op jit(solution)/shard_map/ppermute | solution.py:269
  44.3 1.8 %collective-permute-start.15 = (f32[6,128,128]{2,1,0:T(8,128)S(1)}, f32[6,128,128]{2,1,0:T(8,128)S(1)}, u32[]{:S(2)}, u32[]{:S(2)}) collective-permute-start(f32[6,128,128]{2,1,0:T(8,128)S(1)} %shard_map.90.refs_1_), channel_id=1, source_target_pairs={{0,1},{1,0},{2,3},{3,2},{4,5},{5,4},{6,7},{7,6},{8,9},{9,8},{10,11... | collective-permute-start | bytes 1179656 | tf_op jit(solution)/shard_map/ppermute | solution.py:269
  44.4 16.4 %collective-permute-start.14 = (f32[8,128,128]{2,1,0:T(8,128)S(1)}, f32[8,128,128]{2,1,0:T(8,128)S(1)}, u32[]{:S(2)}, u32[]{:S(2)}) collective-permute-start(f32[8,128,128]{2,1,0:T(8,128)S(1)} %collective-permute-done.9.refs_0_.refs_3_), channel_id=1, source_target_pairs={{0,1},{1,0},{2,3},{3,2},{4,5},{5,4},{6,7},{7,6},{8,9},{9,8},{10,11... | collective-permute-start | bytes 1572872 | tf_op jit(solution)/shard_map/ppermute | solution.py:269
  47.0 13.7 %collective-permute-start.16 = (f32[8,128,128]{2,1,0:T(8,128)S(1)}, f32[8,128,128]{2,1,0:T(8,128)S(1)}, u32[]{:S(2)}, u32[]{:S(2)}) collective-permute-start(f32[8,128,128]{2,1,0:T(8,128)S(1)} %shard_map.92), channel_id=1, source_target_pairs={{0,4},{1,9},{2,6},{3,11},{4,8},{5,13},{6,10},{7,15},{8,12},{9,17},... | collective-permute-start | bytes 1572872 | tf_op jit(solution)/shard_map/ppermute | solution.py:278
  50.0 10.7 %collective-permute-start.13 = (f32[4,128,128]{2,1,0:T(8,128)S(1)}, f32[4,128,128]{2,1,0:T(8,128)S(1)}, u32[]{:S(2)}, u32[]{:S(2)}) collective-permute-start(f32[4,128,128]{2,1,0:T(8,128)S(1)} %get-tuple-element.35.refs_1_), channel_id=1, source_target_pairs={{0,2},{1,3},{2,0},{3,1},{4,6},{5,7},{6,4},{7,5},{8,10},{9,11},{10,... | collective-permute-start | bytes 786440 | tf_op jit(solution)/shard_map/ppermute | solution.py:269
  51.5 9.1 %collective-permute-start.5 = (s32[4,64]{1,0:T(4,128)S(1)}, s32[4,64]{1,0:T(4,128)S(1)}, u32[]{:S(2)}, u32[]{:S(2)}) collective-permute-start(s32[4,64]{1,0:T(4,128)S(1)} %pad_add_fusion.metas), channel_id=1, source_target_pairs={{4,0},{6,2},{8,4},{9,1},{10,6},{11,3},{12,8},{13,5},{14,10},{15,7}... | collective-permute-start | bytes 3080 | tf_op jit(solution)/shard_map/ppermute | solution.py:278
  54.4 6.3 %collective-permute-start.4 = (s32[4,64]{1,0:T(4,128)S(1)}, s32[4,64]{1,0:T(4,128)S(1)}, u32[]{:S(2)}, u32[]{:S(2)}) collective-permute-start(s32[4,64]{1,0:T(4,128)S(1)} %pad_add_fusion.metas), channel_id=1, source_target_pairs={{0,4},{1,9},{2,6},{3,11},{4,8},{5,13},{6,10},{7,15},{8,12},{9,17},... | collective-permute-start | bytes 3080 | tf_op jit(solution)/shard_map/ppermute | solution.py:278
  61.8 2.6 %collective-permute-start.17 = (f32[6,128,128]{2,1,0:T(8,128)S(1)}, f32[6,128,128]{2,1,0:T(8,128)S(1)}, u32[]{:S(2)}, u32[]{:S(2)}) collective-permute-start(f32[6,128,128]{2,1,0:T(8,128)S(1)} %get-tuple-element.39), channel_id=1, source_target_pairs={{0,1},{1,0},{2,3},{3,2},{4,5},{5,4},{6,7},{7,6},{8,9},{9,8},{10,11... | collective-permute-start | bytes 1179656 | tf_op jit(solution)/shard_map/ppermute | solution.py:269
  64.5 11.5 %collective-permute-start.18 = (f32[6,128,128]{2,1,0:T(8,128)S(1)}, f32[6,128,128]{2,1,0:T(8,128)S(1)}, u32[]{:S(2)}, u32[]{:S(2)}) collective-permute-start(f32[6,128,128]{2,1,0:T(8,128)S(1)} %add.32), channel_id=1, source_target_pairs={{0,2},{1,3},{2,0},{3,1},{4,6},{5,7},{6,4},{7,5},{8,10},{9,11},{10,... | collective-permute-start | bytes 1179656 | tf_op jit(solution)/shard_map/ppermute | solution.py:269
  76.1 2.3 %copy-start.2 = (f32[12,32,128]{2,1,0:T(8,128)S(1)}, f32[12,32,128]{2,1,0:T(8,128)}, u32[]{:S(2)}) copy-start(f32[12,32,128]{2,1,0:T(8,128)} %base.1) | copy-start | bytes 589828
  76.6 1.8 %collective-permute-start.19 = (f32[6,128,128]{2,1,0:T(8,128)S(1)}, f32[6,128,128]{2,1,0:T(8,128)S(1)}, u32[]{:S(2)}, u32[]{:S(2)}) collective-permute-start(f32[6,128,128]{2,1,0:T(8,128)S(1)} %shard_map.94), channel_id=1, source_target_pairs={{0,1},{1,0},{2,3},{3,2},{4,5},{5,4},{6,7},{7,6},{8,9},{9,8},{10,11... | collective-permute-start | bytes 1179656 | tf_op jit(solution)/shard_map/ppermute | solution.py:269
  76.6 20.1 %collective-permute-start.20 = (f32[12,128,128]{2,1,0:T(8,128)S(1)}, f32[12,128,128]{2,1,0:T(8,128)S(1)}, u32[]{:S(2)}, u32[]{:S(2)}) collective-permute-start(f32[12,128,128]{2,1,0:T(8,128)S(1)} %get-tuple-element.36.upper.refs_0_), channel_id=1, source_target_pairs={{0,2},{1,3},{2,0},{3,1},{4,6},{5,7},{6,4},{7,5},{8,10},{9,11},{10,... | collective-permute-start | bytes 2359304 | tf_op jit(solution)/shard_map/ppermute | solution.py:269
  78.8 7.1 %collective-permute-start.21 = (f32[12,16,128]{2,1,0:T(8,128)S(1)}, f32[12,16,128]{2,1,0:T(8,128)S(1)}, u32[]{:S(2)}, u32[]{:S(2)}) collective-permute-start(f32[12,16,128]{2,1,0:T(8,128)S(1)} %shard_map.95.x), channel_id=1, source_target_pairs={{0,4},{1,9},{2,6},{3,11},{4,8},{5,13},{6,10},{7,15},{8,12},{9,17},... | collective-permute-start | bytes 294920 | tf_op jit(solution)/shard_map/ppermute | solution.py:278
  86.9 1.4 collective-permute-start.22
  88.2 7.4 %collective-permute-start.23 = (f32[12,16,128]{2,1,0:T(8,128)S(1)}, f32[12,16,128]{2,1,0:T(8,128)S(1)}, u32[]{:S(2)}, u32[]{:S(2)}) collective-permute-start(f32[12,16,128]{2,1,0:T(8,128)S(1)} %add_subtract_fusion.5.x), channel_id=1, source_target_pairs={{0,4},{1,9},{2,6},{3,11},{4,8},{5,13},{6,10},{7,15},{8,12},{9,17},... | collective-permute-start | bytes 294920 | tf_op jit(solution)/shard_map/ppermute | solution.py:278
  96.7 1.4 collective-permute-start.24
  96.7 15.9 %collective-permute-start.27 = (f32[12,128,128]{2,1,0:T(8,128)S(1)}, f32[12,128,128]{2,1,0:T(8,128)S(1)}, u32[]{:S(2)}, u32[]{:S(2)}) collective-permute-start(f32[12,128,128]{2,1,0:T(8,128)S(1)} %collective-permute-done.20.refs_0_.refs_2_), channel_id=1, source_target_pairs={{0,1},{1,0},{2,3},{3,2},{4,5},{5,4},{6,7},{7,6},{8,9},{9,8},{10,11... | collective-permute-start | bytes 2359304 | tf_op jit(solution)/shard_map/ppermute | solution.py:269
  98.0 7.4 %collective-permute-start.25 = (f32[12,16,128]{2,1,0:T(8,128)S(1)}, f32[12,16,128]{2,1,0:T(8,128)S(1)}, u32[]{:S(2)}, u32[]{:S(2)}) collective-permute-start(f32[12,16,128]{2,1,0:T(8,128)S(1)} %add_subtract_fusion.4.x), channel_id=1, source_target_pairs={{0,4},{1,9},{2,6},{3,11},{4,8},{5,13},{6,10},{7,15},{8,12},{9,17},... | collective-permute-start | bytes 294920 | tf_op jit(solution)/shard_map/ppermute | solution.py:278
  106.5 1.4 collective-permute-start.26
  107.8 7.9 %collective-permute-start.28 = (f32[12,16,128]{2,1,0:T(8,128)S(1)}, f32[12,16,128]{2,1,0:T(8,128)S(1)}, u32[]{:S(2)}, u32[]{:S(2)}) collective-permute-start(f32[12,16,128]{2,1,0:T(8,128)S(1)} %add_subtract_fusion.3.x), channel_id=1, source_target_pairs={{4,0},{6,2},{8,4},{9,1},{10,6},{11,3},{12,8},{13,5},{14,10},{15,7}... | collective-permute-start | bytes 294920 | tf_op jit(solution)/shard_map/ppermute | solution.py:278
  116.7 1.4 collective-permute-start.29
  118.1 7.7 %collective-permute-start.30 = (f32[12,16,128]{2,1,0:T(8,128)S(1)}, f32[12,16,128]{2,1,0:T(8,128)S(1)}, u32[]{:S(2)}, u32[]{:S(2)}) collective-permute-start(f32[12,16,128]{2,1,0:T(8,128)S(1)} %add_subtract_fusion.2.x), channel_id=1, source_target_pairs={{4,0},{6,2},{8,4},{9,1},{10,6},{11,3},{12,8},{13,5},{14,10},{15,7}... | collective-permute-start | bytes 294920 | tf_op jit(solution)/shard_map/ppermute | solution.py:278
  126.8 1.4 collective-permute-start.31
  128.2 7.4 %collective-permute-start.32 = (f32[12,16,128]{2,1,0:T(8,128)S(1)}, f32[12,16,128]{2,1,0:T(8,128)S(1)}, u32[]{:S(2)}, u32[]{:S(2)}) collective-permute-start(f32[12,16,128]{2,1,0:T(8,128)S(1)} %add_subtract_fusion.1.x), channel_id=1, source_target_pairs={{4,0},{6,2},{8,4},{9,1},{10,6},{11,3},{12,8},{13,5},{14,10},{15,7}... | collective-permute-start | bytes 294920 | tf_op jit(solution)/shard_map/ppermute | solution.py:278
  136.6 1.4 collective-permute-start.33
  138.0 4.9 %collective-permute-start.34 = (f32[12,16,128]{2,1,0:T(8,128)S(1)}, f32[12,16,128]{2,1,0:T(8,128)S(1)}, u32[]{:S(2)}, u32[]{:S(2)}) collective-permute-start(f32[12,16,128]{2,1,0:T(8,128)S(1)} %add_subtract_fusion), channel_id=1, source_target_pairs={{0,2},{1,3},{2,0},{3,1},{4,6},{5,7},{6,4},{7,5},{8,10},{9,11},{10,... | collective-permute-start | bytes 294920 | tf_op jit(solution)/shard_map/ppermute | solution.py:269

commit v5 on v4

--- a/solution.py
+++ b/solution.py
@@ -10,6 +10,7 @@
 FSWEEPS = 2
 LSWEEPS = 3
 USWEEPS = 3
+PARTS = 2
 F32 = jnp.float32
 BF16 = jnp.bfloat16
 
@@ -30,6 +31,18 @@
 
 def matmul(a, b):
     return matmul_parts(*split(a), *split(b))
+
+
+def matmul_nt_parts(ah, al, bh, bl):
+    lhs = jnp.concatenate([ah, al], 1)
+    rhs = jnp.concatenate([jnp.concatenate([bh, bh], 1), jnp.concatenate([bl, bl], 1)], 0)
+    out = lax.dot_general(lhs, rhs, (((1,), (1,)), ((), ())), preferred_element_type=F32)
+    n = bh.shape[0]
+    return out[:, :n] + out[:, n:]
+
+
+def matmul_nt(a, b):
+    return matmul_nt_parts(*split(a), *split(b))
 
 
 def times_tile(x, wide):
@@ -51,7 +64,7 @@
         self.pairs = max(1, (self.slots - 4 * cap) // 2)
         self.listed_slots = n_tile * cap
         self.local_slots = n_tile // 2 * self.pairs
-        self.table = 2 * (self.listed_slots + self.local_slots)
+        self.table = self.listed_slots + 2 * self.local_slots
 
     def kind(self, meta, s):
         return meta[s]
@@ -91,13 +104,13 @@
     return pl.BlockSpec(memory_space=pltpu.VMEM)
 
 
-def call(body, outs, scalars, arrays, flops=0, scratch=(), early=(), to_smem=False):
+def call(body, outs, scalars, arrays, flops=0, scratch=(), early=(), to_smem=0):
     moved = sum(a.size * a.dtype.itemsize for a in arrays) + sum(o.size * o.dtype.itemsize for o in outs)
     return pl.pallas_call(
         body if not early else lambda *refs: body(*refs[len(early) :]),
         out_shape=outs,
         in_specs=[pl.BlockSpec(memory_space=pl.ANY)] * len(early) + [smem()] * len(scalars) + [vmem()] * len(arrays),
-        out_specs=[smem() if to_smem else vmem()] * len(outs),
+        out_specs=[smem()] * to_smem + [vmem()] * (len(outs) - to_smem),
         scratch_shapes=list(scratch),
         compiler_params=pltpu.CompilerParams(vmem_limit_bytes=8 << 20),
         cost_estimate=pl.CostEstimate(flops=flops, bytes_accessed=moved, transcendentals=0),
@@ -108,30 +121,38 @@
     for which in range(2):
         for j in range(lay.cap):
             s, live, _ = lay.lookup(meta, 4 - 2 * side + which, side, j)
-            out[which * lay.cap + j] = jnp.where(live, tiles[s], 0.0)
-
-
-def outgoing_kernel(lay, me, mine, mates, inverse, tiles, mate_tiles, out, lower):
+            tile = jnp.where(live, tiles[s], 0.0)
+            out[which * lay.cap + j] = tile if side == 1 else tile.T
+
+
+def outgoing_kernel(lay, near, inverse, tiles, mate_tiles, *refs):
+    outs, lower = refs[:-1], refs[-1]
+    me, mine, mates = near.at[0], near.at[1], near.at[2]
     role = me[0] % 2
     for g, (meta, source) in enumerate(((mine, tiles), (mates, mate_tiles))):
         for j in range(lay.cap):
             s, live, _ = lay.lookup(meta, role, 2, j)
             tile = jnp.where(live, source[s], 0.0)
-            out[g * lay.cap + j] = matmul(inverse[lay.place(s // lay.width, me[0])], tile)
+            product = matmul(inverse[lay.place(s // lay.width, me[0])], tile).T
+            for h, out in enumerate(outs):
+                out[g * lay.cap + j] = product[h * out.shape[1] : (h + 1) * out.shape[1]]
     listed_tiles(lay, mine, 1, tiles, lower)
 
 
-def next_outgoing_kernel(lay, me, mine, mates, inverse, upper, mate_upper, out):
+def next_outgoing_kernel(lay, near, inverse, upper, mate_upper, *outs):
+    me, mine, mates = near.at[0], near.at[1], near.at[2]
     role = me[0] % 2
     for g, (meta, source) in enumerate(((mine, upper), (mates, mate_upper))):
         for j in range(lay.cap):
             r = lay.listed(meta, role, j) // lay.width
-            out[g * lay.cap + j] = matmul(inverse[lay.place(r, me[0])], source[role * lay.cap + j])
-
-
-def local_terms(lay, me, mine, inverse, diag, tiles, out):
-    out[: lay.own_rows] = -diag[...]
-    out[lay.own_rows :] = jnp.zeros((lay.rows - lay.own_rows,) + diag.shape[1:], F32)
+            product = matmul_nt(source[role * lay.cap + j], inverse[lay.place(r, me[0])])
+            for h, out in enumerate(outs):
+                out[g * lay.cap + j] = product[h * out.shape[1] : (h + 1) * out.shape[1]]
+
+
+def local_terms(lay, me, mine, inverse, diag, tiles, outs, total):
+    total[: lay.own_rows] = -diag[...]
+    total[lay.own_rows :] = jnp.zeros((lay.rows - lay.own_rows,) + diag.shape[1:], F32)
 
     @pl.loop(0, lay.slots)
     def _(s):
@@ -139,13 +160,18 @@
         def _():
             v = lay.link(mine, s)
             q = matmul(inverse[lay.place(v // lay.width, me[0])], tiles[v])
-            out[lay.place(s // lay.width, me[0])] += matmul(tiles[s], q)
-
-
-def local_pivot_kernel(
-    lay, me, mine, mates, inverse, diag, tiles, mate_tiles, out, mate_lower, lower_local, upper, mate_upper, places
-):
-    local_terms(lay, me, mine, inverse, diag, tiles, out)
+            total[lay.place(s // lay.width, me[0])] += matmul(tiles[s], q)
+
+    for r in range(lay.rows):
+        turned = total[r].T
+        for h, out in enumerate(outs):
+            out[r] = turned[h * out.shape[1] : (h + 1) * out.shape[1]]
+
+
+def local_pivot_kernel(lay, parts, near, inverse, diag, tiles, mate_tiles, *refs):
+    outs, (mate_lower, lower_local, upper, mate_upper, total, places) = refs[:parts], refs[parts:]
+    me, mine, mates = near.at[0], near.at[1], near.at[2]
+    local_terms(lay, me, mine, inverse, diag, tiles, outs, total)
     listed_tiles(lay, mates, 1, mate_tiles, mate_lower)
     listed_tiles(lay, mates, 2, mate_tiles, mate_upper)
     listed_tiles(lay, mine, 2, tiles, upper)
@@ -153,21 +179,23 @@
         count = lay.scan(mine, side, places)
         for i in range(lay.pairs):
             live = i < count
-            target[start + i] = jnp.where(live, tiles[jnp.where(live, places[i], 0)], 0.0)
-
-
-def next_local_pivot_kernel(lay, me, mine, inverse, diag, tiles, out):
-    local_terms(lay, me, mine, inverse, diag, tiles, out)
-
-
-def incoming_kernel(lay, me, mine, mates, local, lower, mate_lower, arrived, keep, give, total):
+            tile = jnp.where(live, tiles[jnp.where(live, places[i], 0)], 0.0)
+            target[start + i] = tile if side == 1 else tile.T
+
+
+def next_local_pivot_kernel(lay, near, inverse, diag, tiles, *refs):
+    local_terms(lay, near.at[0], near.at[1], inverse, diag, tiles, refs[:-1], refs[-1])
+
+
+def incoming_kernel(lay, near, local, lower, mate_lower, arrived, keep, give, total):
+    me, mine, mates = near.at[0], near.at[1], near.at[2]
     role = me[0] % 2
     places, terms = [], []
     for g, (meta, source) in enumerate(((mine, lower), (mates, mate_lower))):
         for j in range(lay.cap):
             s, _, v = lay.lookup(meta, 2 + role, 1, j)
             places.append(lay.place(s // lay.width, me[0]))
-            terms.append(matmul(source[role * lay.cap + j], arrived[g * lay.cap + v]))
+            terms.append(matmul_nt(arrived[g * lay.cap + v], source[role * lay.cap + j]))
     total[...] = local[...]
     for place, term in zip(places, terms):
         total[place] += term
@@ -176,16 +204,20 @@
     give[...] = total[half:]
 
 
-def newton_kernel(inverse, sums, out):
+def newton_kernel(inverse, *refs):
+    sums, out = refs[:-1], refs[-1]
     for i in range(out.shape[0]):
         x = inverse[i]
         xh, xl = split(x)
-        product = matmul_parts(xh, xl, *split(sums[i]))
+        product = matmul_nt_parts(xh, xl, *split(jnp.concatenate([part[i] for part in sums], 0)))
         out[i] = 2.0 * x + matmul_parts(*split(product), xh, xl)
 
 
-def table_kernel(lay, me, metas, peers_below, peers_above, out, places):
+def table_kernel(lay, me, metas, peers_below, peers_above, out, *refs):
+    masks, places = refs[:4], refs[4]
     role = me[0] % 2
+    out[2 * lay.table] = me[0]
+    row = lax.broadcasted_iota(jnp.int32, masks[0].shape[1:], 0)
     for side in (1, 2):
         start = (side - 1) * lay.table
         base, peers = ((2, peers_below), (0, peers_above))[side - 1]
@@ -193,12 +225,13 @@
             a, meta, peer = q ^ me[0], metas.at[q], peers.at[q]
             for j in range(lay.cap):
                 s, _, v = lay.lookup(meta, base + role, side, j)
-                k = start + a * lay.cap + j
-                out[k] = s // lay.width
-                out[lay.listed_slots + k] = lay.listed(peer, 2 - base + role, v) // lay.width
+                out[start + a * lay.cap + j] = s // lay.width
+                source = lay.listed(peer, 2 - base + role, v) // lay.width
+                masks[2 * side - 2][a * lay.cap + j] = (row == s // lay.width).astype(F32)
+                masks[2 * side - 1][a * lay.cap + j] = (row == source).astype(F32)
         for q in range(0, lay.n_tile, 2):
             meta = metas.at[q]
-            begin = start + 2 * lay.listed_slots + ((q ^ me[0]) >> 1) * lay.pairs
+            begin = start + lay.listed_slots + ((q ^ me[0]) >> 1) * lay.pairs
             count = lay.scan(meta, side, places)
             for i in range(lay.pairs):
                 s = jnp.where(i < count, places[i], 0)
@@ -207,27 +240,29 @@
                 out[begin + lay.local_slots + i] = v // lay.width
 
 
-def scaled_kernel(lay, side, me, table, inverse, *refs):
+def scaled_kernel(lay, side, table, inverse, *refs):
     sources, (listed, local) = refs[:-2], refs[-2:]
-    role = me[0] % 2
+    me = table[2 * lay.table]
+    role = me % 2
     start = (side - 1) * lay.table
 
     def scaled(row, tile):
-        return widen(matmul(inverse[lay.place(row, me[0])], tile))
+        x = inverse[lay.place(row, me)]
+        return widen(matmul(x, tile) if side == 1 else matmul_nt(x, tile))
 
     at = 0
     for q in range(lay.n_tile):
         lists = sources[at]
         for j in range(lay.cap):
-            k = (q ^ me[0]) * lay.cap + j
+            k = (q ^ me) * lay.cap + j
             listed[k] = scaled(table[start + k], lists[role * lay.cap + j])
         at += 1
         if q % 2 == 0:
             pairs, first = (lists, 2 * lay.cap) if side == 2 else (sources[at], 0)
             at += side == 1
             for i in range(lay.pairs):
-                k = ((q ^ me[0]) >> 1) * lay.pairs + i
-                local[k] = scaled(table[start + 2 * lay.listed_slots + k], pairs[first + i])
+                k = ((q ^ me) >> 1) * lay.pairs + i
+                local[k] = scaled(table[start + lay.listed_slots + k], pairs[first + i])
 
 
 def first_kernel(lay, me, base, inverse, out):
@@ -238,19 +273,21 @@
 
 
 def local_sum_kernel(lay, side, table, x, tiles, out):
-    start = (side - 1) * lay.table + 2 * lay.listed_slots
+    start = (side - 1) * lay.table + lay.listed_slots
     terms = [times_tile(x[table[start + lay.local_slots + k]], tiles[k]) for k in range(lay.local_slots)]
     out[...] = jnp.zeros_like(out)
     for k, value in enumerate(terms):
         out[table[start + k]] += value
 
 
-def listed_sum_kernel(lay, side, table, local, tiles, arrived, out):
-    start = (side - 1) * lay.table
-    terms = [times_tile(arrived[table[start + lay.listed_slots + k]], tiles[k]) for k in range(lay.listed_slots)]
-    out[...] = local[...]
-    for k, value in enumerate(terms):
-        out[table[start + k]] += value
+def listed_sum_kernel(lay, tiles, picks, sources, local, arrived, out):
+    rows = [arrived[r] for r in range(lay.rows)]
+    terms = []
+    for k in range(lay.listed_slots):
+        x = sum(sources[k, r : r + 1] * rows[r] for r in range(lay.rows))
+        terms.append(times_tile(x, tiles[k]))
+    for r in range(lay.rows):
+        out[r] = local[r] + sum(picks[k, r : r + 1] * terms[k] for k in range(lay.listed_slots))
 
 
 def local(krylov_block, diag_block, inverse_prev, coupling_tiles, slot_kind, slot_link, send_slots):
@@ -304,65 +341,68 @@
     arriving, held, both = lax.optimization_barrier((arriving, held, both))
     mates = both[0]
     metas = jnp.stack([one for pair in zip(held, both) for one in pair])
+    near = jnp.stack([jnp.broadcast_to(me, mine.shape), mine, mates])
     kept = jnp.concatenate(arriving, 0)
     mated = jnp.concatenate([swap(x, 1) for x in arriving], 0)
     half = rows // 2
     lists, local_list = shape(2 * cap, n, n), shape(lay.pairs, n, n)
+    sent, summands = [shape(2 * cap, n // PARTS, n)] * PARTS, [shape(rows, n // PARTS, n)] * PARTS
     places = pltpu.SMEM((lay.slots + 1,), jnp.int32)
+    total = pltpu.VMEM((rows, n, n), F32)
     for sweep in range(FSWEEPS):
         inverse = jnp.concatenate([kept, mated], 0)
         early, later = [], []
         if sweep == 0:
-            out, lower = call(
-                kernel(outgoing_kernel), [lists] * 2, (me, mine, mates), (inverse, tiles, mate_tiles)
-            )
-            arrived = along(out, 1)
+            *out, lower = call(kernel(outgoing_kernel), sent + [lists], (near,), (inverse, tiles, mate_tiles))
+            arrived = [along(part, 1) for part in out]
             lowers = over_chips(lower)
-            here, mate_lower, lower_local, upper, mate_upper = call(
-                kernel(local_pivot_kernel),
-                [shape(rows, n, n), lists, local_list, shape(2 * cap + lay.pairs, n, n), lists],
-                (me, mine, mates),
+            *here, mate_lower, lower_local, upper, mate_upper = call(
+                kernel(local_pivot_kernel, PARTS),
+                summands + [lists, local_list, shape(2 * cap + lay.pairs, n, n), lists],
+                (near,),
                 (inverse, diag_block, tiles, mate_tiles),
                 flops=product * rows,
-                scratch=(places,),
+                scratch=(total, places),
             )
             early += lowers[1:]
         else:
-            (out,) = call(
-                kernel(next_outgoing_kernel), [lists], (me, mine, mates), (inverse, upper, mate_upper)
-            )
-            arrived = along(out, 1)
-            (here,) = call(
+            out = call(kernel(next_outgoing_kernel), sent, (near,), (inverse, upper, mate_upper))
+            arrived = [along(part, 1) for part in out]
+            here = call(
                 kernel(next_local_pivot_kernel),
-                [shape(rows, n, n)],
-                (me, mine),
+                summands,
+                (near,),
                 (inverse, diag_block, tiles),
                 flops=product * rows,
+                scratch=(total,),
             )
         if sweep == FSWEEPS - 1:
             lower_locals = over_chips(lower_local)
             mate_lowers = [mate_lower] + [swap(x, 1) for x in lowers[1:]]
             below, above = along(metas, 1), along(metas, -1)
-            (table,) = call(
+            mask = shape(lay.listed_slots, rows, n)
+            table, *masks = call(
                 kernel(table_kernel),
-                [shape(2 * lay.table, dtype=jnp.int32)],
+                [shape(2 * lay.table + 1, dtype=jnp.int32)] + [mask] * 4,
                 (me, metas, below, above),
                 (),
                 scratch=(places,),
-                to_smem=True,
+                to_smem=1,
             )
             early += [*lower_locals[1:], *mate_lowers[1:], below, above]
             later += [table]
-        keep, give = call(
-            kernel(incoming_kernel),
-            [shape(half, n, n)] * 2,
-            (me, mine, mates),
-            (here, lower, mate_lower, arrived),
-            scratch=(pltpu.VMEM((rows, n, n), F32),),
-            early=early,
-        )
-        sums = summed(keep + swap(give, 1))
-        (kept,) = call(newton_kernel, [shape(half, n, n)], (), (kept, sums), early=later)
+        sums = []
+        for part in range(PARTS):
+            keep, give = call(
+                kernel(incoming_kernel),
+                [shape(half, n // PARTS, n)] * 2,
+                (near,),
+                (here[part], lower, mate_lower, arrived[part]),
+                scratch=(pltpu.VMEM((rows, n // PARTS, n), F32),),
+                early=early if part == PARTS - 1 else (),
+            )
+            sums.append(summed(keep + swap(give, 1)))
+        (kept,) = call(newton_kernel, [shape(half, n, n)], (), (kept, *sums), early=later)
         mated = swap(kept, 1)
     inverse = jnp.concatenate([kept, mated], 0)
 
@@ -373,7 +413,7 @@
                 shape(lay.listed_slots, 2 * n, n, dtype=BF16),
                 shape(lay.local_slots, 2 * n, n, dtype=BF16),
             ],
-            (me, table),
+            (table,),
             (inverse, *sources),
             flops=product * 24,
         )
@@ -390,10 +430,10 @@
                 kernel(local_sum_kernel, side), [block], (table,), (x, local), flops=8 * n**2 * vectors * rows
             )
             (part,) = call(
-                kernel(listed_sum_kernel, side),
+                kernel(listed_sum_kernel),
                 [block],
-                (table,),
-                (here, listed, arrived),
+                (),
+                (listed, *masks[2 * side - 2 : 2 * side], here, arrived),
                 early=early if sweep == count - 1 else (),
             )
             x = base - (part + swap(part, 1))

time: 145 us -> 151 us (1.041)
  starting transfers between devices: 51.7 us -> 62.5 us
  waiting for transfers between devices: 59.6 us -> 52.9 us
  Pallas kernels: 25.6 us -> 27.8 us
    ppermute x10 -> x12, starting transfers between devices: 37 us -> 48 us  [along(): return lax.ppermute(x, ('dom', 'tile'), route)]
    ppermute x25 -> x29, waiting for transfers between devices: 38.6 us -> 31.2 us  [swap(): return lax.ppermute(x, 'tile', [(i, i ^ bit) for i in range(n_tile)])]
    pallas_call x24 -> x26, Pallas kernels: 25.6 us -> 27.8 us  [call(): pl.pallas_call(body if not early else lambda *refs: body(*refs[len(early)...]
    ppermute x10 -> x12, waiting for transfers between devices: 21 us -> 21.7 us  [along(): return lax.ppermute(x, ('dom', 'tile'), route)]
    ppermute x25 -> x29, starting transfers between devices: 14.6 us -> 14.6 us  [swap(): return lax.ppermute(x, 'tile', [(i, i ^ bit) for i in range(n_tile)])]
  transfers between devices with their start and end apart: 35 -> 41, of which waited for: 26 -> 30; matrix products, arithmetic and copies ran while one was open for 3% -> 3% of each run, Pallas kernels for 13% -> 15%
where the time goes in v5:
time: 151 us; the launch traced here: 150 us
  starting transfers between devices  62.5 us (41%)
  waiting for transfers between devices  52.9 us (35%)
  Pallas kernels  27.8 us (18%)
  local copies, waits for them, and re-layouts  4.22 us (3%)
    ppermute x12, starting transfers between devices, along(): return lax.ppermute(x, ('dom', 'tile'), route)  48 us
    ppermute x29, waiting for transfers between devices, swap(): return lax.ppermute(x, 'tile', [(i, i ^ bit) for i in range(n_tile)])  31.2 us
    pallas_call x26, Pallas kernels, call(): pl.pallas_call(body if not early else lambda *refs: body(*refs[len(early)...  27.8 us
    ppermute x12, waiting for transfers between devices, along(): return lax.ppermute(x, ('dom', 'tile'), route)  21.7 us
    ppermute x29, starting transfers between devices, swap(): return lax.ppermute(x, 'tile', [(i, i ^ bit) for i in range(n_tile)])  14.6 us
  transfers between devices with their start and end apart: 41, of which 30 were waited for; matrix products, arithmetic and copies ran while one was open for 3% of the time, Pallas kernels for 15%

profile of v5, /device:TPU:18, one launch (start us, length us, event | category | flops | bytes accessed | tf_op | source)
XLA Modules:
  0.0 150.1 jit_solution(7280837574749389155)
XLA Ops:
  0.7 1.6 %collective-permute-start = (f32[3,128,128]{2,1,0:T(8,128)}, f32[3,128,128]{2,1,0:T(8,128)S(1)}, u32[]{:S(2)}, u32[]{:S(2)}) collective-permute-start(f32[3,128,128]{2,1,0:T(8,128)} %param.9), channel_id=1, source_target_pairs={{0,2},{1,3},{2,0},{3,1},{4,6},{5,7},{6,4},{7,5},{8,10},{9,11},{10,... | collective-permute-start | bytes 589832 | tf_op jit(solution)/shard_map/ppermute | solution.py:306
  5.4 3.0 %collective-permute-done.1 = s32[64]{0:T(128)S(1)} collective-permute-done((s32[64]{0:T(128)S(1)}, s32[64]{0:T(128)S(1)}, u32[]{:S(2)}, u32[]{:S(2)}) %collective-permute-start.1) | collective-permute-done | bytes 288 | tf_op jit(solution)/shard_map/ppermute | solution.py:306
  8.4 1.1 collective-permute-done.3
  12.3 3.5 %collective-permute-start.9 = (f32[8,64,128]{2,1,0:T(8,128)S(1)}, f32[8,64,128]{2,1,0:T(8,128)S(1)}, u32[]{:S(2)}, u32[]{:S(2)}) collective-permute-start(f32[8,64,128]{2,1,0:T(8,128)S(1)} %get-tuple-element.48), channel_id=1, source_target_pairs={{0,4},{1,9},{2,6},{3,11},{4,8},{5,13},{6,10},{7,15},{8,12},{9,17},... | collective-permute-start | bytes 786440 | tf_op jit(solution)/shard_map/ppermute | solution.py:315
  15.8 1.5 collective-permute-start.12
  17.3 3.1 %shard_map.87 = (f32[12,64,128]{2,1,0:T(8,128)S(1)}, f32[12,64,128]{2,1,0:T(8,128)S(1)}, f32[8,128,128]{2,1,0:T(8,128)S(1)}, f32[4,128,128]{2,1,0:T(8,128)S(1)},...) custom-call(s32[3,64]{1,0:T(4,128)S(1)} %pad_add_fusion.1.near.refs_1_.refs_4_, ...), custom_call_target="tpu_custom_call" | custom-call | flops 201326592 | bytes 7012352 | tf_op jit(solution)/shard_map/pallas_call | solution.py:109
  20.4 1.4 collective-permute-done.9.arrived
  23.2 5.0 %collective-permute-start.13 = (f32[8,64,128]{2,1,0:T(8,128)S(1)}, f32[8,64,128]{2,1,0:T(8,128)S(1)}, u32[]{:S(2)}, u32[]{:S(2)}) collective-permute-start(f32[8,64,128]{2,1,0:T(8,128)S(1)} %get-tuple-element.52), channel_id=1, source_target_pairs={{0,4},{1,9},{2,6},{3,11},{4,8},{5,13},{6,10},{7,15},{8,12},{9,17},... | collective-permute-start | bytes 786440 | tf_op jit(solution)/shard_map/ppermute | solution.py:315
  28.2 1.5 collective-permute-start.11
  29.8 2.7 %collective-permute-done.13.refs_5_ = f32[8,64,128]{2,1,0:T(8,128)S(1)} collective-permute-done((f32[8,64,128]{2,1,0:T(8,128)S(1)}, f32[8,64,128]{2,1,0:T(8,128)S(1)}, u32[]{:S(2)}, u32[]{:S(2)}) %collective-permute-start.13) | collective-permute-done | bytes 262176 | tf_op jit(solution)/shard_map/ppermute | solution.py:315
  35.0 1.5 %collective-permute-start.15 = (f32[6,64,128]{2,1,0:T(8,128)S(1)}, f32[6,64,128]{2,1,0:T(8,128)S(1)}, u32[]{:S(2)}, u32[]{:S(2)}) collective-permute-start(f32[6,64,128]{2,1,0:T(8,128)S(1)} %add.44), channel_id=1, source_target_pairs={{0,2},{1,3},{2,0},{3,1},{4,6},{5,7},{6,4},{7,5},{8,10},{9,11},{10,... | collective-permute-start | bytes 589832 | tf_op jit(solution)/shard_map/ppermute | solution.py:306
  36.5 5.5 %collective-permute-done.15 = f32[6,64,128]{2,1,0:T(8,128)S(1)} collective-permute-done((f32[6,64,128]{2,1,0:T(8,128)S(1)}, f32[6,64,128]{2,1,0:T(8,128)S(1)}, u32[]{:S(2)}, u32[]{:S(2)}) %collective-permute-start.15) | collective-permute-done | bytes 196640 | tf_op jit(solution)/shard_map/ppermute | solution.py:306
  42.1 1.3 shard_map.91.refs_1_
  44.0 1.2 collective-permute-done.16
  45.3 1.1 shard_map.93
  46.3 5.3 %collective-permute-start.17 = (f32[8,64,128]{2,1,0:T(8,128)S(1)}, f32[8,64,128]{2,1,0:T(8,128)S(1)}, u32[]{:S(2)}, u32[]{:S(2)}) collective-permute-start(f32[8,64,128]{2,1,0:T(8,128)S(1)} %get-tuple-element.58), channel_id=1, source_target_pairs={{0,4},{1,9},{2,6},{3,11},{4,8},{5,13},{6,10},{7,15},{8,12},{9,17},... | collective-permute-start | bytes 786440 | tf_op jit(solution)/shard_map/ppermute | solution.py:315
  51.6 1.5 %collective-permute-start.20 = (f32[4,128,128]{2,1,0:T(8,128)S(1)}, f32[4,128,128]{2,1,0:T(8,128)S(1)}, u32[]{:S(2)}, u32[]{:S(2)}) collective-permute-start(f32[4,128,128]{2,1,0:T(8,128)S(1)} %get-tuple-element.61.refs_1_), channel_id=1, source_target_pairs={{0,2},{1,3},{2,0},{3,1},{4,6},{5,7},{6,4},{7,5},{8,10},{9,11},{10,... | collective-permute-start | bytes 786440 | tf_op jit(solution)/shard_map/ppermute | solution.py:306
  53.1 1.9 %collective-permute-start.22 = (f32[8,64,128]{2,1,0:T(8,128)S(1)}, f32[8,64,128]{2,1,0:T(8,128)S(1)}, u32[]{:S(2)}, u32[]{:S(2)}) collective-permute-start(f32[8,64,128]{2,1,0:T(8,128)S(1)} %get-tuple-element.63), channel_id=1, source_target_pairs={{0,4},{1,9},{2,6},{3,11},{4,8},{5,13},{6,10},{7,15},{8,12},{9,17},... | collective-permute-start | bytes 786440 | tf_op jit(solution)/shard_map/ppermute | solution.py:315
  55.1 2.6 %shard_map.92 = (f32[12,64,128]{2,1,0:T(8,128)S(1)}, f32[12,64,128]{2,1,0:T(8,128)S(1)}) custom-call(s32[3,64]{1,0:T(4,128)S(1)} %pad_add_fusion.1.near.refs_1_.refs_4_, f32[12,128,128]{2,1,0:T(8,128)S(1)} %pad_maximum_fusion.inverse, f32[3,128,128]{2,1,0:T(8,128)S(1)} %copy-done.1, f32[24,128,128]{2,1,0:T(8,128)S(1)} %bitcast.23), custom_call_target="tpu_custom_call" | custom-call | flops 201326592 | bytes 3342336 | tf_op jit(solution)/shard_map/pallas_call | solution.py:109
  59.0 4.2 %collective-permute-start.5 = (s32[4,64]{1,0:T(4,128)S(1)}, s32[4,64]{1,0:T(4,128)S(1)}, u32[]{:S(2)}, u32[]{:S(2)}) collective-permute-start(s32[4,64]{1,0:T(4,128)S(1)} %pad_add_fusion.metas), channel_id=1, source_target_pairs={{4,0},{6,2},{8,4},{9,1},{10,6},{11,3},{12,8},{13,5},{14,10},{15,7}... | collective-permute-start | bytes 3080 | tf_op jit(solution)/shard_map/ppermute | solution.py:315
  63.3 2.6 %collective-permute-done.5.peers_above.refs_3_ = s32[4,64]{1,0:T(4,128)S(1)} collective-permute-done((s32[4,64]{1,0:T(4,128)S(1)}, s32[4,64]{1,0:T(4,128)S(1)}, u32[]{:S(2)}, u32[]{:S(2)}) %collective-permute-start.5) | collective-permute-done | bytes 1056 | tf_op jit(solution)/shard_map/ppermute | solution.py:315
  65.9 3.9 %collective-permute-start.4 = (s32[4,64]{1,0:T(4,128)S(1)}, s32[4,64]{1,0:T(4,128)S(1)}, u32[]{:S(2)}, u32[]{:S(2)}) collective-permute-start(s32[4,64]{1,0:T(4,128)S(1)} %pad_add_fusion.metas), channel_id=1, source_target_pairs={{0,4},{1,9},{2,6},{3,11},{4,8},{5,13},{6,10},{7,15},{8,12},{9,17},... | collective-permute-start | bytes 3080 | tf_op jit(solution)/shard_map/ppermute | solution.py:315
  69.8 1.5 %collective-permute-done.4.peers_below.refs_2_ = s32[4,64]{1,0:T(4,128)S(1)} collective-permute-done((s32[4,64]{1,0:T(4,128)S(1)}, s32[4,64]{1,0:T(4,128)S(1)}, u32[]{:S(2)}, u32[]{:S(2)}) %collective-permute-start.4) | collective-permute-done | bytes 1056 | tf_op jit(solution)/shard_map/ppermute | solution.py:315
  72.6 1.2 collective-permute-start.19
  73.7 2.1 %shard_map.86 = (s32[65]{0:T(128)S(1)}, f32[16,12,128]{2,1,0:T(8,128)S(1)}, f32[16,12,128]{2,1,0:T(8,128)S(1)}, f32[16,12,128]{2,1,0:T(8,128)S(1)}, f32[16,12,128]{2,1,0:T(8,128)S(1)}) custom-call(s32[1]{0:T(128)} %bitcast.me, s32[4,64]{1,0:T(4,128)S(1)} %pad_add_fusion.metas, s32[4,64]{1,0:T(4,128)S(1)} %collective-permute-done.4.peers_below.refs_2_, ...), custom_call_target="tpu_custom_call" | custom-call | bytes 393476 | tf_op jit(solution)/shard_map/pallas_call | solution.py:109
  76.9 3.4 %collective-permute-done.19 = f32[6,64,128]{2,1,0:T(8,128)S(1)} collective-permute-done((f32[6,64,128]{2,1,0:T(8,128)S(1)}, f32[6,64,128]{2,1,0:T(8,128)S(1)}, u32[]{:S(2)}, u32[]{:S(2)}) %collective-permute-start.19) | collective-permute-done | bytes 196640 | tf_op jit(solution)/shard_map/ppermute | solution.py:306
  80.4 3.7 %collective-permute-done.24 = f32[6,64,128]{2,1,0:T(8,128)S(1)} collective-permute-done((f32[6,64,128]{2,1,0:T(8,128)S(1)}, f32[6,64,128]{2,1,0:T(8,128)S(1)}, u32[]{:S(2)}, u32[]{:S(2)}) %collective-permute-start.24) | collective-permute-done | bytes 196640 | tf_op jit(solution)/shard_map/ppermute | solution.py:306
  84.2 1.3 shard_map.96
  85.6 1.2 collective-permute-start.26
  87.7 4.8 %collective-permute-start.27 = (f32[12,16,128]{2,1,0:T(8,128)S(1)}, f32[12,16,128]{2,1,0:T(8,128)S(1)}, u32[]{:S(2)}, u32[]{:S(2)}) collective-permute-start(f32[12,16,128]{2,1,0:T(8,128)S(1)} %shard_map.97.x), channel_id=1, source_target_pairs={{0,4},{1,9},{2,6},{3,11},{4,8},{5,13},{6,10},{7,15},{8,12},{9,17},... | collective-permute-start | bytes 294920 | tf_op jit(solution)/shard_map/ppermute | solution.py:315
  92.6 1.3 shard_map.98
  95.4 1.3 collective-permute-done.28
  96.7 5.2 %collective-permute-start.29 = (f32[12,16,128]{2,1,0:T(8,128)S(1)}, f32[12,16,128]{2,1,0:T(8,128)S(1)}, u32[]{:S(2)}, u32[]{:S(2)}) collective-permute-start(f32[12,16,128]{2,1,0:T(8,128)S(1)} %add_subtract_fusion.5.x), channel_id=1, source_target_pairs={{0,4},{1,9},{2,6},{3,11},{4,8},{5,13},{6,10},{7,15},{8,12},{9,17},... | collective-permute-start | bytes 294920 | tf_op jit(solution)/shard_map/ppermute | solution.py:315
  102.7 1.4 collective-permute-done.29.arrived
  105.9 5.2 %collective-permute-start.31 = (f32[12,16,128]{2,1,0:T(8,128)S(1)}, f32[12,16,128]{2,1,0:T(8,128)S(1)}, u32[]{:S(2)}, u32[]{:S(2)}) collective-permute-start(f32[12,16,128]{2,1,0:T(8,128)S(1)} %add_subtract_fusion.4.x), channel_id=1, source_target_pairs={{0,4},{1,9},{2,6},{3,11},{4,8},{5,13},{6,10},{7,15},{8,12},{9,17},... | collective-permute-start | bytes 294920 | tf_op jit(solution)/shard_map/ppermute | solution.py:315
  112.0 1.4 collective-permute-done.31.refs_5_
  113.9 1.3 collective-permute-done.32
  115.2 4.8 %collective-permute-start.34 = (f32[12,16,128]{2,1,0:T(8,128)S(1)}, f32[12,16,128]{2,1,0:T(8,128)S(1)}, u32[]{:S(2)}, u32[]{:S(2)}) collective-permute-start(f32[12,16,128]{2,1,0:T(8,128)S(1)} %add_subtract_fusion.3.x), channel_id=1, source_target_pairs={{4,0},{6,2},{8,4},{9,1},{10,6},{11,3},{12,8},{13,5},{14,10},{15,7}... | collective-permute-start | bytes 294920 | tf_op jit(solution)/shard_map/ppermute | solution.py:315
  120.0 1.7 %shard_map.105 = (bf16[16,256,128]{2,1,0:T(8,128)(2,1)S(1)}, bf16[8,256,128]{2,1,0:T(8,128)(2,1)S(1)}) custom-call(s32[65]{0:T(128)S(1)} %get-tuple-element.42.refs_0_.table, f32[12,128,128]{2,1,0:T(8,128)S(1)} %pad_maximum_fusion.1.inverse, f32[12,128,128]{2,1,0:T(8,128)S(1)} %get-tuple-element.56.upper.refs_0_, ...), custom_call_target="tpu_custom_call" | custom-call | flops 402653184 | bytes 5242880 | tf_op jit(solution)/shard_map/pallas_call | solution.py:109
  122.6 1.5 collective-permute-done.34.arrived
  124.6 1.3 collective-permute-done.35
  125.9 2.3 %collective-permute-start.36 = (f32[12,16,128]{2,1,0:T(8,128)S(1)}, f32[12,16,128]{2,1,0:T(8,128)S(1)}, u32[]{:S(2)}, u32[]{:S(2)}) collective-permute-start(f32[12,16,128]{2,1,0:T(8,128)S(1)} %add_subtract_fusion.2.x), channel_id=1, source_target_pairs={{4,0},{6,2},{8,4},{9,1},{10,6},{11,3},{12,8},{13,5},{14,10},{15,7}... | collective-permute-start | bytes 294920 | tf_op jit(solution)/shard_map/ppermute | solution.py:315
  129.0 4.3 %collective-permute-done.36.arrived = f32[12,16,128]{2,1,0:T(8,128)S(1)} collective-permute-done((f32[12,16,128]{2,1,0:T(8,128)S(1)}, f32[12,16,128]{2,1,0:T(8,128)S(1)}, u32[]{:S(2)}, u32[]{:S(2)}) %collective-permute-start.36) | collective-permute-done | bytes 98336 | tf_op jit(solution)/shard_map/ppermute | solution.py:315
  133.9 1.3 collective-permute-done.37
  135.2 1.9 %collective-permute-start.38 = (f32[12,16,128]{2,1,0:T(8,128)S(1)}, f32[12,16,128]{2,1,0:T(8,128)S(1)}, u32[]{:S(2)}, u32[]{:S(2)}) collective-permute-start(f32[12,16,128]{2,1,0:T(8,128)S(1)} %add_subtract_fusion.1.x), channel_id=1, source_target_pairs={{4,0},{6,2},{8,4},{9,1},{10,6},{11,3},{12,8},{13,5},{14,10},{15,7}... | collective-permute-start | bytes 294920 | tf_op jit(solution)/shard_map/ppermute | solution.py:315
  138.0 4.7 %collective-permute-done.38.arrived = f32[12,16,128]{2,1,0:T(8,128)S(1)} collective-permute-done((f32[12,16,128]{2,1,0:T(8,128)S(1)}, f32[12,16,128]{2,1,0:T(8,128)S(1)}, u32[]{:S(2)}, u32[]{:S(2)}) %collective-permute-start.38) | collective-permute-done | bytes 98336 | tf_op jit(solution)/shard_map/ppermute | solution.py:315
  143.2 1.3 collective-permute-done.39
  146.1 3.4 %collective-permute-done.40 = f32[12,16,128]{2,1,0:T(8,128)S(1)} collective-permute-done((f32[12,16,128]{2,1,0:T(8,128)S(1)}, f32[12,16,128]{2,1,0:T(8,128)S(1)}, u32[]{:S(2)}, u32[]{:S(2)}) %collective-permute-start.40) | collective-permute-done | bytes 98336 | tf_op jit(solution)/shard_map/ppermute | solution.py:306
  (108 shorter events, 27.2 us)
Async XLA Ops:
  0.6 10.7 %copy-start = (f32[12,2,128,128]{3,2,1,0:T(8,128)S(1)}, f32[12,2,128,128]{3,2,1,0:T(8,128)}, u32[]{:S(2)}) copy-start(f32[12,2,128,128]{3,2,1,0:T(8,128)} %param.10) | copy-start | bytes 4718596
  0.6 10.6 %collective-permute-start.8 = (f32[24,128,128]{2,1,0:T(8,128)}, f32[24,128,128]{2,1,0:T(8,128)S(1)}, u32[]{:S(2)}, u32[]{:S(2)}) collective-permute-start(f32[24,128,128]{2,1,0:T(8,128)} %bitcast.20), channel_id=1, source_target_pairs={{0,1},{1,0},{2,3},{3,2},{4,5},{5,4},{6,7},{7,6},{8,9},{9,8},{10,11... | collective-permute-start | bytes 4718600 | tf_op jit(solution)/shard_map/ppermute | solution.py:306
  0.7 8.8 %collective-permute-start = (f32[3,128,128]{2,1,0:T(8,128)}, f32[3,128,128]{2,1,0:T(8,128)S(1)}, u32[]{:S(2)}, u32[]{:S(2)}) collective-permute-start(f32[3,128,128]{2,1,0:T(8,128)} %param.9), channel_id=1, source_target_pairs={{0,2},{1,3},{2,0},{3,1},{4,6},{5,7},{6,4},{7,5},{8,10},{9,11},{10,... | collective-permute-start | bytes 589832 | tf_op jit(solution)/shard_map/ppermute | solution.py:306
  4.9 3.5 %collective-permute-start.1 = (s32[64]{0:T(128)S(1)}, s32[64]{0:T(128)S(1)}, u32[]{:S(2)}, u32[]{:S(2)}) collective-permute-start(s32[64]{0:T(128)S(1)} %pad_add_fusion.2), channel_id=1, source_target_pairs={{0,2},{1,3},{2,0},{3,1},{4,6},{5,7},{6,4},{7,5},{8,10},{9,11},{10,... | collective-permute-start | bytes 776 | tf_op jit(solution)/shard_map/ppermute | solution.py:306
  5.4 3.0 %collective-permute-start.2 = (s32[64]{0:T(128)S(1)}, s32[64]{0:T(128)S(1)}, u32[]{:S(2)}, u32[]{:S(2)}) collective-permute-start(s32[64]{0:T(128)S(1)} %pad_add_fusion.2), channel_id=1, source_target_pairs={{0,1},{1,0},{2,3},{3,2},{4,5},{5,4},{6,7},{7,6},{8,9},{9,8},{10,11... | collective-permute-start | bytes 776 | tf_op jit(solution)/shard_map/ppermute | solution.py:306
  8.4 1.1 collective-permute-start.3
  9.5 1.7 %collective-permute-start.6 = (f32[3,128,128]{2,1,0:T(8,128)}, f32[3,128,128]{2,1,0:T(8,128)S(1)}, u32[]{:S(2)}, u32[]{:S(2)}) collective-permute-start(f32[3,128,128]{2,1,0:T(8,128)} %param.9), channel_id=1, source_target_pairs={{0,1},{1,0},{2,3},{3,2},{4,5},{5,4},{6,7},{7,6},{8,9},{9,8},{10,11... | collective-permute-start | bytes 589832 | tf_op jit(solution)/shard_map/ppermute | solution.py:306
  9.7 1.5 %collective-permute-start.7 = (f32[3,128,128]{2,1,0:T(8,128)S(1)}, f32[3,128,128]{2,1,0:T(8,128)S(1)}, u32[]{:S(2)}, u32[]{:S(2)}) collective-permute-start(f32[3,128,128]{2,1,0:T(8,128)S(1)} %collective-permute-done), channel_id=1, source_target_pairs={{0,1},{1,0},{2,3},{3,2},{4,5},{5,4},{6,7},{7,6},{8,9},{9,8},{10,11... | collective-permute-start | bytes 589832 | tf_op jit(solution)/shard_map/ppermute | solution.py:306
  11.3 6.0 %copy-start.1 = (f32[3,128,128]{2,1,0:T(8,128)S(1)}, f32[3,128,128]{2,1,0:T(8,128)}, u32[]{:S(2)}) copy-start(f32[3,128,128]{2,1,0:T(8,128)} %diag.3) | copy-start | bytes 589828
  12.3 9.4 %collective-permute-start.9 = (f32[8,64,128]{2,1,0:T(8,128)S(1)}, f32[8,64,128]{2,1,0:T(8,128)S(1)}, u32[]{:S(2)}, u32[]{:S(2)}) collective-permute-start(f32[8,64,128]{2,1,0:T(8,128)S(1)} %get-tuple-element.48), channel_id=1, source_target_pairs={{0,4},{1,9},{2,6},{3,11},{4,8},{5,13},{6,10},{7,15},{8,12},{9,17},... | collective-permute-start | bytes 786440 | tf_op jit(solution)/shard_map/ppermute | solution.py:315
  15.8 16.6 %collective-permute-start.12 = (f32[8,128,128]{2,1,0:T(8,128)S(1)}, f32[8,128,128]{2,1,0:T(8,128)S(1)}, u32[]{:S(2)}, u32[]{:S(2)}) collective-permute-start(f32[8,128,128]{2,1,0:T(8,128)S(1)} %get-tuple-element.46.lower.refs_3_.refs_6_.refs_0_), channel_id=1, source_target_pairs={{0,2},{1,3},{2,0},{3,1},{4,6},{5,7},{6,4},{7,5},{8,10},{9,11},{10,... | collective-permute-start | bytes 1572872 | tf_op jit(solution)/shard_map/ppermute | solution.py:306
  20.4 9.3 %copy-start.3 = (f32[3,128,128]{2,1,0:T(8,128)S(1)}, f32[3,128,128]{2,1,0:T(8,128)}, u32[]{:S(2)}) copy-start(f32[3,128,128]{2,1,0:T(8,128)} %param.9) | copy-start | bytes 589828
  22.8 5.4 %collective-permute-start.10 = (f32[6,64,128]{2,1,0:T(8,128)S(1)}, f32[6,64,128]{2,1,0:T(8,128)S(1)}, u32[]{:S(2)}, u32[]{:S(2)}) collective-permute-start(f32[6,64,128]{2,1,0:T(8,128)S(1)} %get-tuple-element.50), channel_id=1, source_target_pairs={{0,1},{1,0},{2,3},{3,2},{4,5},{5,4},{6,7},{7,6},{8,9},{9,8},{10,11... | collective-permute-start | bytes 589832 | tf_op jit(solution)/shard_map/ppermute | solution.py:306
  23.2 9.2 %collective-permute-start.13 = (f32[8,64,128]{2,1,0:T(8,128)S(1)}, f32[8,64,128]{2,1,0:T(8,128)S(1)}, u32[]{:S(2)}, u32[]{:S(2)}) collective-permute-start(f32[8,64,128]{2,1,0:T(8,128)S(1)} %get-tuple-element.52), channel_id=1, source_target_pairs={{0,4},{1,9},{2,6},{3,11},{4,8},{5,13},{6,10},{7,15},{8,12},{9,17},... | collective-permute-start | bytes 786440 | tf_op jit(solution)/shard_map/ppermute | solution.py:315
  28.2 5.7 %collective-permute-start.11 = (f32[6,64,128]{2,1,0:T(8,128)S(1)}, f32[6,64,128]{2,1,0:T(8,128)S(1)}, u32[]{:S(2)}, u32[]{:S(2)}) collective-permute-start(f32[6,64,128]{2,1,0:T(8,128)S(1)} %add.42), channel_id=1, source_target_pairs={{0,2},{1,3},{2,0},{3,1},{4,6},{5,7},{6,4},{7,5},{8,10},{9,11},{10,... | collective-permute-start | bytes 589832 | tf_op jit(solution)/shard_map/ppermute | solution.py:306
  33.5 1.5 %collective-permute-start.14 = (f32[6,64,128]{2,1,0:T(8,128)S(1)}, f32[6,64,128]{2,1,0:T(8,128)S(1)}, u32[]{:S(2)}, u32[]{:S(2)}) collective-permute-start(f32[6,64,128]{2,1,0:T(8,128)S(1)} %get-tuple-element.54), channel_id=1, source_target_pairs={{0,1},{1,0},{2,3},{3,2},{4,5},{5,4},{6,7},{7,6},{8,9},{9,8},{10,11... | collective-permute-start | bytes 589832 | tf_op jit(solution)/shard_map/ppermute | solution.py:306
  35.0 7.0 %collective-permute-start.15 = (f32[6,64,128]{2,1,0:T(8,128)S(1)}, f32[6,64,128]{2,1,0:T(8,128)S(1)}, u32[]{:S(2)}, u32[]{:S(2)}) collective-permute-start(f32[6,64,128]{2,1,0:T(8,128)S(1)} %add.44), channel_id=1, source_target_pairs={{0,2},{1,3},{2,0},{3,1},{4,6},{5,7},{6,4},{7,5},{8,10},{9,11},{10,... | collective-permute-start | bytes 589832 | tf_op jit(solution)/shard_map/ppermute | solution.py:306
  43.4 1.8 %collective-permute-start.16 = (f32[6,128,128]{2,1,0:T(8,128)S(1)}, f32[6,128,128]{2,1,0:T(8,128)S(1)}, u32[]{:S(2)}, u32[]{:S(2)}) collective-permute-start(f32[6,128,128]{2,1,0:T(8,128)S(1)} %shard_map.91.refs_1_), channel_id=1, source_target_pairs={{0,1},{1,0},{2,3},{3,2},{4,5},{5,4},{6,7},{7,6},{8,9},{9,8},{10,11... | collective-permute-start | bytes 1179656 | tf_op jit(solution)/shard_map/ppermute | solution.py:306
  43.5 27.9 %collective-permute-start.21 = (f32[8,128,128]{2,1,0:T(8,128)S(1)}, f32[8,128,128]{2,1,0:T(8,128)S(1)}, u32[]{:S(2)}, u32[]{:S(2)}) collective-permute-start(f32[8,128,128]{2,1,0:T(8,128)S(1)} %collective-permute-done.12.refs_0_.refs_3_), channel_id=1, source_target_pairs={{0,1},{1,0},{2,3},{3,2},{4,5},{5,4},{6,7},{7,6},{8,9},{9,8},{10,11... | collective-permute-start | bytes 1572872 | tf_op jit(solution)/shard_map/ppermute | solution.py:306
  46.3 11.5 %collective-permute-start.17 = (f32[8,64,128]{2,1,0:T(8,128)S(1)}, f32[8,64,128]{2,1,0:T(8,128)S(1)}, u32[]{:S(2)}, u32[]{:S(2)}) collective-permute-start(f32[8,64,128]{2,1,0:T(8,128)S(1)} %get-tuple-element.58), channel_id=1, source_target_pairs={{0,4},{1,9},{2,6},{3,11},{4,8},{5,13},{6,10},{7,15},{8,12},{9,17},... | collective-permute-start | bytes 786440 | tf_op jit(solution)/shard_map/ppermute | solution.py:315
  51.6 19.7 %collective-permute-start.20 = (f32[4,128,128]{2,1,0:T(8,128)S(1)}, f32[4,128,128]{2,1,0:T(8,128)S(1)}, u32[]{:S(2)}, u32[]{:S(2)}) collective-permute-start(f32[4,128,128]{2,1,0:T(8,128)S(1)} %get-tuple-element.61.refs_1_), channel_id=1, source_target_pairs={{0,2},{1,3},{2,0},{3,1},{4,6},{5,7},{6,4},{7,5},{8,10},{9,11},{10,... | collective-permute-start | bytes 786440 | tf_op jit(solution)/shard_map/ppermute | solution.py:306
  53.1 18.2 %collective-permute-start.22 = (f32[8,64,128]{2,1,0:T(8,128)S(1)}, f32[8,64,128]{2,1,0:T(8,128)S(1)}, u32[]{:S(2)}, u32[]{:S(2)}) collective-permute-start(f32[8,64,128]{2,1,0:T(8,128)S(1)} %get-tuple-element.63), channel_id=1, source_target_pairs={{0,4},{1,9},{2,6},{3,11},{4,8},{5,13},{6,10},{7,15},{8,12},{9,17},... | collective-permute-start | bytes 786440 | tf_op jit(solution)/shard_map/ppermute | solution.py:315
  58.9 13.6 %collective-permute-start.18 = (f32[6,64,128]{2,1,0:T(8,128)S(1)}, f32[6,64,128]{2,1,0:T(8,128)S(1)}, u32[]{:S(2)}, u32[]{:S(2)}) collective-permute-start(f32[6,64,128]{2,1,0:T(8,128)S(1)} %get-tuple-element.60), channel_id=1, source_target_pairs={{0,1},{1,0},{2,3},{3,2},{4,5},{5,4},{6,7},{7,6},{8,9},{9,8},{10,11... | collective-permute-start | bytes 589832 | tf_op jit(solution)/shard_map/ppermute | solution.py:306
  59.0 6.8 %collective-permute-start.5 = (s32[4,64]{1,0:T(4,128)S(1)}, s32[4,64]{1,0:T(4,128)S(1)}, u32[]{:S(2)}, u32[]{:S(2)}) collective-permute-start(s32[4,64]{1,0:T(4,128)S(1)} %pad_add_fusion.metas), channel_id=1, source_target_pairs={{4,0},{6,2},{8,4},{9,1},{10,6},{11,3},{12,8},{13,5},{14,10},{15,7}... | collective-permute-start | bytes 3080 | tf_op jit(solution)/shard_map/ppermute | solution.py:315
  65.9 5.5 %collective-permute-start.4 = (s32[4,64]{1,0:T(4,128)S(1)}, s32[4,64]{1,0:T(4,128)S(1)}, u32[]{:S(2)}, u32[]{:S(2)}) collective-permute-start(s32[4,64]{1,0:T(4,128)S(1)} %pad_add_fusion.metas), channel_id=1, source_target_pairs={{0,4},{1,9},{2,6},{3,11},{4,8},{5,13},{6,10},{7,15},{8,12},{9,17},... | collective-permute-start | bytes 3080 | tf_op jit(solution)/shard_map/ppermute | solution.py:315
  72.4 3.4 %collective-permute-start.23 = (f32[6,64,128]{2,1,0:T(8,128)S(1)}, f32[6,64,128]{2,1,0:T(8,128)S(1)}, u32[]{:S(2)}, u32[]{:S(2)}) collective-permute-start(f32[6,64,128]{2,1,0:T(8,128)S(1)} %get-tuple-element.65), channel_id=1, source_target_pairs={{0,1},{1,0},{2,3},{3,2},{4,5},{5,4},{6,7},{7,6},{8,9},{9,8},{10,11... | collective-permute-start | bytes 589832 | tf_op jit(solution)/shard_map/ppermute | solution.py:306
  72.6 7.8 %collective-permute-start.19 = (f32[6,64,128]{2,1,0:T(8,128)S(1)}, f32[6,64,128]{2,1,0:T(8,128)S(1)}, u32[]{:S(2)}, u32[]{:S(2)}) collective-permute-start(f32[6,64,128]{2,1,0:T(8,128)S(1)} %add.46), channel_id=1, source_target_pairs={{0,2},{1,3},{2,0},{3,1},{4,6},{5,7},{6,4},{7,5},{8,10},{9,11},{10,... | collective-permute-start | bytes 589832 | tf_op jit(solution)/shard_map/ppermute | solution.py:306
  75.9 8.2 %collective-permute-start.24 = (f32[6,64,128]{2,1,0:T(8,128)S(1)}, f32[6,64,128]{2,1,0:T(8,128)S(1)}, u32[]{:S(2)}, u32[]{:S(2)}) collective-permute-start(f32[6,64,128]{2,1,0:T(8,128)S(1)} %add.48), channel_id=1, source_target_pairs={{0,2},{1,3},{2,0},{3,1},{4,6},{5,7},{6,4},{7,5},{8,10},{9,11},{10,... | collective-permute-start | bytes 589832 | tf_op jit(solution)/shard_map/ppermute | solution.py:306
  84.2 3.2 %copy-start.2 = (f32[12,32,128]{2,1,0:T(8,128)S(1)}, f32[12,32,128]{2,1,0:T(8,128)}, u32[]{:S(2)}) copy-start(f32[12,32,128]{2,1,0:T(8,128)} %base.1) | copy-start | bytes 589828
  85.5 1.8 %collective-permute-start.25 = (f32[6,128,128]{2,1,0:T(8,128)S(1)}, f32[6,128,128]{2,1,0:T(8,128)S(1)}, u32[]{:S(2)}, u32[]{:S(2)}) collective-permute-start(f32[6,128,128]{2,1,0:T(8,128)S(1)} %shard_map.96), channel_id=1, source_target_pairs={{0,1},{1,0},{2,3},{3,2},{4,5},{5,4},{6,7},{7,6},{8,9},{9,8},{10,11... | collective-permute-start | bytes 1179656 | tf_op jit(solution)/shard_map/ppermute | solution.py:306
  85.6 20.0 %collective-permute-start.26 = (f32[12,128,128]{2,1,0:T(8,128)S(1)}, f32[12,128,128]{2,1,0:T(8,128)S(1)}, u32[]{:S(2)}, u32[]{:S(2)}) collective-permute-start(f32[12,128,128]{2,1,0:T(8,128)S(1)} %get-tuple-element.56.upper.refs_0_), channel_id=1, source_target_pairs={{0,2},{1,3},{2,0},{3,1},{4,6},{5,7},{6,4},{7,5},{8,10},{9,11},{10,... | collective-permute-start | bytes 2359304 | tf_op jit(solution)/shard_map/ppermute | solution.py:306
  87.7 7.0 %collective-permute-start.27 = (f32[12,16,128]{2,1,0:T(8,128)S(1)}, f32[12,16,128]{2,1,0:T(8,128)S(1)}, u32[]{:S(2)}, u32[]{:S(2)}) collective-permute-start(f32[12,16,128]{2,1,0:T(8,128)S(1)} %shard_map.97.x), channel_id=1, source_target_pairs={{0,4},{1,9},{2,6},{3,11},{4,8},{5,13},{6,10},{7,15},{8,12},{9,17},... | collective-permute-start | bytes 294920 | tf_op jit(solution)/shard_map/ppermute | solution.py:315
  95.3 1.4 collective-permute-start.28
  96.7 7.4 %collective-permute-start.29 = (f32[12,16,128]{2,1,0:T(8,128)S(1)}, f32[12,16,128]{2,1,0:T(8,128)S(1)}, u32[]{:S(2)}, u32[]{:S(2)}) collective-permute-start(f32[12,16,128]{2,1,0:T(8,128)S(1)} %add_subtract_fusion.5.x), channel_id=1, source_target_pairs={{0,4},{1,9},{2,6},{3,11},{4,8},{5,13},{6,10},{7,15},{8,12},{9,17},... | collective-permute-start | bytes 294920 | tf_op jit(solution)/shard_map/ppermute | solution.py:315
  104.6 1.4 collective-permute-start.30
  105.6 14.5 %collective-permute-start.33 = (f32[12,128,128]{2,1,0:T(8,128)S(1)}, f32[12,128,128]{2,1,0:T(8,128)S(1)}, u32[]{:S(2)}, u32[]{:S(2)}) collective-permute-start(f32[12,128,128]{2,1,0:T(8,128)S(1)} %collective-permute-done.26.refs_0_.refs_2_), channel_id=1, source_target_pairs={{0,1},{1,0},{2,3},{3,2},{4,5},{5,4},{6,7},{7,6},{8,9},{9,8},{10,11... | collective-permute-start | bytes 2359304 | tf_op jit(solution)/shard_map/ppermute | solution.py:306
  105.9 7.4 %collective-permute-start.31 = (f32[12,16,128]{2,1,0:T(8,128)S(1)}, f32[12,16,128]{2,1,0:T(8,128)S(1)}, u32[]{:S(2)}, u32[]{:S(2)}) collective-permute-start(f32[12,16,128]{2,1,0:T(8,128)S(1)} %add_subtract_fusion.4.x), channel_id=1, source_target_pairs={{0,4},{1,9},{2,6},{3,11},{4,8},{5,13},{6,10},{7,15},{8,12},{9,17},... | collective-permute-start | bytes 294920 | tf_op jit(solution)/shard_map/ppermute | solution.py:315
  113.8 1.4 collective-permute-start.32
  115.2 8.8 %collective-permute-start.34 = (f32[12,16,128]{2,1,0:T(8,128)S(1)}, f32[12,16,128]{2,1,0:T(8,128)S(1)}, u32[]{:S(2)}, u32[]{:S(2)}) collective-permute-start(f32[12,16,128]{2,1,0:T(8,128)S(1)} %add_subtract_fusion.3.x), channel_id=1, source_target_pairs={{4,0},{6,2},{8,4},{9,1},{10,6},{11,3},{12,8},{13,5},{14,10},{15,7}... | collective-permute-start | bytes 294920 | tf_op jit(solution)/shard_map/ppermute | solution.py:315
  124.6 1.4 collective-permute-start.35
  125.9 7.4 %collective-permute-start.36 = (f32[12,16,128]{2,1,0:T(8,128)S(1)}, f32[12,16,128]{2,1,0:T(8,128)S(1)}, u32[]{:S(2)}, u32[]{:S(2)}) collective-permute-start(f32[12,16,128]{2,1,0:T(8,128)S(1)} %add_subtract_fusion.2.x), channel_id=1, source_target_pairs={{4,0},{6,2},{8,4},{9,1},{10,6},{11,3},{12,8},{13,5},{14,10},{15,7}... | collective-permute-start | bytes 294920 | tf_op jit(solution)/shard_map/ppermute | solution.py:315
  133.8 1.4 collective-permute-start.37
  135.2 7.4 %collective-permute-start.38 = (f32[12,16,128]{2,1,0:T(8,128)S(1)}, f32[12,16,128]{2,1,0:T(8,128)S(1)}, u32[]{:S(2)}, u32[]{:S(2)}) collective-permute-start(f32[12,16,128]{2,1,0:T(8,128)S(1)} %add_subtract_fusion.1.x), channel_id=1, source_target_pairs={{4,0},{6,2},{8,4},{9,1},{10,6},{11,3},{12,8},{13,5},{14,10},{15,7}... | collective-permute-start | bytes 294920 | tf_op jit(solution)/shard_map/ppermute | solution.py:315
  143.1 1.4 collective-permute-start.39
  144.5 4.9 %collective-permute-start.40 = (f32[12,16,128]{2,1,0:T(8,128)S(1)}, f32[12,16,128]{2,1,0:T(8,128)S(1)}, u32[]{:S(2)}, u32[]{:S(2)}) collective-permute-start(f32[12,16,128]{2,1,0:T(8,128)S(1)} %add_subtract_fusion), channel_id=1, source_target_pairs={{0,2},{1,3},{2,0},{3,1},{4,6},{5,7},{6,4},{7,5},{8,10},{9,11},{10,... | collective-permute-start | bytes 294920 | tf_op jit(solution)/shard_map/ppermute | solution.py:306

commit v6 on v4

--- a/solution.py
+++ b/solution.py
@@ -51,7 +51,7 @@
         self.pairs = max(1, (self.slots - 4 * cap) // 2)
         self.listed_slots = n_tile * cap
         self.local_slots = n_tile // 2 * self.pairs
-        self.table = 2 * (self.listed_slots + self.local_slots)
+        self.table = self.listed_slots + 2 * self.local_slots
 
     def kind(self, meta, s):
         return meta[s]
@@ -91,13 +91,13 @@
     return pl.BlockSpec(memory_space=pltpu.VMEM)
 
 
-def call(body, outs, scalars, arrays, flops=0, scratch=(), early=(), to_smem=False):
+def call(body, outs, scalars, arrays, flops=0, scratch=(), early=(), to_smem=0):
     moved = sum(a.size * a.dtype.itemsize for a in arrays) + sum(o.size * o.dtype.itemsize for o in outs)
     return pl.pallas_call(
         body if not early else lambda *refs: body(*refs[len(early) :]),
         out_shape=outs,
         in_specs=[pl.BlockSpec(memory_space=pl.ANY)] * len(early) + [smem()] * len(scalars) + [vmem()] * len(arrays),
-        out_specs=[smem() if to_smem else vmem()] * len(outs),
+        out_specs=[smem()] * to_smem + [vmem()] * (len(outs) - to_smem),
         scratch_shapes=list(scratch),
         compiler_params=pltpu.CompilerParams(vmem_limit_bytes=8 << 20),
         cost_estimate=pl.CostEstimate(flops=flops, bytes_accessed=moved, transcendentals=0),
@@ -111,7 +111,8 @@
             out[which * lay.cap + j] = jnp.where(live, tiles[s], 0.0)
 
 
-def outgoing_kernel(lay, me, mine, mates, inverse, tiles, mate_tiles, out, lower):
+def outgoing_kernel(lay, near, inverse, tiles, mate_tiles, out, lower):
+    me, mine, mates = near.at[0], near.at[1], near.at[2]
     role = me[0] % 2
     for g, (meta, source) in enumerate(((mine, tiles), (mates, mate_tiles))):
         for j in range(lay.cap):
@@ -121,7 +122,8 @@
     listed_tiles(lay, mine, 1, tiles, lower)
 
 
-def next_outgoing_kernel(lay, me, mine, mates, inverse, upper, mate_upper, out):
+def next_outgoing_kernel(lay, near, inverse, upper, mate_upper, out):
+    me, mine, mates = near.at[0], near.at[1], near.at[2]
     role = me[0] % 2
     for g, (meta, source) in enumerate(((mine, upper), (mates, mate_upper))):
         for j in range(lay.cap):
@@ -143,8 +145,9 @@
 
 
 def local_pivot_kernel(
-    lay, me, mine, mates, inverse, diag, tiles, mate_tiles, out, mate_lower, lower_local, upper, mate_upper, places
+    lay, near, inverse, diag, tiles, mate_tiles, out, mate_lower, lower_local, upper, mate_upper, places
 ):
+    me, mine, mates = near.at[0], near.at[1], near.at[2]
     local_terms(lay, me, mine, inverse, diag, tiles, out)
     listed_tiles(lay, mates, 1, mate_tiles, mate_lower)
     listed_tiles(lay, mates, 2, mate_tiles, mate_upper)
@@ -156,11 +159,12 @@
             target[start + i] = jnp.where(live, tiles[jnp.where(live, places[i], 0)], 0.0)
 
 
-def next_local_pivot_kernel(lay, me, mine, inverse, diag, tiles, out):
-    local_terms(lay, me, mine, inverse, diag, tiles, out)
-
-
-def incoming_kernel(lay, me, mine, mates, local, lower, mate_lower, arrived, keep, give, total):
+def next_local_pivot_kernel(lay, near, inverse, diag, tiles, out):
+    local_terms(lay, near.at[0], near.at[1], inverse, diag, tiles, out)
+
+
+def incoming_kernel(lay, near, local, lower, mate_lower, arrived, keep, give, total):
+    me, mine, mates = near.at[0], near.at[1], near.at[2]
     role = me[0] % 2
     places, terms = [], []
     for g, (meta, source) in enumerate(((mine, lower), (mates, mate_lower))):
@@ -184,8 +188,11 @@
         out[i] = 2.0 * x + matmul_parts(*split(product), xh, xl)
 
 
-def table_kernel(lay, me, metas, peers_below, peers_above, out, places):
+def table_kernel(lay, me, metas, peers_below, peers_above, out, *refs):
+    masks, places = refs[:4], refs[4]
     role = me[0] % 2
+    out[2 * lay.table] = me[0]
+    row = lax.broadcasted_iota(jnp.int32, masks[0].shape[1:], 0)
     for side in (1, 2):
         start = (side - 1) * lay.table
         base, peers = ((2, peers_below), (0, peers_above))[side - 1]
@@ -193,12 +200,13 @@
             a, meta, peer = q ^ me[0], metas.at[q], peers.at[q]
             for j in range(lay.cap):
                 s, _, v = lay.lookup(meta, base + role, side, j)
-                k = start + a * lay.cap + j
-                out[k] = s // lay.width
-                out[lay.listed_slots + k] = lay.listed(peer, 2 - base + role, v) // lay.width
+                out[start + a * lay.cap + j] = s // lay.width
+                source = lay.listed(peer, 2 - base + role, v) // lay.width
+                masks[2 * side - 2][a * lay.cap + j] = (row == s // lay.width).astype(F32)
+                masks[2 * side - 1][a * lay.cap + j] = (row == source).astype(F32)
         for q in range(0, lay.n_tile, 2):
             meta = metas.at[q]
-            begin = start + 2 * lay.listed_slots + ((q ^ me[0]) >> 1) * lay.pairs
+            begin = start + lay.listed_slots + ((q ^ me[0]) >> 1) * lay.pairs
             count = lay.scan(meta, side, places)
             for i in range(lay.pairs):
                 s = jnp.where(i < count, places[i], 0)
@@ -207,27 +215,28 @@
                 out[begin + lay.local_slots + i] = v // lay.width
 
 
-def scaled_kernel(lay, side, me, table, inverse, *refs):
+def scaled_kernel(lay, side, table, inverse, *refs):
     sources, (listed, local) = refs[:-2], refs[-2:]
-    role = me[0] % 2
+    me = table[2 * lay.table]
+    role = me % 2
     start = (side - 1) * lay.table
 
     def scaled(row, tile):
-        return widen(matmul(inverse[lay.place(row, me[0])], tile))
+        return widen(matmul(inverse[lay.place(row, me)], tile))
 
     at = 0
     for q in range(lay.n_tile):
         lists = sources[at]
         for j in range(lay.cap):
-            k = (q ^ me[0]) * lay.cap + j
+            k = (q ^ me) * lay.cap + j
             listed[k] = scaled(table[start + k], lists[role * lay.cap + j])
         at += 1
         if q % 2 == 0:
             pairs, first = (lists, 2 * lay.cap) if side == 2 else (sources[at], 0)
             at += side == 1
             for i in range(lay.pairs):
-                k = ((q ^ me[0]) >> 1) * lay.pairs + i
-                local[k] = scaled(table[start + 2 * lay.listed_slots + k], pairs[first + i])
+                k = ((q ^ me) >> 1) * lay.pairs + i
+                local[k] = scaled(table[start + lay.listed_slots + k], pairs[first + i])
 
 
 def first_kernel(lay, me, base, inverse, out):
@@ -238,19 +247,21 @@
 
 
 def local_sum_kernel(lay, side, table, x, tiles, out):
-    start = (side - 1) * lay.table + 2 * lay.listed_slots
+    start = (side - 1) * lay.table + lay.listed_slots
     terms = [times_tile(x[table[start + lay.local_slots + k]], tiles[k]) for k in range(lay.local_slots)]
     out[...] = jnp.zeros_like(out)
     for k, value in enumerate(terms):
         out[table[start + k]] += value
 
 
-def listed_sum_kernel(lay, side, table, local, tiles, arrived, out):
-    start = (side - 1) * lay.table
-    terms = [times_tile(arrived[table[start + lay.listed_slots + k]], tiles[k]) for k in range(lay.listed_slots)]
-    out[...] = local[...]
-    for k, value in enumerate(terms):
-        out[table[start + k]] += value
+def listed_sum_kernel(lay, tiles, picks, sources, local, arrived, out):
+    rows = [arrived[r] for r in range(lay.rows)]
+    terms = []
+    for k in range(lay.listed_slots):
+        x = sum(sources[k, r : r + 1] * rows[r] for r in range(lay.rows))
+        terms.append(times_tile(x, tiles[k]))
+    for r in range(lay.rows):
+        out[r] = local[r] + sum(picks[k, r : r + 1] * terms[k] for k in range(lay.listed_slots))
 
 
 def local(krylov_block, diag_block, inverse_prev, coupling_tiles, slot_kind, slot_link, send_slots):
@@ -299,11 +310,9 @@
 
     mate_tiles = swap(tiles, 1)
     arriving = over_chips(inverse_prev)
-    held = over_chips(mine)
-    both = [swap(x, 1) for x in held]
-    arriving, held, both = lax.optimization_barrier((arriving, held, both))
-    mates = both[0]
-    metas = jnp.stack([one for pair in zip(held, both) for one in pair])
+    mates = swap(mine, 1)
+    arriving, mine, mates = lax.optimization_barrier((arriving, mine, mates))
+    near = jnp.stack([jnp.broadcast_to(me, mine.shape), mine, mates])
     kept = jnp.concatenate(arriving, 0)
     mated = jnp.concatenate([swap(x, 1) for x in arriving], 0)
     half = rows // 2
@@ -314,28 +323,30 @@
         early, later = [], []
         if sweep == 0:
             out, lower = call(
-                kernel(outgoing_kernel), [lists] * 2, (me, mine, mates), (inverse, tiles, mate_tiles)
+                kernel(outgoing_kernel), [lists] * 2, (near,), (inverse, tiles, mate_tiles)
             )
             arrived = along(out, 1)
             lowers = over_chips(lower)
             here, mate_lower, lower_local, upper, mate_upper = call(
                 kernel(local_pivot_kernel),
                 [shape(rows, n, n), lists, local_list, shape(2 * cap + lay.pairs, n, n), lists],
-                (me, mine, mates),
+                (near,),
                 (inverse, diag_block, tiles, mate_tiles),
                 flops=product * rows,
                 scratch=(places,),
             )
             early += lowers[1:]
+            metas = jnp.concatenate(over_chips(near[1:]), 0)
+            later += [metas]
         else:
             (out,) = call(
-                kernel(next_outgoing_kernel), [lists], (me, mine, mates), (inverse, upper, mate_upper)
+                kernel(next_outgoing_kernel), [lists], (near,), (inverse, upper, mate_upper)
             )
             arrived = along(out, 1)
             (here,) = call(
                 kernel(next_local_pivot_kernel),
                 [shape(rows, n, n)],
-                (me, mine),
+                (near,),
                 (inverse, diag_block, tiles),
                 flops=product * rows,
             )
@@ -343,20 +354,21 @@
             lower_locals = over_chips(lower_local)
             mate_lowers = [mate_lower] + [swap(x, 1) for x in lowers[1:]]
             below, above = along(metas, 1), along(metas, -1)
-            (table,) = call(
+            mask = shape(lay.listed_slots, rows, n)
+            table, *masks = call(
                 kernel(table_kernel),
-                [shape(2 * lay.table, dtype=jnp.int32)],
+                [shape(2 * lay.table + 1, dtype=jnp.int32)] + [mask] * 4,
                 (me, metas, below, above),
                 (),
                 scratch=(places,),
-                to_smem=True,
+                to_smem=1,
             )
             early += [*lower_locals[1:], *mate_lowers[1:], below, above]
             later += [table]
         keep, give = call(
             kernel(incoming_kernel),
             [shape(half, n, n)] * 2,
-            (me, mine, mates),
+            (near,),
             (here, lower, mate_lower, arrived),
             scratch=(pltpu.VMEM((rows, n, n), F32),),
             early=early,
@@ -373,7 +385,7 @@
                 shape(lay.listed_slots, 2 * n, n, dtype=BF16),
                 shape(lay.local_slots, 2 * n, n, dtype=BF16),
             ],
-            (me, table),
+            (table,),
             (inverse, *sources),
             flops=product * 24,
         )
@@ -390,10 +402,10 @@
                 kernel(local_sum_kernel, side), [block], (table,), (x, local), flops=8 * n**2 * vectors * rows
             )
             (part,) = call(
-                kernel(listed_sum_kernel, side),
+                kernel(listed_sum_kernel),
                 [block],
-                (table,),
-                (here, listed, arrived),
+                (),
+                (listed, *masks[2 * side - 2 : 2 * side], here, arrived),
                 early=early if sweep == count - 1 else (),
             )
             x = base - (part + swap(part, 1))

time: 145 us -> 141 us (0.972)
  Pallas kernels: 25.6 us -> 22.1 us
    pallas_call x24, Pallas kernels: 25.6 us -> 22.1 us  [call(): pl.pallas_call(body if not early else lambda *refs: body(*refs[len(early)...]
    ppermute x25 -> x24, waiting for transfers between devices: 38.6 us -> 37.5 us  [swap(): return lax.ppermute(x, 'tile', [(i, i ^ bit) for i in range(n_tile)])]
    ppermute x25 -> x24, starting transfers between devices: 14.6 us -> 14.8 us  [swap(): return lax.ppermute(x, 'tile', [(i, i ^ bit) for i in range(n_tile)])]
  transfers between devices with their start and end apart: 35 -> 34, of which waited for: 26 -> 26; matrix products, arithmetic and copies ran while one was open for 3% -> 3% of each run, Pallas kernels for 13% -> 12%
where the time goes in v6:
time: 141 us; the launch traced here: 140 us
  waiting for transfers between devices  58.9 us (42%)
  starting transfers between devices  51.8 us (37%)
  Pallas kernels  22.1 us (16%)
  local copies, waits for them, and re-layouts  4.22 us (3%)
    ppermute x24, waiting for transfers between devices, swap(): return lax.ppermute(x, 'tile', [(i, i ^ bit) for i in range(n_tile)])  37.5 us
    ppermute x10, starting transfers between devices, along(): return lax.ppermute(x, ('dom', 'tile'), route)  37 us
    pallas_call x24, Pallas kernels, call(): pl.pallas_call(body if not early else lambda *refs: body(*refs[len(early)...  22.1 us
    ppermute x10, waiting for transfers between devices, along(): return lax.ppermute(x, ('dom', 'tile'), route)  21.4 us
    ppermute x24, starting transfers between devices, swap(): return lax.ppermute(x, 'tile', [(i, i ^ bit) for i in range(n_tile)])  14.8 us
  transfers between devices with their start and end apart: 34, of which 26 were waited for; matrix products, arithmetic and copies ran while one was open for 3% of the time, Pallas kernels for 12%

profile of v6, /device:TPU:18, one launch (start us, length us, event | category | flops | bytes accessed | tf_op | source)
XLA Modules:
  0.0 139.6 jit_solution(14442403107970822917)
XLA Ops:
  0.7 1.6 %collective-permute-start = (f32[3,128,128]{2,1,0:T(8,128)}, f32[3,128,128]{2,1,0:T(8,128)S(1)}, u32[]{:S(2)}, u32[]{:S(2)}) collective-permute-start(f32[3,128,128]{2,1,0:T(8,128)} %param.9), channel_id=1, source_target_pairs={{0,2},{1,3},{2,0},{3,1},{4,6},{5,7},{6,4},{7,5},{8,10},{9,11},{10,... | collective-permute-start | bytes 589832 | tf_op jit(solution)/shard_map/ppermute | solution.py:280
  5.0 1.0 collective-permute-done.1
  6.0 2.3 %collective-permute-done = f32[3,128,128]{2,1,0:T(8,128)S(1)} collective-permute-done((f32[3,128,128]{2,1,0:T(8,128)}, f32[3,128,128]{2,1,0:T(8,128)S(1)}, u32[]{:S(2)}, u32[]{:S(2)}) %collective-permute-start) | collective-permute-done | bytes 196640 | tf_op jit(solution)/shard_map/ppermute | solution.py:280
  8.8 0.9 constant_dynamic-update-slice_fusion.3
  10.2 0.9 shard_map.87
  11.2 3.5 %collective-permute-start.9 = (f32[8,128,128]{2,1,0:T(8,128)S(1)}, f32[8,128,128]{2,1,0:T(8,128)S(1)}, u32[]{:S(2)}, u32[]{:S(2)}) collective-permute-start(f32[8,128,128]{2,1,0:T(8,128)S(1)} %get-tuple-element.34), channel_id=1, source_target_pairs={{0,4},{1,9},{2,6},{3,11},{4,8},{5,13},{6,10},{7,15},{8,12},{9,17},... | collective-permute-start | bytes 1572872 | tf_op jit(solution)/shard_map/ppermute | solution.py:289
  14.6 1.6 %collective-permute-start.8 = (f32[8,128,128]{2,1,0:T(8,128)S(1)}, f32[8,128,128]{2,1,0:T(8,128)S(1)}, u32[]{:S(2)}, u32[]{:S(2)}) collective-permute-start(f32[8,128,128]{2,1,0:T(8,128)S(1)} %get-tuple-element.31.refs_3_.refs_6_.refs_0_), channel_id=1, source_target_pairs={{0,2},{1,3},{2,0},{3,1},{4,6},{5,7},{6,4},{7,5},{8,10},{9,11},{10,... | collective-permute-start | bytes 1572872 | tf_op jit(solution)/shard_map/ppermute | solution.py:280
  16.2 2.4 %shard_map.88 = (f32[12,128,128]{2,1,0:T(8,128)S(1)}, f32[8,128,128]{2,1,0:T(8,128)S(1)}, f32[4,128,128]{2,1,0:T(8,128)S(1)}, f32[12,128,128]{2,1,0:T(8,128)S(1)}, f32[8,128,128]{2,1,0:T(8,128)S(1)}) custom-call(s32[3,64]{1,0:T(4,128)S(1)} %pad_add_fusion.1.near.refs_1_.refs_4_, f32[12,128,128]{2,1,0:T(8,128)S(1)} %constant_dynamic-update-slice_fusion.inverse, ...), custom_call_target="tpu_custom_call" | custom-call | flops 201326592 | bytes 7012352 | tf_op jit(solution)/shard_map/pallas_call | solution.py:96
  18.7 7.5 %collective-permute-done.9.refs_5_ = f32[8,128,128]{2,1,0:T(8,128)S(1)} collective-permute-done((f32[8,128,128]{2,1,0:T(8,128)S(1)}, f32[8,128,128]{2,1,0:T(8,128)S(1)}, u32[]{:S(2)}, u32[]{:S(2)}) %collective-permute-start.9) | collective-permute-done | bytes 524320 | tf_op jit(solution)/shard_map/ppermute | solution.py:289
  26.1 2.3 %collective-permute-done.8.refs_0_.refs_3_ = f32[8,128,128]{2,1,0:T(8,128)S(1)} collective-permute-done((f32[8,128,128]{2,1,0:T(8,128)S(1)}, f32[8,128,128]{2,1,0:T(8,128)S(1)}, u32[]{:S(2)}, u32[]{:S(2)}) %collective-permute-start.8) | collective-permute-done | bytes 524320 | tf_op jit(solution)/shard_map/ppermute | solution.py:280
  28.4 1.1 shard_map.89
  29.6 1.7 %collective-permute-done.10 = f32[6,128,128]{2,1,0:T(8,128)S(1)} collective-permute-done((f32[6,128,128]{2,1,0:T(8,128)S(1)}, f32[6,128,128]{2,1,0:T(8,128)S(1)}, u32[]{:S(2)}, u32[]{:S(2)}) %collective-permute-start.10) | collective-permute-done | bytes 393248 | tf_op jit(solution)/shard_map/ppermute | solution.py:280
  31.3 1.6 %collective-permute-start.11 = (f32[6,128,128]{2,1,0:T(8,128)S(1)}, f32[6,128,128]{2,1,0:T(8,128)S(1)}, u32[]{:S(2)}, u32[]{:S(2)}) collective-permute-start(f32[6,128,128]{2,1,0:T(8,128)S(1)} %add.30), channel_id=1, source_target_pairs={{0,2},{1,3},{2,0},{3,1},{4,6},{5,7},{6,4},{7,5},{8,10},{9,11},{10,... | collective-permute-start | bytes 1179656 | tf_op jit(solution)/shard_map/ppermute | solution.py:280
  33.5 9.1 %collective-permute-done.2 = s32[2,64]{1,0:T(2,128)S(1)} collective-permute-done((s32[2,64]{1,0:T(2,128)S(1)}, s32[2,64]{1,0:T(2,128)S(1)}, u32[]{:S(2)}, u32[]{:S(2)}) %collective-permute-start.2) | collective-permute-done | bytes 544 | tf_op jit(solution)/shard_map/ppermute | solution.py:280
  43.8 1.2 collective-permute-done.14
  45.1 0.9 shard_map.92
  46.0 3.0 %collective-permute-start.15 = (f32[8,128,128]{2,1,0:T(8,128)S(1)}, f32[8,128,128]{2,1,0:T(8,128)S(1)}, u32[]{:S(2)}, u32[]{:S(2)}) collective-permute-start(f32[8,128,128]{2,1,0:T(8,128)S(1)} %shard_map.92), channel_id=1, source_target_pairs={{0,4},{1,9},{2,6},{3,11},{4,8},{5,13},{6,10},{7,15},{8,12},{9,17},... | collective-permute-start | bytes 1572872 | tf_op jit(solution)/shard_map/ppermute | solution.py:289
  49.0 1.6 %collective-permute-start.12 = (f32[4,128,128]{2,1,0:T(8,128)S(1)}, f32[4,128,128]{2,1,0:T(8,128)S(1)}, u32[]{:S(2)}, u32[]{:S(2)}) collective-permute-start(f32[4,128,128]{2,1,0:T(8,128)S(1)} %get-tuple-element.37.refs_1_), channel_id=1, source_target_pairs={{0,2},{1,3},{2,0},{3,1},{4,6},{5,7},{6,4},{7,5},{8,10},{9,11},{10,... | collective-permute-start | bytes 786440 | tf_op jit(solution)/shard_map/ppermute | solution.py:280
  50.6 2.8 %collective-permute-start.4 = (s32[4,64]{1,0:T(4,128)S(1)}, s32[4,64]{1,0:T(4,128)S(1)}, u32[]{:S(2)}, u32[]{:S(2)}) collective-permute-start(s32[4,64]{1,0:T(4,128)S(1)} %pad_add_fusion.metas.refs_0_), channel_id=1, source_target_pairs={{4,0},{6,2},{8,4},{9,1},{10,6},{11,3},{12,8},{13,5},{14,10},{15,7}... | collective-permute-start | bytes 3080 | tf_op jit(solution)/shard_map/ppermute | solution.py:289
  53.4 3.9 %collective-permute-start.3 = (s32[4,64]{1,0:T(4,128)S(1)}, s32[4,64]{1,0:T(4,128)S(1)}, u32[]{:S(2)}, u32[]{:S(2)}) collective-permute-start(s32[4,64]{1,0:T(4,128)S(1)} %pad_add_fusion.metas.refs_0_), channel_id=1, source_target_pairs={{0,4},{1,9},{2,6},{3,11},{4,8},{5,13},{6,10},{7,15},{8,12},{9,17},... | collective-permute-start | bytes 3080 | tf_op jit(solution)/shard_map/ppermute | solution.py:289
  57.3 2.0 %shard_map.91.refs_5_ = f32[12,128,128]{2,1,0:T(8,128)S(1)} custom-call(s32[3,64]{1,0:T(4,128)S(1)} %pad_add_fusion.1.near.refs_1_.refs_4_, f32[12,128,128]{2,1,0:T(8,128)S(1)} %pad_maximum_fusion.inverse, f32[3,128,128]{2,1,0:T(8,128)S(1)} %copy-done.1, f32[24,128,128]{2,1,0:T(8,128)S(1)} %bitcast.14), custom_call_target="tpu_custom_call" | custom-call | flops 201326592 | bytes 3342336 | tf_op jit(solution)/shard_map/pallas_call | solution.py:96
  59.7 1.1 shard_map.93
  60.8 1.3 collective-permute-start.16
  62.1 1.3 collective-permute-done.16
  63.5 1.6 %collective-permute-start.17 = (f32[6,128,128]{2,1,0:T(8,128)S(1)}, f32[6,128,128]{2,1,0:T(8,128)S(1)}, u32[]{:S(2)}, u32[]{:S(2)}) collective-permute-start(f32[6,128,128]{2,1,0:T(8,128)S(1)} %add.32), channel_id=1, source_target_pairs={{0,2},{1,3},{2,0},{3,1},{4,6},{5,7},{6,4},{7,5},{8,10},{9,11},{10,... | collective-permute-start | bytes 1179656 | tf_op jit(solution)/shard_map/ppermute | solution.py:280
  65.1 2.1 %shard_map.86 = (s32[65]{0:T(128)S(1)}, f32[16,12,128]{2,1,0:T(8,128)S(1)}, f32[16,12,128]{2,1,0:T(8,128)S(1)}, f32[16,12,128]{2,1,0:T(8,128)S(1)}, f32[16,12,128]{2,1,0:T(8,128)S(1)}) custom-call(s32[1]{0:T(128)} %bitcast.me, s32[4,64]{1,0:T(4,128)S(1)} %pad_add_fusion.metas.refs_0_, s32[4,64]{1,0:T(4,128)S(1)} %collective-permute-done.3.peers_below.refs_2_, ...), custom_call_target="tpu_custom_call" | custom-call | bytes 393476 | tf_op jit(solution)/shard_map/pallas_call | solution.py:96
  67.2 7.7 %collective-permute-done.17 = f32[6,128,128]{2,1,0:T(8,128)S(1)} collective-permute-done((f32[6,128,128]{2,1,0:T(8,128)S(1)}, f32[6,128,128]{2,1,0:T(8,128)S(1)}, u32[]{:S(2)}, u32[]{:S(2)}) %collective-permute-start.17) | collective-permute-done | bytes 393248 | tf_op jit(solution)/shard_map/ppermute | solution.py:280
  75.6 1.6 %collective-permute-start.19 = (f32[12,128,128]{2,1,0:T(8,128)S(1)}, f32[12,128,128]{2,1,0:T(8,128)S(1)}, u32[]{:S(2)}, u32[]{:S(2)}) collective-permute-start(f32[12,128,128]{2,1,0:T(8,128)S(1)} %get-tuple-element.38.upper.refs_0_), channel_id=1, source_target_pairs={{0,2},{1,3},{2,0},{3,1},{4,6},{5,7},{6,4},{7,5},{8,10},{9,11},{10,... | collective-permute-start | bytes 2359304 | tf_op jit(solution)/shard_map/ppermute | solution.py:280
  77.8 4.2 %collective-permute-start.20 = (f32[12,16,128]{2,1,0:T(8,128)S(1)}, f32[12,16,128]{2,1,0:T(8,128)S(1)}, u32[]{:S(2)}, u32[]{:S(2)}) collective-permute-start(f32[12,16,128]{2,1,0:T(8,128)S(1)} %shard_map.95.x), channel_id=1, source_target_pairs={{0,4},{1,9},{2,6},{3,11},{4,8},{5,13},{6,10},{7,15},{8,12},{9,17},... | collective-permute-start | bytes 294920 | tf_op jit(solution)/shard_map/ppermute | solution.py:289
  82.0 1.3 shard_map.96
  85.4 1.3 collective-permute-done.21
  86.7 4.5 %collective-permute-start.22 = (f32[12,16,128]{2,1,0:T(8,128)S(1)}, f32[12,16,128]{2,1,0:T(8,128)S(1)}, u32[]{:S(2)}, u32[]{:S(2)}) collective-permute-start(f32[12,16,128]{2,1,0:T(8,128)S(1)} %add_subtract_fusion.5.x), channel_id=1, source_target_pairs={{0,4},{1,9},{2,6},{3,11},{4,8},{5,13},{6,10},{7,15},{8,12},{9,17},... | collective-permute-start | bytes 294920 | tf_op jit(solution)/shard_map/ppermute | solution.py:289
  92.1 2.0 %collective-permute-done.22.arrived = f32[12,16,128]{2,1,0:T(8,128)S(1)} collective-permute-done((f32[12,16,128]{2,1,0:T(8,128)S(1)}, f32[12,16,128]{2,1,0:T(8,128)S(1)}, u32[]{:S(2)}, u32[]{:S(2)}) %collective-permute-start.22) | collective-permute-done | bytes 98336 | tf_op jit(solution)/shard_map/ppermute | solution.py:289
  96.0 4.6 %collective-permute-start.24 = (f32[12,16,128]{2,1,0:T(8,128)S(1)}, f32[12,16,128]{2,1,0:T(8,128)S(1)}, u32[]{:S(2)}, u32[]{:S(2)}) collective-permute-start(f32[12,16,128]{2,1,0:T(8,128)S(1)} %add_subtract_fusion.4.x), channel_id=1, source_target_pairs={{0,4},{1,9},{2,6},{3,11},{4,8},{5,13},{6,10},{7,15},{8,12},{9,17},... | collective-permute-start | bytes 294920 | tf_op jit(solution)/shard_map/ppermute | solution.py:289
  101.4 2.0 %collective-permute-done.24.refs_5_ = f32[12,16,128]{2,1,0:T(8,128)S(1)} collective-permute-done((f32[12,16,128]{2,1,0:T(8,128)S(1)}, f32[12,16,128]{2,1,0:T(8,128)S(1)}, u32[]{:S(2)}, u32[]{:S(2)}) %collective-permute-start.24) | collective-permute-done | bytes 98336 | tf_op jit(solution)/shard_map/ppermute | solution.py:289
  104.0 1.3 collective-permute-done.25
  105.3 4.8 %collective-permute-start.27 = (f32[12,16,128]{2,1,0:T(8,128)S(1)}, f32[12,16,128]{2,1,0:T(8,128)S(1)}, u32[]{:S(2)}, u32[]{:S(2)}) collective-permute-start(f32[12,16,128]{2,1,0:T(8,128)S(1)} %add_subtract_fusion.3.x), channel_id=1, source_target_pairs={{4,0},{6,2},{8,4},{9,1},{10,6},{11,3},{12,8},{13,5},{14,10},{15,7}... | collective-permute-start | bytes 294920 | tf_op jit(solution)/shard_map/ppermute | solution.py:289
  110.2 1.2 shard_map.103
  112.2 1.0 collective-permute-done.27.arrived
  113.8 1.3 collective-permute-done.28
  115.1 3.4 %collective-permute-start.29 = (f32[12,16,128]{2,1,0:T(8,128)S(1)}, f32[12,16,128]{2,1,0:T(8,128)S(1)}, u32[]{:S(2)}, u32[]{:S(2)}) collective-permute-start(f32[12,16,128]{2,1,0:T(8,128)S(1)} %add_subtract_fusion.2.x), channel_id=1, source_target_pairs={{4,0},{6,2},{8,4},{9,1},{10,6},{11,3},{12,8},{13,5},{14,10},{15,7}... | collective-permute-start | bytes 294920 | tf_op jit(solution)/shard_map/ppermute | solution.py:289
  119.4 3.4 %collective-permute-done.29.arrived = f32[12,16,128]{2,1,0:T(8,128)S(1)} collective-permute-done((f32[12,16,128]{2,1,0:T(8,128)S(1)}, f32[12,16,128]{2,1,0:T(8,128)S(1)}, u32[]{:S(2)}, u32[]{:S(2)}) %collective-permute-start.29) | collective-permute-done | bytes 98336 | tf_op jit(solution)/shard_map/ppermute | solution.py:289
  123.4 1.3 collective-permute-done.30
  124.7 2.2 %collective-permute-start.31 = (f32[12,16,128]{2,1,0:T(8,128)S(1)}, f32[12,16,128]{2,1,0:T(8,128)S(1)}, u32[]{:S(2)}, u32[]{:S(2)}) collective-permute-start(f32[12,16,128]{2,1,0:T(8,128)S(1)} %add_subtract_fusion.1.x), channel_id=1, source_target_pairs={{4,0},{6,2},{8,4},{9,1},{10,6},{11,3},{12,8},{13,5},{14,10},{15,7}... | collective-permute-start | bytes 294920 | tf_op jit(solution)/shard_map/ppermute | solution.py:289
  127.7 4.3 %collective-permute-done.31.arrived = f32[12,16,128]{2,1,0:T(8,128)S(1)} collective-permute-done((f32[12,16,128]{2,1,0:T(8,128)S(1)}, f32[12,16,128]{2,1,0:T(8,128)S(1)}, u32[]{:S(2)}, u32[]{:S(2)}) %collective-permute-start.31) | collective-permute-done | bytes 98336 | tf_op jit(solution)/shard_map/ppermute | solution.py:289
  132.7 1.3 collective-permute-done.32
  134.0 1.6 %collective-permute-start.33 = (f32[12,16,128]{2,1,0:T(8,128)S(1)}, f32[12,16,128]{2,1,0:T(8,128)S(1)}, u32[]{:S(2)}, u32[]{:S(2)}) collective-permute-start(f32[12,16,128]{2,1,0:T(8,128)S(1)} %add_subtract_fusion), channel_id=1, source_target_pairs={{0,2},{1,3},{2,0},{3,1},{4,6},{5,7},{6,4},{7,5},{8,10},{9,11},{10,... | collective-permute-start | bytes 294920 | tf_op jit(solution)/shard_map/ppermute | solution.py:280
  136.2 2.6 %collective-permute-done.33 = f32[12,16,128]{2,1,0:T(8,128)S(1)} collective-permute-done((f32[12,16,128]{2,1,0:T(8,128)S(1)}, f32[12,16,128]{2,1,0:T(8,128)S(1)}, u32[]{:S(2)}, u32[]{:S(2)}) %collective-permute-start.33) | collective-permute-done | bytes 98336 | tf_op jit(solution)/shard_map/ppermute | solution.py:280
  (85 shorter events, 18.9 us)
Async XLA Ops:
  0.6 9.6 %copy-start = (f32[12,2,128,128]{3,2,1,0:T(8,128)S(1)}, f32[12,2,128,128]{3,2,1,0:T(8,128)}, u32[]{:S(2)}) copy-start(f32[12,2,128,128]{3,2,1,0:T(8,128)} %param.10) | copy-start | bytes 4718596
  0.6 9.6 %collective-permute-start.7 = (f32[24,128,128]{2,1,0:T(8,128)}, f32[24,128,128]{2,1,0:T(8,128)S(1)}, u32[]{:S(2)}, u32[]{:S(2)}) collective-permute-start(f32[24,128,128]{2,1,0:T(8,128)} %bitcast.11), channel_id=1, source_target_pairs={{0,1},{1,0},{2,3},{3,2},{4,5},{5,4},{6,7},{7,6},{8,9},{9,8},{10,11... | collective-permute-start | bytes 4718600 | tf_op jit(solution)/shard_map/ppermute | solution.py:280
  0.7 7.5 %collective-permute-start = (f32[3,128,128]{2,1,0:T(8,128)}, f32[3,128,128]{2,1,0:T(8,128)S(1)}, u32[]{:S(2)}, u32[]{:S(2)}) collective-permute-start(f32[3,128,128]{2,1,0:T(8,128)} %param.9), channel_id=1, source_target_pairs={{0,2},{1,3},{2,0},{3,1},{4,6},{5,7},{6,4},{7,5},{8,10},{9,11},{10,... | collective-permute-start | bytes 589832 | tf_op jit(solution)/shard_map/ppermute | solution.py:280
  4.9 1.1 collective-permute-start.1
  8.2 1.9 %collective-permute-start.5 = (f32[3,128,128]{2,1,0:T(8,128)}, f32[3,128,128]{2,1,0:T(8,128)S(1)}, u32[]{:S(2)}, u32[]{:S(2)}) collective-permute-start(f32[3,128,128]{2,1,0:T(8,128)} %param.9), channel_id=1, source_target_pairs={{0,1},{1,0},{2,3},{3,2},{4,5},{5,4},{6,7},{7,6},{8,9},{9,8},{10,11... | collective-permute-start | bytes 589832 | tf_op jit(solution)/shard_map/ppermute | solution.py:280
  8.3 1.9 %collective-permute-start.6 = (f32[3,128,128]{2,1,0:T(8,128)S(1)}, f32[3,128,128]{2,1,0:T(8,128)S(1)}, u32[]{:S(2)}, u32[]{:S(2)}) collective-permute-start(f32[3,128,128]{2,1,0:T(8,128)S(1)} %collective-permute-done), channel_id=1, source_target_pairs={{0,1},{1,0},{2,3},{3,2},{4,5},{5,4},{6,7},{7,6},{8,9},{9,8},{10,11... | collective-permute-start | bytes 589832 | tf_op jit(solution)/shard_map/ppermute | solution.py:280
  10.2 6.0 %copy-start.1 = (f32[3,128,128]{2,1,0:T(8,128)S(1)}, f32[3,128,128]{2,1,0:T(8,128)}, u32[]{:S(2)}) copy-start(f32[3,128,128]{2,1,0:T(8,128)} %diag.3) | copy-start | bytes 589828
  11.2 15.0 %collective-permute-start.9 = (f32[8,128,128]{2,1,0:T(8,128)S(1)}, f32[8,128,128]{2,1,0:T(8,128)S(1)}, u32[]{:S(2)}, u32[]{:S(2)}) collective-permute-start(f32[8,128,128]{2,1,0:T(8,128)S(1)} %get-tuple-element.34), channel_id=1, source_target_pairs={{0,4},{1,9},{2,6},{3,11},{4,8},{5,13},{6,10},{7,15},{8,12},{9,17},... | collective-permute-start | bytes 1572872 | tf_op jit(solution)/shard_map/ppermute | solution.py:289
  14.6 13.8 %collective-permute-start.8 = (f32[8,128,128]{2,1,0:T(8,128)S(1)}, f32[8,128,128]{2,1,0:T(8,128)S(1)}, u32[]{:S(2)}, u32[]{:S(2)}) collective-permute-start(f32[8,128,128]{2,1,0:T(8,128)S(1)} %get-tuple-element.31.refs_3_.refs_6_.refs_0_), channel_id=1, source_target_pairs={{0,2},{1,3},{2,0},{3,1},{4,6},{5,7},{6,4},{7,5},{8,10},{9,11},{10,... | collective-permute-start | bytes 1572872 | tf_op jit(solution)/shard_map/ppermute | solution.py:280
  28.4 5.0 %copy-start.3 = (f32[3,128,128]{2,1,0:T(8,128)S(1)}, f32[3,128,128]{2,1,0:T(8,128)}, u32[]{:S(2)}) copy-start(f32[3,128,128]{2,1,0:T(8,128)} %param.9) | copy-start | bytes 589828
  29.5 1.8 %collective-permute-start.10 = (f32[6,128,128]{2,1,0:T(8,128)S(1)}, f32[6,128,128]{2,1,0:T(8,128)S(1)}, u32[]{:S(2)}, u32[]{:S(2)}) collective-permute-start(f32[6,128,128]{2,1,0:T(8,128)S(1)} %get-tuple-element.36), channel_id=1, source_target_pairs={{0,1},{1,0},{2,3},{3,2},{4,5},{5,4},{6,7},{7,6},{8,9},{9,8},{10,11... | collective-permute-start | bytes 1179656 | tf_op jit(solution)/shard_map/ppermute | solution.py:280
  31.3 11.3 %collective-permute-start.11 = (f32[6,128,128]{2,1,0:T(8,128)S(1)}, f32[6,128,128]{2,1,0:T(8,128)S(1)}, u32[]{:S(2)}, u32[]{:S(2)}) collective-permute-start(f32[6,128,128]{2,1,0:T(8,128)S(1)} %add.30), channel_id=1, source_target_pairs={{0,2},{1,3},{2,0},{3,1},{4,6},{5,7},{6,4},{7,5},{8,10},{9,11},{10,... | collective-permute-start | bytes 1179656 | tf_op jit(solution)/shard_map/ppermute | solution.py:280
  32.9 9.7 %collective-permute-start.2 = (s32[2,64]{1,0:T(2,128)S(1)}, s32[2,64]{1,0:T(2,128)S(1)}, u32[]{:S(2)}, u32[]{:S(2)}) collective-permute-start(s32[2,64]{1,0:T(2,128)S(1)} %pad_add_fusion.2), channel_id=1, source_target_pairs={{0,2},{1,3},{2,0},{3,1},{4,6},{5,7},{6,4},{7,5},{8,10},{9,11},{10,... | collective-permute-start | bytes 1544 | tf_op jit(solution)/shard_map/ppermute | solution.py:280
  43.2 1.8 %collective-permute-start.14 = (f32[6,128,128]{2,1,0:T(8,128)S(1)}, f32[6,128,128]{2,1,0:T(8,128)S(1)}, u32[]{:S(2)}, u32[]{:S(2)}) collective-permute-start(f32[6,128,128]{2,1,0:T(8,128)S(1)} %shard_map.90.refs_1_), channel_id=1, source_target_pairs={{0,1},{1,0},{2,3},{3,2},{4,5},{5,4},{6,7},{7,6},{8,9},{9,8},{10,11... | collective-permute-start | bytes 1179656 | tf_op jit(solution)/shard_map/ppermute | solution.py:280
  43.3 16.4 %collective-permute-start.13 = (f32[8,128,128]{2,1,0:T(8,128)S(1)}, f32[8,128,128]{2,1,0:T(8,128)S(1)}, u32[]{:S(2)}, u32[]{:S(2)}) collective-permute-start(f32[8,128,128]{2,1,0:T(8,128)S(1)} %collective-permute-done.8.refs_0_.refs_3_), channel_id=1, source_target_pairs={{0,1},{1,0},{2,3},{3,2},{4,5},{5,4},{6,7},{7,6},{8,9},{9,8},{10,11... | collective-permute-start | bytes 1572872 | tf_op jit(solution)/shard_map/ppermute | solution.py:280
  46.0 13.7 %collective-permute-start.15 = (f32[8,128,128]{2,1,0:T(8,128)S(1)}, f32[8,128,128]{2,1,0:T(8,128)S(1)}, u32[]{:S(2)}, u32[]{:S(2)}) collective-permute-start(f32[8,128,128]{2,1,0:T(8,128)S(1)} %shard_map.92), channel_id=1, source_target_pairs={{0,4},{1,9},{2,6},{3,11},{4,8},{5,13},{6,10},{7,15},{8,12},{9,17},... | collective-permute-start | bytes 1572872 | tf_op jit(solution)/shard_map/ppermute | solution.py:289
  49.0 10.7 %collective-permute-start.12 = (f32[4,128,128]{2,1,0:T(8,128)S(1)}, f32[4,128,128]{2,1,0:T(8,128)S(1)}, u32[]{:S(2)}, u32[]{:S(2)}) collective-permute-start(f32[4,128,128]{2,1,0:T(8,128)S(1)} %get-tuple-element.37.refs_1_), channel_id=1, source_target_pairs={{0,2},{1,3},{2,0},{3,1},{4,6},{5,7},{6,4},{7,5},{8,10},{9,11},{10,... | collective-permute-start | bytes 786440 | tf_op jit(solution)/shard_map/ppermute | solution.py:280
  50.6 8.8 %collective-permute-start.4 = (s32[4,64]{1,0:T(4,128)S(1)}, s32[4,64]{1,0:T(4,128)S(1)}, u32[]{:S(2)}, u32[]{:S(2)}) collective-permute-start(s32[4,64]{1,0:T(4,128)S(1)} %pad_add_fusion.metas.refs_0_), channel_id=1, source_target_pairs={{4,0},{6,2},{8,4},{9,1},{10,6},{11,3},{12,8},{13,5},{14,10},{15,7}... | collective-permute-start | bytes 3080 | tf_op jit(solution)/shard_map/ppermute | solution.py:289
  53.4 6.3 %collective-permute-start.3 = (s32[4,64]{1,0:T(4,128)S(1)}, s32[4,64]{1,0:T(4,128)S(1)}, u32[]{:S(2)}, u32[]{:S(2)}) collective-permute-start(s32[4,64]{1,0:T(4,128)S(1)} %pad_add_fusion.metas.refs_0_), channel_id=1, source_target_pairs={{0,4},{1,9},{2,6},{3,11},{4,8},{5,13},{6,10},{7,15},{8,12},{9,17},... | collective-permute-start | bytes 3080 | tf_op jit(solution)/shard_map/ppermute | solution.py:289
  60.8 2.6 %collective-permute-start.16 = (f32[6,128,128]{2,1,0:T(8,128)S(1)}, f32[6,128,128]{2,1,0:T(8,128)S(1)}, u32[]{:S(2)}, u32[]{:S(2)}) collective-permute-start(f32[6,128,128]{2,1,0:T(8,128)S(1)} %get-tuple-element.41), channel_id=1, source_target_pairs={{0,1},{1,0},{2,3},{3,2},{4,5},{5,4},{6,7},{7,6},{8,9},{9,8},{10,11... | collective-permute-start | bytes 1179656 | tf_op jit(solution)/shard_map/ppermute | solution.py:280
  63.5 11.5 %collective-permute-start.17 = (f32[6,128,128]{2,1,0:T(8,128)S(1)}, f32[6,128,128]{2,1,0:T(8,128)S(1)}, u32[]{:S(2)}, u32[]{:S(2)}) collective-permute-start(f32[6,128,128]{2,1,0:T(8,128)S(1)} %add.32), channel_id=1, source_target_pairs={{0,2},{1,3},{2,0},{3,1},{4,6},{5,7},{6,4},{7,5},{8,10},{9,11},{10,... | collective-permute-start | bytes 1179656 | tf_op jit(solution)/shard_map/ppermute | solution.py:280
  75.1 2.4 %copy-start.2 = (f32[12,32,128]{2,1,0:T(8,128)S(1)}, f32[12,32,128]{2,1,0:T(8,128)}, u32[]{:S(2)}) copy-start(f32[12,32,128]{2,1,0:T(8,128)} %base.1) | copy-start | bytes 589828
  75.6 1.8 %collective-permute-start.18 = (f32[6,128,128]{2,1,0:T(8,128)S(1)}, f32[6,128,128]{2,1,0:T(8,128)S(1)}, u32[]{:S(2)}, u32[]{:S(2)}) collective-permute-start(f32[6,128,128]{2,1,0:T(8,128)S(1)} %shard_map.94), channel_id=1, source_target_pairs={{0,1},{1,0},{2,3},{3,2},{4,5},{5,4},{6,7},{7,6},{8,9},{9,8},{10,11... | collective-permute-start | bytes 1179656 | tf_op jit(solution)/shard_map/ppermute | solution.py:280
  75.6 20.0 %collective-permute-start.19 = (f32[12,128,128]{2,1,0:T(8,128)S(1)}, f32[12,128,128]{2,1,0:T(8,128)S(1)}, u32[]{:S(2)}, u32[]{:S(2)}) collective-permute-start(f32[12,128,128]{2,1,0:T(8,128)S(1)} %get-tuple-element.38.upper.refs_0_), channel_id=1, source_target_pairs={{0,2},{1,3},{2,0},{3,1},{4,6},{5,7},{6,4},{7,5},{8,10},{9,11},{10,... | collective-permute-start | bytes 2359304 | tf_op jit(solution)/shard_map/ppermute | solution.py:280
  77.8 7.1 %collective-permute-start.20 = (f32[12,16,128]{2,1,0:T(8,128)S(1)}, f32[12,16,128]{2,1,0:T(8,128)S(1)}, u32[]{:S(2)}, u32[]{:S(2)}) collective-permute-start(f32[12,16,128]{2,1,0:T(8,128)S(1)} %shard_map.95.x), channel_id=1, source_target_pairs={{0,4},{1,9},{2,6},{3,11},{4,8},{5,13},{6,10},{7,15},{8,12},{9,17},... | collective-permute-start | bytes 294920 | tf_op jit(solution)/shard_map/ppermute | solution.py:289
  85.4 1.4 collective-permute-start.21
  86.7 7.4 %collective-permute-start.22 = (f32[12,16,128]{2,1,0:T(8,128)S(1)}, f32[12,16,128]{2,1,0:T(8,128)S(1)}, u32[]{:S(2)}, u32[]{:S(2)}) collective-permute-start(f32[12,16,128]{2,1,0:T(8,128)S(1)} %add_subtract_fusion.5.x), channel_id=1, source_target_pairs={{0,4},{1,9},{2,6},{3,11},{4,8},{5,13},{6,10},{7,15},{8,12},{9,17},... | collective-permute-start | bytes 294920 | tf_op jit(solution)/shard_map/ppermute | solution.py:289
  94.6 1.4 collective-permute-start.23
  95.6 14.5 %collective-permute-start.26 = (f32[12,128,128]{2,1,0:T(8,128)S(1)}, f32[12,128,128]{2,1,0:T(8,128)S(1)}, u32[]{:S(2)}, u32[]{:S(2)}) collective-permute-start(f32[12,128,128]{2,1,0:T(8,128)S(1)} %collective-permute-done.19.refs_0_.refs_2_), channel_id=1, source_target_pairs={{0,1},{1,0},{2,3},{3,2},{4,5},{5,4},{6,7},{7,6},{8,9},{9,8},{10,11... | collective-permute-start | bytes 2359304 | tf_op jit(solution)/shard_map/ppermute | solution.py:280
  96.0 7.4 %collective-permute-start.24 = (f32[12,16,128]{2,1,0:T(8,128)S(1)}, f32[12,16,128]{2,1,0:T(8,128)S(1)}, u32[]{:S(2)}, u32[]{:S(2)}) collective-permute-start(f32[12,16,128]{2,1,0:T(8,128)S(1)} %add_subtract_fusion.4.x), channel_id=1, source_target_pairs={{0,4},{1,9},{2,6},{3,11},{4,8},{5,13},{6,10},{7,15},{8,12},{9,17},... | collective-permute-start | bytes 294920 | tf_op jit(solution)/shard_map/ppermute | solution.py:289
  103.9 1.4 collective-permute-start.25
  105.3 7.9 %collective-permute-start.27 = (f32[12,16,128]{2,1,0:T(8,128)S(1)}, f32[12,16,128]{2,1,0:T(8,128)S(1)}, u32[]{:S(2)}, u32[]{:S(2)}) collective-permute-start(f32[12,16,128]{2,1,0:T(8,128)S(1)} %add_subtract_fusion.3.x), channel_id=1, source_target_pairs={{4,0},{6,2},{8,4},{9,1},{10,6},{11,3},{12,8},{13,5},{14,10},{15,7}... | collective-permute-start | bytes 294920 | tf_op jit(solution)/shard_map/ppermute | solution.py:289
  113.7 1.4 collective-permute-start.28
  115.1 7.7 %collective-permute-start.29 = (f32[12,16,128]{2,1,0:T(8,128)S(1)}, f32[12,16,128]{2,1,0:T(8,128)S(1)}, u32[]{:S(2)}, u32[]{:S(2)}) collective-permute-start(f32[12,16,128]{2,1,0:T(8,128)S(1)} %add_subtract_fusion.2.x), channel_id=1, source_target_pairs={{4,0},{6,2},{8,4},{9,1},{10,6},{11,3},{12,8},{13,5},{14,10},{15,7}... | collective-permute-start | bytes 294920 | tf_op jit(solution)/shard_map/ppermute | solution.py:289
  123.3 1.4 collective-permute-start.30
  124.7 7.4 %collective-permute-start.31 = (f32[12,16,128]{2,1,0:T(8,128)S(1)}, f32[12,16,128]{2,1,0:T(8,128)S(1)}, u32[]{:S(2)}, u32[]{:S(2)}) collective-permute-start(f32[12,16,128]{2,1,0:T(8,128)S(1)} %add_subtract_fusion.1.x), channel_id=1, source_target_pairs={{4,0},{6,2},{8,4},{9,1},{10,6},{11,3},{12,8},{13,5},{14,10},{15,7}... | collective-permute-start | bytes 294920 | tf_op jit(solution)/shard_map/ppermute | solution.py:289
  132.6 1.4 collective-permute-start.32
  134.0 4.9 %collective-permute-start.33 = (f32[12,16,128]{2,1,0:T(8,128)S(1)}, f32[12,16,128]{2,1,0:T(8,128)S(1)}, u32[]{:S(2)}, u32[]{:S(2)}) collective-permute-start(f32[12,16,128]{2,1,0:T(8,128)S(1)} %add_subtract_fusion), channel_id=1, source_target_pairs={{0,2},{1,3},{2,0},{3,1},{4,6},{5,7},{6,4},{7,5},{8,10},{9,11},{10,... | collective-permute-start | bytes 294920 | tf_op jit(solution)/shard_map/ppermute | solution.py:280

commit v7 on v6

--- a/solution.py
+++ b/solution.py
@@ -19,13 +19,18 @@
     return hi, (a - hi.astype(F32)).astype(BF16)
 
 
+def beside(a):
+    return jnp.concatenate(split(a), 1)
+
+
+def matmul_beside(lhs, pair):
+    out = jnp.dot(lhs, jnp.concatenate([pair, pair], 0), preferred_element_type=F32)
+    n = pair.shape[1] // 2
+    return out[:, :n] + out[:, n:]
+
+
 def matmul_parts(ah, al, bh, bl):
-    lhs = jnp.concatenate([ah, al], 1)
-    pair = jnp.concatenate([bh, bl], 1)
-    rhs = jnp.concatenate([pair, pair], 0)
-    out = jnp.dot(lhs, rhs, preferred_element_type=F32)
-    n = bh.shape[1]
-    return out[:, :n] + out[:, n:]
+    return matmul_beside(jnp.concatenate([ah, al], 1), jnp.concatenate([bh, bl], 1))
 
 
 def matmul(a, b):
@@ -91,17 +96,17 @@
     return pl.BlockSpec(memory_space=pltpu.VMEM)
 
 
-def call(body, outs, scalars, arrays, flops=0, scratch=(), early=(), to_smem=0):
+def call(body, outs, scalars, arrays, flops=0, scratch=(), early=(), to_smem=0, fetched=()):
     moved = sum(a.size * a.dtype.itemsize for a in arrays) + sum(o.size * o.dtype.itemsize for o in outs)
     return pl.pallas_call(
         body if not early else lambda *refs: body(*refs[len(early) :]),
         out_shape=outs,
-        in_specs=[pl.BlockSpec(memory_space=pl.ANY)] * len(early) + [smem()] * len(scalars) + [vmem()] * len(arrays),
+        in_specs=[pl.BlockSpec(memory_space=pl.ANY)] * (len(early) + len(fetched)) + [smem()] * len(scalars) + [vmem()] * len(arrays),
         out_specs=[smem()] * to_smem + [vmem()] * (len(outs) - to_smem),
         scratch_shapes=list(scratch),
         compiler_params=pltpu.CompilerParams(vmem_limit_bytes=8 << 20),
         cost_estimate=pl.CostEstimate(flops=flops, bytes_accessed=moved, transcendentals=0),
-    )(*early, *scalars, *arrays)
+    )(*early, *fetched, *scalars, *arrays)
 
 
 def listed_tiles(lay, meta, side, tiles, out):
@@ -111,24 +116,31 @@
             out[which * lay.cap + j] = jnp.where(live, tiles[s], 0.0)
 
 
-def outgoing_kernel(lay, near, inverse, tiles, mate_tiles, out, lower):
-    me, mine, mates = near.at[0], near.at[1], near.at[2]
-    role = me[0] % 2
-    for g, (meta, source) in enumerate(((mine, tiles), (mates, mate_tiles))):
+def outgoing_products(lay, inverse, near_source, near, done, halves, tile_of, out):
+    fetch = pltpu.make_async_copy(near_source, near, done)
+    fetch.start()
+    for r in range(lay.rows):
+        halves[r] = beside(inverse[r])
+    fetch.wait()
+    me, metas = near.at[0], (near.at[1], near.at[2])
+    for g, meta in enumerate(metas):
         for j in range(lay.cap):
-            s, live, _ = lay.lookup(meta, role, 2, j)
-            tile = jnp.where(live, source[s], 0.0)
-            out[g * lay.cap + j] = matmul(inverse[lay.place(s // lay.width, me[0])], tile)
-    listed_tiles(lay, mine, 1, tiles, lower)
-
-
-def next_outgoing_kernel(lay, near, inverse, upper, mate_upper, out):
-    me, mine, mates = near.at[0], near.at[1], near.at[2]
-    role = me[0] % 2
-    for g, (meta, source) in enumerate(((mine, upper), (mates, mate_upper))):
-        for j in range(lay.cap):
-            r = lay.listed(meta, role, j) // lay.width
-            out[g * lay.cap + j] = matmul(inverse[lay.place(r, me[0])], source[role * lay.cap + j])
+            s, live, _ = lay.lookup(meta, me[0] % 2, 2, j)
+            tile = tile_of(g, me[0] % 2 * lay.cap + j, s, live)
+            out[g * lay.cap + j] = matmul_beside(halves[lay.place(s // lay.width, me[0])], beside(tile))
+
+
+def outgoing_kernel(lay, near_source, inverse, tiles, mate_tiles, out, lower, halves, near, done):
+    held = (tiles, mate_tiles)
+    outgoing_products(
+        lay, inverse, near_source, near, done, halves, lambda g, k, s, live: jnp.where(live, held[g][s], 0.0), out
+    )
+    listed_tiles(lay, near.at[1], 1, tiles, lower)
+
+
+def next_outgoing_kernel(lay, near_source, inverse, upper, mate_upper, out, halves, near, done):
+    held = (upper, mate_upper)
+    outgoing_products(lay, inverse, near_source, near, done, halves, lambda g, k, s, live: held[g][k], out)
 
 
 def local_terms(lay, me, mine, inverse, diag, tiles, out):
@@ -163,7 +175,13 @@
     local_terms(lay, near.at[0], near.at[1], inverse, diag, tiles, out)
 
 
-def incoming_kernel(lay, near, local, lower, mate_lower, arrived, keep, give, total):
+def incoming_kernel(lay, near_source, local, lower, mate_lower, arrived, keep, give, total, halves, near, done):
+    fetch = pltpu.make_async_copy(near_source, near, done)
+    fetch.start()
+    total[...] = local[...]
+    for k in range(2 * lay.cap):
+        halves[k] = beside(arrived[k])
+    fetch.wait()
     me, mine, mates = near.at[0], near.at[1], near.at[2]
     role = me[0] % 2
     places, terms = [], []
@@ -171,8 +189,7 @@
         for j in range(lay.cap):
             s, _, v = lay.lookup(meta, 2 + role, 1, j)
             places.append(lay.place(s // lay.width, me[0]))
-            terms.append(matmul(source[role * lay.cap + j], arrived[g * lay.cap + v]))
-    total[...] = local[...]
+            terms.append(matmul_beside(beside(source[role * lay.cap + j]), halves[g * lay.cap + v]))
     for place, term in zip(places, terms):
         total[place] += term
     half = keep.shape[0]
@@ -318,12 +335,19 @@
     half = rows // 2
     lists, local_list = shape(2 * cap, n, n), shape(lay.pairs, n, n)
     places = pltpu.SMEM((lay.slots + 1,), jnp.int32)
+    fetching = (pltpu.SMEM(near.shape, jnp.int32), pltpu.SemaphoreType.DMA)
+    split_rows, whole_rows = pltpu.VMEM((rows, n, 2 * n), BF16), pltpu.VMEM((rows, n, n), F32)
     for sweep in range(FSWEEPS):
         inverse = jnp.concatenate([kept, mated], 0)
         early, later = [], []
         if sweep == 0:
             out, lower = call(
-                kernel(outgoing_kernel), [lists] * 2, (near,), (inverse, tiles, mate_tiles)
+                kernel(outgoing_kernel),
+                [lists] * 2,
+                (),
+                (inverse, tiles, mate_tiles),
+                scratch=(split_rows, *fetching),
+                fetched=(near,),
             )
             arrived = along(out, 1)
             lowers = over_chips(lower)
@@ -340,7 +364,12 @@
             later += [metas]
         else:
             (out,) = call(
-                kernel(next_outgoing_kernel), [lists], (near,), (inverse, upper, mate_upper)
+                kernel(next_outgoing_kernel),
+                [lists],
+                (),
+                (inverse, upper, mate_upper),
+                scratch=(split_rows, *fetching),
+                fetched=(near,),
             )
             arrived = along(out, 1)
             (here,) = call(
@@ -368,9 +397,10 @@
         keep, give = call(
             kernel(incoming_kernel),
             [shape(half, n, n)] * 2,
-            (near,),
+            (),
             (here, lower, mate_lower, arrived),
-            scratch=(pltpu.VMEM((rows, n, n), F32),),
+            scratch=(whole_rows, pltpu.VMEM((2 * cap, n, 2 * n), BF16), *fetching),
+            fetched=(near,),
             early=early,
         )
         sums = summed(keep + swap(give, 1))

time: 141 us -> 141 us (level)
  transfers between devices with their start and end apart: 34 -> 34, of which waited for: 26 -> 25; matrix products, arithmetic and copies ran while one was open for 3% -> 3% of each run, Pallas kernels for 12% -> 12%
where the time goes in v7:
time: 141 us; the launch traced here: 140 us
  waiting for transfers between devices  58.2 us (41%)
  starting transfers between devices  51.8 us (37%)
  Pallas kernels  22.7 us (16%)
  local copies, waits for them, and re-layouts  4.22 us (3%)
    ppermute x24, waiting for transfers between devices, swap(): return lax.ppermute(x, 'tile', [(i, i ^ bit) for i in range(n_tile)])  37.5 us
    ppermute x10, starting transfers between devices, along(): return lax.ppermute(x, ('dom', 'tile'), route)  37 us
    pallas_call x24, Pallas kernels, call(): pl.pallas_call(body if not early else lambda *refs: body(*refs[len(early)...  22.7 us
    ppermute x10, waiting for transfers between devices, along(): return lax.ppermute(x, ('dom', 'tile'), route)  20.7 us
    ppermute x24, starting transfers between devices, swap(): return lax.ppermute(x, 'tile', [(i, i ^ bit) for i in range(n_tile)])  14.8 us
  transfers between devices with their start and end apart: 34, of which 25 were waited for; matrix products, arithmetic and copies ran while one was open for 3% of the time, Pallas kernels for 12%

profile of v7, /device:TPU:18, one launch (start us, length us, event | category | flops | bytes accessed | tf_op | source)
XLA Modules:
  0.0 139.5 jit_solution(4442122558078340941)
XLA Ops:
  0.7 1.6 %collective-permute-start = (f32[3,128,128]{2,1,0:T(8,128)}, f32[3,128,128]{2,1,0:T(8,128)S(1)}, u32[]{:S(2)}, u32[]{:S(2)}) collective-permute-start(f32[3,128,128]{2,1,0:T(8,128)} %param.9), channel_id=1, source_target_pairs={{0,2},{1,3},{2,0},{3,1},{4,6},{5,7},{6,4},{7,5},{8,10},{9,11},{10,... | collective-permute-start | bytes 589832 | tf_op jit(solution)/shard_map/ppermute | solution.py:297
  5.0 1.0 collective-permute-done.1
  6.0 2.3 %collective-permute-done = f32[3,128,128]{2,1,0:T(8,128)S(1)} collective-permute-done((f32[3,128,128]{2,1,0:T(8,128)}, f32[3,128,128]{2,1,0:T(8,128)S(1)}, u32[]{:S(2)}, u32[]{:S(2)}) %collective-permute-start) | collective-permute-done | bytes 196640 | tf_op jit(solution)/shard_map/ppermute | solution.py:297
  8.8 0.9 constant_dynamic-update-slice_fusion.3
  10.2 0.9 shard_map.87
  11.2 3.5 %collective-permute-start.9 = (f32[8,128,128]{2,1,0:T(8,128)S(1)}, f32[8,128,128]{2,1,0:T(8,128)S(1)}, u32[]{:S(2)}, u32[]{:S(2)}) collective-permute-start(f32[8,128,128]{2,1,0:T(8,128)S(1)} %get-tuple-element.34), channel_id=1, source_target_pairs={{0,4},{1,9},{2,6},{3,11},{4,8},{5,13},{6,10},{7,15},{8,12},{9,17},... | collective-permute-start | bytes 1572872 | tf_op jit(solution)/shard_map/ppermute | solution.py:306
  14.6 1.6 %collective-permute-start.8 = (f32[8,128,128]{2,1,0:T(8,128)S(1)}, f32[8,128,128]{2,1,0:T(8,128)S(1)}, u32[]{:S(2)}, u32[]{:S(2)}) collective-permute-start(f32[8,128,128]{2,1,0:T(8,128)S(1)} %get-tuple-element.31.refs_3_.refs_6_.refs_0_), channel_id=1, source_target_pairs={{0,2},{1,3},{2,0},{3,1},{4,6},{5,7},{6,4},{7,5},{8,10},{9,11},{10,... | collective-permute-start | bytes 1572872 | tf_op jit(solution)/shard_map/ppermute | solution.py:297
  16.2 2.8 %shard_map.88 = (f32[12,128,128]{2,1,0:T(8,128)S(1)}, f32[8,128,128]{2,1,0:T(8,128)S(1)}, f32[4,128,128]{2,1,0:T(8,128)S(1)}, f32[12,128,128]{2,1,0:T(8,128)S(1)}, f32[8,128,128]{2,1,0:T(8,128)S(1)}) custom-call(s32[3,64]{1,0:T(4,128)S(1)} %pad_add_fusion.1.near_source.near.refs_1_.refs_4_, f32[12,128,128]{2,1,0:T(8,128)S(1)} %constant_dynamic-update-slice_fusion.inverse, ...), custom_call_target="tpu_custom_call" | custom-call | flops 201326592 | bytes 7012352 | tf_op jit(solution)/shard_map/pallas_call | solution.py:101
  19.0 7.1 %collective-permute-done.9.refs_5_ = f32[8,128,128]{2,1,0:T(8,128)S(1)} collective-permute-done((f32[8,128,128]{2,1,0:T(8,128)S(1)}, f32[8,128,128]{2,1,0:T(8,128)S(1)}, u32[]{:S(2)}, u32[]{:S(2)}) %collective-permute-start.9) | collective-permute-done | bytes 524320 | tf_op jit(solution)/shard_map/ppermute | solution.py:306
  26.1 2.3 %collective-permute-done.8.refs_0_.refs_3_ = f32[8,128,128]{2,1,0:T(8,128)S(1)} collective-permute-done((f32[8,128,128]{2,1,0:T(8,128)S(1)}, f32[8,128,128]{2,1,0:T(8,128)S(1)}, u32[]{:S(2)}, u32[]{:S(2)}) %collective-permute-start.8) | collective-permute-done | bytes 524320 | tf_op jit(solution)/shard_map/ppermute | solution.py:297
  28.4 1.0 shard_map.89
  29.6 1.7 %collective-permute-done.10 = f32[6,128,128]{2,1,0:T(8,128)S(1)} collective-permute-done((f32[6,128,128]{2,1,0:T(8,128)S(1)}, f32[6,128,128]{2,1,0:T(8,128)S(1)}, u32[]{:S(2)}, u32[]{:S(2)}) %collective-permute-start.10) | collective-permute-done | bytes 393248 | tf_op jit(solution)/shard_map/ppermute | solution.py:297
  31.3 1.6 %collective-permute-start.11 = (f32[6,128,128]{2,1,0:T(8,128)S(1)}, f32[6,128,128]{2,1,0:T(8,128)S(1)}, u32[]{:S(2)}, u32[]{:S(2)}) collective-permute-start(f32[6,128,128]{2,1,0:T(8,128)S(1)} %add.30), channel_id=1, source_target_pairs={{0,2},{1,3},{2,0},{3,1},{4,6},{5,7},{6,4},{7,5},{8,10},{9,11},{10,... | collective-permute-start | bytes 1179656 | tf_op jit(solution)/shard_map/ppermute | solution.py:297
  33.5 9.1 %collective-permute-done.2 = s32[2,64]{1,0:T(2,128)S(1)} collective-permute-done((s32[2,64]{1,0:T(2,128)S(1)}, s32[2,64]{1,0:T(2,128)S(1)}, u32[]{:S(2)}, u32[]{:S(2)}) %collective-permute-start.2) | collective-permute-done | bytes 544 | tf_op jit(solution)/shard_map/ppermute | solution.py:297
  43.8 1.2 collective-permute-done.14
  45.1 0.9 shard_map.92
  46.0 3.0 %collective-permute-start.15 = (f32[8,128,128]{2,1,0:T(8,128)S(1)}, f32[8,128,128]{2,1,0:T(8,128)S(1)}, u32[]{:S(2)}, u32[]{:S(2)}) collective-permute-start(f32[8,128,128]{2,1,0:T(8,128)S(1)} %shard_map.92), channel_id=1, source_target_pairs={{0,4},{1,9},{2,6},{3,11},{4,8},{5,13},{6,10},{7,15},{8,12},{9,17},... | collective-permute-start | bytes 1572872 | tf_op jit(solution)/shard_map/ppermute | solution.py:306
  49.0 1.6 %collective-permute-start.12 = (f32[4,128,128]{2,1,0:T(8,128)S(1)}, f32[4,128,128]{2,1,0:T(8,128)S(1)}, u32[]{:S(2)}, u32[]{:S(2)}) collective-permute-start(f32[4,128,128]{2,1,0:T(8,128)S(1)} %get-tuple-element.37.refs_1_), channel_id=1, source_target_pairs={{0,2},{1,3},{2,0},{3,1},{4,6},{5,7},{6,4},{7,5},{8,10},{9,11},{10,... | collective-permute-start | bytes 786440 | tf_op jit(solution)/shard_map/ppermute | solution.py:297
  50.6 2.8 %collective-permute-start.4 = (s32[4,64]{1,0:T(4,128)S(1)}, s32[4,64]{1,0:T(4,128)S(1)}, u32[]{:S(2)}, u32[]{:S(2)}) collective-permute-start(s32[4,64]{1,0:T(4,128)S(1)} %pad_add_fusion.metas.refs_0_), channel_id=1, source_target_pairs={{4,0},{6,2},{8,4},{9,1},{10,6},{11,3},{12,8},{13,5},{14,10},{15,7}... | collective-permute-start | bytes 3080 | tf_op jit(solution)/shard_map/ppermute | solution.py:306
  53.4 3.9 %collective-permute-start.3 = (s32[4,64]{1,0:T(4,128)S(1)}, s32[4,64]{1,0:T(4,128)S(1)}, u32[]{:S(2)}, u32[]{:S(2)}) collective-permute-start(s32[4,64]{1,0:T(4,128)S(1)} %pad_add_fusion.metas.refs_0_), channel_id=1, source_target_pairs={{0,4},{1,9},{2,6},{3,11},{4,8},{5,13},{6,10},{7,15},{8,12},{9,17},... | collective-permute-start | bytes 3080 | tf_op jit(solution)/shard_map/ppermute | solution.py:306
  57.3 2.4 %shard_map.91.refs_5_ = f32[12,128,128]{2,1,0:T(8,128)S(1)} custom-call(s32[3,64]{1,0:T(4,128)S(1)} %pad_add_fusion.1.near_source.near.refs_1_.refs_4_, f32[12,128,128]{2,1,0:T(8,128)S(1)} %pad_maximum_fusion.inverse, f32[3,128,128]{2,1,0:T(8,128)S(1)} %copy-done.1, f32[24,128,128]{2,1,0:T(8,128)S(1)} %bitcast.14), custom_call_target="tpu_custom_call" | custom-call | flops 201326592 | bytes 3342336 | tf_op jit(solution)/shard_map/pallas_call | solution.py:101
  59.8 1.1 shard_map.93
  60.8 1.2 collective-permute-start.16
  62.1 1.3 collective-permute-done.16
  63.5 1.6 %collective-permute-start.17 = (f32[6,128,128]{2,1,0:T(8,128)S(1)}, f32[6,128,128]{2,1,0:T(8,128)S(1)}, u32[]{:S(2)}, u32[]{:S(2)}) collective-permute-start(f32[6,128,128]{2,1,0:T(8,128)S(1)} %add.32), channel_id=1, source_target_pairs={{0,2},{1,3},{2,0},{3,1},{4,6},{5,7},{6,4},{7,5},{8,10},{9,11},{10,... | collective-permute-start | bytes 1179656 | tf_op jit(solution)/shard_map/ppermute | solution.py:297
  65.1 2.1 %shard_map.86 = (s32[65]{0:T(128)S(1)}, f32[16,12,128]{2,1,0:T(8,128)S(1)}, f32[16,12,128]{2,1,0:T(8,128)S(1)}, f32[16,12,128]{2,1,0:T(8,128)S(1)}, f32[16,12,128]{2,1,0:T(8,128)S(1)}) custom-call(s32[1]{0:T(128)} %bitcast.me, s32[4,64]{1,0:T(4,128)S(1)} %pad_add_fusion.metas.refs_0_, s32[4,64]{1,0:T(4,128)S(1)} %collective-permute-done.3.peers_below.refs_2_, ...), custom_call_target="tpu_custom_call" | custom-call | bytes 393476 | tf_op jit(solution)/shard_map/pallas_call | solution.py:101
  67.2 7.7 %collective-permute-done.17 = f32[6,128,128]{2,1,0:T(8,128)S(1)} collective-permute-done((f32[6,128,128]{2,1,0:T(8,128)S(1)}, f32[6,128,128]{2,1,0:T(8,128)S(1)}, u32[]{:S(2)}, u32[]{:S(2)}) %collective-permute-start.17) | collective-permute-done | bytes 393248 | tf_op jit(solution)/shard_map/ppermute | solution.py:297
  75.6 1.6 %collective-permute-start.19 = (f32[12,128,128]{2,1,0:T(8,128)S(1)}, f32[12,128,128]{2,1,0:T(8,128)S(1)}, u32[]{:S(2)}, u32[]{:S(2)}) collective-permute-start(f32[12,128,128]{2,1,0:T(8,128)S(1)} %get-tuple-element.38.upper.refs_0_), channel_id=1, source_target_pairs={{0,2},{1,3},{2,0},{3,1},{4,6},{5,7},{6,4},{7,5},{8,10},{9,11},{10,... | collective-permute-start | bytes 2359304 | tf_op jit(solution)/shard_map/ppermute | solution.py:297
  77.8 4.2 %collective-permute-start.20 = (f32[12,16,128]{2,1,0:T(8,128)S(1)}, f32[12,16,128]{2,1,0:T(8,128)S(1)}, u32[]{:S(2)}, u32[]{:S(2)}) collective-permute-start(f32[12,16,128]{2,1,0:T(8,128)S(1)} %shard_map.95.x), channel_id=1, source_target_pairs={{0,4},{1,9},{2,6},{3,11},{4,8},{5,13},{6,10},{7,15},{8,12},{9,17},... | collective-permute-start | bytes 294920 | tf_op jit(solution)/shard_map/ppermute | solution.py:306
  82.0 1.3 shard_map.96
  85.4 1.3 collective-permute-done.21
  86.7 4.5 %collective-permute-start.22 = (f32[12,16,128]{2,1,0:T(8,128)S(1)}, f32[12,16,128]{2,1,0:T(8,128)S(1)}, u32[]{:S(2)}, u32[]{:S(2)}) collective-permute-start(f32[12,16,128]{2,1,0:T(8,128)S(1)} %add_subtract_fusion.5.x), channel_id=1, source_target_pairs={{0,4},{1,9},{2,6},{3,11},{4,8},{5,13},{6,10},{7,15},{8,12},{9,17},... | collective-permute-start | bytes 294920 | tf_op jit(solution)/shard_map/ppermute | solution.py:306
  92.1 2.0 %collective-permute-done.22.arrived = f32[12,16,128]{2,1,0:T(8,128)S(1)} collective-permute-done((f32[12,16,128]{2,1,0:T(8,128)S(1)}, f32[12,16,128]{2,1,0:T(8,128)S(1)}, u32[]{:S(2)}, u32[]{:S(2)}) %collective-permute-start.22) | collective-permute-done | bytes 98336 | tf_op jit(solution)/shard_map/ppermute | solution.py:306
  96.0 4.5 %collective-permute-start.24 = (f32[12,16,128]{2,1,0:T(8,128)S(1)}, f32[12,16,128]{2,1,0:T(8,128)S(1)}, u32[]{:S(2)}, u32[]{:S(2)}) collective-permute-start(f32[12,16,128]{2,1,0:T(8,128)S(1)} %add_subtract_fusion.4.x), channel_id=1, source_target_pairs={{0,4},{1,9},{2,6},{3,11},{4,8},{5,13},{6,10},{7,15},{8,12},{9,17},... | collective-permute-start | bytes 294920 | tf_op jit(solution)/shard_map/ppermute | solution.py:306
  101.4 2.0 %collective-permute-done.24.refs_5_ = f32[12,16,128]{2,1,0:T(8,128)S(1)} collective-permute-done((f32[12,16,128]{2,1,0:T(8,128)S(1)}, f32[12,16,128]{2,1,0:T(8,128)S(1)}, u32[]{:S(2)}, u32[]{:S(2)}) %collective-permute-start.24) | collective-permute-done | bytes 98336 | tf_op jit(solution)/shard_map/ppermute | solution.py:306
  104.0 1.3 collective-permute-done.25
  105.3 4.8 %collective-permute-start.27 = (f32[12,16,128]{2,1,0:T(8,128)S(1)}, f32[12,16,128]{2,1,0:T(8,128)S(1)}, u32[]{:S(2)}, u32[]{:S(2)}) collective-permute-start(f32[12,16,128]{2,1,0:T(8,128)S(1)} %add_subtract_fusion.3.x), channel_id=1, source_target_pairs={{4,0},{6,2},{8,4},{9,1},{10,6},{11,3},{12,8},{13,5},{14,10},{15,7}... | collective-permute-start | bytes 294920 | tf_op jit(solution)/shard_map/ppermute | solution.py:306
  110.1 1.2 shard_map.103
  112.2 1.0 collective-permute-done.27.arrived
  113.7 1.3 collective-permute-done.28
  115.0 3.4 %collective-permute-start.29 = (f32[12,16,128]{2,1,0:T(8,128)S(1)}, f32[12,16,128]{2,1,0:T(8,128)S(1)}, u32[]{:S(2)}, u32[]{:S(2)}) collective-permute-start(f32[12,16,128]{2,1,0:T(8,128)S(1)} %add_subtract_fusion.2.x), channel_id=1, source_target_pairs={{4,0},{6,2},{8,4},{9,1},{10,6},{11,3},{12,8},{13,5},{14,10},{15,7}... | collective-permute-start | bytes 294920 | tf_op jit(solution)/shard_map/ppermute | solution.py:306
  119.3 3.4 %collective-permute-done.29.arrived = f32[12,16,128]{2,1,0:T(8,128)S(1)} collective-permute-done((f32[12,16,128]{2,1,0:T(8,128)S(1)}, f32[12,16,128]{2,1,0:T(8,128)S(1)}, u32[]{:S(2)}, u32[]{:S(2)}) %collective-permute-start.29) | collective-permute-done | bytes 98336 | tf_op jit(solution)/shard_map/ppermute | solution.py:306
  123.3 1.3 collective-permute-done.30
  124.6 2.2 %collective-permute-start.31 = (f32[12,16,128]{2,1,0:T(8,128)S(1)}, f32[12,16,128]{2,1,0:T(8,128)S(1)}, u32[]{:S(2)}, u32[]{:S(2)}) collective-permute-start(f32[12,16,128]{2,1,0:T(8,128)S(1)} %add_subtract_fusion.1.x), channel_id=1, source_target_pairs={{4,0},{6,2},{8,4},{9,1},{10,6},{11,3},{12,8},{13,5},{14,10},{15,7}... | collective-permute-start | bytes 294920 | tf_op jit(solution)/shard_map/ppermute | solution.py:306
  127.7 4.3 %collective-permute-done.31.arrived = f32[12,16,128]{2,1,0:T(8,128)S(1)} collective-permute-done((f32[12,16,128]{2,1,0:T(8,128)S(1)}, f32[12,16,128]{2,1,0:T(8,128)S(1)}, u32[]{:S(2)}, u32[]{:S(2)}) %collective-permute-start.31) | collective-permute-done | bytes 98336 | tf_op jit(solution)/shard_map/ppermute | solution.py:306
  132.6 1.3 collective-permute-done.32
  133.9 1.6 %collective-permute-start.33 = (f32[12,16,128]{2,1,0:T(8,128)S(1)}, f32[12,16,128]{2,1,0:T(8,128)S(1)}, u32[]{:S(2)}, u32[]{:S(2)}) collective-permute-start(f32[12,16,128]{2,1,0:T(8,128)S(1)} %add_subtract_fusion), channel_id=1, source_target_pairs={{0,2},{1,3},{2,0},{3,1},{4,6},{5,7},{6,4},{7,5},{8,10},{9,11},{10,... | collective-permute-start | bytes 294920 | tf_op jit(solution)/shard_map/ppermute | solution.py:297
  136.2 2.6 %collective-permute-done.33 = f32[12,16,128]{2,1,0:T(8,128)S(1)} collective-permute-done((f32[12,16,128]{2,1,0:T(8,128)S(1)}, f32[12,16,128]{2,1,0:T(8,128)S(1)}, u32[]{:S(2)}, u32[]{:S(2)}) %collective-permute-start.33) | collective-permute-done | bytes 98336 | tf_op jit(solution)/shard_map/ppermute | solution.py:297
  (85 shorter events, 18.6 us)
Async XLA Ops:
  0.6 9.6 %copy-start = (f32[12,2,128,128]{3,2,1,0:T(8,128)S(1)}, f32[12,2,128,128]{3,2,1,0:T(8,128)}, u32[]{:S(2)}) copy-start(f32[12,2,128,128]{3,2,1,0:T(8,128)} %param.10) | copy-start | bytes 4718596
  0.6 9.6 %collective-permute-start.7 = (f32[24,128,128]{2,1,0:T(8,128)}, f32[24,128,128]{2,1,0:T(8,128)S(1)}, u32[]{:S(2)}, u32[]{:S(2)}) collective-permute-start(f32[24,128,128]{2,1,0:T(8,128)} %bitcast.11), channel_id=1, source_target_pairs={{0,1},{1,0},{2,3},{3,2},{4,5},{5,4},{6,7},{7,6},{8,9},{9,8},{10,11... | collective-permute-start | bytes 4718600 | tf_op jit(solution)/shard_map/ppermute | solution.py:297
  0.7 7.5 %collective-permute-start = (f32[3,128,128]{2,1,0:T(8,128)}, f32[3,128,128]{2,1,0:T(8,128)S(1)}, u32[]{:S(2)}, u32[]{:S(2)}) collective-permute-start(f32[3,128,128]{2,1,0:T(8,128)} %param.9), channel_id=1, source_target_pairs={{0,2},{1,3},{2,0},{3,1},{4,6},{5,7},{6,4},{7,5},{8,10},{9,11},{10,... | collective-permute-start | bytes 589832 | tf_op jit(solution)/shard_map/ppermute | solution.py:297
  4.9 1.1 collective-permute-start.1
  8.2 1.9 %collective-permute-start.5 = (f32[3,128,128]{2,1,0:T(8,128)}, f32[3,128,128]{2,1,0:T(8,128)S(1)}, u32[]{:S(2)}, u32[]{:S(2)}) collective-permute-start(f32[3,128,128]{2,1,0:T(8,128)} %param.9), channel_id=1, source_target_pairs={{0,1},{1,0},{2,3},{3,2},{4,5},{5,4},{6,7},{7,6},{8,9},{9,8},{10,11... | collective-permute-start | bytes 589832 | tf_op jit(solution)/shard_map/ppermute | solution.py:297
  8.3 1.9 %collective-permute-start.6 = (f32[3,128,128]{2,1,0:T(8,128)S(1)}, f32[3,128,128]{2,1,0:T(8,128)S(1)}, u32[]{:S(2)}, u32[]{:S(2)}) collective-permute-start(f32[3,128,128]{2,1,0:T(8,128)S(1)} %collective-permute-done), channel_id=1, source_target_pairs={{0,1},{1,0},{2,3},{3,2},{4,5},{5,4},{6,7},{7,6},{8,9},{9,8},{10,11... | collective-permute-start | bytes 589832 | tf_op jit(solution)/shard_map/ppermute | solution.py:297
  10.2 6.0 %copy-start.1 = (f32[3,128,128]{2,1,0:T(8,128)S(1)}, f32[3,128,128]{2,1,0:T(8,128)}, u32[]{:S(2)}) copy-start(f32[3,128,128]{2,1,0:T(8,128)} %diag.3) | copy-start | bytes 589828
  11.2 15.0 %collective-permute-start.9 = (f32[8,128,128]{2,1,0:T(8,128)S(1)}, f32[8,128,128]{2,1,0:T(8,128)S(1)}, u32[]{:S(2)}, u32[]{:S(2)}) collective-permute-start(f32[8,128,128]{2,1,0:T(8,128)S(1)} %get-tuple-element.34), channel_id=1, source_target_pairs={{0,4},{1,9},{2,6},{3,11},{4,8},{5,13},{6,10},{7,15},{8,12},{9,17},... | collective-permute-start | bytes 1572872 | tf_op jit(solution)/shard_map/ppermute | solution.py:306
  14.6 13.8 %collective-permute-start.8 = (f32[8,128,128]{2,1,0:T(8,128)S(1)}, f32[8,128,128]{2,1,0:T(8,128)S(1)}, u32[]{:S(2)}, u32[]{:S(2)}) collective-permute-start(f32[8,128,128]{2,1,0:T(8,128)S(1)} %get-tuple-element.31.refs_3_.refs_6_.refs_0_), channel_id=1, source_target_pairs={{0,2},{1,3},{2,0},{3,1},{4,6},{5,7},{6,4},{7,5},{8,10},{9,11},{10,... | collective-permute-start | bytes 1572872 | tf_op jit(solution)/shard_map/ppermute | solution.py:297
  28.4 5.0 %copy-start.3 = (f32[3,128,128]{2,1,0:T(8,128)S(1)}, f32[3,128,128]{2,1,0:T(8,128)}, u32[]{:S(2)}) copy-start(f32[3,128,128]{2,1,0:T(8,128)} %param.9) | copy-start | bytes 589828
  29.5 1.8 %collective-permute-start.10 = (f32[6,128,128]{2,1,0:T(8,128)S(1)}, f32[6,128,128]{2,1,0:T(8,128)S(1)}, u32[]{:S(2)}, u32[]{:S(2)}) collective-permute-start(f32[6,128,128]{2,1,0:T(8,128)S(1)} %get-tuple-element.36), channel_id=1, source_target_pairs={{0,1},{1,0},{2,3},{3,2},{4,5},{5,4},{6,7},{7,6},{8,9},{9,8},{10,11... | collective-permute-start | bytes 1179656 | tf_op jit(solution)/shard_map/ppermute | solution.py:297
  31.3 11.3 %collective-permute-start.11 = (f32[6,128,128]{2,1,0:T(8,128)S(1)}, f32[6,128,128]{2,1,0:T(8,128)S(1)}, u32[]{:S(2)}, u32[]{:S(2)}) collective-permute-start(f32[6,128,128]{2,1,0:T(8,128)S(1)} %add.30), channel_id=1, source_target_pairs={{0,2},{1,3},{2,0},{3,1},{4,6},{5,7},{6,4},{7,5},{8,10},{9,11},{10,... | collective-permute-start | bytes 1179656 | tf_op jit(solution)/shard_map/ppermute | solution.py:297
  32.9 9.7 %collective-permute-start.2 = (s32[2,64]{1,0:T(2,128)S(1)}, s32[2,64]{1,0:T(2,128)S(1)}, u32[]{:S(2)}, u32[]{:S(2)}) collective-permute-start(s32[2,64]{1,0:T(2,128)S(1)} %pad_add_fusion.2), channel_id=1, source_target_pairs={{0,2},{1,3},{2,0},{3,1},{4,6},{5,7},{6,4},{7,5},{8,10},{9,11},{10,... | collective-permute-start | bytes 1544 | tf_op jit(solution)/shard_map/ppermute | solution.py:297
  43.2 1.8 %collective-permute-start.14 = (f32[6,128,128]{2,1,0:T(8,128)S(1)}, f32[6,128,128]{2,1,0:T(8,128)S(1)}, u32[]{:S(2)}, u32[]{:S(2)}) collective-permute-start(f32[6,128,128]{2,1,0:T(8,128)S(1)} %shard_map.90.refs_1_), channel_id=1, source_target_pairs={{0,1},{1,0},{2,3},{3,2},{4,5},{5,4},{6,7},{7,6},{8,9},{9,8},{10,11... | collective-permute-start | bytes 1179656 | tf_op jit(solution)/shard_map/ppermute | solution.py:297
  43.3 16.4 %collective-permute-start.13 = (f32[8,128,128]{2,1,0:T(8,128)S(1)}, f32[8,128,128]{2,1,0:T(8,128)S(1)}, u32[]{:S(2)}, u32[]{:S(2)}) collective-permute-start(f32[8,128,128]{2,1,0:T(8,128)S(1)} %collective-permute-done.8.refs_0_.refs_3_), channel_id=1, source_target_pairs={{0,1},{1,0},{2,3},{3,2},{4,5},{5,4},{6,7},{7,6},{8,9},{9,8},{10,11... | collective-permute-start | bytes 1572872 | tf_op jit(solution)/shard_map/ppermute | solution.py:297
  46.0 13.8 %collective-permute-start.15 = (f32[8,128,128]{2,1,0:T(8,128)S(1)}, f32[8,128,128]{2,1,0:T(8,128)S(1)}, u32[]{:S(2)}, u32[]{:S(2)}) collective-permute-start(f32[8,128,128]{2,1,0:T(8,128)S(1)} %shard_map.92), channel_id=1, source_target_pairs={{0,4},{1,9},{2,6},{3,11},{4,8},{5,13},{6,10},{7,15},{8,12},{9,17},... | collective-permute-start | bytes 1572872 | tf_op jit(solution)/shard_map/ppermute | solution.py:306
  49.0 10.7 %collective-permute-start.12 = (f32[4,128,128]{2,1,0:T(8,128)S(1)}, f32[4,128,128]{2,1,0:T(8,128)S(1)}, u32[]{:S(2)}, u32[]{:S(2)}) collective-permute-start(f32[4,128,128]{2,1,0:T(8,128)S(1)} %get-tuple-element.37.refs_1_), channel_id=1, source_target_pairs={{0,2},{1,3},{2,0},{3,1},{4,6},{5,7},{6,4},{7,5},{8,10},{9,11},{10,... | collective-permute-start | bytes 786440 | tf_op jit(solution)/shard_map/ppermute | solution.py:297
  50.6 9.1 %collective-permute-start.4 = (s32[4,64]{1,0:T(4,128)S(1)}, s32[4,64]{1,0:T(4,128)S(1)}, u32[]{:S(2)}, u32[]{:S(2)}) collective-permute-start(s32[4,64]{1,0:T(4,128)S(1)} %pad_add_fusion.metas.refs_0_), channel_id=1, source_target_pairs={{4,0},{6,2},{8,4},{9,1},{10,6},{11,3},{12,8},{13,5},{14,10},{15,7}... | collective-permute-start | bytes 3080 | tf_op jit(solution)/shard_map/ppermute | solution.py:306
  53.4 6.3 %collective-permute-start.3 = (s32[4,64]{1,0:T(4,128)S(1)}, s32[4,64]{1,0:T(4,128)S(1)}, u32[]{:S(2)}, u32[]{:S(2)}) collective-permute-start(s32[4,64]{1,0:T(4,128)S(1)} %pad_add_fusion.metas.refs_0_), channel_id=1, source_target_pairs={{0,4},{1,9},{2,6},{3,11},{4,8},{5,13},{6,10},{7,15},{8,12},{9,17},... | collective-permute-start | bytes 3080 | tf_op jit(solution)/shard_map/ppermute | solution.py:306
  60.8 2.6 %collective-permute-start.16 = (f32[6,128,128]{2,1,0:T(8,128)S(1)}, f32[6,128,128]{2,1,0:T(8,128)S(1)}, u32[]{:S(2)}, u32[]{:S(2)}) collective-permute-start(f32[6,128,128]{2,1,0:T(8,128)S(1)} %get-tuple-element.41), channel_id=1, source_target_pairs={{0,1},{1,0},{2,3},{3,2},{4,5},{5,4},{6,7},{7,6},{8,9},{9,8},{10,11... | collective-permute-start | bytes 1179656 | tf_op jit(solution)/shard_map/ppermute | solution.py:297
  63.5 11.5 %collective-permute-start.17 = (f32[6,128,128]{2,1,0:T(8,128)S(1)}, f32[6,128,128]{2,1,0:T(8,128)S(1)}, u32[]{:S(2)}, u32[]{:S(2)}) collective-permute-start(f32[6,128,128]{2,1,0:T(8,128)S(1)} %add.32), channel_id=1, source_target_pairs={{0,2},{1,3},{2,0},{3,1},{4,6},{5,7},{6,4},{7,5},{8,10},{9,11},{10,... | collective-permute-start | bytes 1179656 | tf_op jit(solution)/shard_map/ppermute | solution.py:297
  75.0 2.4 %copy-start.2 = (f32[12,32,128]{2,1,0:T(8,128)S(1)}, f32[12,32,128]{2,1,0:T(8,128)}, u32[]{:S(2)}) copy-start(f32[12,32,128]{2,1,0:T(8,128)} %base.1) | copy-start | bytes 589828
  75.5 1.8 %collective-permute-start.18 = (f32[6,128,128]{2,1,0:T(8,128)S(1)}, f32[6,128,128]{2,1,0:T(8,128)S(1)}, u32[]{:S(2)}, u32[]{:S(2)}) collective-permute-start(f32[6,128,128]{2,1,0:T(8,128)S(1)} %shard_map.94), channel_id=1, source_target_pairs={{0,1},{1,0},{2,3},{3,2},{4,5},{5,4},{6,7},{7,6},{8,9},{9,8},{10,11... | collective-permute-start | bytes 1179656 | tf_op jit(solution)/shard_map/ppermute | solution.py:297
  75.6 20.0 %collective-permute-start.19 = (f32[12,128,128]{2,1,0:T(8,128)S(1)}, f32[12,128,128]{2,1,0:T(8,128)S(1)}, u32[]{:S(2)}, u32[]{:S(2)}) collective-permute-start(f32[12,128,128]{2,1,0:T(8,128)S(1)} %get-tuple-element.38.upper.refs_0_), channel_id=1, source_target_pairs={{0,2},{1,3},{2,0},{3,1},{4,6},{5,7},{6,4},{7,5},{8,10},{9,11},{10,... | collective-permute-start | bytes 2359304 | tf_op jit(solution)/shard_map/ppermute | solution.py:297
  77.8 7.1 %collective-permute-start.20 = (f32[12,16,128]{2,1,0:T(8,128)S(1)}, f32[12,16,128]{2,1,0:T(8,128)S(1)}, u32[]{:S(2)}, u32[]{:S(2)}) collective-permute-start(f32[12,16,128]{2,1,0:T(8,128)S(1)} %shard_map.95.x), channel_id=1, source_target_pairs={{0,4},{1,9},{2,6},{3,11},{4,8},{5,13},{6,10},{7,15},{8,12},{9,17},... | collective-permute-start | bytes 294920 | tf_op jit(solution)/shard_map/ppermute | solution.py:306
  85.3 1.4 collective-permute-start.21
  86.7 7.4 %collective-permute-start.22 = (f32[12,16,128]{2,1,0:T(8,128)S(1)}, f32[12,16,128]{2,1,0:T(8,128)S(1)}, u32[]{:S(2)}, u32[]{:S(2)}) collective-permute-start(f32[12,16,128]{2,1,0:T(8,128)S(1)} %add_subtract_fusion.5.x), channel_id=1, source_target_pairs={{0,4},{1,9},{2,6},{3,11},{4,8},{5,13},{6,10},{7,15},{8,12},{9,17},... | collective-permute-start | bytes 294920 | tf_op jit(solution)/shard_map/ppermute | solution.py:306
  94.6 1.4 collective-permute-start.23
  95.6 14.5 %collective-permute-start.26 = (f32[12,128,128]{2,1,0:T(8,128)S(1)}, f32[12,128,128]{2,1,0:T(8,128)S(1)}, u32[]{:S(2)}, u32[]{:S(2)}) collective-permute-start(f32[12,128,128]{2,1,0:T(8,128)S(1)} %collective-permute-done.19.refs_0_.refs_2_), channel_id=1, source_target_pairs={{0,1},{1,0},{2,3},{3,2},{4,5},{5,4},{6,7},{7,6},{8,9},{9,8},{10,11... | collective-permute-start | bytes 2359304 | tf_op jit(solution)/shard_map/ppermute | solution.py:297
  96.0 7.4 %collective-permute-start.24 = (f32[12,16,128]{2,1,0:T(8,128)S(1)}, f32[12,16,128]{2,1,0:T(8,128)S(1)}, u32[]{:S(2)}, u32[]{:S(2)}) collective-permute-start(f32[12,16,128]{2,1,0:T(8,128)S(1)} %add_subtract_fusion.4.x), channel_id=1, source_target_pairs={{0,4},{1,9},{2,6},{3,11},{4,8},{5,13},{6,10},{7,15},{8,12},{9,17},... | collective-permute-start | bytes 294920 | tf_op jit(solution)/shard_map/ppermute | solution.py:306
  103.9 1.4 collective-permute-start.25
  105.3 7.9 %collective-permute-start.27 = (f32[12,16,128]{2,1,0:T(8,128)S(1)}, f32[12,16,128]{2,1,0:T(8,128)S(1)}, u32[]{:S(2)}, u32[]{:S(2)}) collective-permute-start(f32[12,16,128]{2,1,0:T(8,128)S(1)} %add_subtract_fusion.3.x), channel_id=1, source_target_pairs={{4,0},{6,2},{8,4},{9,1},{10,6},{11,3},{12,8},{13,5},{14,10},{15,7}... | collective-permute-start | bytes 294920 | tf_op jit(solution)/shard_map/ppermute | solution.py:306
  113.7 1.4 collective-permute-start.28
  115.0 7.7 %collective-permute-start.29 = (f32[12,16,128]{2,1,0:T(8,128)S(1)}, f32[12,16,128]{2,1,0:T(8,128)S(1)}, u32[]{:S(2)}, u32[]{:S(2)}) collective-permute-start(f32[12,16,128]{2,1,0:T(8,128)S(1)} %add_subtract_fusion.2.x), channel_id=1, source_target_pairs={{4,0},{6,2},{8,4},{9,1},{10,6},{11,3},{12,8},{13,5},{14,10},{15,7}... | collective-permute-start | bytes 294920 | tf_op jit(solution)/shard_map/ppermute | solution.py:306
  123.3 1.4 collective-permute-start.30
  124.6 7.4 %collective-permute-start.31 = (f32[12,16,128]{2,1,0:T(8,128)S(1)}, f32[12,16,128]{2,1,0:T(8,128)S(1)}, u32[]{:S(2)}, u32[]{:S(2)}) collective-permute-start(f32[12,16,128]{2,1,0:T(8,128)S(1)} %add_subtract_fusion.1.x), channel_id=1, source_target_pairs={{4,0},{6,2},{8,4},{9,1},{10,6},{11,3},{12,8},{13,5},{14,10},{15,7}... | collective-permute-start | bytes 294920 | tf_op jit(solution)/shard_map/ppermute | solution.py:306
  132.5 1.4 collective-permute-start.32
  133.9 4.9 %collective-permute-start.33 = (f32[12,16,128]{2,1,0:T(8,128)S(1)}, f32[12,16,128]{2,1,0:T(8,128)S(1)}, u32[]{:S(2)}, u32[]{:S(2)}) collective-permute-start(f32[12,16,128]{2,1,0:T(8,128)S(1)} %add_subtract_fusion), channel_id=1, source_target_pairs={{0,2},{1,3},{2,0},{3,1},{4,6},{5,7},{6,4},{7,5},{8,10},{9,11},{10,... | collective-permute-start | bytes 294920 | tf_op jit(solution)/shard_map/ppermute | solution.py:297

commit v8 on v7

--- a/solution.py
+++ b/solution.py
@@ -207,7 +207,7 @@
 
 def table_kernel(lay, me, metas, peers_below, peers_above, out, *refs):
     masks, places = refs[:4], refs[4]
-    role = me[0] % 2
+    role = 1 - me[0] % 2
     out[2 * lay.table] = me[0]
     row = lax.broadcasted_iota(jnp.int32, masks[0].shape[1:], 0)
     for side in (1, 2):
@@ -235,7 +235,7 @@
 def scaled_kernel(lay, side, table, inverse, *refs):
     sources, (listed, local) = refs[:-2], refs[-2:]
     me = table[2 * lay.table]
-    role = me % 2
+    role = 1 - me % 2
     start = (side - 1) * lay.table
 
     def scaled(row, tile):
@@ -296,11 +296,11 @@
     def swap(x, bit):
         return lax.ppermute(x, "tile", [(i, i ^ bit) for i in range(n_tile)])
 
-    def along(x, sign):
+    def along(x, sign, swapped=0):
         route = []
         for d in range(n_dom):
             for t in range(n_tile):
-                to = d + sign * (1 + t % 2)
+                to = d + sign * (1 + (t + swapped) % 2)
                 if 0 <= to < n_dom:
                     route.append((d * n_tile + t, to * n_tile + t))
         return lax.ppermute(x, ("dom", "tile"), route)
@@ -328,10 +328,11 @@
     mate_tiles = swap(tiles, 1)
     arriving = over_chips(inverse_prev)
     mates = swap(mine, 1)
-    arriving, mine, mates = lax.optimization_barrier((arriving, mine, mates))
+    given = swap(inverse_prev, 1)
+    arriving, mine, mates, given = lax.optimization_barrier((arriving, mine, mates, given))
     near = jnp.stack([jnp.broadcast_to(me, mine.shape), mine, mates])
     kept = jnp.concatenate(arriving, 0)
-    mated = jnp.concatenate([swap(x, 1) for x in arriving], 0)
+    mated = jnp.concatenate([given] + [swap(x, 1) for x in arriving[1:]], 0)
     half = rows // 2
     lists, local_list = shape(2 * cap, n, n), shape(lay.pairs, n, n)
     places = pltpu.SMEM((lay.slots + 1,), jnp.int32)
@@ -382,7 +383,7 @@
         if sweep == FSWEEPS - 1:
             lower_locals = over_chips(lower_local)
             mate_lowers = [mate_lower] + [swap(x, 1) for x in lowers[1:]]
-            below, above = along(metas, 1), along(metas, -1)
+            below, above = along(metas, 1, 1), along(metas, -1, 1)
             mask = shape(lay.listed_slots, rows, n)
             table, *masks = call(
                 kernel(table_kernel),
@@ -427,7 +428,7 @@
     def sweeps(x, side, count, listed, local, early=()):
         base = x
         for sweep in range(count):
-            arrived = along(x, 1 if side == 1 else -1)
+            arrived = along(x, 1 if side == 1 else -1, 1)
             (here,) = call(
                 kernel(local_sum_kernel, side), [block], (table,), (x, local), flops=8 * n**2 * vectors * rows
             )

time: 141 us -> 141 us (level)
  starting transfers between devices: 51.8 us -> 42 us
  waiting for transfers between devices: 58.2 us -> 65.9 us
    ppermute x10, starting transfers between devices: 37 us -> 26 us  [along(): return lax.ppermute(x, ('dom', 'tile'), route)]
    ppermute x10, waiting for transfers between devices: 20.7 us -> 30.6 us  [along(): return lax.ppermute(x, ('dom', 'tile'), route)]
    ppermute x24, waiting for transfers between devices: 37.5 us -> 35.3 us  [swap(): return lax.ppermute(x, 'tile', [(i, i ^ bit) for i in range(n_tile)])]
  transfers between devices with their start and end apart: 34 -> 34, of which waited for: 25 -> 26; matrix products, arithmetic and copies ran while one was open for 3% -> 4% of each run, Pallas kernels for 12% -> 12%
where the time goes in v8:
time: 141 us; the launch traced here: 139 us
  waiting for transfers between devices  65.9 us (47%)
  starting transfers between devices  42 us (30%)
  Pallas kernels  22.7 us (16%)
  local copies, waits for them, and re-layouts  4.74 us (3%)
  other arithmetic  1.99 us (1%)
    ppermute x24, waiting for transfers between devices, swap(): return lax.ppermute(x, 'tile', [(i, i ^ bit) for i in range(n_tile)])  35.3 us
    ppermute x10, waiting for transfers between devices, along(): return lax.ppermute(x, ('dom', 'tile'), route)  30.6 us
    ppermute x10, starting transfers between devices, along(): return lax.ppermute(x, ('dom', 'tile'), route)  26 us
    pallas_call x24, Pallas kernels, call(): pl.pallas_call(body if not early else lambda *refs: body(*refs[len(early)...  22.7 us
    ppermute x24, starting transfers between devices, swap(): return lax.ppermute(x, 'tile', [(i, i ^ bit) for i in range(n_tile)])  16.1 us
  transfers between devices with their start and end apart: 34, of which 26 were waited for; matrix products, arithmetic and copies ran while one was open for 4% of the time, Pallas kernels for 12%

profile of v8, /device:TPU:18, one launch (start us, length us, event | category | flops | bytes accessed | tf_op | source)
XLA Modules:
  0.0 138.6 jit_solution(13905607072433532410)
XLA Ops:
  0.7 1.6 %collective-permute-start = (f32[3,128,128]{2,1,0:T(8,128)}, f32[3,128,128]{2,1,0:T(8,128)S(1)}, u32[]{:S(2)}, u32[]{:S(2)}) collective-permute-start(f32[3,128,128]{2,1,0:T(8,128)} %param.9), channel_id=1, source_target_pairs={{0,2},{1,3},{2,0},{3,1},{4,6},{5,7},{6,4},{7,5},{8,10},{9,11},{10,... | collective-permute-start | bytes 589832 | tf_op jit(solution)/shard_map/ppermute | solution.py:297
  8.3 0.9 constant_dynamic-update-slice_fusion.3
  9.7 0.9 shard_map.87
  10.7 3.5 %collective-permute-start.9 = (f32[8,128,128]{2,1,0:T(8,128)S(1)}, f32[8,128,128]{2,1,0:T(8,128)S(1)}, u32[]{:S(2)}, u32[]{:S(2)}) collective-permute-start(f32[8,128,128]{2,1,0:T(8,128)S(1)} %get-tuple-element.36), channel_id=1, source_target_pairs={{0,4},{1,9},{2,6},{3,11},{4,8},{5,13},{6,10},{7,15},{8,12},{9,17},... | collective-permute-start | bytes 1572872 | tf_op jit(solution)/shard_map/ppermute | solution.py:306
  14.2 1.6 %collective-permute-start.8 = (f32[8,128,128]{2,1,0:T(8,128)S(1)}, f32[8,128,128]{2,1,0:T(8,128)S(1)}, u32[]{:S(2)}, u32[]{:S(2)}) collective-permute-start(f32[8,128,128]{2,1,0:T(8,128)S(1)} %get-tuple-element.33.refs_3_.refs_6_.refs_0_), channel_id=1, source_target_pairs={{0,2},{1,3},{2,0},{3,1},{4,6},{5,7},{6,4},{7,5},{8,10},{9,11},{10,... | collective-permute-start | bytes 1572872 | tf_op jit(solution)/shard_map/ppermute | solution.py:297
  15.7 2.8 %shard_map.88 = (f32[12,128,128]{2,1,0:T(8,128)S(1)}, f32[8,128,128]{2,1,0:T(8,128)S(1)}, f32[4,128,128]{2,1,0:T(8,128)S(1)}, f32[12,128,128]{2,1,0:T(8,128)S(1)}, f32[8,128,128]{2,1,0:T(8,128)S(1)}) custom-call(s32[3,64]{1,0:T(4,128)S(1)} %pad_add_fusion.1.near_source.near.refs_1_.refs_4_, f32[12,128,128]{2,1,0:T(8,128)S(1)} %constant_dynamic-update-slice_fusion.inverse, ...), custom_call_target="tpu_custom_call" | custom-call | flops 201326592 | bytes 7012352 | tf_op jit(solution)/shard_map/pallas_call | solution.py:101
  18.5 7.1 %collective-permute-done.9.refs_5_ = f32[8,128,128]{2,1,0:T(8,128)S(1)} collective-permute-done((f32[8,128,128]{2,1,0:T(8,128)S(1)}, f32[8,128,128]{2,1,0:T(8,128)S(1)}, u32[]{:S(2)}, u32[]{:S(2)}) %collective-permute-start.9) | collective-permute-done | bytes 524320 | tf_op jit(solution)/shard_map/ppermute | solution.py:306
  25.6 2.3 %collective-permute-done.8.refs_0_.refs_3_ = f32[8,128,128]{2,1,0:T(8,128)S(1)} collective-permute-done((f32[8,128,128]{2,1,0:T(8,128)S(1)}, f32[8,128,128]{2,1,0:T(8,128)S(1)}, u32[]{:S(2)}, u32[]{:S(2)}) %collective-permute-start.8) | collective-permute-done | bytes 524320 | tf_op jit(solution)/shard_map/ppermute | solution.py:297
  27.9 1.1 shard_map.89
  29.1 1.7 %collective-permute-done.10 = f32[6,128,128]{2,1,0:T(8,128)S(1)} collective-permute-done((f32[6,128,128]{2,1,0:T(8,128)S(1)}, f32[6,128,128]{2,1,0:T(8,128)S(1)}, u32[]{:S(2)}, u32[]{:S(2)}) %collective-permute-start.10) | collective-permute-done | bytes 393248 | tf_op jit(solution)/shard_map/ppermute | solution.py:297
  30.8 1.6 %collective-permute-start.11 = (f32[6,128,128]{2,1,0:T(8,128)S(1)}, f32[6,128,128]{2,1,0:T(8,128)S(1)}, u32[]{:S(2)}, u32[]{:S(2)}) collective-permute-start(f32[6,128,128]{2,1,0:T(8,128)S(1)} %add.30), channel_id=1, source_target_pairs={{0,2},{1,3},{2,0},{3,1},{4,6},{5,7},{6,4},{7,5},{8,10},{9,11},{10,... | collective-permute-start | bytes 1179656 | tf_op jit(solution)/shard_map/ppermute | solution.py:297
  33.0 9.1 %collective-permute-done.3 = s32[2,64]{1,0:T(2,128)S(1)} collective-permute-done((s32[2,64]{1,0:T(2,128)S(1)}, s32[2,64]{1,0:T(2,128)S(1)}, u32[]{:S(2)}, u32[]{:S(2)}) %collective-permute-start.3) | collective-permute-done | bytes 544 | tf_op jit(solution)/shard_map/ppermute | solution.py:297
  43.3 1.2 collective-permute-done.14
  45.5 3.0 %collective-permute-start.15 = (f32[8,128,128]{2,1,0:T(8,128)S(1)}, f32[8,128,128]{2,1,0:T(8,128)S(1)}, u32[]{:S(2)}, u32[]{:S(2)}) collective-permute-start(f32[8,128,128]{2,1,0:T(8,128)S(1)} %shard_map.92), channel_id=1, source_target_pairs={{0,4},{1,9},{2,6},{3,11},{4,8},{5,13},{6,10},{7,15},{8,12},{9,17},... | collective-permute-start | bytes 1572872 | tf_op jit(solution)/shard_map/ppermute | solution.py:306
  48.5 1.6 %collective-permute-start.12 = (f32[4,128,128]{2,1,0:T(8,128)S(1)}, f32[4,128,128]{2,1,0:T(8,128)S(1)}, u32[]{:S(2)}, u32[]{:S(2)}) collective-permute-start(f32[4,128,128]{2,1,0:T(8,128)S(1)} %get-tuple-element.39.refs_1_), channel_id=1, source_target_pairs={{0,2},{1,3},{2,0},{3,1},{4,6},{5,7},{6,4},{7,5},{8,10},{9,11},{10,... | collective-permute-start | bytes 786440 | tf_op jit(solution)/shard_map/ppermute | solution.py:297
  50.1 2.8 %collective-permute-start.5 = (s32[4,64]{1,0:T(4,128)S(1)}, s32[4,64]{1,0:T(4,128)S(1)}, u32[]{:S(2)}, u32[]{:S(2)}) collective-permute-start(s32[4,64]{1,0:T(4,128)S(1)} %pad_add_fusion.metas.refs_0_), channel_id=1, source_target_pairs={{5,1},{7,3},{8,0},{9,5},{10,2},{11,7},{12,4},{13,9},{14,6},{15,11}... | collective-permute-start | bytes 3080 | tf_op jit(solution)/shard_map/ppermute | solution.py:306
  52.9 3.0 %collective-permute-start.4 = (s32[4,64]{1,0:T(4,128)S(1)}, s32[4,64]{1,0:T(4,128)S(1)}, u32[]{:S(2)}, u32[]{:S(2)}) collective-permute-start(s32[4,64]{1,0:T(4,128)S(1)} %pad_add_fusion.metas.refs_0_), channel_id=1, source_target_pairs={{0,8},{1,5},{2,10},{3,7},{4,12},{5,9},{6,14},{7,11},{8,16},{9,13},... | collective-permute-start | bytes 3080 | tf_op jit(solution)/shard_map/ppermute | solution.py:306
  55.9 2.4 %shard_map.91.refs_5_ = f32[12,128,128]{2,1,0:T(8,128)S(1)} custom-call(s32[3,64]{1,0:T(4,128)S(1)} %pad_add_fusion.1.near_source.near.refs_1_.refs_4_, f32[12,128,128]{2,1,0:T(8,128)S(1)} %pad_maximum_fusion.inverse, f32[3,128,128]{2,1,0:T(8,128)S(1)} %copy-done.1, f32[24,128,128]{2,1,0:T(8,128)S(1)} %bitcast.14), custom_call_target="tpu_custom_call" | custom-call | flops 201326592 | bytes 3342336 | tf_op jit(solution)/shard_map/pallas_call | solution.py:101
  58.3 3.1 %collective-permute-done.4.peers_below.refs_2_ = s32[4,64]{1,0:T(4,128)S(1)} collective-permute-done((s32[4,64]{1,0:T(4,128)S(1)}, s32[4,64]{1,0:T(4,128)S(1)}, u32[]{:S(2)}, u32[]{:S(2)}) %collective-permute-start.4) | collective-permute-done | bytes 1056 | tf_op jit(solution)/shard_map/ppermute | solution.py:306
  61.4 1.1 shard_map.93
  62.6 1.7 %collective-permute-done.16 = f32[6,128,128]{2,1,0:T(8,128)S(1)} collective-permute-done((f32[6,128,128]{2,1,0:T(8,128)S(1)}, f32[6,128,128]{2,1,0:T(8,128)S(1)}, u32[]{:S(2)}, u32[]{:S(2)}) %collective-permute-start.16) | collective-permute-done | bytes 393248 | tf_op jit(solution)/shard_map/ppermute | solution.py:297
  64.3 1.6 %collective-permute-start.17 = (f32[6,128,128]{2,1,0:T(8,128)S(1)}, f32[6,128,128]{2,1,0:T(8,128)S(1)}, u32[]{:S(2)}, u32[]{:S(2)}) collective-permute-start(f32[6,128,128]{2,1,0:T(8,128)S(1)} %add.32), channel_id=1, source_target_pairs={{0,2},{1,3},{2,0},{3,1},{4,6},{5,7},{6,4},{7,5},{8,10},{9,11},{10,... | collective-permute-start | bytes 1179656 | tf_op jit(solution)/shard_map/ppermute | solution.py:297
  65.9 2.1 %shard_map.86 = (s32[65]{0:T(128)S(1)}, f32[16,12,128]{2,1,0:T(8,128)S(1)}, f32[16,12,128]{2,1,0:T(8,128)S(1)}, f32[16,12,128]{2,1,0:T(8,128)S(1)}, f32[16,12,128]{2,1,0:T(8,128)S(1)}) custom-call(s32[1]{0:T(128)} %bitcast.me, s32[4,64]{1,0:T(4,128)S(1)} %pad_add_fusion.metas.refs_0_, s32[4,64]{1,0:T(4,128)S(1)} %collective-permute-done.4.peers_below.refs_2_, ...), custom_call_target="tpu_custom_call" | custom-call | bytes 393476 | tf_op jit(solution)/shard_map/pallas_call | solution.py:101
  68.0 7.5 %collective-permute-done.17 = f32[6,128,128]{2,1,0:T(8,128)S(1)} collective-permute-done((f32[6,128,128]{2,1,0:T(8,128)S(1)}, f32[6,128,128]{2,1,0:T(8,128)S(1)}, u32[]{:S(2)}, u32[]{:S(2)}) %collective-permute-start.17) | collective-permute-done | bytes 393248 | tf_op jit(solution)/shard_map/ppermute | solution.py:297
  76.2 1.6 %collective-permute-start.19 = (f32[12,128,128]{2,1,0:T(8,128)S(1)}, f32[12,128,128]{2,1,0:T(8,128)S(1)}, u32[]{:S(2)}, u32[]{:S(2)}) collective-permute-start(f32[12,128,128]{2,1,0:T(8,128)S(1)} %get-tuple-element.40.upper.refs_0_), channel_id=1, source_target_pairs={{0,2},{1,3},{2,0},{3,1},{4,6},{5,7},{6,4},{7,5},{8,10},{9,11},{10,... | collective-permute-start | bytes 2359304 | tf_op jit(solution)/shard_map/ppermute | solution.py:297
  78.4 2.2 %collective-permute-start.20 = (f32[12,16,128]{2,1,0:T(8,128)S(1)}, f32[12,16,128]{2,1,0:T(8,128)S(1)}, u32[]{:S(2)}, u32[]{:S(2)}) collective-permute-start(f32[12,16,128]{2,1,0:T(8,128)S(1)} %shard_map.95.x), channel_id=1, source_target_pairs={{0,8},{1,5},{2,10},{3,7},{4,12},{5,9},{6,14},{7,11},{8,16},{9,13},... | collective-permute-start | bytes 294920 | tf_op jit(solution)/shard_map/ppermute | solution.py:306
  80.6 1.2 shard_map.96
  82.7 3.3 %collective-permute-done.20.arrived = f32[12,16,128]{2,1,0:T(8,128)S(1)} collective-permute-done((f32[12,16,128]{2,1,0:T(8,128)S(1)}, f32[12,16,128]{2,1,0:T(8,128)S(1)}, u32[]{:S(2)}, u32[]{:S(2)}) %collective-permute-start.20) | collective-permute-done | bytes 98336 | tf_op jit(solution)/shard_map/ppermute | solution.py:306
  86.5 1.3 collective-permute-done.21
  87.8 2.2 %collective-permute-start.22 = (f32[12,16,128]{2,1,0:T(8,128)S(1)}, f32[12,16,128]{2,1,0:T(8,128)S(1)}, u32[]{:S(2)}, u32[]{:S(2)}) collective-permute-start(f32[12,16,128]{2,1,0:T(8,128)S(1)} %add_subtract_fusion.5.x), channel_id=1, source_target_pairs={{0,8},{1,5},{2,10},{3,7},{4,12},{5,9},{6,14},{7,11},{8,16},{9,13},... | collective-permute-start | bytes 294920 | tf_op jit(solution)/shard_map/ppermute | solution.py:306
  90.8 4.3 %collective-permute-done.22.arrived = f32[12,16,128]{2,1,0:T(8,128)S(1)} collective-permute-done((f32[12,16,128]{2,1,0:T(8,128)S(1)}, f32[12,16,128]{2,1,0:T(8,128)S(1)}, u32[]{:S(2)}, u32[]{:S(2)}) %collective-permute-start.22) | collective-permute-done | bytes 98336 | tf_op jit(solution)/shard_map/ppermute | solution.py:306
  97.0 2.2 %collective-permute-start.24 = (f32[12,16,128]{2,1,0:T(8,128)S(1)}, f32[12,16,128]{2,1,0:T(8,128)S(1)}, u32[]{:S(2)}, u32[]{:S(2)}) collective-permute-start(f32[12,16,128]{2,1,0:T(8,128)S(1)} %add_subtract_fusion.4.x), channel_id=1, source_target_pairs={{0,8},{1,5},{2,10},{3,7},{4,12},{5,9},{6,14},{7,11},{8,16},{9,13},... | collective-permute-start | bytes 294920 | tf_op jit(solution)/shard_map/ppermute | solution.py:306
  100.0 4.1 %collective-permute-done.24.refs_5_ = f32[12,16,128]{2,1,0:T(8,128)S(1)} collective-permute-done((f32[12,16,128]{2,1,0:T(8,128)S(1)}, f32[12,16,128]{2,1,0:T(8,128)S(1)}, u32[]{:S(2)}, u32[]{:S(2)}) %collective-permute-start.24) | collective-permute-done | bytes 98336 | tf_op jit(solution)/shard_map/ppermute | solution.py:306
  104.7 1.3 collective-permute-done.25
  106.0 2.4 %collective-permute-start.27 = (f32[12,16,128]{2,1,0:T(8,128)S(1)}, f32[12,16,128]{2,1,0:T(8,128)S(1)}, u32[]{:S(2)}, u32[]{:S(2)}) collective-permute-start(f32[12,16,128]{2,1,0:T(8,128)S(1)} %add_subtract_fusion.3.x), channel_id=1, source_target_pairs={{5,1},{7,3},{8,0},{9,5},{10,2},{11,7},{12,4},{13,9},{14,6},{15,11}... | collective-permute-start | bytes 294920 | tf_op jit(solution)/shard_map/ppermute | solution.py:306
  108.4 1.3 shard_map.103
  110.5 2.0 %collective-permute-done.27.arrived = f32[12,16,128]{2,1,0:T(8,128)S(1)} collective-permute-done((f32[12,16,128]{2,1,0:T(8,128)S(1)}, f32[12,16,128]{2,1,0:T(8,128)S(1)}, u32[]{:S(2)}, u32[]{:S(2)}) %collective-permute-start.27) | collective-permute-done | bytes 98336 | tf_op jit(solution)/shard_map/ppermute | solution.py:306
  113.0 1.0 collective-permute-start.28
  114.0 0.9 collective-permute-done.28
  115.0 2.4 %collective-permute-start.29 = (f32[12,16,128]{2,1,0:T(8,128)S(1)}, f32[12,16,128]{2,1,0:T(8,128)S(1)}, u32[]{:S(2)}, u32[]{:S(2)}) collective-permute-start(f32[12,16,128]{2,1,0:T(8,128)S(1)} %add_subtract_fusion.2.x), channel_id=1, source_target_pairs={{5,1},{7,3},{8,0},{9,5},{10,2},{11,7},{12,4},{13,9},{14,6},{15,11}... | collective-permute-start | bytes 294920 | tf_op jit(solution)/shard_map/ppermute | solution.py:306
  118.2 3.3 %collective-permute-done.29.arrived = f32[12,16,128]{2,1,0:T(8,128)S(1)} collective-permute-done((f32[12,16,128]{2,1,0:T(8,128)S(1)}, f32[12,16,128]{2,1,0:T(8,128)S(1)}, u32[]{:S(2)}, u32[]{:S(2)}) %collective-permute-start.29) | collective-permute-done | bytes 98336 | tf_op jit(solution)/shard_map/ppermute | solution.py:306
  122.0 1.0 collective-permute-start.30
  123.0 0.9 collective-permute-done.30
  124.0 2.4 %collective-permute-start.31 = (f32[12,16,128]{2,1,0:T(8,128)S(1)}, f32[12,16,128]{2,1,0:T(8,128)S(1)}, u32[]{:S(2)}, u32[]{:S(2)}) collective-permute-start(f32[12,16,128]{2,1,0:T(8,128)S(1)} %add_subtract_fusion.1.x), channel_id=1, source_target_pairs={{5,1},{7,3},{8,0},{9,5},{10,2},{11,7},{12,4},{13,9},{14,6},{15,11}... | collective-permute-start | bytes 294920 | tf_op jit(solution)/shard_map/ppermute | solution.py:306
  127.2 3.3 %collective-permute-done.31.arrived = f32[12,16,128]{2,1,0:T(8,128)S(1)} collective-permute-done((f32[12,16,128]{2,1,0:T(8,128)S(1)}, f32[12,16,128]{2,1,0:T(8,128)S(1)}, u32[]{:S(2)}, u32[]{:S(2)}) %collective-permute-start.31) | collective-permute-done | bytes 98336 | tf_op jit(solution)/shard_map/ppermute | solution.py:306
  131.8 0.9 collective-permute-done.32
  132.8 1.6 %collective-permute-start.33 = (f32[12,16,128]{2,1,0:T(8,128)S(1)}, f32[12,16,128]{2,1,0:T(8,128)S(1)}, u32[]{:S(2)}, u32[]{:S(2)}) collective-permute-start(f32[12,16,128]{2,1,0:T(8,128)S(1)} %add_subtract_fusion), channel_id=1, source_target_pairs={{0,2},{1,3},{2,0},{3,1},{4,6},{5,7},{6,4},{7,5},{8,10},{9,11},{10,... | collective-permute-start | bytes 294920 | tf_op jit(solution)/shard_map/ppermute | solution.py:297
  135.1 2.8 %collective-permute-done.33 = f32[12,16,128]{2,1,0:T(8,128)S(1)} collective-permute-done((f32[12,16,128]{2,1,0:T(8,128)S(1)}, f32[12,16,128]{2,1,0:T(8,128)S(1)}, u32[]{:S(2)}, u32[]{:S(2)}) %collective-permute-start.33) | collective-permute-done | bytes 98336 | tf_op jit(solution)/shard_map/ppermute | solution.py:297
  (85 shorter events, 22.1 us)
Async XLA Ops:
  0.6 9.1 %copy-start = (f32[12,2,128,128]{3,2,1,0:T(8,128)S(1)}, f32[12,2,128,128]{3,2,1,0:T(8,128)}, u32[]{:S(2)}) copy-start(f32[12,2,128,128]{3,2,1,0:T(8,128)} %param.10) | copy-start | bytes 4718596
  0.6 9.1 %collective-permute-start.7 = (f32[24,128,128]{2,1,0:T(8,128)}, f32[24,128,128]{2,1,0:T(8,128)S(1)}, u32[]{:S(2)}, u32[]{:S(2)}) collective-permute-start(f32[24,128,128]{2,1,0:T(8,128)} %bitcast.11), channel_id=1, source_target_pairs={{0,1},{1,0},{2,3},{3,2},{4,5},{5,4},{6,7},{7,6},{8,9},{9,8},{10,11... | collective-permute-start | bytes 4718600 | tf_op jit(solution)/shard_map/ppermute | solution.py:297
  0.7 7.5 %collective-permute-start = (f32[3,128,128]{2,1,0:T(8,128)}, f32[3,128,128]{2,1,0:T(8,128)S(1)}, u32[]{:S(2)}, u32[]{:S(2)}) collective-permute-start(f32[3,128,128]{2,1,0:T(8,128)} %param.9), channel_id=1, source_target_pairs={{0,2},{1,3},{2,0},{3,1},{4,6},{5,7},{6,4},{7,5},{8,10},{9,11},{10,... | collective-permute-start | bytes 589832 | tf_op jit(solution)/shard_map/ppermute | solution.py:297
  2.3 5.9 %collective-permute-start.2 = (f32[3,128,128]{2,1,0:T(8,128)}, f32[3,128,128]{2,1,0:T(8,128)S(1)}, u32[]{:S(2)}, u32[]{:S(2)}) collective-permute-start(f32[3,128,128]{2,1,0:T(8,128)} %param.9), channel_id=1, source_target_pairs={{0,1},{1,0},{2,3},{3,2},{4,5},{5,4},{6,7},{7,6},{8,9},{9,8},{10,11... | collective-permute-start | bytes 589832 | tf_op jit(solution)/shard_map/ppermute | solution.py:297
  6.2 1.2 collective-permute-start.1
  8.3 1.4 %collective-permute-start.6 = (f32[3,128,128]{2,1,0:T(8,128)S(1)}, f32[3,128,128]{2,1,0:T(8,128)S(1)}, u32[]{:S(2)}, u32[]{:S(2)}) collective-permute-start(f32[3,128,128]{2,1,0:T(8,128)S(1)} %collective-permute-done), channel_id=1, source_target_pairs={{0,1},{1,0},{2,3},{3,2},{4,5},{5,4},{6,7},{7,6},{8,9},{9,8},{10,11... | collective-permute-start | bytes 589832 | tf_op jit(solution)/shard_map/ppermute | solution.py:297
  9.7 6.0 %copy-start.1 = (f32[3,128,128]{2,1,0:T(8,128)S(1)}, f32[3,128,128]{2,1,0:T(8,128)}, u32[]{:S(2)}) copy-start(f32[3,128,128]{2,1,0:T(8,128)} %diag.3) | copy-start | bytes 589828
  10.7 14.9 %collective-permute-start.9 = (f32[8,128,128]{2,1,0:T(8,128)S(1)}, f32[8,128,128]{2,1,0:T(8,128)S(1)}, u32[]{:S(2)}, u32[]{:S(2)}) collective-permute-start(f32[8,128,128]{2,1,0:T(8,128)S(1)} %get-tuple-element.36), channel_id=1, source_target_pairs={{0,4},{1,9},{2,6},{3,11},{4,8},{5,13},{6,10},{7,15},{8,12},{9,17},... | collective-permute-start | bytes 1572872 | tf_op jit(solution)/shard_map/ppermute | solution.py:306
  14.2 13.8 %collective-permute-start.8 = (f32[8,128,128]{2,1,0:T(8,128)S(1)}, f32[8,128,128]{2,1,0:T(8,128)S(1)}, u32[]{:S(2)}, u32[]{:S(2)}) collective-permute-start(f32[8,128,128]{2,1,0:T(8,128)S(1)} %get-tuple-element.33.refs_3_.refs_6_.refs_0_), channel_id=1, source_target_pairs={{0,2},{1,3},{2,0},{3,1},{4,6},{5,7},{6,4},{7,5},{8,10},{9,11},{10,... | collective-permute-start | bytes 1572872 | tf_op jit(solution)/shard_map/ppermute | solution.py:297
  27.9 5.0 %copy-start.3 = (f32[3,128,128]{2,1,0:T(8,128)S(1)}, f32[3,128,128]{2,1,0:T(8,128)}, u32[]{:S(2)}) copy-start(f32[3,128,128]{2,1,0:T(8,128)} %param.9) | copy-start | bytes 589828
  29.0 1.8 %collective-permute-start.10 = (f32[6,128,128]{2,1,0:T(8,128)S(1)}, f32[6,128,128]{2,1,0:T(8,128)S(1)}, u32[]{:S(2)}, u32[]{:S(2)}) collective-permute-start(f32[6,128,128]{2,1,0:T(8,128)S(1)} %get-tuple-element.38), channel_id=1, source_target_pairs={{0,1},{1,0},{2,3},{3,2},{4,5},{5,4},{6,7},{7,6},{8,9},{9,8},{10,11... | collective-permute-start | bytes 1179656 | tf_op jit(solution)/shard_map/ppermute | solution.py:297
  30.8 11.3 %collective-permute-start.11 = (f32[6,128,128]{2,1,0:T(8,128)S(1)}, f32[6,128,128]{2,1,0:T(8,128)S(1)}, u32[]{:S(2)}, u32[]{:S(2)}) collective-permute-start(f32[6,128,128]{2,1,0:T(8,128)S(1)} %add.30), channel_id=1, source_target_pairs={{0,2},{1,3},{2,0},{3,1},{4,6},{5,7},{6,4},{7,5},{8,10},{9,11},{10,... | collective-permute-start | bytes 1179656 | tf_op jit(solution)/shard_map/ppermute | solution.py:297
  32.4 9.7 %collective-permute-start.3 = (s32[2,64]{1,0:T(2,128)S(1)}, s32[2,64]{1,0:T(2,128)S(1)}, u32[]{:S(2)}, u32[]{:S(2)}) collective-permute-start(s32[2,64]{1,0:T(2,128)S(1)} %pad_add_fusion.2), channel_id=1, source_target_pairs={{0,2},{1,3},{2,0},{3,1},{4,6},{5,7},{6,4},{7,5},{8,10},{9,11},{10,... | collective-permute-start | bytes 1544 | tf_op jit(solution)/shard_map/ppermute | solution.py:297
  42.7 1.8 %collective-permute-start.14 = (f32[6,128,128]{2,1,0:T(8,128)S(1)}, f32[6,128,128]{2,1,0:T(8,128)S(1)}, u32[]{:S(2)}, u32[]{:S(2)}) collective-permute-start(f32[6,128,128]{2,1,0:T(8,128)S(1)} %shard_map.90.refs_1_), channel_id=1, source_target_pairs={{0,1},{1,0},{2,3},{3,2},{4,5},{5,4},{6,7},{7,6},{8,9},{9,8},{10,11... | collective-permute-start | bytes 1179656 | tf_op jit(solution)/shard_map/ppermute | solution.py:297
  42.8 18.6 %collective-permute-start.13 = (f32[8,128,128]{2,1,0:T(8,128)S(1)}, f32[8,128,128]{2,1,0:T(8,128)S(1)}, u32[]{:S(2)}, u32[]{:S(2)}) collective-permute-start(f32[8,128,128]{2,1,0:T(8,128)S(1)} %collective-permute-done.8.refs_0_.refs_3_), channel_id=1, source_target_pairs={{0,1},{1,0},{2,3},{3,2},{4,5},{5,4},{6,7},{7,6},{8,9},{9,8},{10,11... | collective-permute-start | bytes 1572872 | tf_op jit(solution)/shard_map/ppermute | solution.py:297
  45.5 15.9 %collective-permute-start.15 = (f32[8,128,128]{2,1,0:T(8,128)S(1)}, f32[8,128,128]{2,1,0:T(8,128)S(1)}, u32[]{:S(2)}, u32[]{:S(2)}) collective-permute-start(f32[8,128,128]{2,1,0:T(8,128)S(1)} %shard_map.92), channel_id=1, source_target_pairs={{0,4},{1,9},{2,6},{3,11},{4,8},{5,13},{6,10},{7,15},{8,12},{9,17},... | collective-permute-start | bytes 1572872 | tf_op jit(solution)/shard_map/ppermute | solution.py:306
  48.5 12.9 %collective-permute-start.12 = (f32[4,128,128]{2,1,0:T(8,128)S(1)}, f32[4,128,128]{2,1,0:T(8,128)S(1)}, u32[]{:S(2)}, u32[]{:S(2)}) collective-permute-start(f32[4,128,128]{2,1,0:T(8,128)S(1)} %get-tuple-element.39.refs_1_), channel_id=1, source_target_pairs={{0,2},{1,3},{2,0},{3,1},{4,6},{5,7},{6,4},{7,5},{8,10},{9,11},{10,... | collective-permute-start | bytes 786440 | tf_op jit(solution)/shard_map/ppermute | solution.py:297
  50.1 8.2 %collective-permute-start.5 = (s32[4,64]{1,0:T(4,128)S(1)}, s32[4,64]{1,0:T(4,128)S(1)}, u32[]{:S(2)}, u32[]{:S(2)}) collective-permute-start(s32[4,64]{1,0:T(4,128)S(1)} %pad_add_fusion.metas.refs_0_), channel_id=1, source_target_pairs={{5,1},{7,3},{8,0},{9,5},{10,2},{11,7},{12,4},{13,9},{14,6},{15,11}... | collective-permute-start | bytes 3080 | tf_op jit(solution)/shard_map/ppermute | solution.py:306
  52.9 8.5 %collective-permute-start.4 = (s32[4,64]{1,0:T(4,128)S(1)}, s32[4,64]{1,0:T(4,128)S(1)}, u32[]{:S(2)}, u32[]{:S(2)}) collective-permute-start(s32[4,64]{1,0:T(4,128)S(1)} %pad_add_fusion.metas.refs_0_), channel_id=1, source_target_pairs={{0,8},{1,5},{2,10},{3,7},{4,12},{5,9},{6,14},{7,11},{8,16},{9,13},... | collective-permute-start | bytes 3080 | tf_op jit(solution)/shard_map/ppermute | solution.py:306
  62.5 1.8 %collective-permute-start.16 = (f32[6,128,128]{2,1,0:T(8,128)S(1)}, f32[6,128,128]{2,1,0:T(8,128)S(1)}, u32[]{:S(2)}, u32[]{:S(2)}) collective-permute-start(f32[6,128,128]{2,1,0:T(8,128)S(1)} %get-tuple-element.43), channel_id=1, source_target_pairs={{0,1},{1,0},{2,3},{3,2},{4,5},{5,4},{6,7},{7,6},{8,9},{9,8},{10,11... | collective-permute-start | bytes 1179656 | tf_op jit(solution)/shard_map/ppermute | solution.py:297
  64.3 11.2 %collective-permute-start.17 = (f32[6,128,128]{2,1,0:T(8,128)S(1)}, f32[6,128,128]{2,1,0:T(8,128)S(1)}, u32[]{:S(2)}, u32[]{:S(2)}) collective-permute-start(f32[6,128,128]{2,1,0:T(8,128)S(1)} %add.32), channel_id=1, source_target_pairs={{0,2},{1,3},{2,0},{3,1},{4,6},{5,7},{6,4},{7,5},{8,10},{9,11},{10,... | collective-permute-start | bytes 1179656 | tf_op jit(solution)/shard_map/ppermute | solution.py:297
  75.6 2.4 %copy-start.2 = (f32[12,32,128]{2,1,0:T(8,128)S(1)}, f32[12,32,128]{2,1,0:T(8,128)}, u32[]{:S(2)}) copy-start(f32[12,32,128]{2,1,0:T(8,128)} %base.1) | copy-start | bytes 589828
  76.1 1.8 %collective-permute-start.18 = (f32[6,128,128]{2,1,0:T(8,128)S(1)}, f32[6,128,128]{2,1,0:T(8,128)S(1)}, u32[]{:S(2)}, u32[]{:S(2)}) collective-permute-start(f32[6,128,128]{2,1,0:T(8,128)S(1)} %shard_map.94), channel_id=1, source_target_pairs={{0,1},{1,0},{2,3},{3,2},{4,5},{5,4},{6,7},{7,6},{8,9},{9,8},{10,11... | collective-permute-start | bytes 1179656 | tf_op jit(solution)/shard_map/ppermute | solution.py:297
  76.2 20.0 %collective-permute-start.19 = (f32[12,128,128]{2,1,0:T(8,128)S(1)}, f32[12,128,128]{2,1,0:T(8,128)S(1)}, u32[]{:S(2)}, u32[]{:S(2)}) collective-permute-start(f32[12,128,128]{2,1,0:T(8,128)S(1)} %get-tuple-element.40.upper.refs_0_), channel_id=1, source_target_pairs={{0,2},{1,3},{2,0},{3,1},{4,6},{5,7},{6,4},{7,5},{8,10},{9,11},{10,... | collective-permute-start | bytes 2359304 | tf_op jit(solution)/shard_map/ppermute | solution.py:297
  78.4 7.6 %collective-permute-start.20 = (f32[12,16,128]{2,1,0:T(8,128)S(1)}, f32[12,16,128]{2,1,0:T(8,128)S(1)}, u32[]{:S(2)}, u32[]{:S(2)}) collective-permute-start(f32[12,16,128]{2,1,0:T(8,128)S(1)} %shard_map.95.x), channel_id=1, source_target_pairs={{0,8},{1,5},{2,10},{3,7},{4,12},{5,9},{6,14},{7,11},{8,16},{9,13},... | collective-permute-start | bytes 294920 | tf_op jit(solution)/shard_map/ppermute | solution.py:306
  86.4 1.4 collective-permute-start.21
  87.8 7.3 %collective-permute-start.22 = (f32[12,16,128]{2,1,0:T(8,128)S(1)}, f32[12,16,128]{2,1,0:T(8,128)S(1)}, u32[]{:S(2)}, u32[]{:S(2)}) collective-permute-start(f32[12,16,128]{2,1,0:T(8,128)S(1)} %add_subtract_fusion.5.x), channel_id=1, source_target_pairs={{0,8},{1,5},{2,10},{3,7},{4,12},{5,9},{6,14},{7,11},{8,16},{9,13},... | collective-permute-start | bytes 294920 | tf_op jit(solution)/shard_map/ppermute | solution.py:306
  95.6 1.4 collective-permute-start.23
  96.2 12.2 %collective-permute-start.26 = (f32[12,128,128]{2,1,0:T(8,128)S(1)}, f32[12,128,128]{2,1,0:T(8,128)S(1)}, u32[]{:S(2)}, u32[]{:S(2)}) collective-permute-start(f32[12,128,128]{2,1,0:T(8,128)S(1)} %collective-permute-done.19.refs_0_.refs_2_), channel_id=1, source_target_pairs={{0,1},{1,0},{2,3},{3,2},{4,5},{5,4},{6,7},{7,6},{8,9},{9,8},{10,11... | collective-permute-start | bytes 2359304 | tf_op jit(solution)/shard_map/ppermute | solution.py:297
  97.0 7.2 %collective-permute-start.24 = (f32[12,16,128]{2,1,0:T(8,128)S(1)}, f32[12,16,128]{2,1,0:T(8,128)S(1)}, u32[]{:S(2)}, u32[]{:S(2)}) collective-permute-start(f32[12,16,128]{2,1,0:T(8,128)S(1)} %add_subtract_fusion.4.x), channel_id=1, source_target_pairs={{0,8},{1,5},{2,10},{3,7},{4,12},{5,9},{6,14},{7,11},{8,16},{9,13},... | collective-permute-start | bytes 294920 | tf_op jit(solution)/shard_map/ppermute | solution.py:306
  104.7 1.4 collective-permute-start.25
  106.0 6.5 %collective-permute-start.27 = (f32[12,16,128]{2,1,0:T(8,128)S(1)}, f32[12,16,128]{2,1,0:T(8,128)S(1)}, u32[]{:S(2)}, u32[]{:S(2)}) collective-permute-start(f32[12,16,128]{2,1,0:T(8,128)S(1)} %add_subtract_fusion.3.x), channel_id=1, source_target_pairs={{5,1},{7,3},{8,0},{9,5},{10,2},{11,7},{12,4},{13,9},{14,6},{15,11}... | collective-permute-start | bytes 294920 | tf_op jit(solution)/shard_map/ppermute | solution.py:306
  113.0 1.9 %collective-permute-start.28 = (f32[12,16,128]{2,1,0:T(8,128)S(1)}, f32[12,16,128]{2,1,0:T(8,128)S(1)}, u32[]{:S(2)}, u32[]{:S(2)}) collective-permute-start(f32[12,16,128]{2,1,0:T(8,128)S(1)} %shard_map.105), channel_id=1, source_target_pairs={{0,1},{1,0},{2,3},{3,2},{4,5},{5,4},{6,7},{7,6},{8,9},{9,8},{10,11... | collective-permute-start | bytes 294920 | tf_op jit(solution)/shard_map/ppermute | solution.py:297
  115.0 6.5 %collective-permute-start.29 = (f32[12,16,128]{2,1,0:T(8,128)S(1)}, f32[12,16,128]{2,1,0:T(8,128)S(1)}, u32[]{:S(2)}, u32[]{:S(2)}) collective-permute-start(f32[12,16,128]{2,1,0:T(8,128)S(1)} %add_subtract_fusion.2.x), channel_id=1, source_target_pairs={{5,1},{7,3},{8,0},{9,5},{10,2},{11,7},{12,4},{13,9},{14,6},{15,11}... | collective-permute-start | bytes 294920 | tf_op jit(solution)/shard_map/ppermute | solution.py:306
  122.0 2.0 %collective-permute-start.30 = (f32[12,16,128]{2,1,0:T(8,128)S(1)}, f32[12,16,128]{2,1,0:T(8,128)S(1)}, u32[]{:S(2)}, u32[]{:S(2)}) collective-permute-start(f32[12,16,128]{2,1,0:T(8,128)S(1)} %shard_map.107), channel_id=1, source_target_pairs={{0,1},{1,0},{2,3},{3,2},{4,5},{5,4},{6,7},{7,6},{8,9},{9,8},{10,11... | collective-permute-start | bytes 294920 | tf_op jit(solution)/shard_map/ppermute | solution.py:297
  124.0 6.5 %collective-permute-start.31 = (f32[12,16,128]{2,1,0:T(8,128)S(1)}, f32[12,16,128]{2,1,0:T(8,128)S(1)}, u32[]{:S(2)}, u32[]{:S(2)}) collective-permute-start(f32[12,16,128]{2,1,0:T(8,128)S(1)} %add_subtract_fusion.1.x), channel_id=1, source_target_pairs={{5,1},{7,3},{8,0},{9,5},{10,2},{11,7},{12,4},{13,9},{14,6},{15,11}... | collective-permute-start | bytes 294920 | tf_op jit(solution)/shard_map/ppermute | solution.py:306
  131.0 1.8 %collective-permute-start.32 = (f32[12,16,128]{2,1,0:T(8,128)S(1)}, f32[12,16,128]{2,1,0:T(8,128)S(1)}, u32[]{:S(2)}, u32[]{:S(2)}) collective-permute-start(f32[12,16,128]{2,1,0:T(8,128)S(1)} %shard_map.109), channel_id=1, source_target_pairs={{0,1},{1,0},{2,3},{3,2},{4,5},{5,4},{6,7},{7,6},{8,9},{9,8},{10,11... | collective-permute-start | bytes 294920 | tf_op jit(solution)/shard_map/ppermute | solution.py:297
  132.8 5.1 %collective-permute-start.33 = (f32[12,16,128]{2,1,0:T(8,128)S(1)}, f32[12,16,128]{2,1,0:T(8,128)S(1)}, u32[]{:S(2)}, u32[]{:S(2)}) collective-permute-start(f32[12,16,128]{2,1,0:T(8,128)S(1)} %add_subtract_fusion), channel_id=1, source_target_pairs={{0,2},{1,3},{2,0},{3,1},{4,6},{5,7},{6,4},{7,5},{8,10},{9,11},{10,... | collective-permute-start | bytes 294920 | tf_op jit(solution)/shard_map/ppermute | solution.py:297

commit v9 on v8

--- a/solution.py
+++ b/solution.py
@@ -205,12 +205,16 @@
         out[i] = 2.0 * x + matmul_parts(*split(product), xh, xl)
 
 
+def vector_role(side, me):
+    return (me + side) % 2
+
+
 def table_kernel(lay, me, metas, peers_below, peers_above, out, *refs):
     masks, places = refs[:4], refs[4]
-    role = 1 - me[0] % 2
     out[2 * lay.table] = me[0]
     row = lax.broadcasted_iota(jnp.int32, masks[0].shape[1:], 0)
     for side in (1, 2):
+        role = vector_role(side, me[0])
         start = (side - 1) * lay.table
         base, peers = ((2, peers_below), (0, peers_above))[side - 1]
         for q in range(lay.n_tile):
@@ -235,7 +239,7 @@
 def scaled_kernel(lay, side, table, inverse, *refs):
     sources, (listed, local) = refs[:-2], refs[-2:]
     me = table[2 * lay.table]
-    role = 1 - me % 2
+    role = vector_role(side, me)
     start = (side - 1) * lay.table
 
     def scaled(row, tile):
@@ -383,7 +387,7 @@
         if sweep == FSWEEPS - 1:
             lower_locals = over_chips(lower_local)
             mate_lowers = [mate_lower] + [swap(x, 1) for x in lowers[1:]]
-            below, above = along(metas, 1, 1), along(metas, -1, 1)
+            below, above = along(metas, 1, 1), along(metas, -1)
             mask = shape(lay.listed_slots, rows, n)
             table, *masks = call(
                 kernel(table_kernel),
@@ -428,7 +432,7 @@
     def sweeps(x, side, count, listed, local, early=()):
         base = x
         for sweep in range(count):
-            arrived = along(x, 1 if side == 1 else -1, 1)
+            arrived = along(x, 1, 1) if side == 1 else along(x, -1)
             (here,) = call(
                 kernel(local_sum_kernel, side), [block], (table,), (x, local), flops=8 * n**2 * vectors * rows
             )

time: 141 us -> 140 us (level); the launches traced: 139 us -> 140 us
  waiting for transfers between devices: 65.9 us -> 71.9 us
  starting transfers between devices: 42 us -> 37.6 us
    ppermute x10, waiting for transfers between devices: 30.6 us -> 35.8 us  [along(): return lax.ppermute(x, ('dom', 'tile'), route)]
    ppermute x24, starting transfers between devices: 16.1 us -> 13.4 us  [swap(): return lax.ppermute(x, 'tile', [(i, i ^ bit) for i in range(n_tile)])]
    ppermute x10, starting transfers between devices: 26 us -> 24.1 us  [along(): return lax.ppermute(x, ('dom', 'tile'), route)]
where the time goes in v9:
time: 140 us
  waiting for transfers between devices  71.9 us (51%)
  starting transfers between devices  37.6 us (27%)
  Pallas kernels  22 us (16%)
  local copies, waits for them, and re-layouts  4.74 us (3%)
  other arithmetic  1.99 us (1%)
    ppermute x24, waiting for transfers between devices, swap(): return lax.ppermute(x, 'tile', [(i, i ^ bit) for i in range(n_tile)])  36.1 us
    ppermute x10, waiting for transfers between devices, along(): return lax.ppermute(x, ('dom', 'tile'), route)  35.8 us
    ppermute x10, starting transfers between devices, along(): return lax.ppermute(x, ('dom', 'tile'), route)  24.1 us
    pallas_call x24, Pallas kernels, call(): pl.pallas_call(body if not early else lambda *refs: body(*refs[len(early)...  22 us
    ppermute x24, starting transfers between devices, swap(): return lax.ppermute(x, 'tile', [(i, i ^ bit) for i in range(n_tile)])  13.4 us
  transfers between devices with their start and end apart: 34, of which 26 were waited for; matrix products, arithmetic and copies ran while one was open for 4% of the time, Pallas kernels for 12%

profile of v9, /device:TPU:18, one launch (start us, length us, event | category | flops | bytes accessed | tf_op | source)
XLA Modules:
  0.0 139.5 jit_solution(3685724929205729836)
XLA Ops:
  0.7 1.6 %collective-permute-start = (f32[3,128,128]{2,1,0:T(8,128)}, f32[3,128,128]{2,1,0:T(8,128)S(1)}, u32[]{:S(2)}, u32[]{:S(2)}) collective-permute-start(f32[3,128,128]{2,1,0:T(8,128)} %param.9), channel_id=1, source_target_pairs={{0,2},{1,3},{2,0},{3,1},{4,6},{5,7},{6,4},{7,5},{8,10},{9,11},{10,... | collective-permute-start | bytes 589832 | tf_op jit(solution)/shard_map/ppermute | solution.py:301
  7.3 0.9 collective-permute-done
  8.3 0.9 constant_dynamic-update-slice_fusion.3
  9.7 0.9 shard_map.87
  10.7 3.5 %collective-permute-start.9 = (f32[8,128,128]{2,1,0:T(8,128)S(1)}, f32[8,128,128]{2,1,0:T(8,128)S(1)}, u32[]{:S(2)}, u32[]{:S(2)}) collective-permute-start(f32[8,128,128]{2,1,0:T(8,128)S(1)} %get-tuple-element.36), channel_id=1, source_target_pairs={{0,4},{1,9},{2,6},{3,11},{4,8},{5,13},{6,10},{7,15},{8,12},{9,17},... | collective-permute-start | bytes 1572872 | tf_op jit(solution)/shard_map/ppermute | solution.py:310
  14.2 1.6 %collective-permute-start.8 = (f32[8,128,128]{2,1,0:T(8,128)S(1)}, f32[8,128,128]{2,1,0:T(8,128)S(1)}, u32[]{:S(2)}, u32[]{:S(2)}) collective-permute-start(f32[8,128,128]{2,1,0:T(8,128)S(1)} %get-tuple-element.33.refs_3_.refs_6_.refs_0_), channel_id=1, source_target_pairs={{0,2},{1,3},{2,0},{3,1},{4,6},{5,7},{6,4},{7,5},{8,10},{9,11},{10,... | collective-permute-start | bytes 1572872 | tf_op jit(solution)/shard_map/ppermute | solution.py:301
  15.7 2.4 %shard_map.88 = (f32[12,128,128]{2,1,0:T(8,128)S(1)}, f32[8,128,128]{2,1,0:T(8,128)S(1)}, f32[4,128,128]{2,1,0:T(8,128)S(1)}, f32[12,128,128]{2,1,0:T(8,128)S(1)}, f32[8,128,128]{2,1,0:T(8,128)S(1)}) custom-call(s32[3,64]{1,0:T(4,128)S(1)} %pad_add_fusion.1.near_source.near.refs_1_.refs_4_, f32[12,128,128]{2,1,0:T(8,128)S(1)} %constant_dynamic-update-slice_fusion.inverse, ...), custom_call_target="tpu_custom_call" | custom-call | flops 201326592 | bytes 7012352 | tf_op jit(solution)/shard_map/pallas_call | solution.py:101
  18.2 7.5 %collective-permute-done.9.refs_5_ = f32[8,128,128]{2,1,0:T(8,128)S(1)} collective-permute-done((f32[8,128,128]{2,1,0:T(8,128)S(1)}, f32[8,128,128]{2,1,0:T(8,128)S(1)}, u32[]{:S(2)}, u32[]{:S(2)}) %collective-permute-start.9) | collective-permute-done | bytes 524320 | tf_op jit(solution)/shard_map/ppermute | solution.py:310
  25.6 2.3 %collective-permute-done.8.refs_0_.refs_3_ = f32[8,128,128]{2,1,0:T(8,128)S(1)} collective-permute-done((f32[8,128,128]{2,1,0:T(8,128)S(1)}, f32[8,128,128]{2,1,0:T(8,128)S(1)}, u32[]{:S(2)}, u32[]{:S(2)}) %collective-permute-start.8) | collective-permute-done | bytes 524320 | tf_op jit(solution)/shard_map/ppermute | solution.py:301
  27.9 1.1 shard_map.89
  29.1 1.7 %collective-permute-done.10 = f32[6,128,128]{2,1,0:T(8,128)S(1)} collective-permute-done((f32[6,128,128]{2,1,0:T(8,128)S(1)}, f32[6,128,128]{2,1,0:T(8,128)S(1)}, u32[]{:S(2)}, u32[]{:S(2)}) %collective-permute-start.10) | collective-permute-done | bytes 393248 | tf_op jit(solution)/shard_map/ppermute | solution.py:301
  30.8 1.6 %collective-permute-start.11 = (f32[6,128,128]{2,1,0:T(8,128)S(1)}, f32[6,128,128]{2,1,0:T(8,128)S(1)}, u32[]{:S(2)}, u32[]{:S(2)}) collective-permute-start(f32[6,128,128]{2,1,0:T(8,128)S(1)} %add.30), channel_id=1, source_target_pairs={{0,2},{1,3},{2,0},{3,1},{4,6},{5,7},{6,4},{7,5},{8,10},{9,11},{10,... | collective-permute-start | bytes 1179656 | tf_op jit(solution)/shard_map/ppermute | solution.py:301
  33.0 9.1 %collective-permute-done.3 = s32[2,64]{1,0:T(2,128)S(1)} collective-permute-done((s32[2,64]{1,0:T(2,128)S(1)}, s32[2,64]{1,0:T(2,128)S(1)}, u32[]{:S(2)}, u32[]{:S(2)}) %collective-permute-start.3) | collective-permute-done | bytes 544 | tf_op jit(solution)/shard_map/ppermute | solution.py:301
  43.3 1.2 collective-permute-done.14
  44.6 0.9 shard_map.92
  45.5 3.0 %collective-permute-start.15 = (f32[8,128,128]{2,1,0:T(8,128)S(1)}, f32[8,128,128]{2,1,0:T(8,128)S(1)}, u32[]{:S(2)}, u32[]{:S(2)}) collective-permute-start(f32[8,128,128]{2,1,0:T(8,128)S(1)} %shard_map.92), channel_id=1, source_target_pairs={{0,4},{1,9},{2,6},{3,11},{4,8},{5,13},{6,10},{7,15},{8,12},{9,17},... | collective-permute-start | bytes 1572872 | tf_op jit(solution)/shard_map/ppermute | solution.py:310
  48.5 1.6 %collective-permute-start.12 = (f32[4,128,128]{2,1,0:T(8,128)S(1)}, f32[4,128,128]{2,1,0:T(8,128)S(1)}, u32[]{:S(2)}, u32[]{:S(2)}) collective-permute-start(f32[4,128,128]{2,1,0:T(8,128)S(1)} %get-tuple-element.39.refs_1_), channel_id=1, source_target_pairs={{0,2},{1,3},{2,0},{3,1},{4,6},{5,7},{6,4},{7,5},{8,10},{9,11},{10,... | collective-permute-start | bytes 786440 | tf_op jit(solution)/shard_map/ppermute | solution.py:301
  50.1 2.8 %collective-permute-start.5 = (s32[4,64]{1,0:T(4,128)S(1)}, s32[4,64]{1,0:T(4,128)S(1)}, u32[]{:S(2)}, u32[]{:S(2)}) collective-permute-start(s32[4,64]{1,0:T(4,128)S(1)} %pad_add_fusion.metas.refs_0_), channel_id=1, source_target_pairs={{4,0},{6,2},{8,4},{9,1},{10,6},{11,3},{12,8},{13,5},{14,10},{15,7}... | collective-permute-start | bytes 3080 | tf_op jit(solution)/shard_map/ppermute | solution.py:310
  52.9 1.9 %collective-permute-start.4 = (s32[4,64]{1,0:T(4,128)S(1)}, s32[4,64]{1,0:T(4,128)S(1)}, u32[]{:S(2)}, u32[]{:S(2)}) collective-permute-start(s32[4,64]{1,0:T(4,128)S(1)} %pad_add_fusion.metas.refs_0_), channel_id=1, source_target_pairs={{0,8},{1,5},{2,10},{3,7},{4,12},{5,9},{6,14},{7,11},{8,16},{9,13},... | collective-permute-start | bytes 3080 | tf_op jit(solution)/shard_map/ppermute | solution.py:310
  54.9 2.0 %shard_map.91.refs_5_ = f32[12,128,128]{2,1,0:T(8,128)S(1)} custom-call(s32[3,64]{1,0:T(4,128)S(1)} %pad_add_fusion.1.near_source.near.refs_1_.refs_4_, f32[12,128,128]{2,1,0:T(8,128)S(1)} %pad_maximum_fusion.inverse, f32[3,128,128]{2,1,0:T(8,128)S(1)} %copy-done.1, f32[24,128,128]{2,1,0:T(8,128)S(1)} %bitcast.14), custom_call_target="tpu_custom_call" | custom-call | flops 201326592 | bytes 3342336 | tf_op jit(solution)/shard_map/pallas_call | solution.py:101
  56.9 4.5 %collective-permute-done.4.peers_below.refs_2_ = s32[4,64]{1,0:T(4,128)S(1)} collective-permute-done((s32[4,64]{1,0:T(4,128)S(1)}, s32[4,64]{1,0:T(4,128)S(1)}, u32[]{:S(2)}, u32[]{:S(2)}) %collective-permute-start.4) | collective-permute-done | bytes 1056 | tf_op jit(solution)/shard_map/ppermute | solution.py:310
  61.4 1.1 shard_map.93
  62.6 1.7 %collective-permute-done.16 = f32[6,128,128]{2,1,0:T(8,128)S(1)} collective-permute-done((f32[6,128,128]{2,1,0:T(8,128)S(1)}, f32[6,128,128]{2,1,0:T(8,128)S(1)}, u32[]{:S(2)}, u32[]{:S(2)}) %collective-permute-start.16) | collective-permute-done | bytes 393248 | tf_op jit(solution)/shard_map/ppermute | solution.py:301
  64.3 1.6 %collective-permute-start.17 = (f32[6,128,128]{2,1,0:T(8,128)S(1)}, f32[6,128,128]{2,1,0:T(8,128)S(1)}, u32[]{:S(2)}, u32[]{:S(2)}) collective-permute-start(f32[6,128,128]{2,1,0:T(8,128)S(1)} %add.32), channel_id=1, source_target_pairs={{0,2},{1,3},{2,0},{3,1},{4,6},{5,7},{6,4},{7,5},{8,10},{9,11},{10,... | collective-permute-start | bytes 1179656 | tf_op jit(solution)/shard_map/ppermute | solution.py:301
  65.9 2.1 %shard_map.86 = (s32[65]{0:T(128)S(1)}, f32[16,12,128]{2,1,0:T(8,128)S(1)}, f32[16,12,128]{2,1,0:T(8,128)S(1)}, f32[16,12,128]{2,1,0:T(8,128)S(1)}, f32[16,12,128]{2,1,0:T(8,128)S(1)}) custom-call(s32[1]{0:T(128)} %bitcast.me, s32[4,64]{1,0:T(4,128)S(1)} %pad_add_fusion.metas.refs_0_, s32[4,64]{1,0:T(4,128)S(1)} %collective-permute-done.4.peers_below.refs_2_, ...), custom_call_target="tpu_custom_call" | custom-call | bytes 393476 | tf_op jit(solution)/shard_map/pallas_call | solution.py:101
  68.0 7.5 %collective-permute-done.17 = f32[6,128,128]{2,1,0:T(8,128)S(1)} collective-permute-done((f32[6,128,128]{2,1,0:T(8,128)S(1)}, f32[6,128,128]{2,1,0:T(8,128)S(1)}, u32[]{:S(2)}, u32[]{:S(2)}) %collective-permute-start.17) | collective-permute-done | bytes 393248 | tf_op jit(solution)/shard_map/ppermute | solution.py:301
  76.2 1.6 %collective-permute-start.19 = (f32[12,128,128]{2,1,0:T(8,128)S(1)}, f32[12,128,128]{2,1,0:T(8,128)S(1)}, u32[]{:S(2)}, u32[]{:S(2)}) collective-permute-start(f32[12,128,128]{2,1,0:T(8,128)S(1)} %get-tuple-element.40.upper.refs_0_), channel_id=1, source_target_pairs={{0,2},{1,3},{2,0},{3,1},{4,6},{5,7},{6,4},{7,5},{8,10},{9,11},{10,... | collective-permute-start | bytes 2359304 | tf_op jit(solution)/shard_map/ppermute | solution.py:301
  78.4 2.2 %collective-permute-start.20 = (f32[12,16,128]{2,1,0:T(8,128)S(1)}, f32[12,16,128]{2,1,0:T(8,128)S(1)}, u32[]{:S(2)}, u32[]{:S(2)}) collective-permute-start(f32[12,16,128]{2,1,0:T(8,128)S(1)} %shard_map.95.x), channel_id=1, source_target_pairs={{0,8},{1,5},{2,10},{3,7},{4,12},{5,9},{6,14},{7,11},{8,16},{9,13},... | collective-permute-start | bytes 294920 | tf_op jit(solution)/shard_map/ppermute | solution.py:310
  80.6 1.2 shard_map.96
  82.7 3.3 %collective-permute-done.20.arrived = f32[12,16,128]{2,1,0:T(8,128)S(1)} collective-permute-done((f32[12,16,128]{2,1,0:T(8,128)S(1)}, f32[12,16,128]{2,1,0:T(8,128)S(1)}, u32[]{:S(2)}, u32[]{:S(2)}) %collective-permute-start.20) | collective-permute-done | bytes 98336 | tf_op jit(solution)/shard_map/ppermute | solution.py:310
  86.5 1.3 collective-permute-done.21
  87.8 2.2 %collective-permute-start.22 = (f32[12,16,128]{2,1,0:T(8,128)S(1)}, f32[12,16,128]{2,1,0:T(8,128)S(1)}, u32[]{:S(2)}, u32[]{:S(2)}) collective-permute-start(f32[12,16,128]{2,1,0:T(8,128)S(1)} %add_subtract_fusion.5.x), channel_id=1, source_target_pairs={{0,8},{1,5},{2,10},{3,7},{4,12},{5,9},{6,14},{7,11},{8,16},{9,13},... | collective-permute-start | bytes 294920 | tf_op jit(solution)/shard_map/ppermute | solution.py:310
  90.8 4.3 %collective-permute-done.22.arrived = f32[12,16,128]{2,1,0:T(8,128)S(1)} collective-permute-done((f32[12,16,128]{2,1,0:T(8,128)S(1)}, f32[12,16,128]{2,1,0:T(8,128)S(1)}, u32[]{:S(2)}, u32[]{:S(2)}) %collective-permute-start.22) | collective-permute-done | bytes 98336 | tf_op jit(solution)/shard_map/ppermute | solution.py:310
  97.0 2.2 %collective-permute-start.24 = (f32[12,16,128]{2,1,0:T(8,128)S(1)}, f32[12,16,128]{2,1,0:T(8,128)S(1)}, u32[]{:S(2)}, u32[]{:S(2)}) collective-permute-start(f32[12,16,128]{2,1,0:T(8,128)S(1)} %add_subtract_fusion.4.x), channel_id=1, source_target_pairs={{0,8},{1,5},{2,10},{3,7},{4,12},{5,9},{6,14},{7,11},{8,16},{9,13},... | collective-permute-start | bytes 294920 | tf_op jit(solution)/shard_map/ppermute | solution.py:310
  100.0 4.1 %collective-permute-done.24.refs_5_ = f32[12,16,128]{2,1,0:T(8,128)S(1)} collective-permute-done((f32[12,16,128]{2,1,0:T(8,128)S(1)}, f32[12,16,128]{2,1,0:T(8,128)S(1)}, u32[]{:S(2)}, u32[]{:S(2)}) %collective-permute-start.24) | collective-permute-done | bytes 98336 | tf_op jit(solution)/shard_map/ppermute | solution.py:310
  104.7 1.3 collective-permute-done.25
  106.0 2.5 %collective-permute-start.27 = (f32[12,16,128]{2,1,0:T(8,128)S(1)}, f32[12,16,128]{2,1,0:T(8,128)S(1)}, u32[]{:S(2)}, u32[]{:S(2)}) collective-permute-start(f32[12,16,128]{2,1,0:T(8,128)S(1)} %add_subtract_fusion.3.x), channel_id=1, source_target_pairs={{4,0},{6,2},{8,4},{9,1},{10,6},{11,3},{12,8},{13,5},{14,10},{15,7}... | collective-permute-start | bytes 294920 | tf_op jit(solution)/shard_map/ppermute | solution.py:310
  108.6 1.3 shard_map.103
  110.7 2.8 %collective-permute-done.27.arrived = f32[12,16,128]{2,1,0:T(8,128)S(1)} collective-permute-done((f32[12,16,128]{2,1,0:T(8,128)S(1)}, f32[12,16,128]{2,1,0:T(8,128)S(1)}, u32[]{:S(2)}, u32[]{:S(2)}) %collective-permute-start.27) | collective-permute-done | bytes 98336 | tf_op jit(solution)/shard_map/ppermute | solution.py:310
  114.0 1.3 collective-permute-done.28
  115.3 1.9 %collective-permute-start.29 = (f32[12,16,128]{2,1,0:T(8,128)S(1)}, f32[12,16,128]{2,1,0:T(8,128)S(1)}, u32[]{:S(2)}, u32[]{:S(2)}) collective-permute-start(f32[12,16,128]{2,1,0:T(8,128)S(1)} %add_subtract_fusion.2.x), channel_id=1, source_target_pairs={{4,0},{6,2},{8,4},{9,1},{10,6},{11,3},{12,8},{13,5},{14,10},{15,7}... | collective-permute-start | bytes 294920 | tf_op jit(solution)/shard_map/ppermute | solution.py:310
  118.1 4.7 %collective-permute-done.29.arrived = f32[12,16,128]{2,1,0:T(8,128)S(1)} collective-permute-done((f32[12,16,128]{2,1,0:T(8,128)S(1)}, f32[12,16,128]{2,1,0:T(8,128)S(1)}, u32[]{:S(2)}, u32[]{:S(2)}) %collective-permute-start.29) | collective-permute-done | bytes 98336 | tf_op jit(solution)/shard_map/ppermute | solution.py:310
  123.3 1.3 collective-permute-done.30
  124.6 1.9 %collective-permute-start.31 = (f32[12,16,128]{2,1,0:T(8,128)S(1)}, f32[12,16,128]{2,1,0:T(8,128)S(1)}, u32[]{:S(2)}, u32[]{:S(2)}) collective-permute-start(f32[12,16,128]{2,1,0:T(8,128)S(1)} %add_subtract_fusion.1.x), channel_id=1, source_target_pairs={{4,0},{6,2},{8,4},{9,1},{10,6},{11,3},{12,8},{13,5},{14,10},{15,7}... | collective-permute-start | bytes 294920 | tf_op jit(solution)/shard_map/ppermute | solution.py:310
  127.4 4.7 %collective-permute-done.31.arrived = f32[12,16,128]{2,1,0:T(8,128)S(1)} collective-permute-done((f32[12,16,128]{2,1,0:T(8,128)S(1)}, f32[12,16,128]{2,1,0:T(8,128)S(1)}, u32[]{:S(2)}, u32[]{:S(2)}) %collective-permute-start.31) | collective-permute-done | bytes 98336 | tf_op jit(solution)/shard_map/ppermute | solution.py:310
  132.6 1.3 collective-permute-done.32
  133.9 1.6 %collective-permute-start.33 = (f32[12,16,128]{2,1,0:T(8,128)S(1)}, f32[12,16,128]{2,1,0:T(8,128)S(1)}, u32[]{:S(2)}, u32[]{:S(2)}) collective-permute-start(f32[12,16,128]{2,1,0:T(8,128)S(1)} %add_subtract_fusion), channel_id=1, source_target_pairs={{0,2},{1,3},{2,0},{3,1},{4,6},{5,7},{6,4},{7,5},{8,10},{9,11},{10,... | collective-permute-start | bytes 294920 | tf_op jit(solution)/shard_map/ppermute | solution.py:301
  136.2 2.6 %collective-permute-done.33 = f32[12,16,128]{2,1,0:T(8,128)S(1)} collective-permute-done((f32[12,16,128]{2,1,0:T(8,128)S(1)}, f32[12,16,128]{2,1,0:T(8,128)S(1)}, u32[]{:S(2)}, u32[]{:S(2)}) %collective-permute-start.33) | collective-permute-done | bytes 98336 | tf_op jit(solution)/shard_map/ppermute | solution.py:301
  (85 shorter events, 19.7 us)
Async XLA Ops:
  0.6 9.1 %copy-start = (f32[12,2,128,128]{3,2,1,0:T(8,128)S(1)}, f32[12,2,128,128]{3,2,1,0:T(8,128)}, u32[]{:S(2)}) copy-start(f32[12,2,128,128]{3,2,1,0:T(8,128)} %param.10) | copy-start | bytes 4718596
  0.6 9.1 %collective-permute-start.7 = (f32[24,128,128]{2,1,0:T(8,128)}, f32[24,128,128]{2,1,0:T(8,128)S(1)}, u32[]{:S(2)}, u32[]{:S(2)}) collective-permute-start(f32[24,128,128]{2,1,0:T(8,128)} %bitcast.11), channel_id=1, source_target_pairs={{0,1},{1,0},{2,3},{3,2},{4,5},{5,4},{6,7},{7,6},{8,9},{9,8},{10,11... | collective-permute-start | bytes 4718600 | tf_op jit(solution)/shard_map/ppermute | solution.py:301
  0.7 7.5 %collective-permute-start = (f32[3,128,128]{2,1,0:T(8,128)}, f32[3,128,128]{2,1,0:T(8,128)S(1)}, u32[]{:S(2)}, u32[]{:S(2)}) collective-permute-start(f32[3,128,128]{2,1,0:T(8,128)} %param.9), channel_id=1, source_target_pairs={{0,2},{1,3},{2,0},{3,1},{4,6},{5,7},{6,4},{7,5},{8,10},{9,11},{10,... | collective-permute-start | bytes 589832 | tf_op jit(solution)/shard_map/ppermute | solution.py:301
  2.3 5.9 %collective-permute-start.2 = (f32[3,128,128]{2,1,0:T(8,128)}, f32[3,128,128]{2,1,0:T(8,128)S(1)}, u32[]{:S(2)}, u32[]{:S(2)}) collective-permute-start(f32[3,128,128]{2,1,0:T(8,128)} %param.9), channel_id=1, source_target_pairs={{0,1},{1,0},{2,3},{3,2},{4,5},{5,4},{6,7},{7,6},{8,9},{9,8},{10,11... | collective-permute-start | bytes 589832 | tf_op jit(solution)/shard_map/ppermute | solution.py:301
  6.2 1.2 collective-permute-start.1
  8.3 1.4 %collective-permute-start.6 = (f32[3,128,128]{2,1,0:T(8,128)S(1)}, f32[3,128,128]{2,1,0:T(8,128)S(1)}, u32[]{:S(2)}, u32[]{:S(2)}) collective-permute-start(f32[3,128,128]{2,1,0:T(8,128)S(1)} %collective-permute-done), channel_id=1, source_target_pairs={{0,1},{1,0},{2,3},{3,2},{4,5},{5,4},{6,7},{7,6},{8,9},{9,8},{10,11... | collective-permute-start | bytes 589832 | tf_op jit(solution)/shard_map/ppermute | solution.py:301
  9.7 6.0 %copy-start.1 = (f32[3,128,128]{2,1,0:T(8,128)S(1)}, f32[3,128,128]{2,1,0:T(8,128)}, u32[]{:S(2)}) copy-start(f32[3,128,128]{2,1,0:T(8,128)} %diag.3) | copy-start | bytes 589828
  10.7 14.9 %collective-permute-start.9 = (f32[8,128,128]{2,1,0:T(8,128)S(1)}, f32[8,128,128]{2,1,0:T(8,128)S(1)}, u32[]{:S(2)}, u32[]{:S(2)}) collective-permute-start(f32[8,128,128]{2,1,0:T(8,128)S(1)} %get-tuple-element.36), channel_id=1, source_target_pairs={{0,4},{1,9},{2,6},{3,11},{4,8},{5,13},{6,10},{7,15},{8,12},{9,17},... | collective-permute-start | bytes 1572872 | tf_op jit(solution)/shard_map/ppermute | solution.py:310
  14.2 13.8 %collective-permute-start.8 = (f32[8,128,128]{2,1,0:T(8,128)S(1)}, f32[8,128,128]{2,1,0:T(8,128)S(1)}, u32[]{:S(2)}, u32[]{:S(2)}) collective-permute-start(f32[8,128,128]{2,1,0:T(8,128)S(1)} %get-tuple-element.33.refs_3_.refs_6_.refs_0_), channel_id=1, source_target_pairs={{0,2},{1,3},{2,0},{3,1},{4,6},{5,7},{6,4},{7,5},{8,10},{9,11},{10,... | collective-permute-start | bytes 1572872 | tf_op jit(solution)/shard_map/ppermute | solution.py:301
  27.9 5.0 %copy-start.3 = (f32[3,128,128]{2,1,0:T(8,128)S(1)}, f32[3,128,128]{2,1,0:T(8,128)}, u32[]{:S(2)}) copy-start(f32[3,128,128]{2,1,0:T(8,128)} %param.9) | copy-start | bytes 589828
  29.0 1.8 %collective-permute-start.10 = (f32[6,128,128]{2,1,0:T(8,128)S(1)}, f32[6,128,128]{2,1,0:T(8,128)S(1)}, u32[]{:S(2)}, u32[]{:S(2)}) collective-permute-start(f32[6,128,128]{2,1,0:T(8,128)S(1)} %get-tuple-element.38), channel_id=1, source_target_pairs={{0,1},{1,0},{2,3},{3,2},{4,5},{5,4},{6,7},{7,6},{8,9},{9,8},{10,11... | collective-permute-start | bytes 1179656 | tf_op jit(solution)/shard_map/ppermute | solution.py:301
  30.8 11.3 %collective-permute-start.11 = (f32[6,128,128]{2,1,0:T(8,128)S(1)}, f32[6,128,128]{2,1,0:T(8,128)S(1)}, u32[]{:S(2)}, u32[]{:S(2)}) collective-permute-start(f32[6,128,128]{2,1,0:T(8,128)S(1)} %add.30), channel_id=1, source_target_pairs={{0,2},{1,3},{2,0},{3,1},{4,6},{5,7},{6,4},{7,5},{8,10},{9,11},{10,... | collective-permute-start | bytes 1179656 | tf_op jit(solution)/shard_map/ppermute | solution.py:301
  32.4 9.7 %collective-permute-start.3 = (s32[2,64]{1,0:T(2,128)S(1)}, s32[2,64]{1,0:T(2,128)S(1)}, u32[]{:S(2)}, u32[]{:S(2)}) collective-permute-start(s32[2,64]{1,0:T(2,128)S(1)} %pad_add_fusion.2), channel_id=1, source_target_pairs={{0,2},{1,3},{2,0},{3,1},{4,6},{5,7},{6,4},{7,5},{8,10},{9,11},{10,... | collective-permute-start | bytes 1544 | tf_op jit(solution)/shard_map/ppermute | solution.py:301
  42.7 1.8 %collective-permute-start.14 = (f32[6,128,128]{2,1,0:T(8,128)S(1)}, f32[6,128,128]{2,1,0:T(8,128)S(1)}, u32[]{:S(2)}, u32[]{:S(2)}) collective-permute-start(f32[6,128,128]{2,1,0:T(8,128)S(1)} %shard_map.90.refs_1_), channel_id=1, source_target_pairs={{0,1},{1,0},{2,3},{3,2},{4,5},{5,4},{6,7},{7,6},{8,9},{9,8},{10,11... | collective-permute-start | bytes 1179656 | tf_op jit(solution)/shard_map/ppermute | solution.py:301
  42.8 18.6 %collective-permute-start.13 = (f32[8,128,128]{2,1,0:T(8,128)S(1)}, f32[8,128,128]{2,1,0:T(8,128)S(1)}, u32[]{:S(2)}, u32[]{:S(2)}) collective-permute-start(f32[8,128,128]{2,1,0:T(8,128)S(1)} %collective-permute-done.8.refs_0_.refs_3_), channel_id=1, source_target_pairs={{0,1},{1,0},{2,3},{3,2},{4,5},{5,4},{6,7},{7,6},{8,9},{9,8},{10,11... | collective-permute-start | bytes 1572872 | tf_op jit(solution)/shard_map/ppermute | solution.py:301
  45.5 15.9 %collective-permute-start.15 = (f32[8,128,128]{2,1,0:T(8,128)S(1)}, f32[8,128,128]{2,1,0:T(8,128)S(1)}, u32[]{:S(2)}, u32[]{:S(2)}) collective-permute-start(f32[8,128,128]{2,1,0:T(8,128)S(1)} %shard_map.92), channel_id=1, source_target_pairs={{0,4},{1,9},{2,6},{3,11},{4,8},{5,13},{6,10},{7,15},{8,12},{9,17},... | collective-permute-start | bytes 1572872 | tf_op jit(solution)/shard_map/ppermute | solution.py:310
  48.5 12.9 %collective-permute-start.12 = (f32[4,128,128]{2,1,0:T(8,128)S(1)}, f32[4,128,128]{2,1,0:T(8,128)S(1)}, u32[]{:S(2)}, u32[]{:S(2)}) collective-permute-start(f32[4,128,128]{2,1,0:T(8,128)S(1)} %get-tuple-element.39.refs_1_), channel_id=1, source_target_pairs={{0,2},{1,3},{2,0},{3,1},{4,6},{5,7},{6,4},{7,5},{8,10},{9,11},{10,... | collective-permute-start | bytes 786440 | tf_op jit(solution)/shard_map/ppermute | solution.py:301
  50.1 6.8 %collective-permute-start.5 = (s32[4,64]{1,0:T(4,128)S(1)}, s32[4,64]{1,0:T(4,128)S(1)}, u32[]{:S(2)}, u32[]{:S(2)}) collective-permute-start(s32[4,64]{1,0:T(4,128)S(1)} %pad_add_fusion.metas.refs_0_), channel_id=1, source_target_pairs={{4,0},{6,2},{8,4},{9,1},{10,6},{11,3},{12,8},{13,5},{14,10},{15,7}... | collective-permute-start | bytes 3080 | tf_op jit(solution)/shard_map/ppermute | solution.py:310
  52.9 8.5 %collective-permute-start.4 = (s32[4,64]{1,0:T(4,128)S(1)}, s32[4,64]{1,0:T(4,128)S(1)}, u32[]{:S(2)}, u32[]{:S(2)}) collective-permute-start(s32[4,64]{1,0:T(4,128)S(1)} %pad_add_fusion.metas.refs_0_), channel_id=1, source_target_pairs={{0,8},{1,5},{2,10},{3,7},{4,12},{5,9},{6,14},{7,11},{8,16},{9,13},... | collective-permute-start | bytes 3080 | tf_op jit(solution)/shard_map/ppermute | solution.py:310
  62.5 1.8 %collective-permute-start.16 = (f32[6,128,128]{2,1,0:T(8,128)S(1)}, f32[6,128,128]{2,1,0:T(8,128)S(1)}, u32[]{:S(2)}, u32[]{:S(2)}) collective-permute-start(f32[6,128,128]{2,1,0:T(8,128)S(1)} %get-tuple-element.43), channel_id=1, source_target_pairs={{0,1},{1,0},{2,3},{3,2},{4,5},{5,4},{6,7},{7,6},{8,9},{9,8},{10,11... | collective-permute-start | bytes 1179656 | tf_op jit(solution)/shard_map/ppermute | solution.py:301
  64.3 11.2 %collective-permute-start.17 = (f32[6,128,128]{2,1,0:T(8,128)S(1)}, f32[6,128,128]{2,1,0:T(8,128)S(1)}, u32[]{:S(2)}, u32[]{:S(2)}) collective-permute-start(f32[6,128,128]{2,1,0:T(8,128)S(1)} %add.32), channel_id=1, source_target_pairs={{0,2},{1,3},{2,0},{3,1},{4,6},{5,7},{6,4},{7,5},{8,10},{9,11},{10,... | collective-permute-start | bytes 1179656 | tf_op jit(solution)/shard_map/ppermute | solution.py:301
  75.6 2.4 %copy-start.2 = (f32[12,32,128]{2,1,0:T(8,128)S(1)}, f32[12,32,128]{2,1,0:T(8,128)}, u32[]{:S(2)}) copy-start(f32[12,32,128]{2,1,0:T(8,128)} %base.1) | copy-start | bytes 589828
  76.1 1.8 %collective-permute-start.18 = (f32[6,128,128]{2,1,0:T(8,128)S(1)}, f32[6,128,128]{2,1,0:T(8,128)S(1)}, u32[]{:S(2)}, u32[]{:S(2)}) collective-permute-start(f32[6,128,128]{2,1,0:T(8,128)S(1)} %shard_map.94), channel_id=1, source_target_pairs={{0,1},{1,0},{2,3},{3,2},{4,5},{5,4},{6,7},{7,6},{8,9},{9,8},{10,11... | collective-permute-start | bytes 1179656 | tf_op jit(solution)/shard_map/ppermute | solution.py:301
  76.2 20.0 %collective-permute-start.19 = (f32[12,128,128]{2,1,0:T(8,128)S(1)}, f32[12,128,128]{2,1,0:T(8,128)S(1)}, u32[]{:S(2)}, u32[]{:S(2)}) collective-permute-start(f32[12,128,128]{2,1,0:T(8,128)S(1)} %get-tuple-element.40.upper.refs_0_), channel_id=1, source_target_pairs={{0,2},{1,3},{2,0},{3,1},{4,6},{5,7},{6,4},{7,5},{8,10},{9,11},{10,... | collective-permute-start | bytes 2359304 | tf_op jit(solution)/shard_map/ppermute | solution.py:301
  78.4 7.6 %collective-permute-start.20 = (f32[12,16,128]{2,1,0:T(8,128)S(1)}, f32[12,16,128]{2,1,0:T(8,128)S(1)}, u32[]{:S(2)}, u32[]{:S(2)}) collective-permute-start(f32[12,16,128]{2,1,0:T(8,128)S(1)} %shard_map.95.x), channel_id=1, source_target_pairs={{0,8},{1,5},{2,10},{3,7},{4,12},{5,9},{6,14},{7,11},{8,16},{9,13},... | collective-permute-start | bytes 294920 | tf_op jit(solution)/shard_map/ppermute | solution.py:310
  86.4 1.4 collective-permute-start.21
  87.8 7.3 %collective-permute-start.22 = (f32[12,16,128]{2,1,0:T(8,128)S(1)}, f32[12,16,128]{2,1,0:T(8,128)S(1)}, u32[]{:S(2)}, u32[]{:S(2)}) collective-permute-start(f32[12,16,128]{2,1,0:T(8,128)S(1)} %add_subtract_fusion.5.x), channel_id=1, source_target_pairs={{0,8},{1,5},{2,10},{3,7},{4,12},{5,9},{6,14},{7,11},{8,16},{9,13},... | collective-permute-start | bytes 294920 | tf_op jit(solution)/shard_map/ppermute | solution.py:310
  95.6 1.4 collective-permute-start.23
  96.2 12.4 %collective-permute-start.26 = (f32[12,128,128]{2,1,0:T(8,128)S(1)}, f32[12,128,128]{2,1,0:T(8,128)S(1)}, u32[]{:S(2)}, u32[]{:S(2)}) collective-permute-start(f32[12,128,128]{2,1,0:T(8,128)S(1)} %collective-permute-done.19.refs_0_.refs_2_), channel_id=1, source_target_pairs={{0,1},{1,0},{2,3},{3,2},{4,5},{5,4},{6,7},{7,6},{8,9},{9,8},{10,11... | collective-permute-start | bytes 2359304 | tf_op jit(solution)/shard_map/ppermute | solution.py:301
  97.0 7.2 %collective-permute-start.24 = (f32[12,16,128]{2,1,0:T(8,128)S(1)}, f32[12,16,128]{2,1,0:T(8,128)S(1)}, u32[]{:S(2)}, u32[]{:S(2)}) collective-permute-start(f32[12,16,128]{2,1,0:T(8,128)S(1)} %add_subtract_fusion.4.x), channel_id=1, source_target_pairs={{0,8},{1,5},{2,10},{3,7},{4,12},{5,9},{6,14},{7,11},{8,16},{9,13},... | collective-permute-start | bytes 294920 | tf_op jit(solution)/shard_map/ppermute | solution.py:310
  104.7 1.4 collective-permute-start.25
  106.0 7.4 %collective-permute-start.27 = (f32[12,16,128]{2,1,0:T(8,128)S(1)}, f32[12,16,128]{2,1,0:T(8,128)S(1)}, u32[]{:S(2)}, u32[]{:S(2)}) collective-permute-start(f32[12,16,128]{2,1,0:T(8,128)S(1)} %add_subtract_fusion.3.x), channel_id=1, source_target_pairs={{4,0},{6,2},{8,4},{9,1},{10,6},{11,3},{12,8},{13,5},{14,10},{15,7}... | collective-permute-start | bytes 294920 | tf_op jit(solution)/shard_map/ppermute | solution.py:310
  113.9 1.4 collective-permute-start.28
  115.3 7.4 %collective-permute-start.29 = (f32[12,16,128]{2,1,0:T(8,128)S(1)}, f32[12,16,128]{2,1,0:T(8,128)S(1)}, u32[]{:S(2)}, u32[]{:S(2)}) collective-permute-start(f32[12,16,128]{2,1,0:T(8,128)S(1)} %add_subtract_fusion.2.x), channel_id=1, source_target_pairs={{4,0},{6,2},{8,4},{9,1},{10,6},{11,3},{12,8},{13,5},{14,10},{15,7}... | collective-permute-start | bytes 294920 | tf_op jit(solution)/shard_map/ppermute | solution.py:310
  123.2 1.4 collective-permute-start.30
  124.6 7.4 %collective-permute-start.31 = (f32[12,16,128]{2,1,0:T(8,128)S(1)}, f32[12,16,128]{2,1,0:T(8,128)S(1)}, u32[]{:S(2)}, u32[]{:S(2)}) collective-permute-start(f32[12,16,128]{2,1,0:T(8,128)S(1)} %add_subtract_fusion.1.x), channel_id=1, source_target_pairs={{4,0},{6,2},{8,4},{9,1},{10,6},{11,3},{12,8},{13,5},{14,10},{15,7}... | collective-permute-start | bytes 294920 | tf_op jit(solution)/shard_map/ppermute | solution.py:310
  132.5 1.4 collective-permute-start.32
  133.9 4.9 %collective-permute-start.33 = (f32[12,16,128]{2,1,0:T(8,128)S(1)}, f32[12,16,128]{2,1,0:T(8,128)S(1)}, u32[]{:S(2)}, u32[]{:S(2)}) collective-permute-start(f32[12,16,128]{2,1,0:T(8,128)S(1)} %add_subtract_fusion), channel_id=1, source_target_pairs={{0,2},{1,3},{2,0},{3,1},{4,6},{5,7},{6,4},{7,5},{8,10},{9,11},{10,... | collective-permute-start | bytes 294920 | tf_op jit(solution)/shard_map/ppermute | solution.py:301

commit v10 on v9

--- a/solution.py
+++ b/solution.py
@@ -175,7 +175,8 @@
     local_terms(lay, near.at[0], near.at[1], inverse, diag, tiles, out)
 
 
-def incoming_kernel(lay, near_source, local, lower, mate_lower, arrived, keep, give, total, halves, near, done):
+def incoming_kernel(lay, near_source, local, lower, mate_lower, arrived, *refs):
+    *outs, total, halves, near, done = refs
     fetch = pltpu.make_async_copy(near_source, near, done)
     fetch.start()
     total[...] = local[...]
@@ -192,9 +193,8 @@
             terms.append(matmul_beside(beside(source[role * lay.cap + j]), halves[g * lay.cap + v]))
     for place, term in zip(places, terms):
         total[place] += term
-    half = keep.shape[0]
-    keep[...] = total[:half]
-    give[...] = total[half:]
+    for c, out in enumerate(outs):
+        out[...] = total[c * lay.own_rows : (c + 1) * lay.own_rows]
 
 
 def newton_kernel(inverse, sums, out):
@@ -309,13 +309,10 @@
                     route.append((d * n_tile + t, to * n_tile + t))
         return lax.ppermute(x, ("dom", "tile"), route)
 
-    def summed(x):
+    def summed(parts):
         for bit in upper_bits:
-            got = swap(x, bit)
-            near = bit // 2
-            got = got.reshape((n_tile // 2 // (2 * near), 2, near * lay.own_rows) + x.shape[1:])
-            x = x + jnp.concatenate([got[:, 1:], got[:, :1]], 1).reshape(x.shape)
-        return x
+            parts = [part + swap(parts[u ^ (bit // 2)], bit) for u, part in enumerate(parts)]
+        return parts
 
     def shape(*dims, dtype=F32):
         return jax.ShapeDtypeStruct(dims, dtype)
@@ -335,15 +332,15 @@
     given = swap(inverse_prev, 1)
     arriving, mine, mates, given = lax.optimization_barrier((arriving, mine, mates, given))
     near = jnp.stack([jnp.broadcast_to(me, mine.shape), mine, mates])
-    kept = jnp.concatenate(arriving, 0)
-    mated = jnp.concatenate([given] + [swap(x, 1) for x in arriving[1:]], 0)
-    half = rows // 2
+    kept = arriving
+    mated = [given] + [swap(x, 1) for x in arriving[1:]]
+    chunk = shape(lay.own_rows, n, n)
     lists, local_list = shape(2 * cap, n, n), shape(lay.pairs, n, n)
     places = pltpu.SMEM((lay.slots + 1,), jnp.int32)
     fetching = (pltpu.SMEM(near.shape, jnp.int32), pltpu.SemaphoreType.DMA)
     split_rows, whole_rows = pltpu.VMEM((rows, n, 2 * n), BF16), pltpu.VMEM((rows, n, n), F32)
     for sweep in range(FSWEEPS):
-        inverse = jnp.concatenate([kept, mated], 0)
+        inverse = jnp.concatenate(kept + mated, 0)
         early, later = [], []
         if sweep == 0:
             out, lower = call(
@@ -399,19 +396,23 @@
             )
             early += [*lower_locals[1:], *mate_lowers[1:], below, above]
             later += [table]
-        keep, give = call(
+        parts = call(
             kernel(incoming_kernel),
-            [shape(half, n, n)] * 2,
+            [chunk] * n_tile,
             (),
             (here, lower, mate_lower, arrived),
             scratch=(whole_rows, pltpu.VMEM((2 * cap, n, 2 * n), BF16), *fetching),
             fetched=(near,),
             early=early,
         )
-        sums = summed(keep + swap(give, 1))
-        (kept,) = call(newton_kernel, [shape(half, n, n)], (), (kept, sums), early=later)
-        mated = swap(kept, 1)
-    inverse = jnp.concatenate([kept, mated], 0)
+        keep, give = parts[: n_tile // 2], parts[n_tile // 2 :]
+        sums = summed([lax.optimization_barrier(x + swap(y, 1)) for x, y in zip(keep, give)])
+        kept = [
+            call(newton_kernel, [chunk], (), (x, y), early=later if x is kept[0] else ())[0]
+            for x, y in zip(kept, sums)
+        ]
+        mated = [swap(x, 1) for x in kept]
+    inverse = lax.optimization_barrier(jnp.concatenate(kept + mated, 0))
 
     def scale(side, sources):
         return call(
@@ -457,7 +458,7 @@
         solved = jnp.where(
             (me[0] & bit) == 0, jnp.concatenate([solved, got], 1), jnp.concatenate([got, solved], 1)
         )
-    return (kept[: lay.own_rows], solved)
+    return (inverse[: lay.own_rows], solved)
 
 
 def solution(mesh):

time: 140 us -> 140 us (level)
  waiting for transfers between devices: 71.9 us -> 66.8 us
  starting transfers between devices: 37.6 us -> 41.1 us
    ppermute x24 -> x30, waiting for transfers between devices: 36.1 us -> 31.6 us  [swap(): return lax.ppermute(x, 'tile', [(i, i ^ bit) for i in range(n_tile)])]
    ppermute x24 -> x30, starting transfers between devices: 13.4 us -> 16.8 us  [swap(): return lax.ppermute(x, 'tile', [(i, i ^ bit) for i in range(n_tile)])]
    pallas_call x24 -> x26, Pallas kernels: 22 us -> 23.3 us  [call(): pl.pallas_call(body if not early else lambda *refs: body(*refs[len(early)...]
  transfers between devices with their start and end apart: 34 -> 40, of which waited for: 26 -> 27; matrix products, arithmetic and copies ran while one was open for 4% -> 4% of each run, Pallas kernels for 12% -> 14%
where the time goes in v10:
time: 140 us; the launch traced here: 139 us
  waiting for transfers between devices  66.8 us (48%)
  starting transfers between devices  41.1 us (29%)
  Pallas kernels  23.3 us (17%)
  local copies, waits for them, and re-layouts  4.68 us (3%)
  other arithmetic  1.96 us (1%)
    ppermute x10, waiting for transfers between devices, along(): return lax.ppermute(x, ('dom', 'tile'), route)  35.3 us
    ppermute x30, waiting for transfers between devices, swap(): return lax.ppermute(x, 'tile', [(i, i ^ bit) for i in range(n_tile)])  31.6 us
    ppermute x10, starting transfers between devices, along(): return lax.ppermute(x, ('dom', 'tile'), route)  24.4 us
    pallas_call x26, Pallas kernels, call(): pl.pallas_call(body if not early else lambda *refs: body(*refs[len(early)...  23.3 us
    ppermute x30, starting transfers between devices, swap(): return lax.ppermute(x, 'tile', [(i, i ^ bit) for i in range(n_tile)])  16.8 us
  transfers between devices with their start and end apart: 40, of which 27 were waited for; matrix products, arithmetic and copies ran while one was open for 4% of the time, Pallas kernels for 14%

profile of v10, /device:TPU:18, one launch (start us, length us, event | category | flops | bytes accessed | tf_op | source)
XLA Modules:
  0.0 139.1 jit_solution(6781506097704507553)
XLA Ops:
  0.7 1.6 %collective-permute-start = (f32[3,128,128]{2,1,0:T(8,128)}, f32[3,128,128]{2,1,0:T(8,128)S(1)}, u32[]{:S(2)}, u32[]{:S(2)}) collective-permute-start(f32[3,128,128]{2,1,0:T(8,128)} %refs_1_), channel_id=1, source_target_pairs={{0,2},{1,3},{2,0},{3,1},{4,6},{5,7},{6,4},{7,5},{8,10},{9,11},{10,... | collective-permute-start | bytes 589832 | tf_op jit(solution)/shard_map/ppermute | solution.py:301
  7.3 0.9 collective-permute-done.inverse
  8.3 0.9 constant_dynamic-update-slice_fusion.3
  9.7 0.9 shard_map.87
  10.7 3.5 %collective-permute-start.9 = (f32[8,128,128]{2,1,0:T(8,128)S(1)}, f32[8,128,128]{2,1,0:T(8,128)S(1)}, u32[]{:S(2)}, u32[]{:S(2)}) collective-permute-start(f32[8,128,128]{2,1,0:T(8,128)S(1)} %get-tuple-element.40), channel_id=1, source_target_pairs={{0,4},{1,9},{2,6},{3,11},{4,8},{5,13},{6,10},{7,15},{8,12},{9,17},... | collective-permute-start | bytes 1572872 | tf_op jit(solution)/shard_map/ppermute | solution.py:310
  14.2 1.6 %collective-permute-start.8 = (f32[8,128,128]{2,1,0:T(8,128)S(1)}, f32[8,128,128]{2,1,0:T(8,128)S(1)}, u32[]{:S(2)}, u32[]{:S(2)}) collective-permute-start(f32[8,128,128]{2,1,0:T(8,128)S(1)} %get-tuple-element.37.refs_3_.refs_6_.refs_0_), channel_id=1, source_target_pairs={{0,2},{1,3},{2,0},{3,1},{4,6},{5,7},{6,4},{7,5},{8,10},{9,11},{10,... | collective-permute-start | bytes 1572872 | tf_op jit(solution)/shard_map/ppermute | solution.py:301
  15.8 2.8 %shard_map.88 = (f32[12,128,128]{2,1,0:T(8,128)S(1)}, f32[8,128,128]{2,1,0:T(8,128)S(1)}, f32[4,128,128]{2,1,0:T(8,128)S(1)}, f32[12,128,128]{2,1,0:T(8,128)S(1)}, f32[8,128,128]{2,1,0:T(8,128)S(1)}) custom-call(s32[3,64]{1,0:T(4,128)S(1)} %pad_add_fusion.1.near_source.near.refs_1_.refs_4_, f32[12,128,128]{2,1,0:T(8,128)S(1)} %constant_dynamic-update-slice_fusion.inverse, ...), custom_call_target="tpu_custom_call" | custom-call | flops 201326592 | bytes 7012352 | tf_op jit(solution)/shard_map/pallas_call | solution.py:101
  18.5 7.1 %collective-permute-done.9.refs_5_ = f32[8,128,128]{2,1,0:T(8,128)S(1)} collective-permute-done((f32[8,128,128]{2,1,0:T(8,128)S(1)}, f32[8,128,128]{2,1,0:T(8,128)S(1)}, u32[]{:S(2)}, u32[]{:S(2)}) %collective-permute-start.9) | collective-permute-done | bytes 524320 | tf_op jit(solution)/shard_map/ppermute | solution.py:310
  25.7 2.3 %collective-permute-done.8.refs_0_.refs_3_ = f32[8,128,128]{2,1,0:T(8,128)S(1)} collective-permute-done((f32[8,128,128]{2,1,0:T(8,128)S(1)}, f32[8,128,128]{2,1,0:T(8,128)S(1)}, u32[]{:S(2)}, u32[]{:S(2)}) %collective-permute-start.8) | collective-permute-done | bytes 524320 | tf_op jit(solution)/shard_map/ppermute | solution.py:301
  27.9 1.0 shard_map.89
  29.6 0.9 collective-permute-done.10
  30.6 1.6 %collective-permute-start.15 = (f32[3,128,128]{2,1,0:T(8,128)S(1)}, f32[3,128,128]{2,1,0:T(8,128)S(1)}, u32[]{:S(2)}, u32[]{:S(2)}) collective-permute-start(f32[3,128,128]{2,1,0:T(8,128)S(1)} %add.42), channel_id=1, source_target_pairs={{0,2},{1,3},{2,0},{3,1},{4,6},{5,7},{6,4},{7,5},{8,10},{9,11},{10,... | collective-permute-start | bytes 589832 | tf_op jit(solution)/shard_map/ppermute | solution.py:301
  32.7 1.5 %collective-permute-start.3 = (s32[2,64]{1,0:T(2,128)S(1)}, s32[2,64]{1,0:T(2,128)S(1)}, u32[]{:S(2)}, u32[]{:S(2)}) collective-permute-start(s32[2,64]{1,0:T(2,128)S(1)} %pad_add_fusion.2), channel_id=1, source_target_pairs={{0,2},{1,3},{2,0},{3,1},{4,6},{5,7},{6,4},{7,5},{8,10},{9,11},{10,... | collective-permute-start | bytes 1544 | tf_op jit(solution)/shard_map/ppermute | solution.py:301
  34.3 7.6 %collective-permute-done.3 = s32[2,64]{1,0:T(2,128)S(1)} collective-permute-done((s32[2,64]{1,0:T(2,128)S(1)}, s32[2,64]{1,0:T(2,128)S(1)}, u32[]{:S(2)}, u32[]{:S(2)}) %collective-permute-start.3) | collective-permute-done | bytes 544 | tf_op jit(solution)/shard_map/ppermute | solution.py:301
  45.4 3.0 %collective-permute-start.18 = (f32[8,128,128]{2,1,0:T(8,128)S(1)}, f32[8,128,128]{2,1,0:T(8,128)S(1)}, u32[]{:S(2)}, u32[]{:S(2)}) collective-permute-start(f32[8,128,128]{2,1,0:T(8,128)S(1)} %shard_map.93), channel_id=1, source_target_pairs={{0,4},{1,9},{2,6},{3,11},{4,8},{5,13},{6,10},{7,15},{8,12},{9,17},... | collective-permute-start | bytes 1572872 | tf_op jit(solution)/shard_map/ppermute | solution.py:310
  48.4 1.6 %collective-permute-start.13 = (f32[4,128,128]{2,1,0:T(8,128)S(1)}, f32[4,128,128]{2,1,0:T(8,128)S(1)}, u32[]{:S(2)}, u32[]{:S(2)}) collective-permute-start(f32[4,128,128]{2,1,0:T(8,128)S(1)} %get-tuple-element.45.refs_1_), channel_id=1, source_target_pairs={{0,2},{1,3},{2,0},{3,1},{4,6},{5,7},{6,4},{7,5},{8,10},{9,11},{10,... | collective-permute-start | bytes 786440 | tf_op jit(solution)/shard_map/ppermute | solution.py:301
  50.0 2.8 %collective-permute-start.5 = (s32[4,64]{1,0:T(4,128)S(1)}, s32[4,64]{1,0:T(4,128)S(1)}, u32[]{:S(2)}, u32[]{:S(2)}) collective-permute-start(s32[4,64]{1,0:T(4,128)S(1)} %pad_add_fusion.metas.refs_0_), channel_id=1, source_target_pairs={{4,0},{6,2},{8,4},{9,1},{10,6},{11,3},{12,8},{13,5},{14,10},{15,7}... | collective-permute-start | bytes 3080 | tf_op jit(solution)/shard_map/ppermute | solution.py:310
  52.8 1.9 %collective-permute-start.4 = (s32[4,64]{1,0:T(4,128)S(1)}, s32[4,64]{1,0:T(4,128)S(1)}, u32[]{:S(2)}, u32[]{:S(2)}) collective-permute-start(s32[4,64]{1,0:T(4,128)S(1)} %pad_add_fusion.metas.refs_0_), channel_id=1, source_target_pairs={{0,8},{1,5},{2,10},{3,7},{4,12},{5,9},{6,14},{7,11},{8,16},{9,13},... | collective-permute-start | bytes 3080 | tf_op jit(solution)/shard_map/ppermute | solution.py:310
  54.7 2.4 %shard_map.92.refs_5_ = f32[12,128,128]{2,1,0:T(8,128)S(1)} custom-call(s32[3,64]{1,0:T(4,128)S(1)} %pad_add_fusion.1.near_source.near.refs_1_.refs_4_, f32[12,128,128]{2,1,0:T(8,128)S(1)} %pad_maximum_fusion.inverse, f32[3,128,128]{2,1,0:T(8,128)S(1)} %copy-done.1, f32[24,128,128]{2,1,0:T(8,128)S(1)} %bitcast.8), custom_call_target="tpu_custom_call" | custom-call | flops 201326592 | bytes 3342336 | tf_op jit(solution)/shard_map/pallas_call | solution.py:101
  57.1 4.4 %collective-permute-done.4.peers_below.refs_2_ = s32[4,64]{1,0:T(4,128)S(1)} collective-permute-done((s32[4,64]{1,0:T(4,128)S(1)}, s32[4,64]{1,0:T(4,128)S(1)}, u32[]{:S(2)}, u32[]{:S(2)}) %collective-permute-start.4) | collective-permute-done | bytes 1056 | tf_op jit(solution)/shard_map/ppermute | solution.py:310
  61.5 1.1 shard_map.94
  63.1 0.9 collective-permute-done.19
  64.1 1.6 %collective-permute-start.22 = (f32[3,128,128]{2,1,0:T(8,128)S(1)}, f32[3,128,128]{2,1,0:T(8,128)S(1)}, u32[]{:S(2)}, u32[]{:S(2)}) collective-permute-start(f32[3,128,128]{2,1,0:T(8,128)S(1)} %add.46), channel_id=1, source_target_pairs={{0,2},{1,3},{2,0},{3,1},{4,6},{5,7},{6,4},{7,5},{8,10},{9,11},{10,... | collective-permute-start | bytes 589832 | tf_op jit(solution)/shard_map/ppermute | solution.py:301
  66.3 2.1 %shard_map.86 = (s32[65]{0:T(128)S(1)}, f32[16,12,128]{2,1,0:T(8,128)S(1)}, f32[16,12,128]{2,1,0:T(8,128)S(1)}, f32[16,12,128]{2,1,0:T(8,128)S(1)}, f32[16,12,128]{2,1,0:T(8,128)S(1)}) custom-call(s32[1]{0:T(128)} %bitcast.me, s32[4,64]{1,0:T(4,128)S(1)} %pad_add_fusion.metas.refs_0_, s32[4,64]{1,0:T(4,128)S(1)} %collective-permute-done.4.peers_below.refs_2_, ...), custom_call_target="tpu_custom_call" | custom-call | bytes 393476 | tf_op jit(solution)/shard_map/pallas_call | solution.py:101
  68.4 3.5 %collective-permute-done.22 = f32[3,128,128]{2,1,0:T(8,128)S(1)} collective-permute-done((f32[3,128,128]{2,1,0:T(8,128)S(1)}, f32[3,128,128]{2,1,0:T(8,128)S(1)}, u32[]{:S(2)}, u32[]{:S(2)}) %collective-permute-start.22) | collective-permute-done | bytes 196640 | tf_op jit(solution)/shard_map/ppermute | solution.py:301
  72.4 2.9 %collective-permute-done.21 = f32[3,128,128]{2,1,0:T(8,128)S(1)} collective-permute-done((f32[3,128,128]{2,1,0:T(8,128)S(1)}, f32[3,128,128]{2,1,0:T(8,128)S(1)}, u32[]{:S(2)}, u32[]{:S(2)}) %collective-permute-start.21) | collective-permute-done | bytes 196640 | tf_op jit(solution)/shard_map/ppermute | solution.py:301
  75.8 1.6 %collective-permute-start.25 = (f32[12,128,128]{2,1,0:T(8,128)S(1)}, f32[12,128,128]{2,1,0:T(8,128)S(1)}, u32[]{:S(2)}, u32[]{:S(2)}) collective-permute-start(f32[12,128,128]{2,1,0:T(8,128)S(1)} %get-tuple-element.46.upper.refs_0_), channel_id=1, source_target_pairs={{0,2},{1,3},{2,0},{3,1},{4,6},{5,7},{6,4},{7,5},{8,10},{9,11},{10,... | collective-permute-start | bytes 2359304 | tf_op jit(solution)/shard_map/ppermute | solution.py:301
  77.9 2.2 %collective-permute-start.26 = (f32[12,16,128]{2,1,0:T(8,128)S(1)}, f32[12,16,128]{2,1,0:T(8,128)S(1)}, u32[]{:S(2)}, u32[]{:S(2)}) collective-permute-start(f32[12,16,128]{2,1,0:T(8,128)S(1)} %shard_map.97.x), channel_id=1, source_target_pairs={{0,8},{1,5},{2,10},{3,7},{4,12},{5,9},{6,14},{7,11},{8,16},{9,13},... | collective-permute-start | bytes 294920 | tf_op jit(solution)/shard_map/ppermute | solution.py:310
  80.1 1.2 shard_map.98
  82.1 3.2 %collective-permute-done.26.arrived = f32[12,16,128]{2,1,0:T(8,128)S(1)} collective-permute-done((f32[12,16,128]{2,1,0:T(8,128)S(1)}, f32[12,16,128]{2,1,0:T(8,128)S(1)}, u32[]{:S(2)}, u32[]{:S(2)}) %collective-permute-start.26) | collective-permute-done | bytes 98336 | tf_op jit(solution)/shard_map/ppermute | solution.py:310
  85.9 1.3 collective-permute-done.27
  87.3 2.2 %collective-permute-start.28 = (f32[12,16,128]{2,1,0:T(8,128)S(1)}, f32[12,16,128]{2,1,0:T(8,128)S(1)}, u32[]{:S(2)}, u32[]{:S(2)}) collective-permute-start(f32[12,16,128]{2,1,0:T(8,128)S(1)} %add_subtract_fusion.5.x), channel_id=1, source_target_pairs={{0,8},{1,5},{2,10},{3,7},{4,12},{5,9},{6,14},{7,11},{8,16},{9,13},... | collective-permute-start | bytes 294920 | tf_op jit(solution)/shard_map/ppermute | solution.py:310
  90.3 4.3 %collective-permute-done.28.arrived = f32[12,16,128]{2,1,0:T(8,128)S(1)} collective-permute-done((f32[12,16,128]{2,1,0:T(8,128)S(1)}, f32[12,16,128]{2,1,0:T(8,128)S(1)}, u32[]{:S(2)}, u32[]{:S(2)}) %collective-permute-start.28) | collective-permute-done | bytes 98336 | tf_op jit(solution)/shard_map/ppermute | solution.py:310
  96.5 2.2 %collective-permute-start.30 = (f32[12,16,128]{2,1,0:T(8,128)S(1)}, f32[12,16,128]{2,1,0:T(8,128)S(1)}, u32[]{:S(2)}, u32[]{:S(2)}) collective-permute-start(f32[12,16,128]{2,1,0:T(8,128)S(1)} %add_subtract_fusion.4.x), channel_id=1, source_target_pairs={{0,8},{1,5},{2,10},{3,7},{4,12},{5,9},{6,14},{7,11},{8,16},{9,13},... | collective-permute-start | bytes 294920 | tf_op jit(solution)/shard_map/ppermute | solution.py:310
  99.5 4.2 %collective-permute-done.30.refs_5_ = f32[12,16,128]{2,1,0:T(8,128)S(1)} collective-permute-done((f32[12,16,128]{2,1,0:T(8,128)S(1)}, f32[12,16,128]{2,1,0:T(8,128)S(1)}, u32[]{:S(2)}, u32[]{:S(2)}) %collective-permute-start.30) | collective-permute-done | bytes 98336 | tf_op jit(solution)/shard_map/ppermute | solution.py:310
  104.3 1.3 collective-permute-done.31
  105.6 2.7 %collective-permute-start.33 = (f32[12,16,128]{2,1,0:T(8,128)S(1)}, f32[12,16,128]{2,1,0:T(8,128)S(1)}, u32[]{:S(2)}, u32[]{:S(2)}) collective-permute-start(f32[12,16,128]{2,1,0:T(8,128)S(1)} %add_subtract_fusion.3.x), channel_id=1, source_target_pairs={{4,0},{6,2},{8,4},{9,1},{10,6},{11,3},{12,8},{13,5},{14,10},{15,7}... | collective-permute-start | bytes 294920 | tf_op jit(solution)/shard_map/ppermute | solution.py:310
  108.4 1.2 shard_map.105
  110.4 2.6 %collective-permute-done.33.arrived = f32[12,16,128]{2,1,0:T(8,128)S(1)} collective-permute-done((f32[12,16,128]{2,1,0:T(8,128)S(1)}, f32[12,16,128]{2,1,0:T(8,128)S(1)}, u32[]{:S(2)}, u32[]{:S(2)}) %collective-permute-start.33) | collective-permute-done | bytes 98336 | tf_op jit(solution)/shard_map/ppermute | solution.py:310
  113.6 1.3 collective-permute-done.34
  114.9 1.9 %collective-permute-start.35 = (f32[12,16,128]{2,1,0:T(8,128)S(1)}, f32[12,16,128]{2,1,0:T(8,128)S(1)}, u32[]{:S(2)}, u32[]{:S(2)}) collective-permute-start(f32[12,16,128]{2,1,0:T(8,128)S(1)} %add_subtract_fusion.2.x), channel_id=1, source_target_pairs={{4,0},{6,2},{8,4},{9,1},{10,6},{11,3},{12,8},{13,5},{14,10},{15,7}... | collective-permute-start | bytes 294920 | tf_op jit(solution)/shard_map/ppermute | solution.py:310
  117.7 4.7 %collective-permute-done.35.arrived = f32[12,16,128]{2,1,0:T(8,128)S(1)} collective-permute-done((f32[12,16,128]{2,1,0:T(8,128)S(1)}, f32[12,16,128]{2,1,0:T(8,128)S(1)}, u32[]{:S(2)}, u32[]{:S(2)}) %collective-permute-start.35) | collective-permute-done | bytes 98336 | tf_op jit(solution)/shard_map/ppermute | solution.py:310
  122.9 1.3 collective-permute-done.36
  124.2 1.9 %collective-permute-start.37 = (f32[12,16,128]{2,1,0:T(8,128)S(1)}, f32[12,16,128]{2,1,0:T(8,128)S(1)}, u32[]{:S(2)}, u32[]{:S(2)}) collective-permute-start(f32[12,16,128]{2,1,0:T(8,128)S(1)} %add_subtract_fusion.1.x), channel_id=1, source_target_pairs={{4,0},{6,2},{8,4},{9,1},{10,6},{11,3},{12,8},{13,5},{14,10},{15,7}... | collective-permute-start | bytes 294920 | tf_op jit(solution)/shard_map/ppermute | solution.py:310
  127.0 4.7 %collective-permute-done.37.arrived = f32[12,16,128]{2,1,0:T(8,128)S(1)} collective-permute-done((f32[12,16,128]{2,1,0:T(8,128)S(1)}, f32[12,16,128]{2,1,0:T(8,128)S(1)}, u32[]{:S(2)}, u32[]{:S(2)}) %collective-permute-start.37) | collective-permute-done | bytes 98336 | tf_op jit(solution)/shard_map/ppermute | solution.py:310
  132.2 1.3 collective-permute-done.38
  133.5 1.6 %collective-permute-start.39 = (f32[12,16,128]{2,1,0:T(8,128)S(1)}, f32[12,16,128]{2,1,0:T(8,128)S(1)}, u32[]{:S(2)}, u32[]{:S(2)}) collective-permute-start(f32[12,16,128]{2,1,0:T(8,128)S(1)} %add_subtract_fusion), channel_id=1, source_target_pairs={{0,2},{1,3},{2,0},{3,1},{4,6},{5,7},{6,4},{7,5},{8,10},{9,11},{10,... | collective-permute-start | bytes 294920 | tf_op jit(solution)/shard_map/ppermute | solution.py:301
  135.8 2.6 %collective-permute-done.39 = f32[12,16,128]{2,1,0:T(8,128)S(1)} collective-permute-done((f32[12,16,128]{2,1,0:T(8,128)S(1)}, f32[12,16,128]{2,1,0:T(8,128)S(1)}, u32[]{:S(2)}, u32[]{:S(2)}) %collective-permute-start.39) | collective-permute-done | bytes 98336 | tf_op jit(solution)/shard_map/ppermute | solution.py:301
  (98 shorter events, 23.8 us)
Async XLA Ops:
  0.6 9.1 %copy-start = (f32[12,2,128,128]{3,2,1,0:T(8,128)S(1)}, f32[12,2,128,128]{3,2,1,0:T(8,128)}, u32[]{:S(2)}) copy-start(f32[12,2,128,128]{3,2,1,0:T(8,128)} %param.10) | copy-start | bytes 4718596
  0.6 9.1 %collective-permute-start.7 = (f32[24,128,128]{2,1,0:T(8,128)}, f32[24,128,128]{2,1,0:T(8,128)S(1)}, u32[]{:S(2)}, u32[]{:S(2)}) collective-permute-start(f32[24,128,128]{2,1,0:T(8,128)} %bitcast.5), channel_id=1, source_target_pairs={{0,1},{1,0},{2,3},{3,2},{4,5},{5,4},{6,7},{7,6},{8,9},{9,8},{10,11... | collective-permute-start | bytes 4718600 | tf_op jit(solution)/shard_map/ppermute | solution.py:301
  0.7 7.5 %collective-permute-start = (f32[3,128,128]{2,1,0:T(8,128)}, f32[3,128,128]{2,1,0:T(8,128)S(1)}, u32[]{:S(2)}, u32[]{:S(2)}) collective-permute-start(f32[3,128,128]{2,1,0:T(8,128)} %refs_1_), channel_id=1, source_target_pairs={{0,2},{1,3},{2,0},{3,1},{4,6},{5,7},{6,4},{7,5},{8,10},{9,11},{10,... | collective-permute-start | bytes 589832 | tf_op jit(solution)/shard_map/ppermute | solution.py:301
  2.3 5.9 %collective-permute-start.2 = (f32[3,128,128]{2,1,0:T(8,128)}, f32[3,128,128]{2,1,0:T(8,128)S(1)}, u32[]{:S(2)}, u32[]{:S(2)}) collective-permute-start(f32[3,128,128]{2,1,0:T(8,128)} %refs_1_), channel_id=1, source_target_pairs={{0,1},{1,0},{2,3},{3,2},{4,5},{5,4},{6,7},{7,6},{8,9},{9,8},{10,11... | collective-permute-start | bytes 589832 | tf_op jit(solution)/shard_map/ppermute | solution.py:301
  6.2 1.2 collective-permute-start.1
  8.3 1.4 %collective-permute-start.6 = (f32[3,128,128]{2,1,0:T(8,128)S(1)}, f32[3,128,128]{2,1,0:T(8,128)S(1)}, u32[]{:S(2)}, u32[]{:S(2)}) collective-permute-start(f32[3,128,128]{2,1,0:T(8,128)S(1)} %collective-permute-done.inverse), channel_id=1, source_target_pairs={{0,1},{1,0},{2,3},{3,2},{4,5},{5,4},{6,7},{7,6},{8,9},{9,8},{10,11... | collective-permute-start | bytes 589832 | tf_op jit(solution)/shard_map/ppermute | solution.py:301
  9.7 6.0 %copy-start.1 = (f32[3,128,128]{2,1,0:T(8,128)S(1)}, f32[3,128,128]{2,1,0:T(8,128)}, u32[]{:S(2)}) copy-start(f32[3,128,128]{2,1,0:T(8,128)} %diag.3) | copy-start | bytes 589828
  10.7 15.0 %collective-permute-start.9 = (f32[8,128,128]{2,1,0:T(8,128)S(1)}, f32[8,128,128]{2,1,0:T(8,128)S(1)}, u32[]{:S(2)}, u32[]{:S(2)}) collective-permute-start(f32[8,128,128]{2,1,0:T(8,128)S(1)} %get-tuple-element.40), channel_id=1, source_target_pairs={{0,4},{1,9},{2,6},{3,11},{4,8},{5,13},{6,10},{7,15},{8,12},{9,17},... | collective-permute-start | bytes 1572872 | tf_op jit(solution)/shard_map/ppermute | solution.py:310
  14.2 13.8 %collective-permute-start.8 = (f32[8,128,128]{2,1,0:T(8,128)S(1)}, f32[8,128,128]{2,1,0:T(8,128)S(1)}, u32[]{:S(2)}, u32[]{:S(2)}) collective-permute-start(f32[8,128,128]{2,1,0:T(8,128)S(1)} %get-tuple-element.37.refs_3_.refs_6_.refs_0_), channel_id=1, source_target_pairs={{0,2},{1,3},{2,0},{3,1},{4,6},{5,7},{6,4},{7,5},{8,10},{9,11},{10,... | collective-permute-start | bytes 1572872 | tf_op jit(solution)/shard_map/ppermute | solution.py:301
  29.0 13.4 %copy-start.2 = (f32[3,128,128]{2,1,0:T(8,128)S(1)}, f32[3,128,128]{2,1,0:T(8,128)}, u32[]{:S(2)}) copy-start(f32[3,128,128]{2,1,0:T(8,128)} %refs_1_) | copy-start | bytes 589828
  29.0 1.5 %collective-permute-start.10 = (f32[3,128,128]{2,1,0:T(8,128)S(1)}, f32[3,128,128]{2,1,0:T(8,128)S(1)}, u32[]{:S(2)}, u32[]{:S(2)}) collective-permute-start(f32[3,128,128]{2,1,0:T(8,128)S(1)} %get-tuple-element.42), channel_id=1, source_target_pairs={{0,1},{1,0},{2,3},{3,2},{4,5},{5,4},{6,7},{7,6},{8,9},{9,8},{10,11... | collective-permute-start | bytes 589832 | tf_op jit(solution)/shard_map/ppermute | solution.py:301
  29.1 3.0 %collective-permute-start.11 = (f32[3,128,128]{2,1,0:T(8,128)S(1)}, f32[3,128,128]{2,1,0:T(8,128)S(1)}, u32[]{:S(2)}, u32[]{:S(2)}) collective-permute-start(f32[3,128,128]{2,1,0:T(8,128)S(1)} %get-tuple-element.44), channel_id=1, source_target_pairs={{0,1},{1,0},{2,3},{3,2},{4,5},{5,4},{6,7},{7,6},{8,9},{9,8},{10,11... | collective-permute-start | bytes 589832 | tf_op jit(solution)/shard_map/ppermute | solution.py:301
  30.6 11.3 %collective-permute-start.15 = (f32[3,128,128]{2,1,0:T(8,128)S(1)}, f32[3,128,128]{2,1,0:T(8,128)S(1)}, u32[]{:S(2)}, u32[]{:S(2)}) collective-permute-start(f32[3,128,128]{2,1,0:T(8,128)S(1)} %add.42), channel_id=1, source_target_pairs={{0,2},{1,3},{2,0},{3,1},{4,6},{5,7},{6,4},{7,5},{8,10},{9,11},{10,... | collective-permute-start | bytes 589832 | tf_op jit(solution)/shard_map/ppermute | solution.py:301
  32.2 10.2 %collective-permute-start.12 = (f32[3,128,128]{2,1,0:T(8,128)S(1)}, f32[3,128,128]{2,1,0:T(8,128)S(1)}, u32[]{:S(2)}, u32[]{:S(2)}) collective-permute-start(f32[3,128,128]{2,1,0:T(8,128)S(1)} %add.43), channel_id=1, source_target_pairs={{0,2},{1,3},{2,0},{3,1},{4,6},{5,7},{6,4},{7,5},{8,10},{9,11},{10,... | collective-permute-start | bytes 589832 | tf_op jit(solution)/shard_map/ppermute | solution.py:301
  32.7 9.1 %collective-permute-start.3 = (s32[2,64]{1,0:T(2,128)S(1)}, s32[2,64]{1,0:T(2,128)S(1)}, u32[]{:S(2)}, u32[]{:S(2)}) collective-permute-start(s32[2,64]{1,0:T(2,128)S(1)} %pad_add_fusion.2), channel_id=1, source_target_pairs={{0,2},{1,3},{2,0},{3,1},{4,6},{5,7},{6,4},{7,5},{8,10},{9,11},{10,... | collective-permute-start | bytes 1544 | tf_op jit(solution)/shard_map/ppermute | solution.py:301
  42.3 1.5 %collective-permute-start.17 = (f32[3,128,128]{2,1,0:T(8,128)S(1)}, f32[3,128,128]{2,1,0:T(8,128)S(1)}, u32[]{:S(2)}, u32[]{:S(2)}) collective-permute-start(f32[3,128,128]{2,1,0:T(8,128)S(1)} %shard_map.91.inverse), channel_id=1, source_target_pairs={{0,1},{1,0},{2,3},{3,2},{4,5},{5,4},{6,7},{7,6},{8,9},{9,8},{10,11... | collective-permute-start | bytes 589832 | tf_op jit(solution)/shard_map/ppermute | solution.py:301
  42.8 1.6 %collective-permute-start.16 = (f32[3,128,128]{2,1,0:T(8,128)S(1)}, f32[3,128,128]{2,1,0:T(8,128)S(1)}, u32[]{:S(2)}, u32[]{:S(2)}) collective-permute-start(f32[3,128,128]{2,1,0:T(8,128)S(1)} %shard_map.90.refs_1_), channel_id=1, source_target_pairs={{0,1},{1,0},{2,3},{3,2},{4,5},{5,4},{6,7},{7,6},{8,9},{9,8},{10,11... | collective-permute-start | bytes 589832 | tf_op jit(solution)/shard_map/ppermute | solution.py:301
  43.3 18.2 %collective-permute-start.14 = (f32[8,128,128]{2,1,0:T(8,128)S(1)}, f32[8,128,128]{2,1,0:T(8,128)S(1)}, u32[]{:S(2)}, u32[]{:S(2)}) collective-permute-start(f32[8,128,128]{2,1,0:T(8,128)S(1)} %collective-permute-done.8.refs_0_.refs_3_), channel_id=1, source_target_pairs={{0,1},{1,0},{2,3},{3,2},{4,5},{5,4},{6,7},{7,6},{8,9},{9,8},{10,11... | collective-permute-start | bytes 1572872 | tf_op jit(solution)/shard_map/ppermute | solution.py:301
  45.4 16.1 %collective-permute-start.18 = (f32[8,128,128]{2,1,0:T(8,128)S(1)}, f32[8,128,128]{2,1,0:T(8,128)S(1)}, u32[]{:S(2)}, u32[]{:S(2)}) collective-permute-start(f32[8,128,128]{2,1,0:T(8,128)S(1)} %shard_map.93), channel_id=1, source_target_pairs={{0,4},{1,9},{2,6},{3,11},{4,8},{5,13},{6,10},{7,15},{8,12},{9,17},... | collective-permute-start | bytes 1572872 | tf_op jit(solution)/shard_map/ppermute | solution.py:310
  48.4 13.1 %collective-permute-start.13 = (f32[4,128,128]{2,1,0:T(8,128)S(1)}, f32[4,128,128]{2,1,0:T(8,128)S(1)}, u32[]{:S(2)}, u32[]{:S(2)}) collective-permute-start(f32[4,128,128]{2,1,0:T(8,128)S(1)} %get-tuple-element.45.refs_1_), channel_id=1, source_target_pairs={{0,2},{1,3},{2,0},{3,1},{4,6},{5,7},{6,4},{7,5},{8,10},{9,11},{10,... | collective-permute-start | bytes 786440 | tf_op jit(solution)/shard_map/ppermute | solution.py:301
  50.0 7.1 %collective-permute-start.5 = (s32[4,64]{1,0:T(4,128)S(1)}, s32[4,64]{1,0:T(4,128)S(1)}, u32[]{:S(2)}, u32[]{:S(2)}) collective-permute-start(s32[4,64]{1,0:T(4,128)S(1)} %pad_add_fusion.metas.refs_0_), channel_id=1, source_target_pairs={{4,0},{6,2},{8,4},{9,1},{10,6},{11,3},{12,8},{13,5},{14,10},{15,7}... | collective-permute-start | bytes 3080 | tf_op jit(solution)/shard_map/ppermute | solution.py:310
  52.8 8.7 %collective-permute-start.4 = (s32[4,64]{1,0:T(4,128)S(1)}, s32[4,64]{1,0:T(4,128)S(1)}, u32[]{:S(2)}, u32[]{:S(2)}) collective-permute-start(s32[4,64]{1,0:T(4,128)S(1)} %pad_add_fusion.metas.refs_0_), channel_id=1, source_target_pairs={{0,8},{1,5},{2,10},{3,7},{4,12},{5,9},{6,14},{7,11},{8,16},{9,13},... | collective-permute-start | bytes 3080 | tf_op jit(solution)/shard_map/ppermute | solution.py:310
  62.6 1.5 %collective-permute-start.19 = (f32[3,128,128]{2,1,0:T(8,128)S(1)}, f32[3,128,128]{2,1,0:T(8,128)S(1)}, u32[]{:S(2)}, u32[]{:S(2)}) collective-permute-start(f32[3,128,128]{2,1,0:T(8,128)S(1)} %get-tuple-element.49), channel_id=1, source_target_pairs={{0,1},{1,0},{2,3},{3,2},{4,5},{5,4},{6,7},{7,6},{8,9},{9,8},{10,11... | collective-permute-start | bytes 589832 | tf_op jit(solution)/shard_map/ppermute | solution.py:301
  62.6 3.1 %collective-permute-start.20 = (f32[3,128,128]{2,1,0:T(8,128)S(1)}, f32[3,128,128]{2,1,0:T(8,128)S(1)}, u32[]{:S(2)}, u32[]{:S(2)}) collective-permute-start(f32[3,128,128]{2,1,0:T(8,128)S(1)} %get-tuple-element.51), channel_id=1, source_target_pairs={{0,1},{1,0},{2,3},{3,2},{4,5},{5,4},{6,7},{7,6},{8,9},{9,8},{10,11... | collective-permute-start | bytes 589832 | tf_op jit(solution)/shard_map/ppermute | solution.py:301
  64.1 7.8 %collective-permute-start.22 = (f32[3,128,128]{2,1,0:T(8,128)S(1)}, f32[3,128,128]{2,1,0:T(8,128)S(1)}, u32[]{:S(2)}, u32[]{:S(2)}) collective-permute-start(f32[3,128,128]{2,1,0:T(8,128)S(1)} %add.46), channel_id=1, source_target_pairs={{0,2},{1,3},{2,0},{3,1},{4,6},{5,7},{6,4},{7,5},{8,10},{9,11},{10,... | collective-permute-start | bytes 589832 | tf_op jit(solution)/shard_map/ppermute | solution.py:301
  65.7 9.6 %collective-permute-start.21 = (f32[3,128,128]{2,1,0:T(8,128)S(1)}, f32[3,128,128]{2,1,0:T(8,128)S(1)}, u32[]{:S(2)}, u32[]{:S(2)}) collective-permute-start(f32[3,128,128]{2,1,0:T(8,128)S(1)} %add.47), channel_id=1, source_target_pairs={{0,2},{1,3},{2,0},{3,1},{4,6},{5,7},{6,4},{7,5},{8,10},{9,11},{10,... | collective-permute-start | bytes 589832 | tf_op jit(solution)/shard_map/ppermute | solution.py:301
  71.9 5.5 %copy-start.3 = (f32[12,32,128]{2,1,0:T(8,128)S(1)}, f32[12,32,128]{2,1,0:T(8,128)}, u32[]{:S(2)}) copy-start(f32[12,32,128]{2,1,0:T(8,128)} %base.1) | copy-start | bytes 589828
  72.3 5.1 %collective-permute-start.24 = (f32[3,128,128]{2,1,0:T(8,128)S(1)}, f32[3,128,128]{2,1,0:T(8,128)S(1)}, u32[]{:S(2)}, u32[]{:S(2)}) collective-permute-start(f32[3,128,128]{2,1,0:T(8,128)S(1)} %shard_map.96), channel_id=1, source_target_pairs={{0,1},{1,0},{2,3},{3,2},{4,5},{5,4},{6,7},{7,6},{8,9},{9,8},{10,11... | collective-permute-start | bytes 589832 | tf_op jit(solution)/shard_map/ppermute | solution.py:301
  75.7 1.7 %collective-permute-start.23 = (f32[3,128,128]{2,1,0:T(8,128)S(1)}, f32[3,128,128]{2,1,0:T(8,128)S(1)}, u32[]{:S(2)}, u32[]{:S(2)}) collective-permute-start(f32[3,128,128]{2,1,0:T(8,128)S(1)} %shard_map.95), channel_id=1, source_target_pairs={{0,1},{1,0},{2,3},{3,2},{4,5},{5,4},{6,7},{7,6},{8,9},{9,8},{10,11... | collective-permute-start | bytes 589832 | tf_op jit(solution)/shard_map/ppermute | solution.py:301
  75.8 20.0 %collective-permute-start.25 = (f32[12,128,128]{2,1,0:T(8,128)S(1)}, f32[12,128,128]{2,1,0:T(8,128)S(1)}, u32[]{:S(2)}, u32[]{:S(2)}) collective-permute-start(f32[12,128,128]{2,1,0:T(8,128)S(1)} %get-tuple-element.46.upper.refs_0_), channel_id=1, source_target_pairs={{0,2},{1,3},{2,0},{3,1},{4,6},{5,7},{6,4},{7,5},{8,10},{9,11},{10,... | collective-permute-start | bytes 2359304 | tf_op jit(solution)/shard_map/ppermute | solution.py:301
  77.9 7.5 %collective-permute-start.26 = (f32[12,16,128]{2,1,0:T(8,128)S(1)}, f32[12,16,128]{2,1,0:T(8,128)S(1)}, u32[]{:S(2)}, u32[]{:S(2)}) collective-permute-start(f32[12,16,128]{2,1,0:T(8,128)S(1)} %shard_map.97.x), channel_id=1, source_target_pairs={{0,8},{1,5},{2,10},{3,7},{4,12},{5,9},{6,14},{7,11},{8,16},{9,13},... | collective-permute-start | bytes 294920 | tf_op jit(solution)/shard_map/ppermute | solution.py:310
  85.9 1.4 collective-permute-start.27
  87.3 7.4 %collective-permute-start.28 = (f32[12,16,128]{2,1,0:T(8,128)S(1)}, f32[12,16,128]{2,1,0:T(8,128)S(1)}, u32[]{:S(2)}, u32[]{:S(2)}) collective-permute-start(f32[12,16,128]{2,1,0:T(8,128)S(1)} %add_subtract_fusion.5.x), channel_id=1, source_target_pairs={{0,8},{1,5},{2,10},{3,7},{4,12},{5,9},{6,14},{7,11},{8,16},{9,13},... | collective-permute-start | bytes 294920 | tf_op jit(solution)/shard_map/ppermute | solution.py:310
  95.1 1.4 collective-permute-start.29
  95.8 12.6 %collective-permute-start.32 = (f32[12,128,128]{2,1,0:T(8,128)S(1)}, f32[12,128,128]{2,1,0:T(8,128)S(1)}, u32[]{:S(2)}, u32[]{:S(2)}) collective-permute-start(f32[12,128,128]{2,1,0:T(8,128)S(1)} %collective-permute-done.25.refs_0_.refs_2_), channel_id=1, source_target_pairs={{0,1},{1,0},{2,3},{3,2},{4,5},{5,4},{6,7},{7,6},{8,9},{9,8},{10,11... | collective-permute-start | bytes 2359304 | tf_op jit(solution)/shard_map/ppermute | solution.py:301
  96.5 7.3 %collective-permute-start.30 = (f32[12,16,128]{2,1,0:T(8,128)S(1)}, f32[12,16,128]{2,1,0:T(8,128)S(1)}, u32[]{:S(2)}, u32[]{:S(2)}) collective-permute-start(f32[12,16,128]{2,1,0:T(8,128)S(1)} %add_subtract_fusion.4.x), channel_id=1, source_target_pairs={{0,8},{1,5},{2,10},{3,7},{4,12},{5,9},{6,14},{7,11},{8,16},{9,13},... | collective-permute-start | bytes 294920 | tf_op jit(solution)/shard_map/ppermute | solution.py:310
  104.3 1.4 collective-permute-start.31
  105.6 7.4 %collective-permute-start.33 = (f32[12,16,128]{2,1,0:T(8,128)S(1)}, f32[12,16,128]{2,1,0:T(8,128)S(1)}, u32[]{:S(2)}, u32[]{:S(2)}) collective-permute-start(f32[12,16,128]{2,1,0:T(8,128)S(1)} %add_subtract_fusion.3.x), channel_id=1, source_target_pairs={{4,0},{6,2},{8,4},{9,1},{10,6},{11,3},{12,8},{13,5},{14,10},{15,7}... | collective-permute-start | bytes 294920 | tf_op jit(solution)/shard_map/ppermute | solution.py:310
  113.5 1.4 collective-permute-start.34
  114.9 7.4 %collective-permute-start.35 = (f32[12,16,128]{2,1,0:T(8,128)S(1)}, f32[12,16,128]{2,1,0:T(8,128)S(1)}, u32[]{:S(2)}, u32[]{:S(2)}) collective-permute-start(f32[12,16,128]{2,1,0:T(8,128)S(1)} %add_subtract_fusion.2.x), channel_id=1, source_target_pairs={{4,0},{6,2},{8,4},{9,1},{10,6},{11,3},{12,8},{13,5},{14,10},{15,7}... | collective-permute-start | bytes 294920 | tf_op jit(solution)/shard_map/ppermute | solution.py:310
  122.8 1.4 collective-permute-start.36
  124.2 7.4 %collective-permute-start.37 = (f32[12,16,128]{2,1,0:T(8,128)S(1)}, f32[12,16,128]{2,1,0:T(8,128)S(1)}, u32[]{:S(2)}, u32[]{:S(2)}) collective-permute-start(f32[12,16,128]{2,1,0:T(8,128)S(1)} %add_subtract_fusion.1.x), channel_id=1, source_target_pairs={{4,0},{6,2},{8,4},{9,1},{10,6},{11,3},{12,8},{13,5},{14,10},{15,7}... | collective-permute-start | bytes 294920 | tf_op jit(solution)/shard_map/ppermute | solution.py:310
  132.1 1.4 collective-permute-start.38
  133.5 4.9 %collective-permute-start.39 = (f32[12,16,128]{2,1,0:T(8,128)S(1)}, f32[12,16,128]{2,1,0:T(8,128)S(1)}, u32[]{:S(2)}, u32[]{:S(2)}) collective-permute-start(f32[12,16,128]{2,1,0:T(8,128)S(1)} %add_subtract_fusion), channel_id=1, source_target_pairs={{0,2},{1,3},{2,0},{3,1},{4,6},{5,7},{6,4},{7,5},{8,10},{9,11},{10,... | collective-permute-start | bytes 294920 | tf_op jit(solution)/shard_map/ppermute | solution.py:301

commit v11 on v10

--- a/solution.py
+++ b/solution.py
@@ -362,8 +362,7 @@
                 scratch=(places,),
             )
             early += lowers[1:]
-            metas = jnp.concatenate(over_chips(near[1:]), 0)
-            later += [metas]
+            later = over_chips(near[1:])
         else:
             (out,) = call(
                 kernel(next_outgoing_kernel),
@@ -407,10 +406,11 @@
         )
         keep, give = parts[: n_tile // 2], parts[n_tile // 2 :]
         sums = summed([lax.optimization_barrier(x + swap(y, 1)) for x, y in zip(keep, give)])
-        kept = [
-            call(newton_kernel, [chunk], (), (x, y), early=later if x is kept[0] else ())[0]
-            for x, y in zip(kept, sums)
-        ]
+        fresh = [call(newton_kernel, [chunk], (), (x, y))[0] for x, y in zip(kept[1:], sums[1:])]
+        if sweep == 0:
+            metas = jnp.concatenate(lax.optimization_barrier((later, fresh))[0], 0)
+            later = [metas]
+        kept = [*call(newton_kernel, [chunk], (), (kept[0], sums[0]), early=later), *fresh]
         mated = [swap(x, 1) for x in kept]
     inverse = lax.optimization_barrier(jnp.concatenate(kept + mated, 0))
 

time: 140 us -> 139 us (level)
  Pallas kernels: 23.3 us -> 21.9 us
    pallas_call x26, Pallas kernels: 23.3 us -> 21.9 us  [call(): pl.pallas_call(body if not early else lambda *refs: body(*refs[len(early)...]
  transfers between devices with their start and end apart: 40 -> 40, of which waited for: 27 -> 28; matrix products, arithmetic and copies ran while one was open for 4% -> 4% of each run, Pallas kernels for 14% -> 12%
where the time goes in v11:
time: 139 us
  waiting for transfers between devices  67.8 us (49%)
  starting transfers between devices  41.1 us (30%)
  Pallas kernels  21.9 us (16%)
  local copies, waits for them, and re-layouts  4.68 us (3%)
  other arithmetic  1.95 us (1%)
    ppermute x10, waiting for transfers between devices, along(): return lax.ppermute(x, ('dom', 'tile'), route)  36.5 us
    ppermute x30, waiting for transfers between devices, swap(): return lax.ppermute(x, 'tile', [(i, i ^ bit) for i in range(n_tile)])  31.3 us
    ppermute x10, starting transfers between devices, along(): return lax.ppermute(x, ('dom', 'tile'), route)  24.4 us
    pallas_call x26, Pallas kernels, call(): pl.pallas_call(body if not early else lambda *refs: body(*refs[len(early)...  21.9 us
    ppermute x30, starting transfers between devices, swap(): return lax.ppermute(x, 'tile', [(i, i ^ bit) for i in range(n_tile)])  16.7 us
  transfers between devices with their start and end apart: 40, of which 28 were waited for; matrix products, arithmetic and copies ran while one was open for 4% of the time, Pallas kernels for 12%

profile of v11, /device:TPU:18, one launch (start us, length us, event | category | flops | bytes accessed | tf_op | source)
XLA Modules:
  0.0 138.7 jit_solution(7684418111993037454)
XLA Ops:
  0.7 1.6 %collective-permute-start = (f32[3,128,128]{2,1,0:T(8,128)}, f32[3,128,128]{2,1,0:T(8,128)S(1)}, u32[]{:S(2)}, u32[]{:S(2)}) collective-permute-start(f32[3,128,128]{2,1,0:T(8,128)} %refs_1_), channel_id=1, source_target_pairs={{0,2},{1,3},{2,0},{3,1},{4,6},{5,7},{6,4},{7,5},{8,10},{9,11},{10,... | collective-permute-start | bytes 589832 | tf_op jit(solution)/shard_map/ppermute | solution.py:301
  8.3 0.9 constant_dynamic-update-slice_fusion.3
  9.7 0.9 shard_map.86
  10.7 3.5 %collective-permute-start.7 = (f32[8,128,128]{2,1,0:T(8,128)S(1)}, f32[8,128,128]{2,1,0:T(8,128)S(1)}, u32[]{:S(2)}, u32[]{:S(2)}) collective-permute-start(f32[8,128,128]{2,1,0:T(8,128)S(1)} %get-tuple-element.41), channel_id=1, source_target_pairs={{0,4},{1,9},{2,6},{3,11},{4,8},{5,13},{6,10},{7,15},{8,12},{9,17},... | collective-permute-start | bytes 1572872 | tf_op jit(solution)/shard_map/ppermute | solution.py:310
  14.2 1.6 %collective-permute-start.6 = (f32[8,128,128]{2,1,0:T(8,128)S(1)}, f32[8,128,128]{2,1,0:T(8,128)S(1)}, u32[]{:S(2)}, u32[]{:S(2)}) collective-permute-start(f32[8,128,128]{2,1,0:T(8,128)S(1)} %get-tuple-element.38.refs_3_.refs_6_.refs_0_), channel_id=1, source_target_pairs={{0,2},{1,3},{2,0},{3,1},{4,6},{5,7},{6,4},{7,5},{8,10},{9,11},{10,... | collective-permute-start | bytes 1572872 | tf_op jit(solution)/shard_map/ppermute | solution.py:301
  15.8 2.1 %shard_map.87 = (f32[12,128,128]{2,1,0:T(8,128)S(1)}, f32[8,128,128]{2,1,0:T(8,128)S(1)}, f32[4,128,128]{2,1,0:T(8,128)S(1)}, f32[12,128,128]{2,1,0:T(8,128)S(1)}, f32[8,128,128]{2,1,0:T(8,128)S(1)}) custom-call(s32[3,64]{1,0:T(4,128)S(1)} %pad_add_fusion.near_source.near.refs_1_.refs_4_, f32[12,128,128]{2,1,0:T(8,128)S(1)} %constant_dynamic-update-slice_fusion.inverse, ...), custom_call_target="tpu_custom_call" | custom-call | flops 201326592 | bytes 7012352 | tf_op jit(solution)/shard_map/pallas_call | solution.py:101
  17.8 7.8 %collective-permute-done.7.refs_5_ = f32[8,128,128]{2,1,0:T(8,128)S(1)} collective-permute-done((f32[8,128,128]{2,1,0:T(8,128)S(1)}, f32[8,128,128]{2,1,0:T(8,128)S(1)}, u32[]{:S(2)}, u32[]{:S(2)}) %collective-permute-start.7) | collective-permute-done | bytes 524320 | tf_op jit(solution)/shard_map/ppermute | solution.py:310
  25.7 2.3 %collective-permute-done.6.refs_0_.refs_3_ = f32[8,128,128]{2,1,0:T(8,128)S(1)} collective-permute-done((f32[8,128,128]{2,1,0:T(8,128)S(1)}, f32[8,128,128]{2,1,0:T(8,128)S(1)}, u32[]{:S(2)}, u32[]{:S(2)}) %collective-permute-start.6) | collective-permute-done | bytes 524320 | tf_op jit(solution)/shard_map/ppermute | solution.py:301
  27.9 1.0 shard_map.88
  29.6 0.9 collective-permute-done.9
  30.6 1.6 %collective-permute-start.10 = (f32[3,128,128]{2,1,0:T(8,128)S(1)}, f32[3,128,128]{2,1,0:T(8,128)S(1)}, u32[]{:S(2)}, u32[]{:S(2)}) collective-permute-start(f32[3,128,128]{2,1,0:T(8,128)S(1)} %add.43), channel_id=1, source_target_pairs={{0,2},{1,3},{2,0},{3,1},{4,6},{5,7},{6,4},{7,5},{8,10},{9,11},{10,... | collective-permute-start | bytes 589832 | tf_op jit(solution)/shard_map/ppermute | solution.py:301
  32.7 1.5 %collective-permute-start.3 = (s32[2,64]{1,0:T(2,128)S(1)}, s32[2,64]{1,0:T(2,128)S(1)}, u32[]{:S(2)}, u32[]{:S(2)}) collective-permute-start(s32[2,64]{1,0:T(2,128)S(1)} %pad_add_fusion.2), channel_id=1, source_target_pairs={{0,2},{1,3},{2,0},{3,1},{4,6},{5,7},{6,4},{7,5},{8,10},{9,11},{10,... | collective-permute-start | bytes 1544 | tf_op jit(solution)/shard_map/ppermute | solution.py:301
  34.3 4.1 %collective-permute-done.10 = f32[3,128,128]{2,1,0:T(8,128)S(1)} collective-permute-done((f32[3,128,128]{2,1,0:T(8,128)S(1)}, f32[3,128,128]{2,1,0:T(8,128)S(1)}, u32[]{:S(2)}, u32[]{:S(2)}) %collective-permute-start.10) | collective-permute-done | bytes 196640 | tf_op jit(solution)/shard_map/ppermute | solution.py:301
  38.8 3.1 %collective-permute-done.3 = s32[2,64]{1,0:T(2,128)S(1)} collective-permute-done((s32[2,64]{1,0:T(2,128)S(1)}, s32[2,64]{1,0:T(2,128)S(1)}, u32[]{:S(2)}, u32[]{:S(2)}) %collective-permute-start.3) | collective-permute-done | bytes 544 | tf_op jit(solution)/shard_map/ppermute | solution.py:301
  45.0 3.0 %collective-permute-start.18 = (f32[8,128,128]{2,1,0:T(8,128)S(1)}, f32[8,128,128]{2,1,0:T(8,128)S(1)}, u32[]{:S(2)}, u32[]{:S(2)}) collective-permute-start(f32[8,128,128]{2,1,0:T(8,128)S(1)} %shard_map.93), channel_id=1, source_target_pairs={{0,4},{1,9},{2,6},{3,11},{4,8},{5,13},{6,10},{7,15},{8,12},{9,17},... | collective-permute-start | bytes 1572872 | tf_op jit(solution)/shard_map/ppermute | solution.py:310
  48.0 1.6 %collective-permute-start.14 = (f32[4,128,128]{2,1,0:T(8,128)S(1)}, f32[4,128,128]{2,1,0:T(8,128)S(1)}, u32[]{:S(2)}, u32[]{:S(2)}) collective-permute-start(f32[4,128,128]{2,1,0:T(8,128)S(1)} %get-tuple-element.49.refs_1_), channel_id=1, source_target_pairs={{0,2},{1,3},{2,0},{3,1},{4,6},{5,7},{6,4},{7,5},{8,10},{9,11},{10,... | collective-permute-start | bytes 786440 | tf_op jit(solution)/shard_map/ppermute | solution.py:301
  49.6 2.8 %collective-permute-start.12 = (s32[4,64]{1,0:T(4,128)S(1)}, s32[4,64]{1,0:T(4,128)S(1)}, u32[]{:S(2)}, u32[]{:S(2)}) collective-permute-start(s32[4,64]{1,0:T(4,128)S(1)} %pad_add_fusion.1.metas.refs_0_), channel_id=1, source_target_pairs={{4,0},{6,2},{8,4},{9,1},{10,6},{11,3},{12,8},{13,5},{14,10},{15,7}... | collective-permute-start | bytes 3080 | tf_op jit(solution)/shard_map/ppermute | solution.py:310
  52.4 1.9 %collective-permute-start.11 = (s32[4,64]{1,0:T(4,128)S(1)}, s32[4,64]{1,0:T(4,128)S(1)}, u32[]{:S(2)}, u32[]{:S(2)}) collective-permute-start(s32[4,64]{1,0:T(4,128)S(1)} %pad_add_fusion.1.metas.refs_0_), channel_id=1, source_target_pairs={{0,8},{1,5},{2,10},{3,7},{4,12},{5,9},{6,14},{7,11},{8,16},{9,13},... | collective-permute-start | bytes 3080 | tf_op jit(solution)/shard_map/ppermute | solution.py:310
  54.4 1.7 %shard_map.92.refs_5_ = f32[12,128,128]{2,1,0:T(8,128)S(1)} custom-call(s32[3,64]{1,0:T(4,128)S(1)} %pad_add_fusion.near_source.near.refs_1_.refs_4_, f32[12,128,128]{2,1,0:T(8,128)S(1)} %pad_maximum_fusion.inverse, f32[3,128,128]{2,1,0:T(8,128)S(1)} %copy-done.1, f32[24,128,128]{2,1,0:T(8,128)S(1)} %bitcast.8), custom_call_target="tpu_custom_call" | custom-call | flops 201326592 | bytes 3342336 | tf_op jit(solution)/shard_map/pallas_call | solution.py:101
  56.1 4.9 %collective-permute-done.11.peers_below.refs_2_ = s32[4,64]{1,0:T(4,128)S(1)} collective-permute-done((s32[4,64]{1,0:T(4,128)S(1)}, s32[4,64]{1,0:T(4,128)S(1)}, u32[]{:S(2)}, u32[]{:S(2)}) %collective-permute-start.11) | collective-permute-done | bytes 1056 | tf_op jit(solution)/shard_map/ppermute | solution.py:310
  61.0 1.0 shard_map.94
  62.7 0.9 collective-permute-done.19
  63.6 1.6 %collective-permute-start.22 = (f32[3,128,128]{2,1,0:T(8,128)S(1)}, f32[3,128,128]{2,1,0:T(8,128)S(1)}, u32[]{:S(2)}, u32[]{:S(2)}) collective-permute-start(f32[3,128,128]{2,1,0:T(8,128)S(1)} %add.46), channel_id=1, source_target_pairs={{0,2},{1,3},{2,0},{3,1},{4,6},{5,7},{6,4},{7,5},{8,10},{9,11},{10,... | collective-permute-start | bytes 589832 | tf_op jit(solution)/shard_map/ppermute | solution.py:301
  65.8 2.1 %shard_map.90 = (s32[65]{0:T(128)S(1)}, f32[16,12,128]{2,1,0:T(8,128)S(1)}, f32[16,12,128]{2,1,0:T(8,128)S(1)}, f32[16,12,128]{2,1,0:T(8,128)S(1)}, f32[16,12,128]{2,1,0:T(8,128)S(1)}) custom-call(s32[1]{0:T(128)} %bitcast.me, s32[4,64]{1,0:T(4,128)S(1)} %pad_add_fusion.1.metas.refs_0_, s32[4,64]{1,0:T(4,128)S(1)} %collective-permute-done.11.peers_below.refs_2_, ...), custom_call_target="tpu_custom_call" | custom-call | bytes 393476 | tf_op jit(solution)/shard_map/pallas_call | solution.py:101
  68.0 3.5 %collective-permute-done.22 = f32[3,128,128]{2,1,0:T(8,128)S(1)} collective-permute-done((f32[3,128,128]{2,1,0:T(8,128)S(1)}, f32[3,128,128]{2,1,0:T(8,128)S(1)}, u32[]{:S(2)}, u32[]{:S(2)}) %collective-permute-start.22) | collective-permute-done | bytes 196640 | tf_op jit(solution)/shard_map/ppermute | solution.py:301
  71.9 2.9 %collective-permute-done.21 = f32[3,128,128]{2,1,0:T(8,128)S(1)} collective-permute-done((f32[3,128,128]{2,1,0:T(8,128)S(1)}, f32[3,128,128]{2,1,0:T(8,128)S(1)}, u32[]{:S(2)}, u32[]{:S(2)}) %collective-permute-start.21) | collective-permute-done | bytes 196640 | tf_op jit(solution)/shard_map/ppermute | solution.py:301
  75.3 1.6 %collective-permute-start.25 = (f32[12,128,128]{2,1,0:T(8,128)S(1)}, f32[12,128,128]{2,1,0:T(8,128)S(1)}, u32[]{:S(2)}, u32[]{:S(2)}) collective-permute-start(f32[12,128,128]{2,1,0:T(8,128)S(1)} %get-tuple-element.50.upper.refs_0_), channel_id=1, source_target_pairs={{0,2},{1,3},{2,0},{3,1},{4,6},{5,7},{6,4},{7,5},{8,10},{9,11},{10,... | collective-permute-start | bytes 2359304 | tf_op jit(solution)/shard_map/ppermute | solution.py:301
  77.4 2.2 %collective-permute-start.26 = (f32[12,16,128]{2,1,0:T(8,128)S(1)}, f32[12,16,128]{2,1,0:T(8,128)S(1)}, u32[]{:S(2)}, u32[]{:S(2)}) collective-permute-start(f32[12,16,128]{2,1,0:T(8,128)S(1)} %shard_map.97.x), channel_id=1, source_target_pairs={{0,8},{1,5},{2,10},{3,7},{4,12},{5,9},{6,14},{7,11},{8,16},{9,13},... | collective-permute-start | bytes 294920 | tf_op jit(solution)/shard_map/ppermute | solution.py:310
  79.6 1.2 shard_map.98
  81.6 3.2 %collective-permute-done.26.arrived = f32[12,16,128]{2,1,0:T(8,128)S(1)} collective-permute-done((f32[12,16,128]{2,1,0:T(8,128)S(1)}, f32[12,16,128]{2,1,0:T(8,128)S(1)}, u32[]{:S(2)}, u32[]{:S(2)}) %collective-permute-start.26) | collective-permute-done | bytes 98336 | tf_op jit(solution)/shard_map/ppermute | solution.py:310
  85.4 1.3 collective-permute-done.27
  86.8 2.2 %collective-permute-start.28 = (f32[12,16,128]{2,1,0:T(8,128)S(1)}, f32[12,16,128]{2,1,0:T(8,128)S(1)}, u32[]{:S(2)}, u32[]{:S(2)}) collective-permute-start(f32[12,16,128]{2,1,0:T(8,128)S(1)} %add_subtract_fusion.5.x), channel_id=1, source_target_pairs={{0,8},{1,5},{2,10},{3,7},{4,12},{5,9},{6,14},{7,11},{8,16},{9,13},... | collective-permute-start | bytes 294920 | tf_op jit(solution)/shard_map/ppermute | solution.py:310
  89.8 4.3 %collective-permute-done.28.arrived = f32[12,16,128]{2,1,0:T(8,128)S(1)} collective-permute-done((f32[12,16,128]{2,1,0:T(8,128)S(1)}, f32[12,16,128]{2,1,0:T(8,128)S(1)}, u32[]{:S(2)}, u32[]{:S(2)}) %collective-permute-start.28) | collective-permute-done | bytes 98336 | tf_op jit(solution)/shard_map/ppermute | solution.py:310
  96.0 2.2 %collective-permute-start.30 = (f32[12,16,128]{2,1,0:T(8,128)S(1)}, f32[12,16,128]{2,1,0:T(8,128)S(1)}, u32[]{:S(2)}, u32[]{:S(2)}) collective-permute-start(f32[12,16,128]{2,1,0:T(8,128)S(1)} %add_subtract_fusion.4.x), channel_id=1, source_target_pairs={{0,8},{1,5},{2,10},{3,7},{4,12},{5,9},{6,14},{7,11},{8,16},{9,13},... | collective-permute-start | bytes 294920 | tf_op jit(solution)/shard_map/ppermute | solution.py:310
  99.0 4.2 %collective-permute-done.30.refs_5_ = f32[12,16,128]{2,1,0:T(8,128)S(1)} collective-permute-done((f32[12,16,128]{2,1,0:T(8,128)S(1)}, f32[12,16,128]{2,1,0:T(8,128)S(1)}, u32[]{:S(2)}, u32[]{:S(2)}) %collective-permute-start.30) | collective-permute-done | bytes 98336 | tf_op jit(solution)/shard_map/ppermute | solution.py:310
  103.9 1.3 collective-permute-done.31
  105.2 2.7 %collective-permute-start.33 = (f32[12,16,128]{2,1,0:T(8,128)S(1)}, f32[12,16,128]{2,1,0:T(8,128)S(1)}, u32[]{:S(2)}, u32[]{:S(2)}) collective-permute-start(f32[12,16,128]{2,1,0:T(8,128)S(1)} %add_subtract_fusion.3.x), channel_id=1, source_target_pairs={{4,0},{6,2},{8,4},{9,1},{10,6},{11,3},{12,8},{13,5},{14,10},{15,7}... | collective-permute-start | bytes 294920 | tf_op jit(solution)/shard_map/ppermute | solution.py:310
  107.9 1.2 shard_map.105
  110.0 2.6 %collective-permute-done.33.arrived = f32[12,16,128]{2,1,0:T(8,128)S(1)} collective-permute-done((f32[12,16,128]{2,1,0:T(8,128)S(1)}, f32[12,16,128]{2,1,0:T(8,128)S(1)}, u32[]{:S(2)}, u32[]{:S(2)}) %collective-permute-start.33) | collective-permute-done | bytes 98336 | tf_op jit(solution)/shard_map/ppermute | solution.py:310
  113.2 1.3 collective-permute-done.34
  114.5 1.9 %collective-permute-start.35 = (f32[12,16,128]{2,1,0:T(8,128)S(1)}, f32[12,16,128]{2,1,0:T(8,128)S(1)}, u32[]{:S(2)}, u32[]{:S(2)}) collective-permute-start(f32[12,16,128]{2,1,0:T(8,128)S(1)} %add_subtract_fusion.2.x), channel_id=1, source_target_pairs={{4,0},{6,2},{8,4},{9,1},{10,6},{11,3},{12,8},{13,5},{14,10},{15,7}... | collective-permute-start | bytes 294920 | tf_op jit(solution)/shard_map/ppermute | solution.py:310
  117.2 4.7 %collective-permute-done.35.arrived = f32[12,16,128]{2,1,0:T(8,128)S(1)} collective-permute-done((f32[12,16,128]{2,1,0:T(8,128)S(1)}, f32[12,16,128]{2,1,0:T(8,128)S(1)}, u32[]{:S(2)}, u32[]{:S(2)}) %collective-permute-start.35) | collective-permute-done | bytes 98336 | tf_op jit(solution)/shard_map/ppermute | solution.py:310
  122.4 1.3 collective-permute-done.36
  123.8 1.9 %collective-permute-start.37 = (f32[12,16,128]{2,1,0:T(8,128)S(1)}, f32[12,16,128]{2,1,0:T(8,128)S(1)}, u32[]{:S(2)}, u32[]{:S(2)}) collective-permute-start(f32[12,16,128]{2,1,0:T(8,128)S(1)} %add_subtract_fusion.1.x), channel_id=1, source_target_pairs={{4,0},{6,2},{8,4},{9,1},{10,6},{11,3},{12,8},{13,5},{14,10},{15,7}... | collective-permute-start | bytes 294920 | tf_op jit(solution)/shard_map/ppermute | solution.py:310
  126.5 4.7 %collective-permute-done.37.arrived = f32[12,16,128]{2,1,0:T(8,128)S(1)} collective-permute-done((f32[12,16,128]{2,1,0:T(8,128)S(1)}, f32[12,16,128]{2,1,0:T(8,128)S(1)}, u32[]{:S(2)}, u32[]{:S(2)}) %collective-permute-start.37) | collective-permute-done | bytes 98336 | tf_op jit(solution)/shard_map/ppermute | solution.py:310
  131.7 1.3 collective-permute-done.38
  133.1 1.6 %collective-permute-start.39 = (f32[12,16,128]{2,1,0:T(8,128)S(1)}, f32[12,16,128]{2,1,0:T(8,128)S(1)}, u32[]{:S(2)}, u32[]{:S(2)}) collective-permute-start(f32[12,16,128]{2,1,0:T(8,128)S(1)} %add_subtract_fusion), channel_id=1, source_target_pairs={{0,2},{1,3},{2,0},{3,1},{4,6},{5,7},{6,4},{7,5},{8,10},{9,11},{10,... | collective-permute-start | bytes 294920 | tf_op jit(solution)/shard_map/ppermute | solution.py:301
  135.3 2.7 %collective-permute-done.39 = f32[12,16,128]{2,1,0:T(8,128)S(1)} collective-permute-done((f32[12,16,128]{2,1,0:T(8,128)S(1)}, f32[12,16,128]{2,1,0:T(8,128)S(1)}, u32[]{:S(2)}, u32[]{:S(2)}) %collective-permute-start.39) | collective-permute-done | bytes 98336 | tf_op jit(solution)/shard_map/ppermute | solution.py:301
  (98 shorter events, 24.8 us)
Async XLA Ops:
  0.6 9.1 %copy-start = (f32[12,2,128,128]{3,2,1,0:T(8,128)S(1)}, f32[12,2,128,128]{3,2,1,0:T(8,128)}, u32[]{:S(2)}) copy-start(f32[12,2,128,128]{3,2,1,0:T(8,128)} %param.10) | copy-start | bytes 4718596
  0.6 9.1 %collective-permute-start.5 = (f32[24,128,128]{2,1,0:T(8,128)}, f32[24,128,128]{2,1,0:T(8,128)S(1)}, u32[]{:S(2)}, u32[]{:S(2)}) collective-permute-start(f32[24,128,128]{2,1,0:T(8,128)} %bitcast.5), channel_id=1, source_target_pairs={{0,1},{1,0},{2,3},{3,2},{4,5},{5,4},{6,7},{7,6},{8,9},{9,8},{10,11... | collective-permute-start | bytes 4718600 | tf_op jit(solution)/shard_map/ppermute | solution.py:301
  0.7 7.5 %collective-permute-start = (f32[3,128,128]{2,1,0:T(8,128)}, f32[3,128,128]{2,1,0:T(8,128)S(1)}, u32[]{:S(2)}, u32[]{:S(2)}) collective-permute-start(f32[3,128,128]{2,1,0:T(8,128)} %refs_1_), channel_id=1, source_target_pairs={{0,2},{1,3},{2,0},{3,1},{4,6},{5,7},{6,4},{7,5},{8,10},{9,11},{10,... | collective-permute-start | bytes 589832 | tf_op jit(solution)/shard_map/ppermute | solution.py:301
  2.3 5.9 %collective-permute-start.2 = (f32[3,128,128]{2,1,0:T(8,128)}, f32[3,128,128]{2,1,0:T(8,128)S(1)}, u32[]{:S(2)}, u32[]{:S(2)}) collective-permute-start(f32[3,128,128]{2,1,0:T(8,128)} %refs_1_), channel_id=1, source_target_pairs={{0,1},{1,0},{2,3},{3,2},{4,5},{5,4},{6,7},{7,6},{8,9},{9,8},{10,11... | collective-permute-start | bytes 589832 | tf_op jit(solution)/shard_map/ppermute | solution.py:301
  6.2 1.2 collective-permute-start.1
  8.3 1.4 %collective-permute-start.4 = (f32[3,128,128]{2,1,0:T(8,128)S(1)}, f32[3,128,128]{2,1,0:T(8,128)S(1)}, u32[]{:S(2)}, u32[]{:S(2)}) collective-permute-start(f32[3,128,128]{2,1,0:T(8,128)S(1)} %collective-permute-done.inverse), channel_id=1, source_target_pairs={{0,1},{1,0},{2,3},{3,2},{4,5},{5,4},{6,7},{7,6},{8,9},{9,8},{10,11... | collective-permute-start | bytes 589832 | tf_op jit(solution)/shard_map/ppermute | solution.py:301
  9.7 6.0 %copy-start.1 = (f32[3,128,128]{2,1,0:T(8,128)S(1)}, f32[3,128,128]{2,1,0:T(8,128)}, u32[]{:S(2)}) copy-start(f32[3,128,128]{2,1,0:T(8,128)} %diag.3) | copy-start | bytes 589828
  10.7 15.0 %collective-permute-start.7 = (f32[8,128,128]{2,1,0:T(8,128)S(1)}, f32[8,128,128]{2,1,0:T(8,128)S(1)}, u32[]{:S(2)}, u32[]{:S(2)}) collective-permute-start(f32[8,128,128]{2,1,0:T(8,128)S(1)} %get-tuple-element.41), channel_id=1, source_target_pairs={{0,4},{1,9},{2,6},{3,11},{4,8},{5,13},{6,10},{7,15},{8,12},{9,17},... | collective-permute-start | bytes 1572872 | tf_op jit(solution)/shard_map/ppermute | solution.py:310
  14.2 13.8 %collective-permute-start.6 = (f32[8,128,128]{2,1,0:T(8,128)S(1)}, f32[8,128,128]{2,1,0:T(8,128)S(1)}, u32[]{:S(2)}, u32[]{:S(2)}) collective-permute-start(f32[8,128,128]{2,1,0:T(8,128)S(1)} %get-tuple-element.38.refs_3_.refs_6_.refs_0_), channel_id=1, source_target_pairs={{0,2},{1,3},{2,0},{3,1},{4,6},{5,7},{6,4},{7,5},{8,10},{9,11},{10,... | collective-permute-start | bytes 1572872 | tf_op jit(solution)/shard_map/ppermute | solution.py:301
  29.0 12.9 %copy-start.2 = (f32[3,128,128]{2,1,0:T(8,128)S(1)}, f32[3,128,128]{2,1,0:T(8,128)}, u32[]{:S(2)}) copy-start(f32[3,128,128]{2,1,0:T(8,128)} %refs_1_) | copy-start | bytes 589828
  29.0 1.5 %collective-permute-start.9 = (f32[3,128,128]{2,1,0:T(8,128)S(1)}, f32[3,128,128]{2,1,0:T(8,128)S(1)}, u32[]{:S(2)}, u32[]{:S(2)}) collective-permute-start(f32[3,128,128]{2,1,0:T(8,128)S(1)} %get-tuple-element.45), channel_id=1, source_target_pairs={{0,1},{1,0},{2,3},{3,2},{4,5},{5,4},{6,7},{7,6},{8,9},{9,8},{10,11... | collective-permute-start | bytes 589832 | tf_op jit(solution)/shard_map/ppermute | solution.py:301
  29.1 3.0 %collective-permute-start.8 = (f32[3,128,128]{2,1,0:T(8,128)S(1)}, f32[3,128,128]{2,1,0:T(8,128)S(1)}, u32[]{:S(2)}, u32[]{:S(2)}) collective-permute-start(f32[3,128,128]{2,1,0:T(8,128)S(1)} %get-tuple-element.43), channel_id=1, source_target_pairs={{0,1},{1,0},{2,3},{3,2},{4,5},{5,4},{6,7},{7,6},{8,9},{9,8},{10,11... | collective-permute-start | bytes 589832 | tf_op jit(solution)/shard_map/ppermute | solution.py:301
  30.6 7.8 %collective-permute-start.10 = (f32[3,128,128]{2,1,0:T(8,128)S(1)}, f32[3,128,128]{2,1,0:T(8,128)S(1)}, u32[]{:S(2)}, u32[]{:S(2)}) collective-permute-start(f32[3,128,128]{2,1,0:T(8,128)S(1)} %add.43), channel_id=1, source_target_pairs={{0,2},{1,3},{2,0},{3,1},{4,6},{5,7},{6,4},{7,5},{8,10},{9,11},{10,... | collective-permute-start | bytes 589832 | tf_op jit(solution)/shard_map/ppermute | solution.py:301
  32.2 9.7 %collective-permute-start.13 = (f32[3,128,128]{2,1,0:T(8,128)S(1)}, f32[3,128,128]{2,1,0:T(8,128)S(1)}, u32[]{:S(2)}, u32[]{:S(2)}) collective-permute-start(f32[3,128,128]{2,1,0:T(8,128)S(1)} %add.42), channel_id=1, source_target_pairs={{0,2},{1,3},{2,0},{3,1},{4,6},{5,7},{6,4},{7,5},{8,10},{9,11},{10,... | collective-permute-start | bytes 589832 | tf_op jit(solution)/shard_map/ppermute | solution.py:301
  32.7 9.1 %collective-permute-start.3 = (s32[2,64]{1,0:T(2,128)S(1)}, s32[2,64]{1,0:T(2,128)S(1)}, u32[]{:S(2)}, u32[]{:S(2)}) collective-permute-start(s32[2,64]{1,0:T(2,128)S(1)} %pad_add_fusion.2), channel_id=1, source_target_pairs={{0,2},{1,3},{2,0},{3,1},{4,6},{5,7},{6,4},{7,5},{8,10},{9,11},{10,... | collective-permute-start | bytes 1544 | tf_op jit(solution)/shard_map/ppermute | solution.py:301
  42.3 1.5 %collective-permute-start.16 = (f32[3,128,128]{2,1,0:T(8,128)S(1)}, f32[3,128,128]{2,1,0:T(8,128)S(1)}, u32[]{:S(2)}, u32[]{:S(2)}) collective-permute-start(f32[3,128,128]{2,1,0:T(8,128)S(1)} %shard_map.91.refs_1_), channel_id=1, source_target_pairs={{0,1},{1,0},{2,3},{3,2},{4,5},{5,4},{6,7},{7,6},{8,9},{9,8},{10,11... | collective-permute-start | bytes 589832 | tf_op jit(solution)/shard_map/ppermute | solution.py:301
  42.3 1.7 %collective-permute-start.17 = (f32[3,128,128]{2,1,0:T(8,128)S(1)}, f32[3,128,128]{2,1,0:T(8,128)S(1)}, u32[]{:S(2)}, u32[]{:S(2)}) collective-permute-start(f32[3,128,128]{2,1,0:T(8,128)S(1)} %shard_map.89.inverse), channel_id=1, source_target_pairs={{0,1},{1,0},{2,3},{3,2},{4,5},{5,4},{6,7},{7,6},{8,9},{9,8},{10,11... | collective-permute-start | bytes 589832 | tf_op jit(solution)/shard_map/ppermute | solution.py:301
  42.8 18.2 %collective-permute-start.15 = (f32[8,128,128]{2,1,0:T(8,128)S(1)}, f32[8,128,128]{2,1,0:T(8,128)S(1)}, u32[]{:S(2)}, u32[]{:S(2)}) collective-permute-start(f32[8,128,128]{2,1,0:T(8,128)S(1)} %collective-permute-done.6.refs_0_.refs_3_), channel_id=1, source_target_pairs={{0,1},{1,0},{2,3},{3,2},{4,5},{5,4},{6,7},{7,6},{8,9},{9,8},{10,11... | collective-permute-start | bytes 1572872 | tf_op jit(solution)/shard_map/ppermute | solution.py:301
  45.0 16.0 %collective-permute-start.18 = (f32[8,128,128]{2,1,0:T(8,128)S(1)}, f32[8,128,128]{2,1,0:T(8,128)S(1)}, u32[]{:S(2)}, u32[]{:S(2)}) collective-permute-start(f32[8,128,128]{2,1,0:T(8,128)S(1)} %shard_map.93), channel_id=1, source_target_pairs={{0,4},{1,9},{2,6},{3,11},{4,8},{5,13},{6,10},{7,15},{8,12},{9,17},... | collective-permute-start | bytes 1572872 | tf_op jit(solution)/shard_map/ppermute | solution.py:310
  48.0 8.0 %collective-permute-start.14 = (f32[4,128,128]{2,1,0:T(8,128)S(1)}, f32[4,128,128]{2,1,0:T(8,128)S(1)}, u32[]{:S(2)}, u32[]{:S(2)}) collective-permute-start(f32[4,128,128]{2,1,0:T(8,128)S(1)} %get-tuple-element.49.refs_1_), channel_id=1, source_target_pairs={{0,2},{1,3},{2,0},{3,1},{4,6},{5,7},{6,4},{7,5},{8,10},{9,11},{10,... | collective-permute-start | bytes 786440 | tf_op jit(solution)/shard_map/ppermute | solution.py:301
  49.6 6.5 %collective-permute-start.12 = (s32[4,64]{1,0:T(4,128)S(1)}, s32[4,64]{1,0:T(4,128)S(1)}, u32[]{:S(2)}, u32[]{:S(2)}) collective-permute-start(s32[4,64]{1,0:T(4,128)S(1)} %pad_add_fusion.1.metas.refs_0_), channel_id=1, source_target_pairs={{4,0},{6,2},{8,4},{9,1},{10,6},{11,3},{12,8},{13,5},{14,10},{15,7}... | collective-permute-start | bytes 3080 | tf_op jit(solution)/shard_map/ppermute | solution.py:310
  52.4 8.6 %collective-permute-start.11 = (s32[4,64]{1,0:T(4,128)S(1)}, s32[4,64]{1,0:T(4,128)S(1)}, u32[]{:S(2)}, u32[]{:S(2)}) collective-permute-start(s32[4,64]{1,0:T(4,128)S(1)} %pad_add_fusion.1.metas.refs_0_), channel_id=1, source_target_pairs={{0,8},{1,5},{2,10},{3,7},{4,12},{5,9},{6,14},{7,11},{8,16},{9,13},... | collective-permute-start | bytes 3080 | tf_op jit(solution)/shard_map/ppermute | solution.py:310
  62.1 1.5 %collective-permute-start.19 = (f32[3,128,128]{2,1,0:T(8,128)S(1)}, f32[3,128,128]{2,1,0:T(8,128)S(1)}, u32[]{:S(2)}, u32[]{:S(2)}) collective-permute-start(f32[3,128,128]{2,1,0:T(8,128)S(1)} %get-tuple-element.53), channel_id=1, source_target_pairs={{0,1},{1,0},{2,3},{3,2},{4,5},{5,4},{6,7},{7,6},{8,9},{9,8},{10,11... | collective-permute-start | bytes 589832 | tf_op jit(solution)/shard_map/ppermute | solution.py:301
  62.2 3.0 %collective-permute-start.20 = (f32[3,128,128]{2,1,0:T(8,128)S(1)}, f32[3,128,128]{2,1,0:T(8,128)S(1)}, u32[]{:S(2)}, u32[]{:S(2)}) collective-permute-start(f32[3,128,128]{2,1,0:T(8,128)S(1)} %get-tuple-element.55), channel_id=1, source_target_pairs={{0,1},{1,0},{2,3},{3,2},{4,5},{5,4},{6,7},{7,6},{8,9},{9,8},{10,11... | collective-permute-start | bytes 589832 | tf_op jit(solution)/shard_map/ppermute | solution.py:301
  63.6 7.8 %collective-permute-start.22 = (f32[3,128,128]{2,1,0:T(8,128)S(1)}, f32[3,128,128]{2,1,0:T(8,128)S(1)}, u32[]{:S(2)}, u32[]{:S(2)}) collective-permute-start(f32[3,128,128]{2,1,0:T(8,128)S(1)} %add.46), channel_id=1, source_target_pairs={{0,2},{1,3},{2,0},{3,1},{4,6},{5,7},{6,4},{7,5},{8,10},{9,11},{10,... | collective-permute-start | bytes 589832 | tf_op jit(solution)/shard_map/ppermute | solution.py:301
  65.2 9.6 %collective-permute-start.21 = (f32[3,128,128]{2,1,0:T(8,128)S(1)}, f32[3,128,128]{2,1,0:T(8,128)S(1)}, u32[]{:S(2)}, u32[]{:S(2)}) collective-permute-start(f32[3,128,128]{2,1,0:T(8,128)S(1)} %add.47), channel_id=1, source_target_pairs={{0,2},{1,3},{2,0},{3,1},{4,6},{5,7},{6,4},{7,5},{8,10},{9,11},{10,... | collective-permute-start | bytes 589832 | tf_op jit(solution)/shard_map/ppermute | solution.py:301
  71.5 5.5 %copy-start.3 = (f32[12,32,128]{2,1,0:T(8,128)S(1)}, f32[12,32,128]{2,1,0:T(8,128)}, u32[]{:S(2)}) copy-start(f32[12,32,128]{2,1,0:T(8,128)} %base.1) | copy-start | bytes 589828
  71.9 5.1 %collective-permute-start.24 = (f32[3,128,128]{2,1,0:T(8,128)S(1)}, f32[3,128,128]{2,1,0:T(8,128)S(1)}, u32[]{:S(2)}, u32[]{:S(2)}) collective-permute-start(f32[3,128,128]{2,1,0:T(8,128)S(1)} %shard_map.96), channel_id=1, source_target_pairs={{0,1},{1,0},{2,3},{3,2},{4,5},{5,4},{6,7},{7,6},{8,9},{9,8},{10,11... | collective-permute-start | bytes 589832 | tf_op jit(solution)/shard_map/ppermute | solution.py:301
  75.3 1.7 %collective-permute-start.23 = (f32[3,128,128]{2,1,0:T(8,128)S(1)}, f32[3,128,128]{2,1,0:T(8,128)S(1)}, u32[]{:S(2)}, u32[]{:S(2)}) collective-permute-start(f32[3,128,128]{2,1,0:T(8,128)S(1)} %shard_map.95), channel_id=1, source_target_pairs={{0,1},{1,0},{2,3},{3,2},{4,5},{5,4},{6,7},{7,6},{8,9},{9,8},{10,11... | collective-permute-start | bytes 589832 | tf_op jit(solution)/shard_map/ppermute | solution.py:301
  75.3 20.0 %collective-permute-start.25 = (f32[12,128,128]{2,1,0:T(8,128)S(1)}, f32[12,128,128]{2,1,0:T(8,128)S(1)}, u32[]{:S(2)}, u32[]{:S(2)}) collective-permute-start(f32[12,128,128]{2,1,0:T(8,128)S(1)} %get-tuple-element.50.upper.refs_0_), channel_id=1, source_target_pairs={{0,2},{1,3},{2,0},{3,1},{4,6},{5,7},{6,4},{7,5},{8,10},{9,11},{10,... | collective-permute-start | bytes 2359304 | tf_op jit(solution)/shard_map/ppermute | solution.py:301
  77.4 7.5 %collective-permute-start.26 = (f32[12,16,128]{2,1,0:T(8,128)S(1)}, f32[12,16,128]{2,1,0:T(8,128)S(1)}, u32[]{:S(2)}, u32[]{:S(2)}) collective-permute-start(f32[12,16,128]{2,1,0:T(8,128)S(1)} %shard_map.97.x), channel_id=1, source_target_pairs={{0,8},{1,5},{2,10},{3,7},{4,12},{5,9},{6,14},{7,11},{8,16},{9,13},... | collective-permute-start | bytes 294920 | tf_op jit(solution)/shard_map/ppermute | solution.py:310
  85.4 1.4 collective-permute-start.27
  86.8 7.4 %collective-permute-start.28 = (f32[12,16,128]{2,1,0:T(8,128)S(1)}, f32[12,16,128]{2,1,0:T(8,128)S(1)}, u32[]{:S(2)}, u32[]{:S(2)}) collective-permute-start(f32[12,16,128]{2,1,0:T(8,128)S(1)} %add_subtract_fusion.5.x), channel_id=1, source_target_pairs={{0,8},{1,5},{2,10},{3,7},{4,12},{5,9},{6,14},{7,11},{8,16},{9,13},... | collective-permute-start | bytes 294920 | tf_op jit(solution)/shard_map/ppermute | solution.py:310
  94.6 1.4 collective-permute-start.29
  95.3 12.6 %collective-permute-start.32 = (f32[12,128,128]{2,1,0:T(8,128)S(1)}, f32[12,128,128]{2,1,0:T(8,128)S(1)}, u32[]{:S(2)}, u32[]{:S(2)}) collective-permute-start(f32[12,128,128]{2,1,0:T(8,128)S(1)} %collective-permute-done.25.refs_0_.refs_2_), channel_id=1, source_target_pairs={{0,1},{1,0},{2,3},{3,2},{4,5},{5,4},{6,7},{7,6},{8,9},{9,8},{10,11... | collective-permute-start | bytes 2359304 | tf_op jit(solution)/shard_map/ppermute | solution.py:301
  96.0 7.3 %collective-permute-start.30 = (f32[12,16,128]{2,1,0:T(8,128)S(1)}, f32[12,16,128]{2,1,0:T(8,128)S(1)}, u32[]{:S(2)}, u32[]{:S(2)}) collective-permute-start(f32[12,16,128]{2,1,0:T(8,128)S(1)} %add_subtract_fusion.4.x), channel_id=1, source_target_pairs={{0,8},{1,5},{2,10},{3,7},{4,12},{5,9},{6,14},{7,11},{8,16},{9,13},... | collective-permute-start | bytes 294920 | tf_op jit(solution)/shard_map/ppermute | solution.py:310
  103.8 1.4 collective-permute-start.31
  105.2 7.4 %collective-permute-start.33 = (f32[12,16,128]{2,1,0:T(8,128)S(1)}, f32[12,16,128]{2,1,0:T(8,128)S(1)}, u32[]{:S(2)}, u32[]{:S(2)}) collective-permute-start(f32[12,16,128]{2,1,0:T(8,128)S(1)} %add_subtract_fusion.3.x), channel_id=1, source_target_pairs={{4,0},{6,2},{8,4},{9,1},{10,6},{11,3},{12,8},{13,5},{14,10},{15,7}... | collective-permute-start | bytes 294920 | tf_op jit(solution)/shard_map/ppermute | solution.py:310
  113.1 1.4 collective-permute-start.34
  114.5 7.4 %collective-permute-start.35 = (f32[12,16,128]{2,1,0:T(8,128)S(1)}, f32[12,16,128]{2,1,0:T(8,128)S(1)}, u32[]{:S(2)}, u32[]{:S(2)}) collective-permute-start(f32[12,16,128]{2,1,0:T(8,128)S(1)} %add_subtract_fusion.2.x), channel_id=1, source_target_pairs={{4,0},{6,2},{8,4},{9,1},{10,6},{11,3},{12,8},{13,5},{14,10},{15,7}... | collective-permute-start | bytes 294920 | tf_op jit(solution)/shard_map/ppermute | solution.py:310
  122.4 1.4 collective-permute-start.36
  123.8 7.4 %collective-permute-start.37 = (f32[12,16,128]{2,1,0:T(8,128)S(1)}, f32[12,16,128]{2,1,0:T(8,128)S(1)}, u32[]{:S(2)}, u32[]{:S(2)}) collective-permute-start(f32[12,16,128]{2,1,0:T(8,128)S(1)} %add_subtract_fusion.1.x), channel_id=1, source_target_pairs={{4,0},{6,2},{8,4},{9,1},{10,6},{11,3},{12,8},{13,5},{14,10},{15,7}... | collective-permute-start | bytes 294920 | tf_op jit(solution)/shard_map/ppermute | solution.py:310
  131.7 1.4 collective-permute-start.38
  133.1 4.9 %collective-permute-start.39 = (f32[12,16,128]{2,1,0:T(8,128)S(1)}, f32[12,16,128]{2,1,0:T(8,128)S(1)}, u32[]{:S(2)}, u32[]{:S(2)}) collective-permute-start(f32[12,16,128]{2,1,0:T(8,128)S(1)} %add_subtract_fusion), channel_id=1, source_target_pairs={{0,2},{1,3},{2,0},{3,1},{4,6},{5,7},{6,4},{7,5},{8,10},{9,11},{10,... | collective-permute-start | bytes 294920 | tf_op jit(solution)/shard_map/ppermute | solution.py:301

commit v12 on v11

--- a/solution.py
+++ b/solution.py
@@ -185,14 +185,11 @@
     fetch.wait()
     me, mine, mates = near.at[0], near.at[1], near.at[2]
     role = me[0] % 2
-    places, terms = [], []
     for g, (meta, source) in enumerate(((mine, lower), (mates, mate_lower))):
         for j in range(lay.cap):
             s, _, v = lay.lookup(meta, 2 + role, 1, j)
-            places.append(lay.place(s // lay.width, me[0]))
-            terms.append(matmul_beside(beside(source[role * lay.cap + j]), halves[g * lay.cap + v]))
-    for place, term in zip(places, terms):
-        total[place] += term
+            place = lay.place(s // lay.width, me[0])
+            total[place] += matmul_beside(beside(source[role * lay.cap + j]), halves[g * lay.cap + v])
     for c, out in enumerate(outs):
         out[...] = total[c * lay.own_rows : (c + 1) * lay.own_rows]
 

time: 139 us -> 139 us (level)
  no operation moved by 1% of the time
where the time goes in v12:
time: 139 us
  waiting for transfers between devices  67.8 us (49%)
  starting transfers between devices  41.1 us (30%)
  Pallas kernels  21.9 us (16%)
  local copies, waits for them, and re-layouts  4.68 us (3%)
  other arithmetic  1.95 us (1%)
    ppermute x10, waiting for transfers between devices, along(): return lax.ppermute(x, ('dom', 'tile'), route)  36.5 us
    ppermute x30, waiting for transfers between devices, swap(): return lax.ppermute(x, 'tile', [(i, i ^ bit) for i in range(n_tile)])  31.3 us
    ppermute x10, starting transfers between devices, along(): return lax.ppermute(x, ('dom', 'tile'), route)  24.4 us
    pallas_call x26, Pallas kernels, call(): pl.pallas_call(body if not early else lambda *refs: body(*refs[len(early)...  21.9 us
    ppermute x30, starting transfers between devices, swap(): return lax.ppermute(x, 'tile', [(i, i ^ bit) for i in range(n_tile)])  16.7 us
  transfers between devices with their start and end apart: 40, of which 28 were waited for; matrix products, arithmetic and copies ran while one was open for 4% of the time, Pallas kernels for 12%

profile of v12, /device:TPU:18, one launch (start us, length us, event | category | flops | bytes accessed | tf_op | source)
XLA Modules:
  0.0 138.7 jit_solution(13954792287048525314)
XLA Ops:
  0.7 1.6 %collective-permute-start = (f32[3,128,128]{2,1,0:T(8,128)}, f32[3,128,128]{2,1,0:T(8,128)S(1)}, u32[]{:S(2)}, u32[]{:S(2)}) collective-permute-start(f32[3,128,128]{2,1,0:T(8,128)} %refs_1_), channel_id=1, source_target_pairs={{0,2},{1,3},{2,0},{3,1},{4,6},{5,7},{6,4},{7,5},{8,10},{9,11},{10,... | collective-permute-start | bytes 589832 | tf_op jit(solution)/shard_map/ppermute | solution.py:298
  8.3 0.9 constant_dynamic-update-slice_fusion.3
  9.7 0.9 shard_map.86
  10.7 3.5 %collective-permute-start.7 = (f32[8,128,128]{2,1,0:T(8,128)S(1)}, f32[8,128,128]{2,1,0:T(8,128)S(1)}, u32[]{:S(2)}, u32[]{:S(2)}) collective-permute-start(f32[8,128,128]{2,1,0:T(8,128)S(1)} %get-tuple-element.41), channel_id=1, source_target_pairs={{0,4},{1,9},{2,6},{3,11},{4,8},{5,13},{6,10},{7,15},{8,12},{9,17},... | collective-permute-start | bytes 1572872 | tf_op jit(solution)/shard_map/ppermute | solution.py:307
  14.2 1.6 %collective-permute-start.6 = (f32[8,128,128]{2,1,0:T(8,128)S(1)}, f32[8,128,128]{2,1,0:T(8,128)S(1)}, u32[]{:S(2)}, u32[]{:S(2)}) collective-permute-start(f32[8,128,128]{2,1,0:T(8,128)S(1)} %get-tuple-element.38.refs_3_.refs_6_.refs_0_), channel_id=1, source_target_pairs={{0,2},{1,3},{2,0},{3,1},{4,6},{5,7},{6,4},{7,5},{8,10},{9,11},{10,... | collective-permute-start | bytes 1572872 | tf_op jit(solution)/shard_map/ppermute | solution.py:298
  15.8 2.1 %shard_map.87 = (f32[12,128,128]{2,1,0:T(8,128)S(1)}, f32[8,128,128]{2,1,0:T(8,128)S(1)}, f32[4,128,128]{2,1,0:T(8,128)S(1)}, f32[12,128,128]{2,1,0:T(8,128)S(1)}, f32[8,128,128]{2,1,0:T(8,128)S(1)}) custom-call(s32[3,64]{1,0:T(4,128)S(1)} %pad_add_fusion.near_source.near.refs_1_.refs_4_, f32[12,128,128]{2,1,0:T(8,128)S(1)} %constant_dynamic-update-slice_fusion.inverse, ...), custom_call_target="tpu_custom_call" | custom-call | flops 201326592 | bytes 7012352 | tf_op jit(solution)/shard_map/pallas_call | solution.py:101
  17.8 7.8 %collective-permute-done.7.refs_5_ = f32[8,128,128]{2,1,0:T(8,128)S(1)} collective-permute-done((f32[8,128,128]{2,1,0:T(8,128)S(1)}, f32[8,128,128]{2,1,0:T(8,128)S(1)}, u32[]{:S(2)}, u32[]{:S(2)}) %collective-permute-start.7) | collective-permute-done | bytes 524320 | tf_op jit(solution)/shard_map/ppermute | solution.py:307
  25.7 2.3 %collective-permute-done.6.refs_0_.refs_3_ = f32[8,128,128]{2,1,0:T(8,128)S(1)} collective-permute-done((f32[8,128,128]{2,1,0:T(8,128)S(1)}, f32[8,128,128]{2,1,0:T(8,128)S(1)}, u32[]{:S(2)}, u32[]{:S(2)}) %collective-permute-start.6) | collective-permute-done | bytes 524320 | tf_op jit(solution)/shard_map/ppermute | solution.py:298
  27.9 1.0 shard_map.88
  29.6 0.9 collective-permute-done.9
  30.5 1.6 %collective-permute-start.10 = (f32[3,128,128]{2,1,0:T(8,128)S(1)}, f32[3,128,128]{2,1,0:T(8,128)S(1)}, u32[]{:S(2)}, u32[]{:S(2)}) collective-permute-start(f32[3,128,128]{2,1,0:T(8,128)S(1)} %add.43), channel_id=1, source_target_pairs={{0,2},{1,3},{2,0},{3,1},{4,6},{5,7},{6,4},{7,5},{8,10},{9,11},{10,... | collective-permute-start | bytes 589832 | tf_op jit(solution)/shard_map/ppermute | solution.py:298
  32.7 1.5 %collective-permute-start.3 = (s32[2,64]{1,0:T(2,128)S(1)}, s32[2,64]{1,0:T(2,128)S(1)}, u32[]{:S(2)}, u32[]{:S(2)}) collective-permute-start(s32[2,64]{1,0:T(2,128)S(1)} %pad_add_fusion.2), channel_id=1, source_target_pairs={{0,2},{1,3},{2,0},{3,1},{4,6},{5,7},{6,4},{7,5},{8,10},{9,11},{10,... | collective-permute-start | bytes 1544 | tf_op jit(solution)/shard_map/ppermute | solution.py:298
  34.3 4.1 %collective-permute-done.10 = f32[3,128,128]{2,1,0:T(8,128)S(1)} collective-permute-done((f32[3,128,128]{2,1,0:T(8,128)S(1)}, f32[3,128,128]{2,1,0:T(8,128)S(1)}, u32[]{:S(2)}, u32[]{:S(2)}) %collective-permute-start.10) | collective-permute-done | bytes 196640 | tf_op jit(solution)/shard_map/ppermute | solution.py:298
  38.8 3.1 %collective-permute-done.3 = s32[2,64]{1,0:T(2,128)S(1)} collective-permute-done((s32[2,64]{1,0:T(2,128)S(1)}, s32[2,64]{1,0:T(2,128)S(1)}, u32[]{:S(2)}, u32[]{:S(2)}) %collective-permute-start.3) | collective-permute-done | bytes 544 | tf_op jit(solution)/shard_map/ppermute | solution.py:298
  45.0 3.0 %collective-permute-start.18 = (f32[8,128,128]{2,1,0:T(8,128)S(1)}, f32[8,128,128]{2,1,0:T(8,128)S(1)}, u32[]{:S(2)}, u32[]{:S(2)}) collective-permute-start(f32[8,128,128]{2,1,0:T(8,128)S(1)} %shard_map.93), channel_id=1, source_target_pairs={{0,4},{1,9},{2,6},{3,11},{4,8},{5,13},{6,10},{7,15},{8,12},{9,17},... | collective-permute-start | bytes 1572872 | tf_op jit(solution)/shard_map/ppermute | solution.py:307
  48.0 1.6 %collective-permute-start.14 = (f32[4,128,128]{2,1,0:T(8,128)S(1)}, f32[4,128,128]{2,1,0:T(8,128)S(1)}, u32[]{:S(2)}, u32[]{:S(2)}) collective-permute-start(f32[4,128,128]{2,1,0:T(8,128)S(1)} %get-tuple-element.49.refs_1_), channel_id=1, source_target_pairs={{0,2},{1,3},{2,0},{3,1},{4,6},{5,7},{6,4},{7,5},{8,10},{9,11},{10,... | collective-permute-start | bytes 786440 | tf_op jit(solution)/shard_map/ppermute | solution.py:298
  49.6 2.8 %collective-permute-start.12 = (s32[4,64]{1,0:T(4,128)S(1)}, s32[4,64]{1,0:T(4,128)S(1)}, u32[]{:S(2)}, u32[]{:S(2)}) collective-permute-start(s32[4,64]{1,0:T(4,128)S(1)} %pad_add_fusion.1.metas.refs_0_), channel_id=1, source_target_pairs={{4,0},{6,2},{8,4},{9,1},{10,6},{11,3},{12,8},{13,5},{14,10},{15,7}... | collective-permute-start | bytes 3080 | tf_op jit(solution)/shard_map/ppermute | solution.py:307
  52.4 1.9 %collective-permute-start.11 = (s32[4,64]{1,0:T(4,128)S(1)}, s32[4,64]{1,0:T(4,128)S(1)}, u32[]{:S(2)}, u32[]{:S(2)}) collective-permute-start(s32[4,64]{1,0:T(4,128)S(1)} %pad_add_fusion.1.metas.refs_0_), channel_id=1, source_target_pairs={{0,8},{1,5},{2,10},{3,7},{4,12},{5,9},{6,14},{7,11},{8,16},{9,13},... | collective-permute-start | bytes 3080 | tf_op jit(solution)/shard_map/ppermute | solution.py:307
  54.4 1.7 %shard_map.92.refs_5_ = f32[12,128,128]{2,1,0:T(8,128)S(1)} custom-call(s32[3,64]{1,0:T(4,128)S(1)} %pad_add_fusion.near_source.near.refs_1_.refs_4_, f32[12,128,128]{2,1,0:T(8,128)S(1)} %pad_maximum_fusion.inverse, f32[3,128,128]{2,1,0:T(8,128)S(1)} %copy-done.1, f32[24,128,128]{2,1,0:T(8,128)S(1)} %bitcast.8), custom_call_target="tpu_custom_call" | custom-call | flops 201326592 | bytes 3342336 | tf_op jit(solution)/shard_map/pallas_call | solution.py:101
  56.1 4.9 %collective-permute-done.11.peers_below.refs_2_ = s32[4,64]{1,0:T(4,128)S(1)} collective-permute-done((s32[4,64]{1,0:T(4,128)S(1)}, s32[4,64]{1,0:T(4,128)S(1)}, u32[]{:S(2)}, u32[]{:S(2)}) %collective-permute-start.11) | collective-permute-done | bytes 1056 | tf_op jit(solution)/shard_map/ppermute | solution.py:307
  61.0 1.0 shard_map.94
  62.7 0.9 collective-permute-done.19
  63.6 1.6 %collective-permute-start.22 = (f32[3,128,128]{2,1,0:T(8,128)S(1)}, f32[3,128,128]{2,1,0:T(8,128)S(1)}, u32[]{:S(2)}, u32[]{:S(2)}) collective-permute-start(f32[3,128,128]{2,1,0:T(8,128)S(1)} %add.46), channel_id=1, source_target_pairs={{0,2},{1,3},{2,0},{3,1},{4,6},{5,7},{6,4},{7,5},{8,10},{9,11},{10,... | collective-permute-start | bytes 589832 | tf_op jit(solution)/shard_map/ppermute | solution.py:298
  65.8 2.1 %shard_map.90 = (s32[65]{0:T(128)S(1)}, f32[16,12,128]{2,1,0:T(8,128)S(1)}, f32[16,12,128]{2,1,0:T(8,128)S(1)}, f32[16,12,128]{2,1,0:T(8,128)S(1)}, f32[16,12,128]{2,1,0:T(8,128)S(1)}) custom-call(s32[1]{0:T(128)} %bitcast.me, s32[4,64]{1,0:T(4,128)S(1)} %pad_add_fusion.1.metas.refs_0_, s32[4,64]{1,0:T(4,128)S(1)} %collective-permute-done.11.peers_below.refs_2_, ...), custom_call_target="tpu_custom_call" | custom-call | bytes 393476 | tf_op jit(solution)/shard_map/pallas_call | solution.py:101
  68.0 3.5 %collective-permute-done.22 = f32[3,128,128]{2,1,0:T(8,128)S(1)} collective-permute-done((f32[3,128,128]{2,1,0:T(8,128)S(1)}, f32[3,128,128]{2,1,0:T(8,128)S(1)}, u32[]{:S(2)}, u32[]{:S(2)}) %collective-permute-start.22) | collective-permute-done | bytes 196640 | tf_op jit(solution)/shard_map/ppermute | solution.py:298
  71.9 2.9 %collective-permute-done.21 = f32[3,128,128]{2,1,0:T(8,128)S(1)} collective-permute-done((f32[3,128,128]{2,1,0:T(8,128)S(1)}, f32[3,128,128]{2,1,0:T(8,128)S(1)}, u32[]{:S(2)}, u32[]{:S(2)}) %collective-permute-start.21) | collective-permute-done | bytes 196640 | tf_op jit(solution)/shard_map/ppermute | solution.py:298
  75.3 1.6 %collective-permute-start.25 = (f32[12,128,128]{2,1,0:T(8,128)S(1)}, f32[12,128,128]{2,1,0:T(8,128)S(1)}, u32[]{:S(2)}, u32[]{:S(2)}) collective-permute-start(f32[12,128,128]{2,1,0:T(8,128)S(1)} %get-tuple-element.50.upper.refs_0_), channel_id=1, source_target_pairs={{0,2},{1,3},{2,0},{3,1},{4,6},{5,7},{6,4},{7,5},{8,10},{9,11},{10,... | collective-permute-start | bytes 2359304 | tf_op jit(solution)/shard_map/ppermute | solution.py:298
  77.4 2.2 %collective-permute-start.26 = (f32[12,16,128]{2,1,0:T(8,128)S(1)}, f32[12,16,128]{2,1,0:T(8,128)S(1)}, u32[]{:S(2)}, u32[]{:S(2)}) collective-permute-start(f32[12,16,128]{2,1,0:T(8,128)S(1)} %shard_map.97.x), channel_id=1, source_target_pairs={{0,8},{1,5},{2,10},{3,7},{4,12},{5,9},{6,14},{7,11},{8,16},{9,13},... | collective-permute-start | bytes 294920 | tf_op jit(solution)/shard_map/ppermute | solution.py:307
  79.6 1.2 shard_map.98
  81.6 3.2 %collective-permute-done.26.arrived = f32[12,16,128]{2,1,0:T(8,128)S(1)} collective-permute-done((f32[12,16,128]{2,1,0:T(8,128)S(1)}, f32[12,16,128]{2,1,0:T(8,128)S(1)}, u32[]{:S(2)}, u32[]{:S(2)}) %collective-permute-start.26) | collective-permute-done | bytes 98336 | tf_op jit(solution)/shard_map/ppermute | solution.py:307
  85.4 1.3 collective-permute-done.27
  86.7 2.2 %collective-permute-start.28 = (f32[12,16,128]{2,1,0:T(8,128)S(1)}, f32[12,16,128]{2,1,0:T(8,128)S(1)}, u32[]{:S(2)}, u32[]{:S(2)}) collective-permute-start(f32[12,16,128]{2,1,0:T(8,128)S(1)} %add_subtract_fusion.5.x), channel_id=1, source_target_pairs={{0,8},{1,5},{2,10},{3,7},{4,12},{5,9},{6,14},{7,11},{8,16},{9,13},... | collective-permute-start | bytes 294920 | tf_op jit(solution)/shard_map/ppermute | solution.py:307
  89.8 4.4 %collective-permute-done.28.arrived = f32[12,16,128]{2,1,0:T(8,128)S(1)} collective-permute-done((f32[12,16,128]{2,1,0:T(8,128)S(1)}, f32[12,16,128]{2,1,0:T(8,128)S(1)}, u32[]{:S(2)}, u32[]{:S(2)}) %collective-permute-start.28) | collective-permute-done | bytes 98336 | tf_op jit(solution)/shard_map/ppermute | solution.py:307
  96.0 2.2 %collective-permute-start.30 = (f32[12,16,128]{2,1,0:T(8,128)S(1)}, f32[12,16,128]{2,1,0:T(8,128)S(1)}, u32[]{:S(2)}, u32[]{:S(2)}) collective-permute-start(f32[12,16,128]{2,1,0:T(8,128)S(1)} %add_subtract_fusion.4.x), channel_id=1, source_target_pairs={{0,8},{1,5},{2,10},{3,7},{4,12},{5,9},{6,14},{7,11},{8,16},{9,13},... | collective-permute-start | bytes 294920 | tf_op jit(solution)/shard_map/ppermute | solution.py:307
  99.0 4.2 %collective-permute-done.30.refs_5_ = f32[12,16,128]{2,1,0:T(8,128)S(1)} collective-permute-done((f32[12,16,128]{2,1,0:T(8,128)S(1)}, f32[12,16,128]{2,1,0:T(8,128)S(1)}, u32[]{:S(2)}, u32[]{:S(2)}) %collective-permute-start.30) | collective-permute-done | bytes 98336 | tf_op jit(solution)/shard_map/ppermute | solution.py:307
  103.9 1.3 collective-permute-done.31
  105.2 2.7 %collective-permute-start.33 = (f32[12,16,128]{2,1,0:T(8,128)S(1)}, f32[12,16,128]{2,1,0:T(8,128)S(1)}, u32[]{:S(2)}, u32[]{:S(2)}) collective-permute-start(f32[12,16,128]{2,1,0:T(8,128)S(1)} %add_subtract_fusion.3.x), channel_id=1, source_target_pairs={{4,0},{6,2},{8,4},{9,1},{10,6},{11,3},{12,8},{13,5},{14,10},{15,7}... | collective-permute-start | bytes 294920 | tf_op jit(solution)/shard_map/ppermute | solution.py:307
  107.9 1.2 shard_map.105
  109.9 2.6 %collective-permute-done.33.arrived = f32[12,16,128]{2,1,0:T(8,128)S(1)} collective-permute-done((f32[12,16,128]{2,1,0:T(8,128)S(1)}, f32[12,16,128]{2,1,0:T(8,128)S(1)}, u32[]{:S(2)}, u32[]{:S(2)}) %collective-permute-start.33) | collective-permute-done | bytes 98336 | tf_op jit(solution)/shard_map/ppermute | solution.py:307
  113.1 1.3 collective-permute-done.34
  114.5 1.9 %collective-permute-start.35 = (f32[12,16,128]{2,1,0:T(8,128)S(1)}, f32[12,16,128]{2,1,0:T(8,128)S(1)}, u32[]{:S(2)}, u32[]{:S(2)}) collective-permute-start(f32[12,16,128]{2,1,0:T(8,128)S(1)} %add_subtract_fusion.2.x), channel_id=1, source_target_pairs={{4,0},{6,2},{8,4},{9,1},{10,6},{11,3},{12,8},{13,5},{14,10},{15,7}... | collective-permute-start | bytes 294920 | tf_op jit(solution)/shard_map/ppermute | solution.py:307
  117.2 4.7 %collective-permute-done.35.arrived = f32[12,16,128]{2,1,0:T(8,128)S(1)} collective-permute-done((f32[12,16,128]{2,1,0:T(8,128)S(1)}, f32[12,16,128]{2,1,0:T(8,128)S(1)}, u32[]{:S(2)}, u32[]{:S(2)}) %collective-permute-start.35) | collective-permute-done | bytes 98336 | tf_op jit(solution)/shard_map/ppermute | solution.py:307
  122.4 1.3 collective-permute-done.36
  123.7 1.9 %collective-permute-start.37 = (f32[12,16,128]{2,1,0:T(8,128)S(1)}, f32[12,16,128]{2,1,0:T(8,128)S(1)}, u32[]{:S(2)}, u32[]{:S(2)}) collective-permute-start(f32[12,16,128]{2,1,0:T(8,128)S(1)} %add_subtract_fusion.1.x), channel_id=1, source_target_pairs={{4,0},{6,2},{8,4},{9,1},{10,6},{11,3},{12,8},{13,5},{14,10},{15,7}... | collective-permute-start | bytes 294920 | tf_op jit(solution)/shard_map/ppermute | solution.py:307
  126.5 4.7 %collective-permute-done.37.arrived = f32[12,16,128]{2,1,0:T(8,128)S(1)} collective-permute-done((f32[12,16,128]{2,1,0:T(8,128)S(1)}, f32[12,16,128]{2,1,0:T(8,128)S(1)}, u32[]{:S(2)}, u32[]{:S(2)}) %collective-permute-start.37) | collective-permute-done | bytes 98336 | tf_op jit(solution)/shard_map/ppermute | solution.py:307
  131.7 1.3 collective-permute-done.38
  133.0 1.6 %collective-permute-start.39 = (f32[12,16,128]{2,1,0:T(8,128)S(1)}, f32[12,16,128]{2,1,0:T(8,128)S(1)}, u32[]{:S(2)}, u32[]{:S(2)}) collective-permute-start(f32[12,16,128]{2,1,0:T(8,128)S(1)} %add_subtract_fusion), channel_id=1, source_target_pairs={{0,2},{1,3},{2,0},{3,1},{4,6},{5,7},{6,4},{7,5},{8,10},{9,11},{10,... | collective-permute-start | bytes 294920 | tf_op jit(solution)/shard_map/ppermute | solution.py:298
  135.3 2.6 %collective-permute-done.39 = f32[12,16,128]{2,1,0:T(8,128)S(1)} collective-permute-done((f32[12,16,128]{2,1,0:T(8,128)S(1)}, f32[12,16,128]{2,1,0:T(8,128)S(1)}, u32[]{:S(2)}, u32[]{:S(2)}) %collective-permute-start.39) | collective-permute-done | bytes 98336 | tf_op jit(solution)/shard_map/ppermute | solution.py:298
  (98 shorter events, 24.8 us)
Async XLA Ops:
  0.6 9.1 %copy-start = (f32[12,2,128,128]{3,2,1,0:T(8,128)S(1)}, f32[12,2,128,128]{3,2,1,0:T(8,128)}, u32[]{:S(2)}) copy-start(f32[12,2,128,128]{3,2,1,0:T(8,128)} %param.10) | copy-start | bytes 4718596
  0.6 9.1 %collective-permute-start.5 = (f32[24,128,128]{2,1,0:T(8,128)}, f32[24,128,128]{2,1,0:T(8,128)S(1)}, u32[]{:S(2)}, u32[]{:S(2)}) collective-permute-start(f32[24,128,128]{2,1,0:T(8,128)} %bitcast.5), channel_id=1, source_target_pairs={{0,1},{1,0},{2,3},{3,2},{4,5},{5,4},{6,7},{7,6},{8,9},{9,8},{10,11... | collective-permute-start | bytes 4718600 | tf_op jit(solution)/shard_map/ppermute | solution.py:298
  0.7 7.5 %collective-permute-start = (f32[3,128,128]{2,1,0:T(8,128)}, f32[3,128,128]{2,1,0:T(8,128)S(1)}, u32[]{:S(2)}, u32[]{:S(2)}) collective-permute-start(f32[3,128,128]{2,1,0:T(8,128)} %refs_1_), channel_id=1, source_target_pairs={{0,2},{1,3},{2,0},{3,1},{4,6},{5,7},{6,4},{7,5},{8,10},{9,11},{10,... | collective-permute-start | bytes 589832 | tf_op jit(solution)/shard_map/ppermute | solution.py:298
  2.3 5.9 %collective-permute-start.2 = (f32[3,128,128]{2,1,0:T(8,128)}, f32[3,128,128]{2,1,0:T(8,128)S(1)}, u32[]{:S(2)}, u32[]{:S(2)}) collective-permute-start(f32[3,128,128]{2,1,0:T(8,128)} %refs_1_), channel_id=1, source_target_pairs={{0,1},{1,0},{2,3},{3,2},{4,5},{5,4},{6,7},{7,6},{8,9},{9,8},{10,11... | collective-permute-start | bytes 589832 | tf_op jit(solution)/shard_map/ppermute | solution.py:298
  6.2 1.2 collective-permute-start.1
  8.3 1.4 %collective-permute-start.4 = (f32[3,128,128]{2,1,0:T(8,128)S(1)}, f32[3,128,128]{2,1,0:T(8,128)S(1)}, u32[]{:S(2)}, u32[]{:S(2)}) collective-permute-start(f32[3,128,128]{2,1,0:T(8,128)S(1)} %collective-permute-done.inverse), channel_id=1, source_target_pairs={{0,1},{1,0},{2,3},{3,2},{4,5},{5,4},{6,7},{7,6},{8,9},{9,8},{10,11... | collective-permute-start | bytes 589832 | tf_op jit(solution)/shard_map/ppermute | solution.py:298
  9.7 6.0 %copy-start.1 = (f32[3,128,128]{2,1,0:T(8,128)S(1)}, f32[3,128,128]{2,1,0:T(8,128)}, u32[]{:S(2)}) copy-start(f32[3,128,128]{2,1,0:T(8,128)} %diag.3) | copy-start | bytes 589828
  10.7 15.0 %collective-permute-start.7 = (f32[8,128,128]{2,1,0:T(8,128)S(1)}, f32[8,128,128]{2,1,0:T(8,128)S(1)}, u32[]{:S(2)}, u32[]{:S(2)}) collective-permute-start(f32[8,128,128]{2,1,0:T(8,128)S(1)} %get-tuple-element.41), channel_id=1, source_target_pairs={{0,4},{1,9},{2,6},{3,11},{4,8},{5,13},{6,10},{7,15},{8,12},{9,17},... | collective-permute-start | bytes 1572872 | tf_op jit(solution)/shard_map/ppermute | solution.py:307
  14.2 13.8 %collective-permute-start.6 = (f32[8,128,128]{2,1,0:T(8,128)S(1)}, f32[8,128,128]{2,1,0:T(8,128)S(1)}, u32[]{:S(2)}, u32[]{:S(2)}) collective-permute-start(f32[8,128,128]{2,1,0:T(8,128)S(1)} %get-tuple-element.38.refs_3_.refs_6_.refs_0_), channel_id=1, source_target_pairs={{0,2},{1,3},{2,0},{3,1},{4,6},{5,7},{6,4},{7,5},{8,10},{9,11},{10,... | collective-permute-start | bytes 1572872 | tf_op jit(solution)/shard_map/ppermute | solution.py:298
  29.0 12.9 %copy-start.2 = (f32[3,128,128]{2,1,0:T(8,128)S(1)}, f32[3,128,128]{2,1,0:T(8,128)}, u32[]{:S(2)}) copy-start(f32[3,128,128]{2,1,0:T(8,128)} %refs_1_) | copy-start | bytes 589828
  29.0 1.5 %collective-permute-start.9 = (f32[3,128,128]{2,1,0:T(8,128)S(1)}, f32[3,128,128]{2,1,0:T(8,128)S(1)}, u32[]{:S(2)}, u32[]{:S(2)}) collective-permute-start(f32[3,128,128]{2,1,0:T(8,128)S(1)} %get-tuple-element.45), channel_id=1, source_target_pairs={{0,1},{1,0},{2,3},{3,2},{4,5},{5,4},{6,7},{7,6},{8,9},{9,8},{10,11... | collective-permute-start | bytes 589832 | tf_op jit(solution)/shard_map/ppermute | solution.py:298
  29.1 3.0 %collective-permute-start.8 = (f32[3,128,128]{2,1,0:T(8,128)S(1)}, f32[3,128,128]{2,1,0:T(8,128)S(1)}, u32[]{:S(2)}, u32[]{:S(2)}) collective-permute-start(f32[3,128,128]{2,1,0:T(8,128)S(1)} %get-tuple-element.43), channel_id=1, source_target_pairs={{0,1},{1,0},{2,3},{3,2},{4,5},{5,4},{6,7},{7,6},{8,9},{9,8},{10,11... | collective-permute-start | bytes 589832 | tf_op jit(solution)/shard_map/ppermute | solution.py:298
  30.5 7.8 %collective-permute-start.10 = (f32[3,128,128]{2,1,0:T(8,128)S(1)}, f32[3,128,128]{2,1,0:T(8,128)S(1)}, u32[]{:S(2)}, u32[]{:S(2)}) collective-permute-start(f32[3,128,128]{2,1,0:T(8,128)S(1)} %add.43), channel_id=1, source_target_pairs={{0,2},{1,3},{2,0},{3,1},{4,6},{5,7},{6,4},{7,5},{8,10},{9,11},{10,... | collective-permute-start | bytes 589832 | tf_op jit(solution)/shard_map/ppermute | solution.py:298
  32.2 9.7 %collective-permute-start.13 = (f32[3,128,128]{2,1,0:T(8,128)S(1)}, f32[3,128,128]{2,1,0:T(8,128)S(1)}, u32[]{:S(2)}, u32[]{:S(2)}) collective-permute-start(f32[3,128,128]{2,1,0:T(8,128)S(1)} %add.42), channel_id=1, source_target_pairs={{0,2},{1,3},{2,0},{3,1},{4,6},{5,7},{6,4},{7,5},{8,10},{9,11},{10,... | collective-permute-start | bytes 589832 | tf_op jit(solution)/shard_map/ppermute | solution.py:298
  32.7 9.1 %collective-permute-start.3 = (s32[2,64]{1,0:T(2,128)S(1)}, s32[2,64]{1,0:T(2,128)S(1)}, u32[]{:S(2)}, u32[]{:S(2)}) collective-permute-start(s32[2,64]{1,0:T(2,128)S(1)} %pad_add_fusion.2), channel_id=1, source_target_pairs={{0,2},{1,3},{2,0},{3,1},{4,6},{5,7},{6,4},{7,5},{8,10},{9,11},{10,... | collective-permute-start | bytes 1544 | tf_op jit(solution)/shard_map/ppermute | solution.py:298
  42.3 1.5 %collective-permute-start.16 = (f32[3,128,128]{2,1,0:T(8,128)S(1)}, f32[3,128,128]{2,1,0:T(8,128)S(1)}, u32[]{:S(2)}, u32[]{:S(2)}) collective-permute-start(f32[3,128,128]{2,1,0:T(8,128)S(1)} %shard_map.91.refs_1_), channel_id=1, source_target_pairs={{0,1},{1,0},{2,3},{3,2},{4,5},{5,4},{6,7},{7,6},{8,9},{9,8},{10,11... | collective-permute-start | bytes 589832 | tf_op jit(solution)/shard_map/ppermute | solution.py:298
  42.3 1.7 %collective-permute-start.17 = (f32[3,128,128]{2,1,0:T(8,128)S(1)}, f32[3,128,128]{2,1,0:T(8,128)S(1)}, u32[]{:S(2)}, u32[]{:S(2)}) collective-permute-start(f32[3,128,128]{2,1,0:T(8,128)S(1)} %shard_map.89.inverse), channel_id=1, source_target_pairs={{0,1},{1,0},{2,3},{3,2},{4,5},{5,4},{6,7},{7,6},{8,9},{9,8},{10,11... | collective-permute-start | bytes 589832 | tf_op jit(solution)/shard_map/ppermute | solution.py:298
  42.8 18.2 %collective-permute-start.15 = (f32[8,128,128]{2,1,0:T(8,128)S(1)}, f32[8,128,128]{2,1,0:T(8,128)S(1)}, u32[]{:S(2)}, u32[]{:S(2)}) collective-permute-start(f32[8,128,128]{2,1,0:T(8,128)S(1)} %collective-permute-done.6.refs_0_.refs_3_), channel_id=1, source_target_pairs={{0,1},{1,0},{2,3},{3,2},{4,5},{5,4},{6,7},{7,6},{8,9},{9,8},{10,11... | collective-permute-start | bytes 1572872 | tf_op jit(solution)/shard_map/ppermute | solution.py:298
  45.0 16.0 %collective-permute-start.18 = (f32[8,128,128]{2,1,0:T(8,128)S(1)}, f32[8,128,128]{2,1,0:T(8,128)S(1)}, u32[]{:S(2)}, u32[]{:S(2)}) collective-permute-start(f32[8,128,128]{2,1,0:T(8,128)S(1)} %shard_map.93), channel_id=1, source_target_pairs={{0,4},{1,9},{2,6},{3,11},{4,8},{5,13},{6,10},{7,15},{8,12},{9,17},... | collective-permute-start | bytes 1572872 | tf_op jit(solution)/shard_map/ppermute | solution.py:307
  48.0 8.0 %collective-permute-start.14 = (f32[4,128,128]{2,1,0:T(8,128)S(1)}, f32[4,128,128]{2,1,0:T(8,128)S(1)}, u32[]{:S(2)}, u32[]{:S(2)}) collective-permute-start(f32[4,128,128]{2,1,0:T(8,128)S(1)} %get-tuple-element.49.refs_1_), channel_id=1, source_target_pairs={{0,2},{1,3},{2,0},{3,1},{4,6},{5,7},{6,4},{7,5},{8,10},{9,11},{10,... | collective-permute-start | bytes 786440 | tf_op jit(solution)/shard_map/ppermute | solution.py:298
  49.6 6.5 %collective-permute-start.12 = (s32[4,64]{1,0:T(4,128)S(1)}, s32[4,64]{1,0:T(4,128)S(1)}, u32[]{:S(2)}, u32[]{:S(2)}) collective-permute-start(s32[4,64]{1,0:T(4,128)S(1)} %pad_add_fusion.1.metas.refs_0_), channel_id=1, source_target_pairs={{4,0},{6,2},{8,4},{9,1},{10,6},{11,3},{12,8},{13,5},{14,10},{15,7}... | collective-permute-start | bytes 3080 | tf_op jit(solution)/shard_map/ppermute | solution.py:307
  52.4 8.6 %collective-permute-start.11 = (s32[4,64]{1,0:T(4,128)S(1)}, s32[4,64]{1,0:T(4,128)S(1)}, u32[]{:S(2)}, u32[]{:S(2)}) collective-permute-start(s32[4,64]{1,0:T(4,128)S(1)} %pad_add_fusion.1.metas.refs_0_), channel_id=1, source_target_pairs={{0,8},{1,5},{2,10},{3,7},{4,12},{5,9},{6,14},{7,11},{8,16},{9,13},... | collective-permute-start | bytes 3080 | tf_op jit(solution)/shard_map/ppermute | solution.py:307
  62.1 1.5 %collective-permute-start.19 = (f32[3,128,128]{2,1,0:T(8,128)S(1)}, f32[3,128,128]{2,1,0:T(8,128)S(1)}, u32[]{:S(2)}, u32[]{:S(2)}) collective-permute-start(f32[3,128,128]{2,1,0:T(8,128)S(1)} %get-tuple-element.53), channel_id=1, source_target_pairs={{0,1},{1,0},{2,3},{3,2},{4,5},{5,4},{6,7},{7,6},{8,9},{9,8},{10,11... | collective-permute-start | bytes 589832 | tf_op jit(solution)/shard_map/ppermute | solution.py:298
  62.2 3.0 %collective-permute-start.20 = (f32[3,128,128]{2,1,0:T(8,128)S(1)}, f32[3,128,128]{2,1,0:T(8,128)S(1)}, u32[]{:S(2)}, u32[]{:S(2)}) collective-permute-start(f32[3,128,128]{2,1,0:T(8,128)S(1)} %get-tuple-element.55), channel_id=1, source_target_pairs={{0,1},{1,0},{2,3},{3,2},{4,5},{5,4},{6,7},{7,6},{8,9},{9,8},{10,11... | collective-permute-start | bytes 589832 | tf_op jit(solution)/shard_map/ppermute | solution.py:298
  63.6 7.8 %collective-permute-start.22 = (f32[3,128,128]{2,1,0:T(8,128)S(1)}, f32[3,128,128]{2,1,0:T(8,128)S(1)}, u32[]{:S(2)}, u32[]{:S(2)}) collective-permute-start(f32[3,128,128]{2,1,0:T(8,128)S(1)} %add.46), channel_id=1, source_target_pairs={{0,2},{1,3},{2,0},{3,1},{4,6},{5,7},{6,4},{7,5},{8,10},{9,11},{10,... | collective-permute-start | bytes 589832 | tf_op jit(solution)/shard_map/ppermute | solution.py:298
  65.2 9.6 %collective-permute-start.21 = (f32[3,128,128]{2,1,0:T(8,128)S(1)}, f32[3,128,128]{2,1,0:T(8,128)S(1)}, u32[]{:S(2)}, u32[]{:S(2)}) collective-permute-start(f32[3,128,128]{2,1,0:T(8,128)S(1)} %add.47), channel_id=1, source_target_pairs={{0,2},{1,3},{2,0},{3,1},{4,6},{5,7},{6,4},{7,5},{8,10},{9,11},{10,... | collective-permute-start | bytes 589832 | tf_op jit(solution)/shard_map/ppermute | solution.py:298
  71.5 5.5 %copy-start.3 = (f32[12,32,128]{2,1,0:T(8,128)S(1)}, f32[12,32,128]{2,1,0:T(8,128)}, u32[]{:S(2)}) copy-start(f32[12,32,128]{2,1,0:T(8,128)} %base.1) | copy-start | bytes 589828
  71.9 5.1 %collective-permute-start.24 = (f32[3,128,128]{2,1,0:T(8,128)S(1)}, f32[3,128,128]{2,1,0:T(8,128)S(1)}, u32[]{:S(2)}, u32[]{:S(2)}) collective-permute-start(f32[3,128,128]{2,1,0:T(8,128)S(1)} %shard_map.96), channel_id=1, source_target_pairs={{0,1},{1,0},{2,3},{3,2},{4,5},{5,4},{6,7},{7,6},{8,9},{9,8},{10,11... | collective-permute-start | bytes 589832 | tf_op jit(solution)/shard_map/ppermute | solution.py:298
  75.3 1.7 %collective-permute-start.23 = (f32[3,128,128]{2,1,0:T(8,128)S(1)}, f32[3,128,128]{2,1,0:T(8,128)S(1)}, u32[]{:S(2)}, u32[]{:S(2)}) collective-permute-start(f32[3,128,128]{2,1,0:T(8,128)S(1)} %shard_map.95), channel_id=1, source_target_pairs={{0,1},{1,0},{2,3},{3,2},{4,5},{5,4},{6,7},{7,6},{8,9},{9,8},{10,11... | collective-permute-start | bytes 589832 | tf_op jit(solution)/shard_map/ppermute | solution.py:298
  75.3 20.0 %collective-permute-start.25 = (f32[12,128,128]{2,1,0:T(8,128)S(1)}, f32[12,128,128]{2,1,0:T(8,128)S(1)}, u32[]{:S(2)}, u32[]{:S(2)}) collective-permute-start(f32[12,128,128]{2,1,0:T(8,128)S(1)} %get-tuple-element.50.upper.refs_0_), channel_id=1, source_target_pairs={{0,2},{1,3},{2,0},{3,1},{4,6},{5,7},{6,4},{7,5},{8,10},{9,11},{10,... | collective-permute-start | bytes 2359304 | tf_op jit(solution)/shard_map/ppermute | solution.py:298
  77.4 7.5 %collective-permute-start.26 = (f32[12,16,128]{2,1,0:T(8,128)S(1)}, f32[12,16,128]{2,1,0:T(8,128)S(1)}, u32[]{:S(2)}, u32[]{:S(2)}) collective-permute-start(f32[12,16,128]{2,1,0:T(8,128)S(1)} %shard_map.97.x), channel_id=1, source_target_pairs={{0,8},{1,5},{2,10},{3,7},{4,12},{5,9},{6,14},{7,11},{8,16},{9,13},... | collective-permute-start | bytes 294920 | tf_op jit(solution)/shard_map/ppermute | solution.py:307
  85.4 1.4 collective-permute-start.27
  86.7 7.4 %collective-permute-start.28 = (f32[12,16,128]{2,1,0:T(8,128)S(1)}, f32[12,16,128]{2,1,0:T(8,128)S(1)}, u32[]{:S(2)}, u32[]{:S(2)}) collective-permute-start(f32[12,16,128]{2,1,0:T(8,128)S(1)} %add_subtract_fusion.5.x), channel_id=1, source_target_pairs={{0,8},{1,5},{2,10},{3,7},{4,12},{5,9},{6,14},{7,11},{8,16},{9,13},... | collective-permute-start | bytes 294920 | tf_op jit(solution)/shard_map/ppermute | solution.py:307
  94.6 1.4 collective-permute-start.29
  95.3 12.6 %collective-permute-start.32 = (f32[12,128,128]{2,1,0:T(8,128)S(1)}, f32[12,128,128]{2,1,0:T(8,128)S(1)}, u32[]{:S(2)}, u32[]{:S(2)}) collective-permute-start(f32[12,128,128]{2,1,0:T(8,128)S(1)} %collective-permute-done.25.refs_0_.refs_2_), channel_id=1, source_target_pairs={{0,1},{1,0},{2,3},{3,2},{4,5},{5,4},{6,7},{7,6},{8,9},{9,8},{10,11... | collective-permute-start | bytes 2359304 | tf_op jit(solution)/shard_map/ppermute | solution.py:298
  96.0 7.3 %collective-permute-start.30 = (f32[12,16,128]{2,1,0:T(8,128)S(1)}, f32[12,16,128]{2,1,0:T(8,128)S(1)}, u32[]{:S(2)}, u32[]{:S(2)}) collective-permute-start(f32[12,16,128]{2,1,0:T(8,128)S(1)} %add_subtract_fusion.4.x), channel_id=1, source_target_pairs={{0,8},{1,5},{2,10},{3,7},{4,12},{5,9},{6,14},{7,11},{8,16},{9,13},... | collective-permute-start | bytes 294920 | tf_op jit(solution)/shard_map/ppermute | solution.py:307
  103.8 1.4 collective-permute-start.31
  105.2 7.4 %collective-permute-start.33 = (f32[12,16,128]{2,1,0:T(8,128)S(1)}, f32[12,16,128]{2,1,0:T(8,128)S(1)}, u32[]{:S(2)}, u32[]{:S(2)}) collective-permute-start(f32[12,16,128]{2,1,0:T(8,128)S(1)} %add_subtract_fusion.3.x), channel_id=1, source_target_pairs={{4,0},{6,2},{8,4},{9,1},{10,6},{11,3},{12,8},{13,5},{14,10},{15,7}... | collective-permute-start | bytes 294920 | tf_op jit(solution)/shard_map/ppermute | solution.py:307
  113.1 1.4 collective-permute-start.34
  114.5 7.4 %collective-permute-start.35 = (f32[12,16,128]{2,1,0:T(8,128)S(1)}, f32[12,16,128]{2,1,0:T(8,128)S(1)}, u32[]{:S(2)}, u32[]{:S(2)}) collective-permute-start(f32[12,16,128]{2,1,0:T(8,128)S(1)} %add_subtract_fusion.2.x), channel_id=1, source_target_pairs={{4,0},{6,2},{8,4},{9,1},{10,6},{11,3},{12,8},{13,5},{14,10},{15,7}... | collective-permute-start | bytes 294920 | tf_op jit(solution)/shard_map/ppermute | solution.py:307
  122.4 1.4 collective-permute-start.36
  123.7 7.4 %collective-permute-start.37 = (f32[12,16,128]{2,1,0:T(8,128)S(1)}, f32[12,16,128]{2,1,0:T(8,128)S(1)}, u32[]{:S(2)}, u32[]{:S(2)}) collective-permute-start(f32[12,16,128]{2,1,0:T(8,128)S(1)} %add_subtract_fusion.1.x), channel_id=1, source_target_pairs={{4,0},{6,2},{8,4},{9,1},{10,6},{11,3},{12,8},{13,5},{14,10},{15,7}... | collective-permute-start | bytes 294920 | tf_op jit(solution)/shard_map/ppermute | solution.py:307
  131.7 1.4 collective-permute-start.38
  133.0 4.9 %collective-permute-start.39 = (f32[12,16,128]{2,1,0:T(8,128)S(1)}, f32[12,16,128]{2,1,0:T(8,128)S(1)}, u32[]{:S(2)}, u32[]{:S(2)}) collective-permute-start(f32[12,16,128]{2,1,0:T(8,128)S(1)} %add_subtract_fusion), channel_id=1, source_target_pairs={{0,2},{1,3},{2,0},{3,1},{4,6},{5,7},{6,4},{7,5},{8,10},{9,11},{10,... | collective-permute-start | bytes 294920 | tf_op jit(solution)/shard_map/ppermute | solution.py:298
